TPU v7x, 32 devices: a whole 2x2x4 slice. The times are simulated.
32 devices in a mesh: gx: 2 (over y), gy: 4 (over x, core), gz: 4 (over z).
Axes of the slice: x: 2, y: 2, z: 4, core: 2. Of those that a mesh axis runs over, the one named last changes fastest.
Arguments:
- rhs: float32 [4, 32, 64, 1024], P(None, 'gz', 'gx', 'gy'), may hold values from -6 to 6
- coef_x: float32 [32, 64, 1024], P('gz', 'gx', 'gy'), may hold values from 0.3 to 3
- coef_y: float32 [32, 64, 1024], P('gz', 'gx', 'gy'), may hold values from 0.3 to 3
- coef_z: float32 [32, 64, 1024], P('gz', 'gx', 'gy'), may hold values from 0.3 to 3
- diag_term: float32 [32, 64, 1024], P('gz', 'gx', 'gy'), may hold values from 0.2 to 2
Outputs:
- ortho_basis: float32 [20, 32, 64, 1024], P(None, 'gz', 'gx', 'gy')
- triangle: float32 [20, 20], replicated
All inputs are finite; a program needn't handle non-finite values.
Results may differ from a plain program's by a relative error of at most 0.0003.
Values sent between devices are 32-bit elements; how exact they have to be, the bound alone decides.
No kernel may reach another device: no remote copies, remote signals or barrier semaphores. Data moves between devices by JAX's collectives and lax.ppermute only.
A program may use at most 128 MiB of HBM per device.

v0:
```python
import functools

import jax
import jax.numpy as jnp
from jax import lax
from jax.experimental import pallas as pl
from jax.experimental.pallas import tpu as pltpu
from jax.sharding import PartitionSpec as P

NRHS = 4
STEPS = 4
COLS = NRHS * (STEPS + 1)
SHIFTS = (3.0, 11.0, 7.0, 1.5)
SCALE = 1.0 / 6.0
FIELDS = NRHS + 4
AXES = ("gx", "gy", "gz")
HIGHEST = lax.Precision.HIGHEST

DEPTH = 4
NZ, NX, NY = 8, 32, 256
EZ = NZ + 2 * DEPTH
ROWS = NX + 8
EROWS = ROWS + 16
LT = 3
FACE = NRHS * 4 + 3 * 4 + 1
F32 = jnp.float32


def params(mb):
    return pltpu.CompilerParams(vmem_limit_bytes=mb << 20)


def vmem():
    return pl.BlockSpec(memory_space=pltpu.VMEM)


def smem():
    return pl.BlockSpec(memory_space=pltpu.SMEM)


def hbm():
    return pl.BlockSpec(memory_space=pl.ANY)


def row_ids(shape):
    return lax.broadcasted_iota(jnp.int32, shape, 0)


def lane_ids(shape):
    return lax.broadcasted_iota(jnp.int32, shape, 1)


def field_of(rhs, cz, cx, cy, dg, f, z):
    return rhs.at[f, z] if f < NRHS else (cz, cx, cy, dg)[f - NRHS].at[z]


def pack_faces(swap, place, rhs, cz, cx, cy, dg, zlo, zhi, *xmsgs):
    n = 0
    for f in range(FIELDS):
        depth = DEPTH if f <= NRHS else DEPTH - 1
        for d in range(depth):
            zlo[n] = field_of(rhs, cz, cx, cy, dg, f, d)[...]
            zhi[n] = field_of(rhs, cz, cx, cy, dg, f, NZ - depth + d)[...]
            n += 1
    low = row_ids((8, NY)) < 4
    up = place[0] == 0
    for f in range(FIELDS):
        for m in range(NZ // 2):
            a = field_of(rhs, cz, cx, cy, dg, f, 2 * m)
            b = field_of(rhs, cz, cx, cy, dg, f, 2 * m + 1)
            first = jnp.where(low, a[0:8], pltpu.roll(b[0:8], 4, 0))
            last = jnp.where(low, pltpu.roll(a[NX - 8 : NX], 4, 0), b[NX - 8 : NX])
            if swap:
                xmsgs[0][f, m] = jnp.where(up, last, first)
            else:
                xmsgs[0][f, m] = first
                xmsgs[1][f, m] = last


def halo_tile(above, below, odd, keep_up, keep_dn):
    low = row_ids(above.shape) < 4
    if odd:
        up, dn = pltpu.roll(above, 4, 0), below
    else:
        up, dn = above, pltpu.roll(below, 4, 0)
    return jnp.where(low, up * keep_up, dn * keep_dn)


def pack_rims(keep, rhs, cz, cx, cy, dg, above, below, ylo, yhi):
    lane = lane_ids((8, 128))
    keep_up, keep_dn = keep[0], keep[1]
    for t in range(ROWS // 8):
        for side, out in ((0, ylo), (1, yhi)):
            lanes = pl.ds(128 * side, 128)
            source = 124 * side
            for half in range(2):
                acc = jnp.zeros((8, 128), F32)
                for zz in range(4):
                    z = 4 * half + zz
                    for f in range(FIELDS):
                        if t < NX // 8:
                            tile = field_of(rhs, cz, cx, cy, dg, f, z)[8 * t : 8 * t + 8, lanes]
                        else:
                            tile = halo_tile(
                                above[f, z // 2, :, lanes], below[f, z // 2, :, lanes], z % 2, keep_up, keep_dn
                            )
                        spot = (zz * FIELDS + f) * 4
                        shift = (spot - source) % 128
                        if shift:
                            tile = pltpu.roll(tile, shift, 1)
                        acc = jnp.where((lane >= spot) & (lane < spot + 4), tile, acc)
                out[8 * t : 8 * t + 8, 128 * half : 128 * half + 128] = acc


def gram_message(read, count, parts, out, unroll=4):
    group = 5
    parts[...] = jnp.zeros_like(parts)
    for gi in range(COLS // group):
        for gj in range(gi, COLS // group):
            pairs = [
                (i, j)
                for i in range(group * gi, group * gi + group)
                for j in range(group * gj, group * gj + group)
                if i <= j
            ]

            def step(n, sums):
                sums = list(sums)
                rows = {i: read(i, n) for i in sorted({i for pair in pairs for i in pair})}
                for k, (i, j) in enumerate(pairs):
                    sums[k] = sums[k] + rows[i] * rows[j]
                return tuple(sums)

            sums = lax.fori_loop(
                0, count, step, tuple(jnp.zeros((8, 128), F32) for _ in pairs), unroll=unroll
            )
            for (i, j), total in zip(pairs, sums):
                line = jnp.sum(total, axis=0, keepdims=True)
                parts[32 * i + j : 32 * i + j + 1, :] = line
                if i != j:
                    parts[32 * j + i : 32 * j + i + 1, :] = line
    flat = lax.dot_general(
        jnp.ones((8, 128), F32), parts[...], (((1,), (1,)), ((), ())), precision=HIGHEST, preferred_element_type=F32
    )
    out[...] = jnp.zeros_like(out)
    for r in range(COLS * 32 // 128):
        out[r : r + 1, :] = flat[0:1, 128 * r : 128 * r + 128]


def krylov(
    keep, rhs, cz, cx, cy, dg, above, below, yup, ydn, facelo, facehi, rimlo, rimhi,
    basis, message,
    store, faces, ysrc, parts, sems,
):
    lane = lane_ids((8, 128))
    keep_up, keep_dn = keep[0], keep[1]
    n_x = 1 if above is below else 2

    def put(f, z, l, t, value):
        store[f, z, l, 8 + 8 * t : 16 + 8 * t, :] = value
        if t == 0:
            store[f, z, l, 8 + ROWS : 16 + ROWS, :] = value
        if t == ROWS // 8 - 1:
            store[f, z, l, 0:8, :] = value

    x_rows = FIELDS * 2 * 8
    for f in range(FIELDS):
        depth = DEPTH if f <= NRHS else DEPTH - 1
        start = f * DEPTH if f <= NRHS else NRHS * DEPTH + DEPTH + (f - NRHS - 1) * (DEPTH - 1)
        for z in range(EZ):
            own = DEPTH <= z < DEPTH + NZ
            if own:
                plane = field_of(rhs, cz, cx, cy, dg, f, z - DEPTH)
            elif z < DEPTH:
                d = z - (DEPTH - depth)
                plane = facelo.at[start + d] if d >= 0 else None
            else:
                d = z - DEPTH - NZ
                plane = facehi.at[start + d] if d < depth else None
            for l in range(2):
                lanes = pl.ds(128 * l, 128)
                for t in range(NX // 8):
                    if plane is None:
                        put(f, z, l, t, jnp.zeros((8, 128), F32))
                    else:
                        put(f, z, l, t, plane[8 * t : 8 * t + 8, lanes])
                if own:
                    m = (z - DEPTH) // 2
                    a, b = above[f, m, :, lanes], below[f, m, :, lanes]
                else:
                    rim, m = (rimlo, z // 2) if z < DEPTH else (rimhi, (z - DEPTH - NZ) // 2)
                    at = (f * 2 + m) * 8
                    a = rim[at : at + 8, lanes]
                    at += x_rows * (n_x - 1)
                    b = rim[at : at + 8, lanes]
                put(f, z, l, NX // 8, halo_tile(a, b, z % 2, keep_up, keep_dn))

    at = x_rows * n_x
    ysrc[0, 0] = rimlo[at : at + ROWS, 0:128]
    ysrc[1, 0] = rimlo[at : at + ROWS, 128:256]
    ysrc[0, 1] = yup[:, 0:128]
    ysrc[0, 2] = yup[:, 128:256]
    ysrc[1, 1] = ydn[:, 0:128]
    ysrc[1, 2] = ydn[:, 128:256]
    ysrc[0, 3] = rimhi[at : at + ROWS, 0:128]
    ysrc[1, 3] = rimhi[at : at + ROWS, 128:256]

    def place_y(q, carry):
        for t in range(ROWS // 8):
            up = ysrc[0, q, 8 * t : 8 * t + 8, :]
            dn = ysrc[1, q, 8 * t : 8 * t + 8, :]
            for zz in range(4):
                for f in range(FIELDS):
                    spot = (zz * FIELDS + f) * 4
                    u = pltpu.roll(up, (-spot) % 128, 1) if spot else up
                    d = pltpu.roll(dn, (124 - spot) % 128, 1) if spot != 124 else dn
                    put(f, 4 * q + zz, 2, t, jnp.where(lane < 4, u, jnp.where(lane >= 124, d, 0.0)))
        return carry

    lax.fori_loop(0, EZ // 4, place_y, 0)

    def tiles(f, z, t, off):
        return [store[f, z, l, pl.ds(8 + 8 * t + off, 8), :] for l in range(LT)]

    def lane_up(tri):
        rolled = [pltpu.roll(v, 127, 1) for v in tri]
        return [jnp.where(lane == 127, rolled[(l + 1) % LT], rolled[l]) for l in range(LT)]

    def lane_dn(tri):
        rolled = [pltpu.roll(v, 1, 1) for v in tri]
        return [jnp.where(lane == 0, rolled[(l - 1) % LT], rolled[l]) for l in range(LT)]

    def coefficients(z, carry):
        for t in range(ROWS // 8):
            kz, kx, ky, kd = (NRHS + i for i in range(4))
            center_z, center_x, center_y = (tiles(k, z, t, 0) for k in (kz, kx, ky))
            diag = tiles(kd, z, t, 0)
            sides = [
                (center_z, tiles(kz, z + 1, t, 0)),
                (center_z, tiles(kz, z - 1, t, 0)),
                (center_x, tiles(kx, z, t, 1)),
                (center_x, tiles(kx, z, t, -1)),
                (center_y, lane_up(center_y)),
                (center_y, lane_dn(center_y)),
            ]
            for l in range(LT):
                inside = diag[l] > 0.0
                total = diag[l] * SCALE
                for k, (mid, side) in enumerate(sides):
                    face = (mid[l] + side[l]) * (0.5 * SCALE)
                    total = total + face
                    faces[k, z, l, 8 * t : 8 * t + 8, :] = jnp.where(inside, face, 0.0)
                faces[6, z, l, 8 * t : 8 * t + 8, :] = jnp.where(inside, total, 0.0)
        return carry

    lax.fori_loop(1, EZ - 1, coefficients, 0)

    copies = []

    def send_block(k):
        copy = pltpu.make_async_copy(
            store.at[pl.ds(k * NRHS + (NRHS if k else 0) * 1, NRHS), pl.ds(DEPTH, NZ), pl.ds(0, 2), pl.ds(8, NX), :],
            basis.at[pl.ds(k * NRHS, NRHS)],
            sems.at[k],
        )
        copy.start()
        copies.append(copy)

    def slot(k):
        return k * NRHS + (NRHS if k else 0)

    send_block(0)
    for k in range(STEPS):

        def apply(z, carry):
            for t in range(ROWS // 8):
                face = [[faces[c, z, l, 8 * t : 8 * t + 8, :] for l in range(LT)] for c in range(7)]
                diag = [face[6][l] - SHIFTS[k] * SCALE for l in range(LT)]
                for r in range(NRHS):
                    f = slot(k) + r
                    mid = tiles(f, z, t, 0)
                    sides = [
                        tiles(f, z + 1, t, 0),
                        tiles(f, z - 1, t, 0),
                        tiles(f, z, t, 1),
                        tiles(f, z, t, -1),
                        lane_up(mid),
                        lane_dn(mid),
                    ]
                    for l in range(LT):
                        value = diag[l] * mid[l]
                        for c in range(6):
                            value = value - face[c][l] * sides[c][l]
                        put(slot(k + 1) + r, z, l, t, value)
            return carry

        lax.fori_loop(k + 1, EZ - 1 - k, apply, 0)
        send_block(k + 1)

    def read(i, n):
        f = slot(i // NRHS) + i % NRHS
        return store[f, DEPTH + n // 8, (n // 4) % 2, pl.ds(pl.multiple_of(8 + 8 * (n % 4), 8), 8), :]

    gram_message(read, NZ * 8, parts, message)
    for copy in copies:
        copy.wait()


def factor_gram(message, cells, gram, work):
    rows = row_ids((24, 128))
    lanes = lane_ids((24, 128))
    gram[...] = jnp.zeros_like(gram)
    for q in range(4):
        turned = pltpu.roll(message, (-32 * q) % 128, 1) if q else message
        for r in range(COLS // 4):
            i = 4 * r + q
            gram[i : i + 1, :] = turned[r : r + 1, :]
    a = jnp.where(lanes < COLS, gram[...] / cells, 0.0)
    a = jnp.where((lanes == rows + 32) & (rows < COLS), 1.0, a)
    for j in range(COLS - 1):
        column = jnp.broadcast_to(a[:, j : j + 1], (24, 128))
        row = jnp.broadcast_to(a[j : j + 1, :], (24, 128))
        pivot = jnp.broadcast_to(column[j : j + 1, :], (24, 128))
        a = a - jnp.where(rows > j, column / pivot, 0.0) * row
    diag = jnp.sum(jnp.where(lanes == rows, a, 0.0), axis=1, keepdims=True)
    diag = jnp.where(rows < COLS, jnp.broadcast_to(diag, (24, 128)), 1.0)
    a = a / jnp.sqrt(diag)
    return jnp.where((lanes >= rows) & (lanes < COLS) | (lanes >= 32) & (lanes <= rows + 32), a, 0.0)


def spread(factor, table):
    for j in range(COLS):
        table[j] = jnp.broadcast_to(factor[:, 32 + j : 33 + j], (24, 128))


def apply_rows(table, read, write):
    group = 5
    pieces = NX // 8
    for g in range(COLS // group):
        mine = range(group * g, group * g + group)
        sums = {i: None for i in mine}
        for j in range(group * g + group):
            value = [read(j, p) for p in range(pieces)]
            for i in mine:
                if j <= i:
                    weight = jnp.broadcast_to(table[j, i : i + 1, :], (8, 128))
                    terms = [weight * v for v in value]
                    sums[i] = terms if sums[i] is None else [s + t for s, t in zip(sums[i], terms)]
        for i in mine:
            for p in range(pieces):
                write(i, p, sums[i][p])


def first_pass(cells, message, basis_hbm, first_hbm, next_message, factor_out, basis, gram, table, parts, sems):
    load = pltpu.make_async_copy(basis_hbm, basis, sems.at[0])
    load.start()
    factor = factor_gram(message[...], cells, gram, None)
    factor_out[...] = factor
    spread(factor, table)
    load.wait()

    def chunk(n, carry):
        z, l = n // 2, n % 2

        def read(j, p):
            return basis[j, z, l, 8 * p : 8 * p + 8, :]

        pending = []
        apply_rows(table, read, lambda i, p, value: pending.append((i, p, value)))
        for i, p, value in pending:
            basis[i, z, l, 8 * p : 8 * p + 8, :] = value
        return carry

    lax.fori_loop(0, NZ * 2, chunk, 0)
    save = pltpu.make_async_copy(basis, first_hbm, sems.at[1])
    save.start()

    def read(i, n):
        return basis[i, n // 8, (n // 4) % 2, pl.ds(pl.multiple_of(8 * (n % 4), 8), 8), :]

    gram_message(read, NZ * 8, parts, next_message)
    save.wait()


def second_pass(cells, message, factor_one, first_hbm, out, triangle, first, gram, table, sems):
    load = pltpu.make_async_copy(first_hbm, first, sems.at[0])
    load.start()
    factor = factor_gram(message[...], cells, gram, None)
    spread(factor, table)
    lanes = lane_ids((24, 128))
    left = jnp.where(lanes < COLS, factor, 0.0)[:, 0:24]
    product = lax.dot_general(
        left, factor_one[...], (((1,), (0,)), ((), ())), precision=HIGHEST, preferred_element_type=F32
    )
    triangle[...] = product[0:COLS, 0:COLS]
    load.wait()

    def chunk(z, carry):
        for l in range(2):

            def read(j, p):
                return first[j, z, l, 8 * p : 8 * p + 8, :]

            def write(i, p, value):
                out[i, z, 8 * p : 8 * p + 8, 128 * l : 128 * l + 128] = value

            apply_rows(table, read, write)
        return carry

    lax.fori_loop(0, NZ, chunk, 0)


def shape(*dims):
    return jax.ShapeDtypeStruct(dims, F32)


def move(value, axis, delta):
    count = lax.axis_size(axis)
    pairs = [(i, i + delta) for i in range(count) if 0 <= i + delta < count]
    return lax.ppermute(value, axis, pairs)


def body(rhs, coef_x, coef_y, coef_z, diag_term):
    n_x = lax.axis_size("gx")
    cells = float(NZ * NX * NY * n_x * lax.axis_size("gy") * lax.axis_size("gz"))
    at_x = lax.axis_index("gx")
    swap = n_x == 2
    fields = (rhs, coef_z, coef_x, coef_y, diag_term)

    x_shape = shape(FIELDS, NZ // 2, 8, NY)
    face_shape = shape(FACE, NX, NY)
    zlo, zhi, *xmsgs = pl.pallas_call(
        functools.partial(pack_faces, swap),
        out_shape=(face_shape, face_shape) + (x_shape,) * (1 if swap else 2),
        in_specs=[smem()] + [vmem()] * 5,
        compiler_params=params(32),
    )(at_x.astype(jnp.int32).reshape(1), *fields)
    facehi = move(zlo, "gz", -1)
    facelo = move(zhi, "gz", 1)
    if swap:
        above = below = lax.ppermute(xmsgs[0], "gx", [(0, 1), (1, 0)])
        x_parts = (above,)
        keep = jnp.stack([1 - at_x, at_x]).astype(F32)
    else:
        above, below = move(xmsgs[0], "gx", -1), move(xmsgs[1], "gx", 1)
        x_parts = (above, below)
        keep = jnp.ones((2,), F32)

    rim_shape = shape(ROWS, NY)
    ylo, yhi = pl.pallas_call(
        pack_rims,
        out_shape=(rim_shape, rim_shape),
        in_specs=[smem()] + [vmem()] * 7,
        compiler_params=params(32),
    )(keep, *fields, above, below)
    yup, ydn = move(ylo, "gy", -1), move(yhi, "gy", 1)

    def rim(half):
        rows = [p[:, 2 * half : 2 * half + 2].reshape(-1, NY) for p in x_parts]
        lanes = slice(128 * half, 128 * half + 128)
        return jnp.concatenate(rows + [jnp.concatenate([yup[:, lanes], ydn[:, lanes]], 1)], 0)

    rimhi, rimlo = move(rim(0), "gz", -1), move(rim(1), "gz", 1)

    block = shape(COLS, NZ, 2, NX, 128)

    def krylov_entry(keep, rhs, cz, cx, cy, dg, *rest):
        if swap:
            rest = (rest[0],) + rest
        krylov(keep, rhs, cz, cx, cy, dg, *rest)

    basis, message = pl.pallas_call(
        krylov_entry,
        out_shape=(block, shape(8, 128)),
        in_specs=[smem()] + [vmem()] * (5 + len(x_parts) + 6),
        out_specs=(hbm(), vmem()),
        scratch_shapes=[
            pltpu.VMEM((COLS + NRHS, EZ, LT, EROWS, 128), F32),
            pltpu.VMEM((7, EZ, LT, ROWS, 128), F32),
            pltpu.VMEM((2, 4, ROWS, 128), F32),
            pltpu.VMEM((32 * COLS, 128), F32),
            pltpu.SemaphoreType.DMA((STEPS + 1,)),
        ],
        compiler_params=params(56),
    )(keep, *fields, *x_parts, yup, ydn, facelo, facehi, rimlo, rimhi)

    message = lax.psum(message, AXES)
    first, message, factor_one = pl.pallas_call(
        functools.partial(first_pass, cells),
        out_shape=(block, shape(8, 128), shape(24, 128)),
        in_specs=[vmem(), hbm()],
        out_specs=(hbm(), vmem(), vmem()),
        scratch_shapes=[
            pltpu.VMEM(block.shape, F32),
            pltpu.VMEM((24, 128), F32),
            pltpu.VMEM((COLS, 24, 128), F32),
            pltpu.VMEM((32 * COLS, 128), F32),
            pltpu.SemaphoreType.DMA((2,)),
        ],
        compiler_params=params(32),
    )(message, basis)

    message = lax.psum(message, AXES)
    return pl.pallas_call(
        functools.partial(second_pass, cells),
        out_shape=(shape(COLS, NZ, NX, NY), shape(COLS, COLS)),
        in_specs=[vmem(), vmem(), hbm()],
        out_specs=(vmem(), vmem()),
        scratch_shapes=[
            pltpu.VMEM(block.shape, F32),
            pltpu.VMEM((24, 128), F32),
            pltpu.VMEM((COLS, 24, 128), F32),
            pltpu.SemaphoreType.DMA((1,)),
        ],
        compiler_params=params(32),
    )(message, factor_one, first)


def solution(mesh):
    return jax.shard_map(
        body,
        mesh=mesh,
        in_specs=(
            P(None, "gz", "gx", "gy"),
            P("gz", "gx", "gy"),
            P("gz", "gx", "gy"),
            P("gz", "gx", "gy"),
            P("gz", "gx", "gy"),
        ),
        out_specs=(P(None, "gz", "gx", "gy"), P()),
        check_vma=False,
    )
```

profile of v0, /device:TPU:0, one launch (start us, length us, event | category | flops | bytes accessed | tf_op | source)
XLA Modules:
  0.0 184.3 jit_solution(3954627041146635560)
XLA Ops:
  0.6 0.0 copy-start
  0.6 1.2 copy-done
  1.9 0.0 copy-start.6
  1.9 0.9 copy-done.6
  2.8 0.0 copy-start.8
  2.8 0.9 copy-done.8
  3.8 0.0 copy-start.10
  3.8 0.9 copy-done.10
  4.7 0.0 copy-start.12
  4.7 0.9 copy-done.12
  5.7 0.2 shard_map.68
  5.8 3.0 %collective-permute-start = (f32[8,4,8,256]{3,2,1,0:T(8,128)S(1)}, f32[8,4,8,256]{3,2,1,0:T(8,128)S(1)}, u32[]{:S(2)}, u32[]{:S(2)}) collective-permute-start(f32[8,4,8,256]{3,2,1,0:T(8,128)S(1)} %get-tuple-element.12), channel_id=1, source_target_pairs={{0,16},{16,0},{1,17},{17,1},{2,18},{18,2},{3,19},{19,3},{4,20},{20... | collective-permute-start | bytes 786440 | tf_op jit(solution)/shard_map/ppermute | solution.py:441
  8.9 3.5 %collective-permute-start.3 = (f32[29,32,256]{2,1,0:T(8,128)S(1)}, f32[29,32,256]{2,1,0:T(8,128)S(1)}, u32[]{:S(2)}, u32[]{:S(2)}) collective-permute-start(f32[29,32,256]{2,1,0:T(8,128)S(1)} %get-tuple-element.15), channel_id=1, source_target_pairs={{0,1},{1,2},{2,3},{4,5},{5,6},{6,7},{8,9},{9,10},{10,11},{12,13},{... | collective-permute-start | bytes 2850824 | tf_op jit(solution)/shard_map/ppermute | solution.py:420
  12.4 1.3 collective-permute-start.4
  13.7 0.1 add_convert_fusion.keep
  13.8 0.0 copy-start.14
  13.8 1.4 collective-permute-done.above.below.rest_0_
  15.2 0.0 copy-start.1
  15.2 1.2 copy-done.1
  16.4 0.0 copy-start.7
  16.4 0.9 copy-done.7
  17.4 0.0 copy-start.9
  17.4 0.9 copy-done.9
  18.3 0.0 copy-start.11
  18.3 0.9 copy-done.11
  19.3 0.0 copy-start.13
  19.3 0.9 copy-done.13
  20.2 0.0 copy-start.5
  20.2 1.3 shard_map.69
  21.5 1.3 collective-permute-start.1
  22.8 3.0 %collective-permute-start.2 = (f32[40,256]{1,0:T(8,128)S(1)}, f32[40,256]{1,0:T(8,128)S(1)}, u32[]{:S(2)}, u32[]{:S(2)}) collective-permute-start(f32[40,256]{1,0:T(8,128)S(1)} %get-tuple-element.14), channel_id=1, source_target_pairs={{0,4},{4,8},{8,12},{1,5},{5,9},{9,13},{2,6},{6,10},{10,14},{3,7},{... | collective-permute-start | bytes 122888 | tf_op jit(solution)/shard_map/ppermute | solution.py:420
  25.8 0.0 collective-permute-done.1.rest_1_
  25.8 0.0 copy-start.18
  25.9 0.8 collective-permute-done.2.rest_2_
  26.7 0.0 copy-start.19
  26.7 3.7 %collective-permute-start.5 = (f32[168,256]{1,0:T(8,128)S(1)}, f32[168,256]{1,0:T(8,128)S(1)}, u32[]{:S(2)}, u32[]{:S(2)}) collective-permute-start(f32[168,256]{1,0:T(8,128)S(1)} %maximum_maximum_fusion), channel_id=1, source_target_pairs={{0,1},{1,2},{2,3},{4,5},{5,6},{6,7},{8,9},{9,10},{10,11},{12,13},{... | collective-permute-start | bytes 516104 | tf_op jit(solution)/shard_map/ppermute | solution.py:420
  30.4 1.3 collective-permute-start.6
  31.7 4.3 %collective-permute-done.5.rest_5_ = f32[168,256]{1,0:T(8,128)S(1)} collective-permute-done((f32[168,256]{1,0:T(8,128)S(1)}, f32[168,256]{1,0:T(8,128)S(1)}, u32[]{:S(2)}, u32[]{:S(2)}) %collective-permute-start.5) | collective-permute-done | bytes 172064 | tf_op jit(solution)/shard_map/ppermute | solution.py:420
  36.0 0.0 copy-start.16
  36.0 4.2 %collective-permute-done.6.rest_6_ = f32[168,256]{1,0:T(8,128)S(1)} collective-permute-done((f32[168,256]{1,0:T(8,128)S(1)}, f32[168,256]{1,0:T(8,128)S(1)}, u32[]{:S(2)}, u32[]{:S(2)}) %collective-permute-start.6) | collective-permute-done | bytes 172064 | tf_op jit(solution)/shard_map/ppermute | solution.py:420
  40.2 0.0 copy-start.17
  40.2 0.0 collective-permute-done.3.rest_3_
  40.2 0.0 copy-start.15
  40.2 0.0 collective-permute-done.4.rest_4_
  40.2 0.0 copy-done.14
  40.2 0.0 copy-done.5
  40.3 0.0 copy-done.18
  40.3 0.0 copy-done.19
  40.3 0.0 copy-done.16
  40.3 0.6 copy-done.17
  40.9 0.4 copy-done.15
  41.3 29.1 %shard_map.70 = (f32[20,8,2,32,128]{4,3,2,1,0:T(8,128)}, f32[8,128]{1,0:T(8,128)}) custom-call(f32[2]{0:T(128)} %copy-done.14, f32[4,8,32,256]{3,2,1,0:T(8,128)} %rhs.5, f32[8,32,256]{2,1,0:T(8,128)} %cz.5, f32[8,32,256]{2,1,0:T(8,128)} %cx.5, f32[8,32,256]{2,1,0:T(8,128)} %cy.5, f32[8,32,256]{2,1,0:T(8,128)} %dg.5, f32[8,4,8,256]{3,2,1,0:T(8,128)} %copy-done.5, ...), custom_call_target="tpu_custom_call" | custom-call | tf_op jit(solution)/shard_map/pallas_call | solution.py:472
  70.4 40.4 %psum.14.message = f32[8,128]{1,0:T(8,128)S(1)} all-reduce(f32[8,128]{1,0:T(8,128)} %get-tuple-element.17), channel_id=1, replica_groups=mesh['gx'=2,'gy'=4,'gz'=4] {'gx','gy','gz'}, use_global_device_ids=true, to_apply=%region_0.0 | all-reduce | flops 1024 | bytes 8192 | tf_op jit(solution)/shard_map/psum | solution.py:487
  110.8 0.0 copy-start.2
  110.8 2.5 %copy-done.2 = f32[20,8,2,32,128]{4,3,2,1,0:T(8,128)S(1)} copy-done((f32[20,8,2,32,128]{4,3,2,1,0:T(8,128)S(1)}, f32[20,8,2,32,128]{4,3,2,1,0:T(8,128)}, u32[]{:S(2)}) %copy-start.2) | copy-done | bytes 5242904
  113.3 17.9 %shard_map.71 = (f32[20,8,2,32,128]{4,3,2,1,0:T(8,128)S(1)}, f32[8,128]{1,0:T(8,128)S(1)}, f32[24,128]{1,0:T(8,128)S(1)}) custom-call(f32[8,128]{1,0:T(8,128)S(1)} %psum.14.message, f32[20,8,2,32,128]{4,3,2,1,0:T(8,128)S(1)} %copy-done.2), custom_call_target="tpu_custom_call" | custom-call | tf_op jit(solution)/shard_map/pallas_call | solution.py:488
  131.2 0.0 copy-start.3
  131.2 2.3 %copy-done.3 = f32[20,8,2,32,128]{4,3,2,1,0:T(8,128)} copy-done((f32[20,8,2,32,128]{4,3,2,1,0:T(8,128)}, f32[20,8,2,32,128]{4,3,2,1,0:T(8,128)S(1)}, u32[]{:S(2)}) %copy-start.3) | copy-done | bytes 5242904
  133.5 39.1 %psum.15.message = f32[8,128]{1,0:T(8,128)S(1)} all-reduce(f32[8,128]{1,0:T(8,128)S(1)} %get-tuple-element.19), channel_id=1, replica_groups=mesh['gx'=2,'gy'=4,'gz'=4] {'gx','gy','gz'}, use_global_device_ids=true, to_apply=%region_1.0 | all-reduce | flops 1024 | bytes 8192 | tf_op jit(solution)/shard_map/psum | solution.py:503
  172.6 0.0 copy-start.4
  172.6 2.5 %copy-done.4 = f32[20,8,2,32,128]{4,3,2,1,0:T(8,128)S(1)} copy-done((f32[20,8,2,32,128]{4,3,2,1,0:T(8,128)S(1)}, f32[20,8,2,32,128]{4,3,2,1,0:T(8,128)}, u32[]{:S(2)}) %copy-start.4) | copy-done | bytes 5242904
  175.1 9.2 %shard_map.72 = (f32[20,8,32,256]{3,2,1,0:T(8,128)}, f32[20,20]{1,0:T(8,128)}) custom-call(f32[8,128]{1,0:T(8,128)S(1)} %psum.15.message, f32[24,128]{1,0:T(8,128)S(1)} %get-tuple-element.20.factor_one, f32[20,8,2,32,128]{4,3,2,1,0:T(8,128)S(1)} %copy-done.4), custom_call_target="tpu_custom_call" | custom-call | tf_op jit(solution)/shard_map/pallas_call | solution.py:504
  (5 shorter events, 0.1 us)
Async XLA Ops:
  0.6 1.2 copy-start
  1.9 0.9 copy-start.6
  2.8 0.9 copy-start.8
  3.8 0.9 copy-start.10
  4.7 0.9 copy-start.12
  5.8 9.3 %collective-permute-start = (f32[8,4,8,256]{3,2,1,0:T(8,128)S(1)}, f32[8,4,8,256]{3,2,1,0:T(8,128)S(1)}, u32[]{:S(2)}, u32[]{:S(2)}) collective-permute-start(f32[8,4,8,256]{3,2,1,0:T(8,128)S(1)} %get-tuple-element.12), channel_id=1, source_target_pairs={{0,16},{16,0},{1,17},{17,1},{2,18},{18,2},{3,19},{19,3},{4,20},{20... | collective-permute-start | bytes 786440 | tf_op jit(solution)/shard_map/ppermute | solution.py:441
  8.9 31.4 %collective-permute-start.3 = (f32[29,32,256]{2,1,0:T(8,128)S(1)}, f32[29,32,256]{2,1,0:T(8,128)S(1)}, u32[]{:S(2)}, u32[]{:S(2)}) collective-permute-start(f32[29,32,256]{2,1,0:T(8,128)S(1)} %get-tuple-element.15), channel_id=1, source_target_pairs={{0,1},{1,2},{2,3},{4,5},{5,6},{6,7},{8,9},{9,10},{10,11},{12,13},{... | collective-permute-start | bytes 2850824 | tf_op jit(solution)/shard_map/ppermute | solution.py:420
  12.4 27.8 %collective-permute-start.4 = (f32[29,32,256]{2,1,0:T(8,128)S(1)}, f32[29,32,256]{2,1,0:T(8,128)}, u32[]{:S(2)}, u32[]{:S(2)}) collective-permute-start(f32[29,32,256]{2,1,0:T(8,128)S(1)} %get-tuple-element.16), channel_id=1, source_target_pairs={{1,0},{2,1},{3,2},{5,4},{6,5},{7,6},{9,8},{10,9},{11,10},{13,12},{... | collective-permute-start | bytes 2850824 | tf_op jit(solution)/shard_map/ppermute | solution.py:420
  13.8 26.4 %copy-start.14 = (f32[2]{0:T(128)}, f32[2]{0:T(128)S(1)}, u32[]{:S(2)}) copy-start(f32[2]{0:T(128)S(1)} %add_convert_fusion.keep) | copy-start | bytes 28
  15.2 1.2 copy-start.1
  16.4 0.9 copy-start.7
  17.4 0.9 copy-start.9
  18.3 0.9 copy-start.11
  19.3 0.9 copy-start.13
  20.2 20.0 %copy-start.5 = (f32[8,4,8,256]{3,2,1,0:T(8,128)}, f32[8,4,8,256]{3,2,1,0:T(8,128)S(1)}, u32[]{:S(2)}) copy-start(f32[8,4,8,256]{3,2,1,0:T(8,128)S(1)} %collective-permute-done.above.below.rest_0_) | copy-start | bytes 786436
  21.5 4.4 %collective-permute-start.1 = (f32[40,256]{1,0:T(8,128)S(1)}, f32[40,256]{1,0:T(8,128)S(1)}, u32[]{:S(2)}, u32[]{:S(2)}) collective-permute-start(f32[40,256]{1,0:T(8,128)S(1)} %get-tuple-element.13), channel_id=1, source_target_pairs={{4,0},{8,4},{12,8},{5,1},{9,5},{13,9},{6,2},{10,6},{14,10},{7,3},{... | collective-permute-start | bytes 122888 | tf_op jit(solution)/shard_map/ppermute | solution.py:420
  22.8 3.9 %collective-permute-start.2 = (f32[40,256]{1,0:T(8,128)S(1)}, f32[40,256]{1,0:T(8,128)S(1)}, u32[]{:S(2)}, u32[]{:S(2)}) collective-permute-start(f32[40,256]{1,0:T(8,128)S(1)} %get-tuple-element.14), channel_id=1, source_target_pairs={{0,4},{4,8},{8,12},{1,5},{5,9},{9,13},{2,6},{6,10},{10,14},{3,7},{... | collective-permute-start | bytes 122888 | tf_op jit(solution)/shard_map/ppermute | solution.py:420
  25.8 14.4 %copy-start.18 = (f32[40,256]{1,0:T(8,128)}, f32[40,256]{1,0:T(8,128)S(1)}, u32[]{:S(2)}) copy-start(f32[40,256]{1,0:T(8,128)S(1)} %collective-permute-done.1.rest_1_) | copy-start | bytes 122884
  26.7 13.6 %copy-start.19 = (f32[40,256]{1,0:T(8,128)}, f32[40,256]{1,0:T(8,128)S(1)}, u32[]{:S(2)}) copy-start(f32[40,256]{1,0:T(8,128)S(1)} %collective-permute-done.2.rest_2_) | copy-start | bytes 122884
  26.7 9.4 %collective-permute-start.5 = (f32[168,256]{1,0:T(8,128)S(1)}, f32[168,256]{1,0:T(8,128)S(1)}, u32[]{:S(2)}, u32[]{:S(2)}) collective-permute-start(f32[168,256]{1,0:T(8,128)S(1)} %maximum_maximum_fusion), channel_id=1, source_target_pairs={{0,1},{1,2},{2,3},{4,5},{5,6},{6,7},{8,9},{9,10},{10,11},{12,13},{... | collective-permute-start | bytes 516104 | tf_op jit(solution)/shard_map/ppermute | solution.py:420
  30.4 9.8 %collective-permute-start.6 = (f32[168,256]{1,0:T(8,128)S(1)}, f32[168,256]{1,0:T(8,128)S(1)}, u32[]{:S(2)}, u32[]{:S(2)}) collective-permute-start(f32[168,256]{1,0:T(8,128)S(1)} %maximum_maximum_fusion.1), channel_id=1, source_target_pairs={{1,0},{2,1},{3,2},{5,4},{6,5},{7,6},{9,8},{10,9},{11,10},{13,12},{... | collective-permute-start | bytes 516104 | tf_op jit(solution)/shard_map/ppermute | solution.py:420
  36.0 4.2 %copy-start.16 = (f32[168,256]{1,0:T(8,128)}, f32[168,256]{1,0:T(8,128)S(1)}, u32[]{:S(2)}) copy-start(f32[168,256]{1,0:T(8,128)S(1)} %collective-permute-done.5.rest_5_) | copy-start | bytes 516100
  40.2 0.7 copy-start.17
  40.2 1.0 copy-start.15
  110.8 2.5 %copy-start.2 = (f32[20,8,2,32,128]{4,3,2,1,0:T(8,128)S(1)}, f32[20,8,2,32,128]{4,3,2,1,0:T(8,128)}, u32[]{:S(2)}) copy-start(f32[20,8,2,32,128]{4,3,2,1,0:T(8,128)} %get-tuple-element.18.basis_hbm) | copy-start | bytes 15728644
  131.2 2.4 %copy-start.3 = (f32[20,8,2,32,128]{4,3,2,1,0:T(8,128)}, f32[20,8,2,32,128]{4,3,2,1,0:T(8,128)S(1)}, u32[]{:S(2)}) copy-start(f32[20,8,2,32,128]{4,3,2,1,0:T(8,128)S(1)} %get-tuple-element.21.first_hbm) | copy-start | bytes 15728644
  172.6 2.5 %copy-start.4 = (f32[20,8,2,32,128]{4,3,2,1,0:T(8,128)S(1)}, f32[20,8,2,32,128]{4,3,2,1,0:T(8,128)}, u32[]{:S(2)}) copy-start(f32[20,8,2,32,128]{4,3,2,1,0:T(8,128)} %copy-done.3) | copy-start | bytes 15728644
where the time goes:
time: 185 us; the launch traced here: 184 us
  blocking collectives  79.5 us (43%)
  Pallas kernels  57.6 us (31%)
  local copies, waits for them, and re-layouts  18.4 us (10%)
  starting transfers between devices  17.2 us (9%)
  waiting for transfers between devices  10.7 us (6%)
    psum x2, blocking collectives, body(): message = lax.psum(message, AXES)  79.5 us
    pallas_call x1, Pallas kernels, body(): pl.pallas_call(krylov_entry, out_shape=(block, shape(8, 128)), in_specs=[...  29.1 us
    unnamed x40, local copies, waits for them, and re-layouts  18.4 us
    pallas_call x1, Pallas kernels, body(): pl.pallas_call(functools.partial(first_pass, cells), out_shape=(block, sh...  17.9 us
    ppermute x6, starting transfers between devices, move(): return lax.ppermute(value, axis, pairs)  14.1 us
    ppermute x6, waiting for transfers between devices, move(): return lax.ppermute(value, axis, pairs)  9.29 us
    pallas_call x1, Pallas kernels, body(): pl.pallas_call(functools.partial(second_pass, cells), out_shape=(shape(CO...  9.16 us
  transfers between devices with their start and end apart: 7, of which 4 were waited for; matrix products, arithmetic and copies ran while one was open for 0% of the time, Pallas kernels for 1%

commit v1 on v0

--- a/solution.py
+++ b/solution.py
@@ -112,45 +112,53 @@
                 out[8 * t : 8 * t + 8, 128 * half : 128 * half + 128] = acc
 
 
-def gram_message(read, count, parts, out, unroll=4):
-    group = 5
-    parts[...] = jnp.zeros_like(parts)
-    for gi in range(COLS // group):
-        for gj in range(gi, COLS // group):
-            pairs = [
-                (i, j)
-                for i in range(group * gi, group * gi + group)
-                for j in range(group * gj, group * gj + group)
-                if i <= j
-            ]
+def gather_rows(values):
+    rows = row_ids((8, 128))
+    width = 1
+    while len(values) > 1:
+        low = (rows & width) == 0
+        merged = []
+        for a, b in zip(values[0::2], values[1::2]):
+            if a is None and b is None:
+                merged.append(None)
+                continue
+            a = jnp.zeros((8, 128), F32) if a is None else a
+            b = jnp.zeros((8, 128), F32) if b is None else b
+            merged.append(jnp.where(low, a, b) + pltpu.roll(jnp.where(low, b, a), width, 0))
+        values = merged
+        width *= 2
+    return values[0]
+
+
+def gram_message(read, count, out, unroll=2):
+    lanes = lane_ids((8, 128))
+    result = jnp.zeros((8, 128), F32)
+    for tile in range(0, COLS, 8):
+        mine = range(tile, min(tile + 8, COLS))
+        columns = [mine] + [range(c, c + 4) for c in range(tile + 8, COLS, 4)]
+        for group in columns:
+            pairs = [(i, j) for j in group for i in mine if i <= j]
 
             def step(n, sums):
-                sums = list(sums)
                 rows = {i: read(i, n) for i in sorted({i for pair in pairs for i in pair})}
-                for k, (i, j) in enumerate(pairs):
-                    sums[k] = sums[k] + rows[i] * rows[j]
-                return tuple(sums)
+                return tuple(s + rows[i] * rows[j] for s, (i, j) in zip(sums, pairs))
 
             sums = lax.fori_loop(
                 0, count, step, tuple(jnp.zeros((8, 128), F32) for _ in pairs), unroll=unroll
             )
-            for (i, j), total in zip(pairs, sums):
-                line = jnp.sum(total, axis=0, keepdims=True)
-                parts[32 * i + j : 32 * i + j + 1, :] = line
-                if i != j:
-                    parts[32 * j + i : 32 * j + i + 1, :] = line
-    flat = lax.dot_general(
-        jnp.ones((8, 128), F32), parts[...], (((1,), (1,)), ((), ())), precision=HIGHEST, preferred_element_type=F32
-    )
-    out[...] = jnp.zeros_like(out)
-    for r in range(COLS * 32 // 128):
-        out[r : r + 1, :] = flat[0:1, 128 * r : 128 * r + 128]
+            sums = dict(zip(pairs, sums))
+            for j in group:
+                total = gather_rows([sums.get((tile + s, j)) for s in range(8)])
+                total = jnp.sum(total, axis=1, keepdims=True)
+                result = jnp.where(lanes == 4 * tile + j, jnp.broadcast_to(total, (8, 128)), result)
+    for n in range(out.shape[0]):
+        out[n] = result
 
 
 def krylov(
     keep, rhs, cz, cx, cy, dg, above, below, yup, ydn, facelo, facehi, rimlo, rimhi,
     basis, message,
-    store, faces, ysrc, parts, sems,
+    store, faces, ysrc, sems,
 ):
     lane = lane_ids((8, 128))
     keep_up, keep_dn = keep[0], keep[1]
@@ -301,21 +309,21 @@
         f = slot(i // NRHS) + i % NRHS
         return store[f, DEPTH + n // 8, (n // 4) % 2, pl.ds(pl.multiple_of(8 + 8 * (n % 4), 8), 8), :]
 
-    gram_message(read, NZ * 8, parts, message)
+    gram_message(read, NZ * 8, message)
     for copy in copies:
         copy.wait()
 
 
-def factor_gram(message, cells, gram, work):
+def factor_gram(messages, cells):
     rows = row_ids((24, 128))
     lanes = lane_ids((24, 128))
-    gram[...] = jnp.zeros_like(gram)
-    for q in range(4):
-        turned = pltpu.roll(message, (-32 * q) % 128, 1) if q else message
-        for r in range(COLS // 4):
-            i = 4 * r + q
-            gram[i : i + 1, :] = turned[r : r + 1, :]
-    a = jnp.where(lanes < COLS, gram[...] / cells, 0.0)
+    message = messages[0]
+    for n in range(1, messages.shape[0]):
+        message = message + messages[n]
+    upper = jnp.concatenate([message] + [pltpu.roll(message, 128 - 32 * k, 1) for k in (1, 2)], 0)
+    upper = jnp.where((lanes < COLS) & (rows < COLS), upper, 0.0)
+    square = jnp.concatenate([upper, jnp.zeros((104, 128), F32)], 0)
+    a = jnp.where(rows <= lanes, upper, square.T[0:24, :]) / cells
     a = jnp.where((lanes == rows + 32) & (rows < COLS), 1.0, a)
     for j in range(COLS - 1):
         column = jnp.broadcast_to(a[:, j : j + 1], (24, 128))
@@ -351,10 +359,10 @@
                 write(i, p, sums[i][p])
 
 
-def first_pass(cells, message, basis_hbm, first_hbm, next_message, factor_out, basis, gram, table, parts, sems):
+def first_pass(cells, message, basis_hbm, first_hbm, next_message, factor_out, basis, table, sems):
     load = pltpu.make_async_copy(basis_hbm, basis, sems.at[0])
     load.start()
-    factor = factor_gram(message[...], cells, gram, None)
+    factor = factor_gram(message, cells)
     factor_out[...] = factor
     spread(factor, table)
     load.wait()
@@ -378,14 +386,14 @@
     def read(i, n):
         return basis[i, n // 8, (n // 4) % 2, pl.ds(pl.multiple_of(8 * (n % 4), 8), 8), :]
 
-    gram_message(read, NZ * 8, parts, next_message)
+    gram_message(read, NZ * 8, next_message)
     save.wait()
 
 
-def second_pass(cells, message, factor_one, first_hbm, out, triangle, first, gram, table, sems):
+def second_pass(cells, message, factor_one, first_hbm, out, triangle, first, table, sems):
     load = pltpu.make_async_copy(first_hbm, first, sems.at[0])
     load.start()
-    factor = factor_gram(message[...], cells, gram, None)
+    factor = factor_gram(message, cells)
     spread(factor, table)
     lanes = lane_ids((24, 128))
     left = jnp.where(lanes < COLS, factor, 0.0)[:, 0:24]
@@ -420,9 +428,14 @@
     return lax.ppermute(value, axis, pairs)
 
 
+def exchange(messages):
+    return lax.all_to_all(messages, AXES, 0, 0, tiled=True)
+
+
 def body(rhs, coef_x, coef_y, coef_z, diag_term):
     n_x = lax.axis_size("gx")
-    cells = float(NZ * NX * NY * n_x * lax.axis_size("gy") * lax.axis_size("gz"))
+    devices = n_x * lax.axis_size("gy") * lax.axis_size("gz")
+    cells = float(NZ * NX * NY * devices)
     at_x = lax.axis_index("gx")
     swap = n_x == 2
     fields = (rhs, coef_z, coef_x, coef_y, diag_term)
@@ -433,7 +446,7 @@
         functools.partial(pack_faces, swap),
         out_shape=(face_shape, face_shape) + (x_shape,) * (1 if swap else 2),
         in_specs=[smem()] + [vmem()] * 5,
-        compiler_params=params(32),
+        compiler_params=params(60),
     )(at_x.astype(jnp.int32).reshape(1), *fields)
     facehi = move(zlo, "gz", -1)
     facelo = move(zhi, "gz", 1)
@@ -451,7 +464,7 @@
         pack_rims,
         out_shape=(rim_shape, rim_shape),
         in_specs=[smem()] + [vmem()] * 7,
-        compiler_params=params(32),
+        compiler_params=params(60),
     )(keep, *fields, above, below)
     yup, ydn = move(ylo, "gy", -1), move(yhi, "gy", 1)
 
@@ -471,36 +484,33 @@
 
     basis, message = pl.pallas_call(
         krylov_entry,
-        out_shape=(block, shape(8, 128)),
+        out_shape=(block, shape(devices, 8, 128)),
         in_specs=[smem()] + [vmem()] * (5 + len(x_parts) + 6),
         out_specs=(hbm(), vmem()),
         scratch_shapes=[
             pltpu.VMEM((COLS + NRHS, EZ, LT, EROWS, 128), F32),
             pltpu.VMEM((7, EZ, LT, ROWS, 128), F32),
             pltpu.VMEM((2, 4, ROWS, 128), F32),
-            pltpu.VMEM((32 * COLS, 128), F32),
             pltpu.SemaphoreType.DMA((STEPS + 1,)),
         ],
-        compiler_params=params(56),
+        compiler_params=params(60),
     )(keep, *fields, *x_parts, yup, ydn, facelo, facehi, rimlo, rimhi)
 
-    message = lax.psum(message, AXES)
+    message = exchange(message)
     first, message, factor_one = pl.pallas_call(
         functools.partial(first_pass, cells),
-        out_shape=(block, shape(8, 128), shape(24, 128)),
+        out_shape=(block, shape(devices, 8, 128), shape(24, 128)),
         in_specs=[vmem(), hbm()],
         out_specs=(hbm(), vmem(), vmem()),
         scratch_shapes=[
             pltpu.VMEM(block.shape, F32),
-            pltpu.VMEM((24, 128), F32),
             pltpu.VMEM((COLS, 24, 128), F32),
-            pltpu.VMEM((32 * COLS, 128), F32),
             pltpu.SemaphoreType.DMA((2,)),
         ],
-        compiler_params=params(32),
+        compiler_params=params(60),
     )(message, basis)
 
-    message = lax.psum(message, AXES)
+    message = exchange(message)
     return pl.pallas_call(
         functools.partial(second_pass, cells),
         out_shape=(shape(COLS, NZ, NX, NY), shape(COLS, COLS)),
@@ -508,11 +518,10 @@
         out_specs=(vmem(), vmem()),
         scratch_shapes=[
             pltpu.VMEM(block.shape, F32),
-            pltpu.VMEM((24, 128), F32),
             pltpu.VMEM((COLS, 24, 128), F32),
             pltpu.SemaphoreType.DMA((1,)),
         ],
-        compiler_params=params(32),
+        compiler_params=params(60),
     )(message, factor_one, first)
 
 

time: 185 us -> 123 us (0.66)
  blocking collectives: 79.5 us -> 24 us
  local copies, waits for them, and re-layouts: 18.4 us -> 3.67 us
  Pallas kernels: 57.6 us -> 63.9 us
    psum x2 -> x0, blocking collectives: 79.5 us -> none  [body(): message = lax.psum(message, AXES)]
    all_to_all x0 -> x2, blocking collectives: none -> 24 us  [exchange(): return lax.all_to_all(messages, AXES, 0, 0, tiled=True)]
    unnamed x40 -> x14, local copies, waits for them, and re-layouts: 18.4 us -> 2.67 us
    pallas_call x1, Pallas kernels: 0.17 us -> 2.92 us  [body(): pl.pallas_call(functools.partial(pack_faces, swap), out_shape=(face_shape...]
  transfers between devices with their start and end apart: 7 -> 7, of which waited for: 4 -> 3; matrix products, arithmetic and copies ran while one was open for 0% -> 1% of each run, Pallas kernels for 1% -> 2%
where the time goes in v1:
time: 123 us; the launch traced here: 122 us
  Pallas kernels  63.9 us (52%)
  blocking collectives  24 us (20%)
  starting transfers between devices  17.1 us (14%)
  waiting for transfers between devices  11.9 us (10%)
  local copies, waits for them, and re-layouts  3.67 us (3%)
    pallas_call x1, Pallas kernels, body(): pl.pallas_call(krylov_entry, out_shape=(block, shape(devices, 8, 128)), i...  28.7 us
    all_to_all x2, blocking collectives, exchange(): return lax.all_to_all(messages, AXES, 0, 0, tiled=True)  24 us
    pallas_call x1, Pallas kernels, body(): pl.pallas_call(functools.partial(first_pass, cells), out_shape=(block, sh...  18.8 us
    ppermute x6, starting transfers between devices, move(): return lax.ppermute(value, axis, pairs)  14.1 us
    ppermute x6, waiting for transfers between devices, move(): return lax.ppermute(value, axis, pairs)  10.9 us
    pallas_call x1, Pallas kernels, body(): pl.pallas_call(functools.partial(second_pass, cells), out_shape=(shape(CO...  10.5 us
    pallas_call x1, Pallas kernels, body(): pl.pallas_call(pack_rims, out_shape=(rim_shape, rim_shape), in_specs=[sme...  3 us
    ppermute x1, starting transfers between devices, body(): above = below = lax.ppermute(xmsgs[0], 'gx', [(0, 1), (1, 0)])  2.97 us
  transfers between devices with their start and end apart: 7, of which 3 were waited for; matrix products, arithmetic and copies ran while one was open for 1% of the time, Pallas kernels for 2%

profile of v1, /device:TPU:0, one launch (start us, length us, event | category | flops | bytes accessed | tf_op | source)
XLA Modules:
  0.0 122.1 jit_solution(9733365316441263660)
XLA Ops:
  0.6 2.9 %shard_map.68 = (f32[29,32,256]{2,1,0:T(8,128)}, f32[29,32,256]{2,1,0:T(8,128)}, f32[8,4,8,256]{3,2,1,0:T(8,128)}) custom-call(s32[1]{0:T(128)} %bitcast.1.place, f32[4,8,32,256]{3,2,1,0:T(8,128)} %rhs.5, f32[8,32,256]{2,1,0:T(8,128)} %cz.5, f32[8,32,256]{2,1,0:T(8,128)} %cx.5, f32[8,32,256]{2,1,0:T(8,128)} %cy.5, f32[8,32,256]{2,1,0:T(8,128)} %dg.5), custom_call_target="tpu_custom_call" | custom-call | tf_op jit(solution)/shard_map/pallas_call | solution.py:445
  3.5 3.0 %collective-permute-start = (f32[8,4,8,256]{3,2,1,0:T(8,128)}, f32[8,4,8,256]{3,2,1,0:T(8,128)S(1)}, u32[]{:S(2)}, u32[]{:S(2)}) collective-permute-start(f32[8,4,8,256]{3,2,1,0:T(8,128)} %get-tuple-element.12), channel_id=1, source_target_pairs={{0,16},{16,0},{1,17},{17,1},{2,18},{18,2},{3,19},{19,3},{4,20},{20... | collective-permute-start | bytes 786440 | tf_op jit(solution)/shard_map/ppermute | solution.py:454
  6.5 3.5 %collective-permute-start.3 = (f32[29,32,256]{2,1,0:T(8,128)}, f32[29,32,256]{2,1,0:T(8,128)S(1)}, u32[]{:S(2)}, u32[]{:S(2)}) collective-permute-start(f32[29,32,256]{2,1,0:T(8,128)} %get-tuple-element.15), channel_id=1, source_target_pairs={{0,1},{1,2},{2,3},{4,5},{5,6},{6,7},{8,9},{9,10},{10,11},{12,13},{... | collective-permute-start | bytes 2850824 | tf_op jit(solution)/shard_map/ppermute | solution.py:428
  10.1 1.3 %collective-permute-start.4 = (f32[29,32,256]{2,1,0:T(8,128)}, f32[29,32,256]{2,1,0:T(8,128)S(1)}, u32[]{:S(2)}, u32[]{:S(2)}) collective-permute-start(f32[29,32,256]{2,1,0:T(8,128)} %get-tuple-element.16), channel_id=1, source_target_pairs={{1,0},{2,1},{3,2},{5,4},{6,5},{7,6},{9,8},{10,9},{11,10},{13,12},{... | collective-permute-start | bytes 2850824 | tf_op jit(solution)/shard_map/ppermute | solution.py:428
  11.4 0.7 add_convert_fusion.keep
  12.0 1.0 collective-permute-done.above.below.rest_0_
  13.0 0.0 copy-start
  13.0 0.7 copy-done
  13.7 3.0 %shard_map.69 = (f32[40,256]{1,0:T(8,128)}, f32[40,256]{1,0:T(8,128)}) custom-call(f32[2]{0:T(128)} %add_convert_fusion.keep, f32[4,8,32,256]{3,2,1,0:T(8,128)} %rhs.5, f32[8,32,256]{2,1,0:T(8,128)} %cz.5, f32[8,32,256]{2,1,0:T(8,128)} %cx.5, f32[8,32,256]{2,1,0:T(8,128)} %cy.5, f32[8,32,256]{2,1,0:T(8,128)} %dg.5, f32[8,4,8,256]{3,2,1,0:T(8,128)} %copy-done, ...), custom_call_target="tpu_custom_call" | custom-call | tf_op jit(solution)/shard_map/pallas_call | solution.py:463
  16.7 1.3 %collective-permute-start.1 = (f32[40,256]{1,0:T(8,128)}, f32[40,256]{1,0:T(8,128)S(1)}, u32[]{:S(2)}, u32[]{:S(2)}) collective-permute-start(f32[40,256]{1,0:T(8,128)} %get-tuple-element.13), channel_id=1, source_target_pairs={{4,0},{8,4},{12,8},{5,1},{9,5},{13,9},{6,2},{10,6},{14,10},{7,3},{... | collective-permute-start | bytes 122888 | tf_op jit(solution)/shard_map/ppermute | solution.py:428
  18.0 3.0 %collective-permute-start.2 = (f32[40,256]{1,0:T(8,128)}, f32[40,256]{1,0:T(8,128)S(1)}, u32[]{:S(2)}, u32[]{:S(2)}) collective-permute-start(f32[40,256]{1,0:T(8,128)} %get-tuple-element.14), channel_id=1, source_target_pairs={{0,4},{4,8},{8,12},{1,5},{5,9},{9,13},{2,6},{6,10},{10,14},{3,7},{... | collective-permute-start | bytes 122888 | tf_op jit(solution)/shard_map/ppermute | solution.py:428
  21.1 1.0 fusion
  22.1 0.0 collective-permute-done.1.rest_1_
  22.1 0.0 copy-start.5
  22.1 0.0 collective-permute-done.2.rest_2_
  22.1 0.0 copy-start.6
  22.1 3.7 %collective-permute-start.5 = (f32[168,256]{1,0:T(8,128)S(1)}, f32[168,256]{1,0:T(8,128)S(1)}, u32[]{:S(2)}, u32[]{:S(2)}) collective-permute-start(f32[168,256]{1,0:T(8,128)S(1)} %maximum_maximum_fusion), channel_id=1, source_target_pairs={{0,1},{1,2},{2,3},{4,5},{5,6},{6,7},{8,9},{9,10},{10,11},{12,13},{... | collective-permute-start | bytes 516104 | tf_op jit(solution)/shard_map/ppermute | solution.py:428
  25.9 1.3 %collective-permute-start.6 = (f32[168,256]{1,0:T(8,128)S(1)}, f32[168,256]{1,0:T(8,128)S(1)}, u32[]{:S(2)}, u32[]{:S(2)}) collective-permute-start(f32[168,256]{1,0:T(8,128)S(1)} %maximum_maximum_fusion.1), channel_id=1, source_target_pairs={{1,0},{2,1},{3,2},{5,4},{6,5},{7,6},{9,8},{10,9},{11,10},{13,12},{... | collective-permute-start | bytes 516104 | tf_op jit(solution)/shard_map/ppermute | solution.py:428
  27.2 6.7 %collective-permute-done.5.rest_5_ = f32[168,256]{1,0:T(8,128)S(1)} collective-permute-done((f32[168,256]{1,0:T(8,128)S(1)}, f32[168,256]{1,0:T(8,128)S(1)}, u32[]{:S(2)}, u32[]{:S(2)}) %collective-permute-start.5) | collective-permute-done | bytes 172064 | tf_op jit(solution)/shard_map/ppermute | solution.py:428
  33.9 0.0 copy-start.3
  33.9 4.2 %collective-permute-done.6.rest_6_ = f32[168,256]{1,0:T(8,128)S(1)} collective-permute-done((f32[168,256]{1,0:T(8,128)S(1)}, f32[168,256]{1,0:T(8,128)S(1)}, u32[]{:S(2)}, u32[]{:S(2)}) %collective-permute-start.6) | collective-permute-done | bytes 172064 | tf_op jit(solution)/shard_map/ppermute | solution.py:428
  38.1 0.0 copy-start.4
  38.1 0.0 collective-permute-done.3.rest_3_
  38.1 0.0 copy-start.1
  38.1 0.0 collective-permute-done.4.rest_4_
  38.1 0.0 copy-done.5
  38.1 0.0 copy-done.6
  38.1 0.0 copy-done.3
  38.1 0.6 copy-done.4
  38.8 0.3 copy-done.1
  39.1 0.0 copy-start.2
  39.1 1.0 copy-done.2
  40.1 28.7 %shard_map.70 = (f32[20,8,2,32,128]{4,3,2,1,0:T(8,128)}, f32[32,8,128]{2,1,0:T(8,128)}) custom-call(f32[2]{0:T(128)} %add_convert_fusion.keep, f32[4,8,32,256]{3,2,1,0:T(8,128)} %rhs.5, f32[8,32,256]{2,1,0:T(8,128)} %cz.5, f32[8,32,256]{2,1,0:T(8,128)} %cx.5, f32[8,32,256]{2,1,0:T(8,128)} %cy.5, f32[8,32,256]{2,1,0:T(8,128)} %dg.5, ...), custom_call_target="tpu_custom_call" | custom-call | tf_op jit(solution)/shard_map/pallas_call | solution.py:485
  68.7 12.4 %all_to_all.10.message = f32[32,8,128]{2,1,0:T(8,128)} all-to-all(f32[32,8,128]{2,1,0:T(8,128)} %get-tuple-element.17), channel_id=1, replica_groups=mesh['gx'=2,'gy'=4,'gz'=4] {'gx','gy','gz'}, dimensions={0} | all-to-all | bytes 262144 | tf_op jit(solution)/shard_map/all_to_all | solution.py:432
  81.1 18.8 %shard_map.71 = (f32[20,8,2,32,128]{4,3,2,1,0:T(8,128)}, f32[32,8,128]{2,1,0:T(8,128)}, f32[24,128]{1,0:T(8,128)}) custom-call(f32[32,8,128]{2,1,0:T(8,128)} %all_to_all.10.message, f32[20,8,2,32,128]{4,3,2,1,0:T(8,128)} %get-tuple-element.18.basis_hbm), custom_call_target="tpu_custom_call" | custom-call | tf_op jit(solution)/shard_map/pallas_call | solution.py:500
  99.9 11.7 %all_to_all.11.message = f32[32,8,128]{2,1,0:T(8,128)} all-to-all(f32[32,8,128]{2,1,0:T(8,128)} %get-tuple-element.19), channel_id=1, replica_groups=mesh['gx'=2,'gy'=4,'gz'=4] {'gx','gy','gz'}, dimensions={0} | all-to-all | bytes 262144 | tf_op jit(solution)/shard_map/all_to_all | solution.py:432
  111.6 10.5 %shard_map.72 = (f32[20,8,32,256]{3,2,1,0:T(8,128)}, f32[20,20]{1,0:T(8,128)}) custom-call(f32[32,8,128]{2,1,0:T(8,128)} %all_to_all.11.message, f32[24,128]{1,0:T(8,128)} %get-tuple-element.20.factor_one, f32[20,8,2,32,128]{4,3,2,1,0:T(8,128)} %get-tuple-element.21.first_hbm), custom_call_target="tpu_custom_call" | custom-call | tf_op jit(solution)/shard_map/pallas_call | solution.py:514
  (4 shorter events, 0.0 us)
Async XLA Ops:
  3.5 9.5 %collective-permute-start = (f32[8,4,8,256]{3,2,1,0:T(8,128)}, f32[8,4,8,256]{3,2,1,0:T(8,128)S(1)}, u32[]{:S(2)}, u32[]{:S(2)}) collective-permute-start(f32[8,4,8,256]{3,2,1,0:T(8,128)} %get-tuple-element.12), channel_id=1, source_target_pairs={{0,16},{16,0},{1,17},{17,1},{2,18},{18,2},{3,19},{19,3},{4,20},{20... | collective-permute-start | bytes 786440 | tf_op jit(solution)/shard_map/ppermute | solution.py:454
  6.5 31.6 %collective-permute-start.3 = (f32[29,32,256]{2,1,0:T(8,128)}, f32[29,32,256]{2,1,0:T(8,128)S(1)}, u32[]{:S(2)}, u32[]{:S(2)}) collective-permute-start(f32[29,32,256]{2,1,0:T(8,128)} %get-tuple-element.15), channel_id=1, source_target_pairs={{0,1},{1,2},{2,3},{4,5},{5,6},{6,7},{8,9},{9,10},{10,11},{12,13},{... | collective-permute-start | bytes 2850824 | tf_op jit(solution)/shard_map/ppermute | solution.py:428
  10.1 28.0 %collective-permute-start.4 = (f32[29,32,256]{2,1,0:T(8,128)}, f32[29,32,256]{2,1,0:T(8,128)S(1)}, u32[]{:S(2)}, u32[]{:S(2)}) collective-permute-start(f32[29,32,256]{2,1,0:T(8,128)} %get-tuple-element.16), channel_id=1, source_target_pairs={{1,0},{2,1},{3,2},{5,4},{6,5},{7,6},{9,8},{10,9},{11,10},{13,12},{... | collective-permute-start | bytes 2850824 | tf_op jit(solution)/shard_map/ppermute | solution.py:428
  13.0 0.7 copy-start
  16.7 5.3 %collective-permute-start.1 = (f32[40,256]{1,0:T(8,128)}, f32[40,256]{1,0:T(8,128)S(1)}, u32[]{:S(2)}, u32[]{:S(2)}) collective-permute-start(f32[40,256]{1,0:T(8,128)} %get-tuple-element.13), channel_id=1, source_target_pairs={{4,0},{8,4},{12,8},{5,1},{9,5},{13,9},{6,2},{10,6},{14,10},{7,3},{... | collective-permute-start | bytes 122888 | tf_op jit(solution)/shard_map/ppermute | solution.py:428
  18.0 4.1 %collective-permute-start.2 = (f32[40,256]{1,0:T(8,128)}, f32[40,256]{1,0:T(8,128)S(1)}, u32[]{:S(2)}, u32[]{:S(2)}) collective-permute-start(f32[40,256]{1,0:T(8,128)} %get-tuple-element.14), channel_id=1, source_target_pairs={{0,4},{4,8},{8,12},{1,5},{5,9},{9,13},{2,6},{6,10},{10,14},{3,7},{... | collective-permute-start | bytes 122888 | tf_op jit(solution)/shard_map/ppermute | solution.py:428
  22.1 16.0 %copy-start.5 = (f32[40,256]{1,0:T(8,128)}, f32[40,256]{1,0:T(8,128)S(1)}, u32[]{:S(2)}) copy-start(f32[40,256]{1,0:T(8,128)S(1)} %collective-permute-done.1.rest_1_) | copy-start | bytes 122884
  22.1 16.0 %copy-start.6 = (f32[40,256]{1,0:T(8,128)}, f32[40,256]{1,0:T(8,128)S(1)}, u32[]{:S(2)}) copy-start(f32[40,256]{1,0:T(8,128)S(1)} %collective-permute-done.2.rest_2_) | copy-start | bytes 122884
  22.1 11.8 %collective-permute-start.5 = (f32[168,256]{1,0:T(8,128)S(1)}, f32[168,256]{1,0:T(8,128)S(1)}, u32[]{:S(2)}, u32[]{:S(2)}) collective-permute-start(f32[168,256]{1,0:T(8,128)S(1)} %maximum_maximum_fusion), channel_id=1, source_target_pairs={{0,1},{1,2},{2,3},{4,5},{5,6},{6,7},{8,9},{9,10},{10,11},{12,13},{... | collective-permute-start | bytes 516104 | tf_op jit(solution)/shard_map/ppermute | solution.py:428
  25.9 12.2 %collective-permute-start.6 = (f32[168,256]{1,0:T(8,128)S(1)}, f32[168,256]{1,0:T(8,128)S(1)}, u32[]{:S(2)}, u32[]{:S(2)}) collective-permute-start(f32[168,256]{1,0:T(8,128)S(1)} %maximum_maximum_fusion.1), channel_id=1, source_target_pairs={{1,0},{2,1},{3,2},{5,4},{6,5},{7,6},{9,8},{10,9},{11,10},{13,12},{... | collective-permute-start | bytes 516104 | tf_op jit(solution)/shard_map/ppermute | solution.py:428
  33.9 4.2 %copy-start.3 = (f32[168,256]{1,0:T(8,128)}, f32[168,256]{1,0:T(8,128)S(1)}, u32[]{:S(2)}) copy-start(f32[168,256]{1,0:T(8,128)S(1)} %collective-permute-done.5.rest_5_) | copy-start | bytes 516100
  38.1 0.7 copy-start.4
  38.1 1.0 copy-start.1
  39.1 1.0 copy-start.2

commit v2 on v1

--- a/solution.py
+++ b/solution.py
@@ -24,6 +24,7 @@
 LT = 3
 FACE = NRHS * 4 + 3 * 4 + 1
 F32 = jnp.float32
+LIMIT = 63
 
 
 def params(mb):
@@ -54,27 +55,41 @@
     return rhs.at[f, z] if f < NRHS else (cz, cx, cy, dg)[f - NRHS].at[z]
 
 
-def pack_faces(swap, place, rhs, cz, cx, cy, dg, zlo, zhi, *xmsgs):
-    n = 0
+def pack_faces(swap, place, rhs, cz, cx, cy, dg, zlo, zhi, *rest):
+    xmsgs, (first_rows, last_rows, sems) = rest[:-3], rest[-3:]
+    edges = []
+    planes = []
+    n = at = 0
     for f in range(FIELDS):
+        src = rhs.at[f] if f < NRHS else (cz, cx, cy, dg)[f - NRHS]
         depth = DEPTH if f <= NRHS else DEPTH - 1
-        for d in range(depth):
-            zlo[n] = field_of(rhs, cz, cx, cy, dg, f, d)[...]
-            zhi[n] = field_of(rhs, cz, cx, cy, dg, f, NZ - depth + d)[...]
-            n += 1
+        for side, rows, out in ((0, first_rows, zlo), (1, last_rows, zhi)):
+            edges.append(pltpu.make_async_copy(src.at[:, pl.ds(side * (NX - 8), 8), :], rows.at[f], sems.at[n]))
+            start = side * (NZ - depth)
+            planes.append(
+                pltpu.make_async_copy(src.at[pl.ds(start, depth)], out.at[pl.ds(at, depth)], sems.at[n + 1])
+            )
+            n += 2
+        at += depth
+    for copy in edges:
+        copy.start()
+    for copy in planes:
+        copy.start()
+    for copy in edges:
+        copy.wait()
     low = row_ids((8, NY)) < 4
     up = place[0] == 0
     for f in range(FIELDS):
         for m in range(NZ // 2):
-            a = field_of(rhs, cz, cx, cy, dg, f, 2 * m)
-            b = field_of(rhs, cz, cx, cy, dg, f, 2 * m + 1)
-            first = jnp.where(low, a[0:8], pltpu.roll(b[0:8], 4, 0))
-            last = jnp.where(low, pltpu.roll(a[NX - 8 : NX], 4, 0), b[NX - 8 : NX])
+            first = jnp.where(low, first_rows[f, 2 * m], pltpu.roll(first_rows[f, 2 * m + 1], 4, 0))
+            last = jnp.where(low, pltpu.roll(last_rows[f, 2 * m], 4, 0), last_rows[f, 2 * m + 1])
             if swap:
                 xmsgs[0][f, m] = jnp.where(up, last, first)
             else:
                 xmsgs[0][f, m] = first
                 xmsgs[1][f, m] = last
+    for copy in planes:
+        copy.wait()
 
 
 def halo_tile(above, below, odd, keep_up, keep_dn):
@@ -86,30 +101,53 @@
     return jnp.where(low, up * keep_up, dn * keep_dn)
 
 
-def pack_rims(keep, rhs, cz, cx, cy, dg, above, below, ylo, yhi):
+def keep_sides(swap, place):
+    if not swap:
+        return 1.0, 1.0
+    first = place[0] == 0
+    return jnp.where(first, 1.0, 0.0), jnp.where(first, 0.0, 1.0)
+
+
+def pack_lanes(tile_of, side):
     lane = lane_ids((8, 128))
-    keep_up, keep_dn = keep[0], keep[1]
-    for t in range(ROWS // 8):
+    source = 124 * side
+    acc = jnp.zeros((8, 128), F32)
+    for zz in range(4):
+        for f in range(FIELDS):
+            tile = tile_of(f, zz)
+            spot = (zz * FIELDS + f) * 4
+            shift = (spot - source) % 128
+            if shift:
+                tile = pltpu.roll(tile, shift, 1)
+            acc = jnp.where((lane >= spot) & (lane < spot + 4), tile, acc)
+    return acc
+
+
+def pack_own_rims(rhs, cz, cx, cy, dg, ylo, yhi):
+    for t in range(NX // 8):
         for side, out in ((0, ylo), (1, yhi)):
-            lanes = pl.ds(128 * side, 128)
-            source = 124 * side
             for half in range(2):
-                acc = jnp.zeros((8, 128), F32)
-                for zz in range(4):
-                    z = 4 * half + zz
-                    for f in range(FIELDS):
-                        if t < NX // 8:
-                            tile = field_of(rhs, cz, cx, cy, dg, f, z)[8 * t : 8 * t + 8, lanes]
-                        else:
-                            tile = halo_tile(
-                                above[f, z // 2, :, lanes], below[f, z // 2, :, lanes], z % 2, keep_up, keep_dn
-                            )
-                        spot = (zz * FIELDS + f) * 4
-                        shift = (spot - source) % 128
-                        if shift:
-                            tile = pltpu.roll(tile, shift, 1)
-                        acc = jnp.where((lane >= spot) & (lane < spot + 4), tile, acc)
-                out[8 * t : 8 * t + 8, 128 * half : 128 * half + 128] = acc
+                out[8 * t : 8 * t + 8, 128 * half : 128 * half + 128] = pack_lanes(
+                    lambda f, zz: field_of(rhs, cz, cx, cy, dg, f, 4 * half + zz)[
+                        8 * t : 8 * t + 8, 128 * side : 128 * side + 128
+                    ],
+                    side,
+                )
+
+
+def pack_rims(swap, place, ylo_own, yhi_own, *refs):
+    above, below, ylo, yhi = refs if not swap else (refs[0],) + refs
+    keep_up, keep_dn = keep_sides(swap, place)
+    for side, own, out in ((0, ylo_own, ylo), (1, yhi_own, yhi)):
+        out[0:NX, :] = own[...]
+        lanes = slice(128 * side, 128 * side + 128)
+        for half in range(2):
+            out[NX:ROWS, 128 * half : 128 * half + 128] = pack_lanes(
+                lambda f, zz: halo_tile(
+                    above[f, 2 * half + zz // 2, :, lanes], below[f, 2 * half + zz // 2, :, lanes], zz % 2, keep_up, keep_dn
+                ),
+                side,
+            )
 
 
 def gather_rows(values):
@@ -130,7 +168,7 @@
     return values[0]
 
 
-def gram_message(read, count, out, unroll=2):
+def gram_message(read, count, out, unroll=8):
     lanes = lane_ids((8, 128))
     result = jnp.zeros((8, 128), F32)
     for tile in range(0, COLS, 8):
@@ -156,13 +194,13 @@
 
 
 def krylov(
-    keep, rhs, cz, cx, cy, dg, above, below, yup, ydn, facelo, facehi, rimlo, rimhi,
+    swap, place, rhs, cz, cx, cy, dg, above, below, yup, ydn, facelo, facehi, rimlo, rimhi,
     basis, message,
     store, faces, ysrc, sems,
 ):
     lane = lane_ids((8, 128))
-    keep_up, keep_dn = keep[0], keep[1]
-    n_x = 1 if above is below else 2
+    keep_up, keep_dn = keep_sides(swap, place)
+    n_x = 1 if swap else 2
 
     def put(f, z, l, t, value):
         store[f, z, l, 8 + 8 * t : 16 + 8 * t, :] = value
@@ -263,19 +301,19 @@
 
     lax.fori_loop(1, EZ - 1, coefficients, 0)
 
+    def slot(k):
+        return k * NRHS + (NRHS if k else 0)
+
     copies = []
 
     def send_block(k):
         copy = pltpu.make_async_copy(
-            store.at[pl.ds(k * NRHS + (NRHS if k else 0) * 1, NRHS), pl.ds(DEPTH, NZ), pl.ds(0, 2), pl.ds(8, NX), :],
+            store.at[pl.ds(slot(k), NRHS), pl.ds(DEPTH, NZ), pl.ds(0, 2), pl.ds(8, NX), :],
             basis.at[pl.ds(k * NRHS, NRHS)],
             sems.at[k],
         )
         copy.start()
         copies.append(copy)
-
-    def slot(k):
-        return k * NRHS + (NRHS if k else 0)
 
     send_block(0)
     for k in range(STEPS):
@@ -344,7 +382,7 @@
 def apply_rows(table, read, write):
     group = 5
     pieces = NX // 8
-    for g in range(COLS // group):
+    for g in reversed(range(COLS // group)):
         mine = range(group * g, group * g + group)
         sums = {i: None for i in mine}
         for j in range(group * g + group):
@@ -359,40 +397,44 @@
                 write(i, p, sums[i][p])
 
 
-def first_pass(cells, message, basis_hbm, first_hbm, next_message, factor_out, basis, table, sems):
-    load = pltpu.make_async_copy(basis_hbm, basis, sems.at[0])
-    load.start()
+def plane_copy(src, dst, sems, z):
+    return pltpu.make_async_copy(src.at[:, z], dst.at[:, z], sems.at[z])
+
+
+def first_pass(cells, message, basis_hbm, first_hbm, next_message, factor_out, basis, table, loads, saves):
+    for z in range(NZ):
+        plane_copy(basis_hbm, basis, loads, z).start()
     factor = factor_gram(message, cells)
     factor_out[...] = factor
     spread(factor, table)
-    load.wait()
-
-    def chunk(n, carry):
-        z, l = n // 2, n % 2
-
-        def read(j, p):
-            return basis[j, z, l, 8 * p : 8 * p + 8, :]
-
-        pending = []
-        apply_rows(table, read, lambda i, p, value: pending.append((i, p, value)))
-        for i, p, value in pending:
-            basis[i, z, l, 8 * p : 8 * p + 8, :] = value
+
+    def chunk(z, carry):
+        plane_copy(basis_hbm, basis, loads, z).wait()
+        for l in range(2):
+
+            def read(j, p):
+                return basis[j, z, l, 8 * p : 8 * p + 8, :]
+
+            def write(i, p, value):
+                basis[i, z, l, 8 * p : 8 * p + 8, :] = value
+
+            apply_rows(table, read, write)
+        plane_copy(basis, first_hbm, saves, z).start()
         return carry
 
-    lax.fori_loop(0, NZ * 2, chunk, 0)
-    save = pltpu.make_async_copy(basis, first_hbm, sems.at[1])
-    save.start()
+    lax.fori_loop(0, NZ, chunk, 0)
 
     def read(i, n):
         return basis[i, n // 8, (n // 4) % 2, pl.ds(pl.multiple_of(8 * (n % 4), 8), 8), :]
 
     gram_message(read, NZ * 8, next_message)
-    save.wait()
-
-
-def second_pass(cells, message, factor_one, first_hbm, out, triangle, first, table, sems):
-    load = pltpu.make_async_copy(first_hbm, first, sems.at[0])
-    load.start()
+    for z in range(NZ):
+        plane_copy(basis, first_hbm, saves, z).wait()
+
+
+def second_pass(cells, message, factor_one, first_hbm, out_hbm, triangle, first, out, table, loads, saves):
+    for z in range(NZ):
+        plane_copy(first_hbm, first, loads, z).start()
     factor = factor_gram(message, cells)
     spread(factor, table)
     lanes = lane_ids((24, 128))
@@ -401,9 +443,9 @@
         left, factor_one[...], (((1,), (0,)), ((), ())), precision=HIGHEST, preferred_element_type=F32
     )
     triangle[...] = product[0:COLS, 0:COLS]
-    load.wait()
 
     def chunk(z, carry):
+        plane_copy(first_hbm, first, loads, z).wait()
         for l in range(2):
 
             def read(j, p):
@@ -413,9 +455,12 @@
                 out[i, z, 8 * p : 8 * p + 8, 128 * l : 128 * l + 128] = value
 
             apply_rows(table, read, write)
+        plane_copy(out, out_hbm, saves, z).start()
         return carry
 
     lax.fori_loop(0, NZ, chunk, 0)
+    for z in range(NZ):
+        plane_copy(out, out_hbm, saves, z).wait()
 
 
 def shape(*dims):
@@ -440,32 +485,42 @@
     swap = n_x == 2
     fields = (rhs, coef_z, coef_x, coef_y, diag_term)
 
+    place = at_x.astype(jnp.int32).reshape(1)
     x_shape = shape(FIELDS, NZ // 2, 8, NY)
     face_shape = shape(FACE, NX, NY)
     zlo, zhi, *xmsgs = pl.pallas_call(
         functools.partial(pack_faces, swap),
         out_shape=(face_shape, face_shape) + (x_shape,) * (1 if swap else 2),
-        in_specs=[smem()] + [vmem()] * 5,
-        compiler_params=params(60),
-    )(at_x.astype(jnp.int32).reshape(1), *fields)
+        in_specs=[smem()] + [hbm()] * 5,
+        out_specs=(hbm(), hbm()) + (vmem(),) * (1 if swap else 2),
+        scratch_shapes=[
+            pltpu.VMEM((FIELDS, NZ, 8, NY), F32),
+            pltpu.VMEM((FIELDS, NZ, 8, NY), F32),
+            pltpu.SemaphoreType.DMA((4 * FIELDS,)),
+        ],
+        compiler_params=params(LIMIT),
+    )(place, *fields)
     facehi = move(zlo, "gz", -1)
     facelo = move(zhi, "gz", 1)
     if swap:
-        above = below = lax.ppermute(xmsgs[0], "gx", [(0, 1), (1, 0)])
-        x_parts = (above,)
-        keep = jnp.stack([1 - at_x, at_x]).astype(F32)
+        x_parts = (lax.ppermute(xmsgs[0], "gx", [(0, 1), (1, 0)]),)
     else:
-        above, below = move(xmsgs[0], "gx", -1), move(xmsgs[1], "gx", 1)
-        x_parts = (above, below)
-        keep = jnp.ones((2,), F32)
-
+        x_parts = (move(xmsgs[0], "gx", -1), move(xmsgs[1], "gx", 1))
+
+    own_shape = shape(NX, NY)
+    own_rims = pl.pallas_call(
+        pack_own_rims,
+        out_shape=(own_shape, own_shape),
+        in_specs=[vmem()] * 5,
+        compiler_params=params(LIMIT),
+    )(*fields)
     rim_shape = shape(ROWS, NY)
     ylo, yhi = pl.pallas_call(
-        pack_rims,
+        functools.partial(pack_rims, swap),
         out_shape=(rim_shape, rim_shape),
-        in_specs=[smem()] + [vmem()] * 7,
-        compiler_params=params(60),
-    )(keep, *fields, above, below)
+        in_specs=[smem()] + [vmem()] * (2 + len(x_parts)),
+        compiler_params=params(LIMIT),
+    )(place, *own_rims, *x_parts)
     yup, ydn = move(ylo, "gy", -1), move(yhi, "gy", 1)
 
     def rim(half):
@@ -477,10 +532,10 @@
 
     block = shape(COLS, NZ, 2, NX, 128)
 
-    def krylov_entry(keep, rhs, cz, cx, cy, dg, *rest):
+    def krylov_entry(place, rhs, cz, cx, cy, dg, *rest):
         if swap:
             rest = (rest[0],) + rest
-        krylov(keep, rhs, cz, cx, cy, dg, *rest)
+        krylov(swap, place, rhs, cz, cx, cy, dg, *rest)
 
     basis, message = pl.pallas_call(
         krylov_entry,
@@ -493,8 +548,8 @@
             pltpu.VMEM((2, 4, ROWS, 128), F32),
             pltpu.SemaphoreType.DMA((STEPS + 1,)),
         ],
-        compiler_params=params(60),
-    )(keep, *fields, *x_parts, yup, ydn, facelo, facehi, rimlo, rimhi)
+        compiler_params=params(LIMIT),
+    )(place, *fields, *x_parts, yup, ydn, facelo, facehi, rimlo, rimhi)
 
     message = exchange(message)
     first, message, factor_one = pl.pallas_call(
@@ -505,9 +560,10 @@
         scratch_shapes=[
             pltpu.VMEM(block.shape, F32),
             pltpu.VMEM((COLS, 24, 128), F32),
-            pltpu.SemaphoreType.DMA((2,)),
+            pltpu.SemaphoreType.DMA((NZ,)),
+            pltpu.SemaphoreType.DMA((NZ,)),
         ],
-        compiler_params=params(60),
+        compiler_params=params(LIMIT),
     )(message, basis)
 
     message = exchange(message)
@@ -515,13 +571,15 @@
         functools.partial(second_pass, cells),
         out_shape=(shape(COLS, NZ, NX, NY), shape(COLS, COLS)),
         in_specs=[vmem(), vmem(), hbm()],
-        out_specs=(vmem(), vmem()),
+        out_specs=(hbm(), vmem()),
         scratch_shapes=[
             pltpu.VMEM(block.shape, F32),
+            pltpu.VMEM((COLS, NZ, NX, NY), F32),
             pltpu.VMEM((COLS, 24, 128), F32),
-            pltpu.SemaphoreType.DMA((1,)),
+            pltpu.SemaphoreType.DMA((NZ,)),
+            pltpu.SemaphoreType.DMA((NZ,)),
         ],
-        compiler_params=params(60),
+        compiler_params=params(LIMIT),
     )(message, factor_one, first)
 
 

time: 123 us -> 171 us (1.39)
  Pallas kernels: 63.9 us -> 115 us
  starting transfers between devices: 17.1 us -> 18.9 us
    pallas_call x1, Pallas kernels: 2.92 us -> 59.7 us  [body(): pl.pallas_call(functools.partial(pack_faces, swap), out_shape=(face_shape...]
    pallas_call x1, Pallas kernels: 18.8 us -> 15.7 us  [body(): pl.pallas_call(functools.partial(first_pass, cells), out_shape=(block, sh...]
    pallas_call x1, Pallas kernels: 28.7 us -> 25.6 us  [body(): pl.pallas_call(krylov_entry, out_shape=(block, shape(devices, 8, 128)), i...]
    ppermute x6, starting transfers between devices: 14.1 us -> 15.9 us  [move(): return lax.ppermute(value, axis, pairs)]
    pallas_call x1 -> x2, Pallas kernels: 3 us -> 4.5 us  [the longest x1 2.7 us: body(): pl.pallas_call(pack_own_rims, out_shape=(own_shape, own_shape), in_specs=...]
  transfers between devices with their start and end apart: 7 -> 7, of which waited for: 3 -> 2; matrix products, arithmetic and copies ran while one was open for 1% -> 1% of each run, Pallas kernels for 2% -> 3%
where the time goes in v2:
time: 171 us; the launch traced here: 170 us
  Pallas kernels  115 us (67%)
  blocking collectives  23.4 us (14%)
  starting transfers between devices  18.9 us (11%)
  waiting for transfers between devices  10.3 us (6%)
  local copies, waits for them, and re-layouts  2.32 us (1%)
    pallas_call x1, Pallas kernels, body(): pl.pallas_call(functools.partial(pack_faces, swap), out_shape=(face_shape...  59.7 us
    pallas_call x1, Pallas kernels, body(): pl.pallas_call(krylov_entry, out_shape=(block, shape(devices, 8, 128)), i...  25.6 us
    all_to_all x2, blocking collectives, exchange(): return lax.all_to_all(messages, AXES, 0, 0, tiled=True)  23.4 us
    ppermute x6, starting transfers between devices, move(): return lax.ppermute(value, axis, pairs)  15.9 us
    pallas_call x1, Pallas kernels, body(): pl.pallas_call(functools.partial(first_pass, cells), out_shape=(block, sh...  15.7 us
    ppermute x6, waiting for transfers between devices, move(): return lax.ppermute(value, axis, pairs)  10.3 us
    pallas_call x1, Pallas kernels, body(): pl.pallas_call(functools.partial(second_pass, cells), out_shape=(shape(CO...  9.33 us
  transfers between devices with their start and end apart: 7, of which 2 were waited for; matrix products, arithmetic and copies ran while one was open for 1% of the time, Pallas kernels for 3%

profile of v2, /device:TPU:0, one launch (start us, length us, event | category | flops | bytes accessed | tf_op | source)
XLA Modules:
  0.0 170.4 jit_solution(9515553911308248694)
XLA Ops:
  0.6 59.7 %shard_map.68 = (f32[29,32,256]{2,1,0:T(8,128)}, f32[29,32,256]{2,1,0:T(8,128)}, f32[8,4,8,256]{3,2,1,0:T(8,128)}) custom-call(s32[1]{0:T(128)} %bitcast.place, f32[4,8,32,256]{3,2,1,0:T(8,128)} %rhs.5, f32[8,32,256]{2,1,0:T(8,128)} %cz.5, f32[8,32,256]{2,1,0:T(8,128)} %cx.5, f32[8,32,256]{2,1,0:T(8,128)} %cy.5, f32[8,32,256]{2,1,0:T(8,128)} %dg.5), custom_call_target="tpu_custom_call" | custom-call | tf_op jit(solution)/shard_map/pallas_call | solution.py:491
  60.3 3.0 %collective-permute-start = (f32[8,4,8,256]{3,2,1,0:T(8,128)}, f32[8,4,8,256]{3,2,1,0:T(8,128)S(1)}, u32[]{:S(2)}, u32[]{:S(2)}) collective-permute-start(f32[8,4,8,256]{3,2,1,0:T(8,128)} %get-tuple-element.14), channel_id=1, source_target_pairs={{0,16},{16,0},{1,17},{17,1},{2,18},{18,2},{3,19},{19,3},{4,20},{20... | collective-permute-start | bytes 786440 | tf_op jit(solution)/shard_map/ppermute | solution.py:506
  63.4 4.4 %collective-permute-start.3 = (f32[29,32,256]{2,1,0:T(8,128)}, f32[29,32,256]{2,1,0:T(8,128)}, u32[]{:S(2)}, u32[]{:S(2)}) collective-permute-start(f32[29,32,256]{2,1,0:T(8,128)} %get-tuple-element.19), channel_id=1, source_target_pairs={{0,1},{1,2},{2,3},{4,5},{5,6},{6,7},{8,9},{9,10},{10,11},{12,13},{... | collective-permute-start | bytes 2850824 | tf_op jit(solution)/shard_map/ppermute | solution.py:473
  67.8 1.3 collective-permute-start.4
  69.1 2.7 %shard_map.69 = (f32[32,256]{1,0:T(8,128)}, f32[32,256]{1,0:T(8,128)}) custom-call(f32[4,8,32,256]{3,2,1,0:T(8,128)} %rhs.5, f32[8,32,256]{2,1,0:T(8,128)} %cz.5, f32[8,32,256]{2,1,0:T(8,128)} %cx.5, f32[8,32,256]{2,1,0:T(8,128)} %cy.5, f32[8,32,256]{2,1,0:T(8,128)} %dg.5), custom_call_target="tpu_custom_call" | custom-call | tf_op jit(solution)/shard_map/pallas_call | solution.py:511
  71.8 0.0 collective-permute-done.refs_0_.rest_0_
  71.8 0.0 copy-start
  71.8 0.7 copy-done
  72.5 1.8 %shard_map.70 = (f32[40,256]{1,0:T(8,128)}, f32[40,256]{1,0:T(8,128)}) custom-call(s32[1]{0:T(128)} %bitcast.place, f32[32,256]{1,0:T(8,128)} %get-tuple-element.15.ylo_own, f32[32,256]{1,0:T(8,128)} %get-tuple-element.16.yhi_own, f32[8,4,8,256]{3,2,1,0:T(8,128)} %copy-done), custom_call_target="tpu_custom_call" | custom-call | tf_op jit(solution)/shard_map/pallas_call | solution.py:518
  74.3 1.3 collective-permute-start.1
  75.6 3.0 %collective-permute-start.2 = (f32[40,256]{1,0:T(8,128)}, f32[40,256]{1,0:T(8,128)S(1)}, u32[]{:S(2)}, u32[]{:S(2)}) collective-permute-start(f32[40,256]{1,0:T(8,128)} %get-tuple-element.18), channel_id=1, source_target_pairs={{0,4},{4,8},{8,12},{1,5},{5,9},{9,13},{2,6},{6,10},{10,14},{3,7},{... | collective-permute-start | bytes 122888 | tf_op jit(solution)/shard_map/ppermute | solution.py:473
  78.6 1.0 fusion
  79.6 0.0 collective-permute-done.1.rest_1_
  79.6 0.0 copy-start.3
  79.6 0.0 collective-permute-done.2.rest_2_
  79.7 0.0 copy-start.4
  79.7 4.6 %collective-permute-start.5 = (f32[168,256]{1,0:T(8,128)S(1)}, f32[168,256]{1,0:T(8,128)S(1)}, u32[]{:S(2)}, u32[]{:S(2)}) collective-permute-start(f32[168,256]{1,0:T(8,128)S(1)} %maximum_maximum_fusion), channel_id=1, source_target_pairs={{0,1},{1,2},{2,3},{4,5},{5,6},{6,7},{8,9},{9,10},{10,11},{12,13},{... | collective-permute-start | bytes 516104 | tf_op jit(solution)/shard_map/ppermute | solution.py:473
  84.3 1.3 collective-permute-start.6
  85.6 5.2 %collective-permute-done.5.rest_5_ = f32[168,256]{1,0:T(8,128)S(1)} collective-permute-done((f32[168,256]{1,0:T(8,128)S(1)}, f32[168,256]{1,0:T(8,128)S(1)}, u32[]{:S(2)}, u32[]{:S(2)}) %collective-permute-start.5) | collective-permute-done | bytes 172064 | tf_op jit(solution)/shard_map/ppermute | solution.py:473
  90.7 0.0 copy-start.1
  90.7 5.0 %collective-permute-done.6.rest_6_ = f32[168,256]{1,0:T(8,128)S(1)} collective-permute-done((f32[168,256]{1,0:T(8,128)S(1)}, f32[168,256]{1,0:T(8,128)S(1)}, u32[]{:S(2)}, u32[]{:S(2)}) %collective-permute-start.6) | collective-permute-done | bytes 172064 | tf_op jit(solution)/shard_map/ppermute | solution.py:473
  95.8 0.0 copy-start.2
  95.8 0.0 collective-permute-done.3.rest_3_
  95.8 0.0 collective-permute-done.4.rest_4_
  95.8 0.0 copy-done.3
  95.8 0.0 copy-done.4
  95.8 0.0 copy-done.1
  95.8 0.6 copy-done.2
  96.4 25.6 %shard_map.71 = (f32[20,8,2,32,128]{4,3,2,1,0:T(8,128)}, f32[32,8,128]{2,1,0:T(8,128)}) custom-call(s32[1]{0:T(128)} %bitcast.place, f32[4,8,32,256]{3,2,1,0:T(8,128)} %rhs.5, f32[8,32,256]{2,1,0:T(8,128)} %cz.5, f32[8,32,256]{2,1,0:T(8,128)} %cx.5, f32[8,32,256]{2,1,0:T(8,128)} %cy.5, f32[8,32,256]{2,1,0:T(8,128)} %dg.5, f32[8,4,8,256]{3,2,1,0:T(8,128)} %copy-done, ...), custom_call_target="tpu_custom_call" | custom-call | tf_op jit(solution)/shard_map/pallas_call | solution.py:540
  122.0 11.7 %all_to_all.10.message = f32[32,8,128]{2,1,0:T(8,128)} all-to-all(f32[32,8,128]{2,1,0:T(8,128)} %get-tuple-element.21), channel_id=1, replica_groups=mesh['gx'=2,'gy'=4,'gz'=4] {'gx','gy','gz'}, dimensions={0} | all-to-all | bytes 262144 | tf_op jit(solution)/shard_map/all_to_all | solution.py:477
  133.7 15.7 %shard_map.72 = (f32[20,8,2,32,128]{4,3,2,1,0:T(8,128)}, f32[32,8,128]{2,1,0:T(8,128)}, f32[24,128]{1,0:T(8,128)}) custom-call(f32[32,8,128]{2,1,0:T(8,128)} %all_to_all.10.message, f32[20,8,2,32,128]{4,3,2,1,0:T(8,128)} %get-tuple-element.22.basis_hbm), custom_call_target="tpu_custom_call" | custom-call | tf_op jit(solution)/shard_map/pallas_call | solution.py:555
  149.4 11.7 %all_to_all.11.message = f32[32,8,128]{2,1,0:T(8,128)} all-to-all(f32[32,8,128]{2,1,0:T(8,128)} %get-tuple-element.23), channel_id=1, replica_groups=mesh['gx'=2,'gy'=4,'gz'=4] {'gx','gy','gz'}, dimensions={0} | all-to-all | bytes 262144 | tf_op jit(solution)/shard_map/all_to_all | solution.py:477
  161.1 9.3 %shard_map.73 = (f32[20,8,32,256]{3,2,1,0:T(8,128)}, f32[20,20]{1,0:T(8,128)}) custom-call(f32[32,8,128]{2,1,0:T(8,128)} %all_to_all.11.message, f32[24,128]{1,0:T(8,128)} %get-tuple-element.24.factor_one, f32[20,8,2,32,128]{4,3,2,1,0:T(8,128)} %get-tuple-element.25.first_hbm), custom_call_target="tpu_custom_call" | custom-call | tf_op jit(solution)/shard_map/pallas_call | solution.py:570
  (4 shorter events, 0.0 us)
Async XLA Ops:
  60.3 11.4 %collective-permute-start = (f32[8,4,8,256]{3,2,1,0:T(8,128)}, f32[8,4,8,256]{3,2,1,0:T(8,128)S(1)}, u32[]{:S(2)}, u32[]{:S(2)}) collective-permute-start(f32[8,4,8,256]{3,2,1,0:T(8,128)} %get-tuple-element.14), channel_id=1, source_target_pairs={{0,16},{16,0},{1,17},{17,1},{2,18},{18,2},{3,19},{19,3},{4,20},{20... | collective-permute-start | bytes 786440 | tf_op jit(solution)/shard_map/ppermute | solution.py:506
  63.4 32.4 %collective-permute-start.3 = (f32[29,32,256]{2,1,0:T(8,128)}, f32[29,32,256]{2,1,0:T(8,128)}, u32[]{:S(2)}, u32[]{:S(2)}) collective-permute-start(f32[29,32,256]{2,1,0:T(8,128)} %get-tuple-element.19), channel_id=1, source_target_pairs={{0,1},{1,2},{2,3},{4,5},{5,6},{6,7},{8,9},{9,10},{10,11},{12,13},{... | collective-permute-start | bytes 2850824 | tf_op jit(solution)/shard_map/ppermute | solution.py:473
  67.8 28.0 %collective-permute-start.4 = (f32[29,32,256]{2,1,0:T(8,128)}, f32[29,32,256]{2,1,0:T(8,128)}, u32[]{:S(2)}, u32[]{:S(2)}) collective-permute-start(f32[29,32,256]{2,1,0:T(8,128)} %get-tuple-element.20), channel_id=1, source_target_pairs={{1,0},{2,1},{3,2},{5,4},{6,5},{7,6},{9,8},{10,9},{11,10},{13,12},{... | collective-permute-start | bytes 2850824 | tf_op jit(solution)/shard_map/ppermute | solution.py:473
  71.8 0.7 copy-start
  74.3 5.3 %collective-permute-start.1 = (f32[40,256]{1,0:T(8,128)}, f32[40,256]{1,0:T(8,128)S(1)}, u32[]{:S(2)}, u32[]{:S(2)}) collective-permute-start(f32[40,256]{1,0:T(8,128)} %get-tuple-element.17), channel_id=1, source_target_pairs={{4,0},{8,4},{12,8},{5,1},{9,5},{13,9},{6,2},{10,6},{14,10},{7,3},{... | collective-permute-start | bytes 122888 | tf_op jit(solution)/shard_map/ppermute | solution.py:473
  75.6 4.1 %collective-permute-start.2 = (f32[40,256]{1,0:T(8,128)}, f32[40,256]{1,0:T(8,128)S(1)}, u32[]{:S(2)}, u32[]{:S(2)}) collective-permute-start(f32[40,256]{1,0:T(8,128)} %get-tuple-element.18), channel_id=1, source_target_pairs={{0,4},{4,8},{8,12},{1,5},{5,9},{9,13},{2,6},{6,10},{10,14},{3,7},{... | collective-permute-start | bytes 122888 | tf_op jit(solution)/shard_map/ppermute | solution.py:473
  79.6 16.2 %copy-start.3 = (f32[40,256]{1,0:T(8,128)}, f32[40,256]{1,0:T(8,128)S(1)}, u32[]{:S(2)}) copy-start(f32[40,256]{1,0:T(8,128)S(1)} %collective-permute-done.1.rest_1_) | copy-start | bytes 122884
  79.7 16.2 %copy-start.4 = (f32[40,256]{1,0:T(8,128)}, f32[40,256]{1,0:T(8,128)S(1)}, u32[]{:S(2)}) copy-start(f32[40,256]{1,0:T(8,128)S(1)} %collective-permute-done.2.rest_2_) | copy-start | bytes 122884
  79.7 11.1 %collective-permute-start.5 = (f32[168,256]{1,0:T(8,128)S(1)}, f32[168,256]{1,0:T(8,128)S(1)}, u32[]{:S(2)}, u32[]{:S(2)}) collective-permute-start(f32[168,256]{1,0:T(8,128)S(1)} %maximum_maximum_fusion), channel_id=1, source_target_pairs={{0,1},{1,2},{2,3},{4,5},{5,6},{6,7},{8,9},{9,10},{10,11},{12,13},{... | collective-permute-start | bytes 516104 | tf_op jit(solution)/shard_map/ppermute | solution.py:473
  84.3 11.5 %collective-permute-start.6 = (f32[168,256]{1,0:T(8,128)S(1)}, f32[168,256]{1,0:T(8,128)S(1)}, u32[]{:S(2)}, u32[]{:S(2)}) collective-permute-start(f32[168,256]{1,0:T(8,128)S(1)} %maximum_maximum_fusion.1), channel_id=1, source_target_pairs={{1,0},{2,1},{3,2},{5,4},{6,5},{7,6},{9,8},{10,9},{11,10},{13,12},{... | collective-permute-start | bytes 516104 | tf_op jit(solution)/shard_map/ppermute | solution.py:473
  90.7 5.1 %copy-start.1 = (f32[168,256]{1,0:T(8,128)}, f32[168,256]{1,0:T(8,128)S(1)}, u32[]{:S(2)}) copy-start(f32[168,256]{1,0:T(8,128)S(1)} %collective-permute-done.5.rest_5_) | copy-start | bytes 516100
  95.8 0.6 copy-start.2

commit v3 on v2

--- a/solution.py
+++ b/solution.py
@@ -56,33 +56,33 @@
 
 
 def pack_faces(swap, place, rhs, cz, cx, cy, dg, zlo, zhi, *rest):
-    xmsgs, (first_rows, last_rows, sems) = rest[:-3], rest[-3:]
-    edges = []
-    planes = []
-    n = at = 0
+    xmsgs, (whole, loads, saves) = rest[:-3], rest[-3:]
+    copies = []
     for f in range(FIELDS):
         src = rhs.at[f] if f < NRHS else (cz, cx, cy, dg)[f - NRHS]
+        copies.append(pltpu.make_async_copy(src, whole.at[f], loads.at[f]))
+        copies[-1].start()
+    low = row_ids((8, NY)) < 4
+    up = place[0] == 0
+    planes = []
+    at = 0
+    for f in range(FIELDS):
+        copies[f].wait()
         depth = DEPTH if f <= NRHS else DEPTH - 1
-        for side, rows, out in ((0, first_rows, zlo), (1, last_rows, zhi)):
-            edges.append(pltpu.make_async_copy(src.at[:, pl.ds(side * (NX - 8), 8), :], rows.at[f], sems.at[n]))
+        for side, out in ((0, zlo), (1, zhi)):
             start = side * (NZ - depth)
             planes.append(
-                pltpu.make_async_copy(src.at[pl.ds(start, depth)], out.at[pl.ds(at, depth)], sems.at[n + 1])
+                pltpu.make_async_copy(
+                    whole.at[f, pl.ds(start, depth)], out.at[pl.ds(at, depth)], saves.at[2 * f + side]
+                )
             )
-            n += 2
+            planes[-1].start()
         at += depth
-    for copy in edges:
-        copy.start()
-    for copy in planes:
-        copy.start()
-    for copy in edges:
-        copy.wait()
-    low = row_ids((8, NY)) < 4
-    up = place[0] == 0
     for f in range(FIELDS):
         for m in range(NZ // 2):
-            first = jnp.where(low, first_rows[f, 2 * m], pltpu.roll(first_rows[f, 2 * m + 1], 4, 0))
-            last = jnp.where(low, pltpu.roll(last_rows[f, 2 * m], 4, 0), last_rows[f, 2 * m + 1])
+            a, b = whole.at[f, 2 * m], whole.at[f, 2 * m + 1]
+            first = jnp.where(low, a[0:8], pltpu.roll(b[0:8], 4, 0))
+            last = jnp.where(low, pltpu.roll(a[NX - 8 : NX], 4, 0), b[NX - 8 : NX])
             if swap:
                 xmsgs[0][f, m] = jnp.where(up, last, first)
             else:
@@ -150,53 +150,83 @@
             )
 
 
-def gather_rows(values):
-    rows = row_ids((8, 128))
-    width = 1
-    while len(values) > 1:
-        low = (rows & width) == 0
-        merged = []
-        for a, b in zip(values[0::2], values[1::2]):
-            if a is None and b is None:
-                merged.append(None)
-                continue
-            a = jnp.zeros((8, 128), F32) if a is None else a
-            b = jnp.zeros((8, 128), F32) if b is None else b
-            merged.append(jnp.where(low, a, b) + pltpu.roll(jnp.where(low, b, a), width, 0))
-        values = merged
-        width *= 2
-    return values[0]
-
-
-def gram_message(read, count, out, unroll=8):
-    lanes = lane_ids((8, 128))
-    result = jnp.zeros((8, 128), F32)
-    for tile in range(0, COLS, 8):
-        mine = range(tile, min(tile + 8, COLS))
-        columns = [mine] + [range(c, c + 4) for c in range(tile + 8, COLS, 4)]
-        for group in columns:
-            pairs = [(i, j) for j in group for i in mine if i <= j]
-
-            def step(n, sums):
-                rows = {i: read(i, n) for i in sorted({i for pair in pairs for i in pair})}
-                return tuple(s + rows[i] * rows[j] for s, (i, j) in zip(sums, pairs))
-
-            sums = lax.fori_loop(
-                0, count, step, tuple(jnp.zeros((8, 128), F32) for _ in pairs), unroll=unroll
-            )
-            sums = dict(zip(pairs, sums))
-            for j in group:
-                total = gather_rows([sums.get((tile + s, j)) for s in range(8)])
-                total = jnp.sum(total, axis=1, keepdims=True)
-                result = jnp.where(lanes == 4 * tile + j, jnp.broadcast_to(total, (8, 128)), result)
+STACK = 8 * COLS
+
+
+def gram_zero(accs):
+    accs[...] = jnp.zeros_like(accs)
+
+
+def gram_add(stacks, accs):
+    left, right = [], []
+    cross_left, cross_right = [], []
+    for stack in stacks:
+        high = stack.astype(jnp.bfloat16)
+        rest = stack - high.astype(F32)
+        mid = rest.astype(jnp.bfloat16)
+        low = (rest - mid.astype(F32)).astype(jnp.bfloat16)
+        left += [high, mid]
+        cross_left += [high, high]
+        cross_right += [mid, low]
+    contract = (((1,), (1,)), ((), ()))
+
+    def product(a, b):
+        return lax.dot_general(jnp.concatenate(a, 1), jnp.concatenate(b, 1), contract, preferred_element_type=F32)
+
+    accs[0] += product(left, left)
+    accs[1] += product(cross_left, cross_right)
+
+
+def gram_message(accs, out):
+    same = (row_ids((STACK, STACK)) & 7) == (lane_ids((STACK, STACK)) & 7)
+    pick = jnp.where((row_ids((STACK, 128)) >> 3) == lane_ids((STACK, 128)), 1.0, 0.0)
+
+    def traces(product):
+        picked = jnp.where(same, product, 0.0)
+        rows = [jnp.sum(picked[8 * i : 8 * i + 8], axis=0, keepdims=True) for i in range(COLS)]
+        rows = jnp.concatenate(rows + [jnp.zeros((128 - COLS, STACK), F32)], 0)
+        return lax.dot_general(
+            rows, pick, (((1,), (0,)), ((), ())), precision=HIGHEST, preferred_element_type=F32
+        )
+
+    cross = traces(accs[1])
+    gram = traces(accs[0]) + cross + cross.T
+    tops = [gram[8 * k : 8 * k + 8] for k in range(3)]
+    rows, lanes = row_ids((8, 128)), lane_ids((8, 128))
+    tile = jnp.where(lanes < COLS, tops[0], pltpu.roll(tops[1], 12, 1))
+    corner = pltpu.roll(pltpu.roll(tops[2], 128 - 16, 1), 4, 0)
+    tile = jnp.where((rows >= 4) & (lanes < 4), corner, tile)
+    packed = tile
+    for q in range(1, 4):
+        turned = pltpu.roll(pltpu.roll(tile, 32 * q, 1), 8 - 2 * q, 0)
+        packed = jnp.where((lanes >> 5) == q, turned, packed)
+    packed = packed[0:2]
     for n in range(out.shape[0]):
-        out[n] = result
+        out[n] = packed
+
+
+def gram_of(messages):
+    total = messages[0]
+    for n in range(1, messages.shape[0]):
+        total = total + messages[n]
+    total = jnp.concatenate([total] * 4, 0)
+    rows, lanes = row_ids((8, 128)), lane_ids((8, 128))
+    tile = total
+    for q in range(1, 4):
+        tile = jnp.where((rows >> 1) == q, pltpu.roll(total, 128 - 32 * q, 1), tile)
+    corner = pltpu.roll(pltpu.roll(tile, 4, 0), 16, 1)
+    tops = [
+        jnp.where((lanes < COLS) & (lanes >= rows), tile, 0.0),
+        jnp.where((lanes < COLS) & (lanes >= rows + 8), pltpu.roll(tile, 128 - 12, 1), 0.0),
+        jnp.where((lanes < COLS) & (lanes >= rows + 16), corner, 0.0),
+    ]
+    return jnp.concatenate(tops, 0)
 
 
 def krylov(
     swap, place, rhs, cz, cx, cy, dg, above, below, yup, ydn, facelo, facehi, rimlo, rimhi,
     basis, message,
-    store, faces, ysrc, sems,
+    store, faces, ysrc, accs, sems,
 ):
     lane = lane_ids((8, 128))
     keep_up, keep_dn = keep_sides(swap, place)
@@ -343,40 +373,51 @@
         lax.fori_loop(k + 1, EZ - 1 - k, apply, 0)
         send_block(k + 1)
 
-    def read(i, n):
-        f = slot(i // NRHS) + i % NRHS
-        return store[f, DEPTH + n // 8, (n // 4) % 2, pl.ds(pl.multiple_of(8 + 8 * (n % 4), 8), 8), :]
-
-    gram_message(read, NZ * 8, message)
+    gram_zero(accs)
+
+    def products(z, carry):
+        def tile(i, t):
+            f = slot(i // NRHS) + i % NRHS
+            return jnp.concatenate([store[f, z, l, 8 + 8 * t : 16 + 8 * t, :] for l in range(2)], 1)
+
+        gram_add([jnp.concatenate([tile(i, t) for i in range(COLS)], 0) for t in range(NX // 8)], accs)
+        return carry
+
+    lax.fori_loop(DEPTH, DEPTH + NZ, products, 0)
+    gram_message(accs, message)
     for copy in copies:
         copy.wait()
 
 
-def factor_gram(messages, cells):
+def factor_gram(messages, cells, table):
     rows = row_ids((24, 128))
     lanes = lane_ids((24, 128))
-    message = messages[0]
-    for n in range(1, messages.shape[0]):
-        message = message + messages[n]
-    upper = jnp.concatenate([message] + [pltpu.roll(message, 128 - 32 * k, 1) for k in (1, 2)], 0)
-    upper = jnp.where((lanes < COLS) & (rows < COLS), upper, 0.0)
-    square = jnp.concatenate([upper, jnp.zeros((104, 128), F32)], 0)
-    a = jnp.where(rows <= lanes, upper, square.T[0:24, :]) / cells
-    a = jnp.where((lanes == rows + 32) & (rows < COLS), 1.0, a)
-    for j in range(COLS - 1):
-        column = jnp.broadcast_to(a[:, j : j + 1], (24, 128))
-        row = jnp.broadcast_to(a[j : j + 1, :], (24, 128))
-        pivot = jnp.broadcast_to(column[j : j + 1, :], (24, 128))
-        a = a - jnp.where(rows > j, column / pivot, 0.0) * row
-    diag = jnp.sum(jnp.where(lanes == rows, a, 0.0), axis=1, keepdims=True)
-    diag = jnp.where(rows < COLS, jnp.broadcast_to(diag, (24, 128)), 1.0)
-    a = a / jnp.sqrt(diag)
-    return jnp.where((lanes >= rows) & (lanes < COLS) | (lanes >= 32) & (lanes <= rows + 32), a, 0.0)
-
-
-def spread(factor, table):
+    upper = gram_of(messages) / cells
+    square = jnp.concatenate([upper, jnp.zeros((104, 128), F32)], 0).T
+    whole = jnp.where(rows <= lanes, upper, square[0:24, :])
+
+    def splat(value):
+        return jnp.broadcast_to(value, (24, 128))
+
+    columns = [splat(whole[:, c : c + 1]) for c in range(COLS)]
+    inverse = [jnp.where(rows == c, 1.0, 0.0) for c in range(COLS)]
+    pivots = jnp.ones((24, 128), F32)
+    factor = jnp.zeros((24, 128), F32)
     for j in range(COLS):
-        table[j] = jnp.broadcast_to(factor[:, 32 + j : 33 + j], (24, 128))
+        pivot = splat(columns[j][j : j + 1, :])
+        pivots = jnp.where(rows == j, pivot, pivots)
+        below = jnp.where(rows > j, columns[j] / pivot, 0.0)
+        for c in range(j, COLS):
+            row = splat(columns[c][j : j + 1, :])
+            factor = jnp.where((rows == j) & (lanes == c), row, factor)
+            if c > j:
+                columns[c] = columns[c] - below * row
+        for c in range(j + 1):
+            inverse[c] = inverse[c] - below * splat(inverse[c][j : j + 1, :])
+    roots = jnp.sqrt(pivots)
+    for c in range(COLS):
+        table[c] = inverse[c] / roots
+    return factor / roots
 
 
 def apply_rows(table, read, write):
@@ -401,12 +442,11 @@
     return pltpu.make_async_copy(src.at[:, z], dst.at[:, z], sems.at[z])
 
 
-def first_pass(cells, message, basis_hbm, first_hbm, next_message, factor_out, basis, table, loads, saves):
+def first_pass(cells, message, basis_hbm, first_hbm, next_message, factor_out, basis, table, accs, loads, saves):
     for z in range(NZ):
         plane_copy(basis_hbm, basis, loads, z).start()
-    factor = factor_gram(message, cells)
-    factor_out[...] = factor
-    spread(factor, table)
+    factor_out[...] = factor_gram(message, cells, table)
+    gram_zero(accs)
 
     def chunk(z, carry):
         plane_copy(basis_hbm, basis, loads, z).wait()
@@ -420,14 +460,16 @@
 
             apply_rows(table, read, write)
         plane_copy(basis, first_hbm, saves, z).start()
+
+        def tile(i, t):
+            return jnp.concatenate([basis[i, z, l, 8 * t : 8 * t + 8, :] for l in range(2)], 1)
+
+        gram_add([jnp.concatenate([tile(i, t) for i in range(COLS)], 0) for t in range(NX // 8)], accs)
         return carry
 
     lax.fori_loop(0, NZ, chunk, 0)
 
-    def read(i, n):
-        return basis[i, n // 8, (n // 4) % 2, pl.ds(pl.multiple_of(8 * (n % 4), 8), 8), :]
-
-    gram_message(read, NZ * 8, next_message)
+    gram_message(accs, next_message)
     for z in range(NZ):
         plane_copy(basis, first_hbm, saves, z).wait()
 
@@ -435,10 +477,7 @@
 def second_pass(cells, message, factor_one, first_hbm, out_hbm, triangle, first, out, table, loads, saves):
     for z in range(NZ):
         plane_copy(first_hbm, first, loads, z).start()
-    factor = factor_gram(message, cells)
-    spread(factor, table)
-    lanes = lane_ids((24, 128))
-    left = jnp.where(lanes < COLS, factor, 0.0)[:, 0:24]
+    left = factor_gram(message, cells, table)[:, 0:24]
     product = lax.dot_general(
         left, factor_one[...], (((1,), (0,)), ((), ())), precision=HIGHEST, preferred_element_type=F32
     )
@@ -494,9 +533,9 @@
         in_specs=[smem()] + [hbm()] * 5,
         out_specs=(hbm(), hbm()) + (vmem(),) * (1 if swap else 2),
         scratch_shapes=[
-            pltpu.VMEM((FIELDS, NZ, 8, NY), F32),
-            pltpu.VMEM((FIELDS, NZ, 8, NY), F32),
-            pltpu.SemaphoreType.DMA((4 * FIELDS,)),
+            pltpu.VMEM((FIELDS, NZ, NX, NY), F32),
+            pltpu.SemaphoreType.DMA((FIELDS,)),
+            pltpu.SemaphoreType.DMA((2 * FIELDS,)),
         ],
         compiler_params=params(LIMIT),
     )(place, *fields)
@@ -539,13 +578,14 @@
 
     basis, message = pl.pallas_call(
         krylov_entry,
-        out_shape=(block, shape(devices, 8, 128)),
+        out_shape=(block, shape(devices, 2, 128)),
         in_specs=[smem()] + [vmem()] * (5 + len(x_parts) + 6),
         out_specs=(hbm(), vmem()),
         scratch_shapes=[
             pltpu.VMEM((COLS + NRHS, EZ, LT, EROWS, 128), F32),
             pltpu.VMEM((7, EZ, LT, ROWS, 128), F32),
             pltpu.VMEM((2, 4, ROWS, 128), F32),
+            pltpu.VMEM((2, STACK, STACK), F32),
             pltpu.SemaphoreType.DMA((STEPS + 1,)),
         ],
         compiler_params=params(LIMIT),
@@ -554,12 +594,13 @@
     message = exchange(message)
     first, message, factor_one = pl.pallas_call(
         functools.partial(first_pass, cells),
-        out_shape=(block, shape(devices, 8, 128), shape(24, 128)),
+        out_shape=(block, shape(devices, 2, 128), shape(24, 128)),
         in_specs=[vmem(), hbm()],
         out_specs=(hbm(), vmem(), vmem()),
         scratch_shapes=[
             pltpu.VMEM(block.shape, F32),
             pltpu.VMEM((COLS, 24, 128), F32),
+            pltpu.VMEM((2, STACK, STACK), F32),
             pltpu.SemaphoreType.DMA((NZ,)),
             pltpu.SemaphoreType.DMA((NZ,)),
         ],

time: 171 us -> 103 us (0.60)
  Pallas kernels: 115 us -> 49.2 us
  blocking collectives: 23.4 us -> 21.1 us
    pallas_call x1, Pallas kernels: 59.7 us -> 3.09 us  [body(): pl.pallas_call(functools.partial(pack_faces, swap), out_shape=(face_shape...]
    pallas_call x1, Pallas kernels: 15.7 us -> 10.6 us  [body(): pl.pallas_call(functools.partial(first_pass, cells), out_shape=(block, sh...]
    pallas_call x1, Pallas kernels: 25.6 us -> 23.1 us  [body(): pl.pallas_call(krylov_entry, out_shape=(block, shape(devices, 2, 128)), i...]
    all_to_all x2, blocking collectives: 23.4 us -> 21.1 us  [exchange(): return lax.all_to_all(messages, AXES, 0, 0, tiled=True)]
  transfers between devices with their start and end apart: 7 -> 7, of which waited for: 2 -> 2; matrix products, arithmetic and copies ran while one was open for 1% -> 1% of each run, Pallas kernels for 3% -> 4%
where the time goes in v3:
time: 103 us
  Pallas kernels  49.2 us (48%)
  blocking collectives  21.1 us (20%)
  starting transfers between devices  18.9 us (18%)
  waiting for transfers between devices  10.3 us (10%)
  local copies, waits for them, and re-layouts  2.32 us (2%)
    pallas_call x1, Pallas kernels, body(): pl.pallas_call(krylov_entry, out_shape=(block, shape(devices, 2, 128)), i...  23.1 us
    all_to_all x2, blocking collectives, exchange(): return lax.all_to_all(messages, AXES, 0, 0, tiled=True)  21.1 us
    ppermute x6, starting transfers between devices, move(): return lax.ppermute(value, axis, pairs)  15.9 us
    pallas_call x1, Pallas kernels, body(): pl.pallas_call(functools.partial(first_pass, cells), out_shape=(block, sh...  10.6 us
    ppermute x6, waiting for transfers between devices, move(): return lax.ppermute(value, axis, pairs)  10.3 us
    pallas_call x1, Pallas kernels, body(): pl.pallas_call(functools.partial(second_pass, cells), out_shape=(shape(CO...  7.86 us
    pallas_call x1, Pallas kernels, body(): pl.pallas_call(functools.partial(pack_faces, swap), out_shape=(face_shape...  3.09 us
    ppermute x1, starting transfers between devices, body(): x_parts = (lax.ppermute(xmsgs[0], 'gx', [(0, 1), (1, 0)]),)  3.03 us
  transfers between devices with their start and end apart: 7, of which 2 were waited for; matrix products, arithmetic and copies ran while one was open for 1% of the time, Pallas kernels for 4%

profile of v3, /device:TPU:0, one launch (start us, length us, event | category | flops | bytes accessed | tf_op | source)
XLA Modules:
  0.0 102.6 jit_solution(3857638815928937244)
XLA Ops:
  0.6 3.1 %shard_map.68 = (f32[29,32,256]{2,1,0:T(8,128)}, f32[29,32,256]{2,1,0:T(8,128)}, f32[8,4,8,256]{3,2,1,0:T(8,128)}) custom-call(s32[1]{0:T(128)} %bitcast.place, f32[4,8,32,256]{3,2,1,0:T(8,128)} %rhs.5, f32[8,32,256]{2,1,0:T(8,128)} %cz.5, f32[8,32,256]{2,1,0:T(8,128)} %cx.5, f32[8,32,256]{2,1,0:T(8,128)} %cy.5, f32[8,32,256]{2,1,0:T(8,128)} %dg.5), custom_call_target="tpu_custom_call" | custom-call | tf_op jit(solution)/shard_map/pallas_call | solution.py:530
  3.7 3.0 %collective-permute-start = (f32[8,4,8,256]{3,2,1,0:T(8,128)}, f32[8,4,8,256]{3,2,1,0:T(8,128)S(1)}, u32[]{:S(2)}, u32[]{:S(2)}) collective-permute-start(f32[8,4,8,256]{3,2,1,0:T(8,128)} %get-tuple-element.14), channel_id=1, source_target_pairs={{0,16},{16,0},{1,17},{17,1},{2,18},{18,2},{3,19},{19,3},{4,20},{20... | collective-permute-start | bytes 786440 | tf_op jit(solution)/shard_map/ppermute | solution.py:545
  6.8 4.4 %collective-permute-start.3 = (f32[29,32,256]{2,1,0:T(8,128)}, f32[29,32,256]{2,1,0:T(8,128)}, u32[]{:S(2)}, u32[]{:S(2)}) collective-permute-start(f32[29,32,256]{2,1,0:T(8,128)} %get-tuple-element.19), channel_id=1, source_target_pairs={{0,1},{1,2},{2,3},{4,5},{5,6},{6,7},{8,9},{9,10},{10,11},{12,13},{... | collective-permute-start | bytes 2850824 | tf_op jit(solution)/shard_map/ppermute | solution.py:512
  11.2 1.3 %collective-permute-start.4 = (f32[29,32,256]{2,1,0:T(8,128)}, f32[29,32,256]{2,1,0:T(8,128)}, u32[]{:S(2)}, u32[]{:S(2)}) collective-permute-start(f32[29,32,256]{2,1,0:T(8,128)} %get-tuple-element.20), channel_id=1, source_target_pairs={{1,0},{2,1},{3,2},{5,4},{6,5},{7,6},{9,8},{10,9},{11,10},{13,12},{... | collective-permute-start | bytes 2850824 | tf_op jit(solution)/shard_map/ppermute | solution.py:512
  12.5 2.7 %shard_map.69 = (f32[32,256]{1,0:T(8,128)}, f32[32,256]{1,0:T(8,128)}) custom-call(f32[4,8,32,256]{3,2,1,0:T(8,128)} %rhs.5, f32[8,32,256]{2,1,0:T(8,128)} %cz.5, f32[8,32,256]{2,1,0:T(8,128)} %cx.5, f32[8,32,256]{2,1,0:T(8,128)} %cy.5, f32[8,32,256]{2,1,0:T(8,128)} %dg.5), custom_call_target="tpu_custom_call" | custom-call | tf_op jit(solution)/shard_map/pallas_call | solution.py:550
  15.2 0.0 collective-permute-done.refs_0_.rest_0_
  15.2 0.0 copy-start
  15.2 0.7 copy-done
  15.9 1.8 %shard_map.70 = (f32[40,256]{1,0:T(8,128)}, f32[40,256]{1,0:T(8,128)}) custom-call(s32[1]{0:T(128)} %bitcast.place, f32[32,256]{1,0:T(8,128)} %get-tuple-element.15.ylo_own, f32[32,256]{1,0:T(8,128)} %get-tuple-element.16.yhi_own, f32[8,4,8,256]{3,2,1,0:T(8,128)} %copy-done), custom_call_target="tpu_custom_call" | custom-call | tf_op jit(solution)/shard_map/pallas_call | solution.py:557
  17.7 1.3 %collective-permute-start.1 = (f32[40,256]{1,0:T(8,128)}, f32[40,256]{1,0:T(8,128)S(1)}, u32[]{:S(2)}, u32[]{:S(2)}) collective-permute-start(f32[40,256]{1,0:T(8,128)} %get-tuple-element.17), channel_id=1, source_target_pairs={{4,0},{8,4},{12,8},{5,1},{9,5},{13,9},{6,2},{10,6},{14,10},{7,3},{... | collective-permute-start | bytes 122888 | tf_op jit(solution)/shard_map/ppermute | solution.py:512
  19.0 3.0 %collective-permute-start.2 = (f32[40,256]{1,0:T(8,128)}, f32[40,256]{1,0:T(8,128)S(1)}, u32[]{:S(2)}, u32[]{:S(2)}) collective-permute-start(f32[40,256]{1,0:T(8,128)} %get-tuple-element.18), channel_id=1, source_target_pairs={{0,4},{4,8},{8,12},{1,5},{5,9},{9,13},{2,6},{6,10},{10,14},{3,7},{... | collective-permute-start | bytes 122888 | tf_op jit(solution)/shard_map/ppermute | solution.py:512
  22.0 1.0 fusion
  23.0 0.0 collective-permute-done.1.rest_1_
  23.0 0.0 copy-start.3
  23.0 0.0 collective-permute-done.2.rest_2_
  23.1 0.0 copy-start.4
  23.1 4.6 %collective-permute-start.5 = (f32[168,256]{1,0:T(8,128)S(1)}, f32[168,256]{1,0:T(8,128)S(1)}, u32[]{:S(2)}, u32[]{:S(2)}) collective-permute-start(f32[168,256]{1,0:T(8,128)S(1)} %maximum_maximum_fusion), channel_id=1, source_target_pairs={{0,1},{1,2},{2,3},{4,5},{5,6},{6,7},{8,9},{9,10},{10,11},{12,13},{... | collective-permute-start | bytes 516104 | tf_op jit(solution)/shard_map/ppermute | solution.py:512
  27.7 1.3 %collective-permute-start.6 = (f32[168,256]{1,0:T(8,128)S(1)}, f32[168,256]{1,0:T(8,128)S(1)}, u32[]{:S(2)}, u32[]{:S(2)}) collective-permute-start(f32[168,256]{1,0:T(8,128)S(1)} %maximum_maximum_fusion.1), channel_id=1, source_target_pairs={{1,0},{2,1},{3,2},{5,4},{6,5},{7,6},{9,8},{10,9},{11,10},{13,12},{... | collective-permute-start | bytes 516104 | tf_op jit(solution)/shard_map/ppermute | solution.py:512
  29.0 5.2 %collective-permute-done.5.rest_5_ = f32[168,256]{1,0:T(8,128)S(1)} collective-permute-done((f32[168,256]{1,0:T(8,128)S(1)}, f32[168,256]{1,0:T(8,128)S(1)}, u32[]{:S(2)}, u32[]{:S(2)}) %collective-permute-start.5) | collective-permute-done | bytes 172064 | tf_op jit(solution)/shard_map/ppermute | solution.py:512
  34.1 0.0 copy-start.1
  34.2 5.0 %collective-permute-done.6.rest_6_ = f32[168,256]{1,0:T(8,128)S(1)} collective-permute-done((f32[168,256]{1,0:T(8,128)S(1)}, f32[168,256]{1,0:T(8,128)S(1)}, u32[]{:S(2)}, u32[]{:S(2)}) %collective-permute-start.6) | collective-permute-done | bytes 172064 | tf_op jit(solution)/shard_map/ppermute | solution.py:512
  39.2 0.0 copy-start.2
  39.2 0.0 collective-permute-done.3.rest_3_
  39.2 0.0 collective-permute-done.4.rest_4_
  39.2 0.0 copy-done.3
  39.2 0.0 copy-done.4
  39.2 0.0 copy-done.1
  39.2 0.6 copy-done.2
  39.8 23.1 %shard_map.71 = (f32[20,8,2,32,128]{4,3,2,1,0:T(8,128)}, f32[32,2,128]{2,1,0:T(2,128)}) custom-call(s32[1]{0:T(128)} %bitcast.place, f32[4,8,32,256]{3,2,1,0:T(8,128)} %rhs.5, f32[8,32,256]{2,1,0:T(8,128)} %cz.5, f32[8,32,256]{2,1,0:T(8,128)} %cx.5, f32[8,32,256]{2,1,0:T(8,128)} %cy.5, f32[8,32,256]{2,1,0:T(8,128)} %dg.5, f32[8,4,8,256]{3,2,1,0:T(8,128)} %copy-done, ...), custom_call_target="tpu_custom_call" | custom-call | tf_op jit(solution)/shard_map/pallas_call | solution.py:579
  63.0 10.6 %all_to_all.10.message = f32[32,2,128]{2,1,0:T(2,128)} all-to-all(f32[32,2,128]{2,1,0:T(2,128)} %get-tuple-element.21), channel_id=1, replica_groups=mesh['gx'=2,'gy'=4,'gz'=4] {'gx','gy','gz'}, dimensions={0} | all-to-all | bytes 65536 | tf_op jit(solution)/shard_map/all_to_all | solution.py:516
  73.5 10.6 %shard_map.72 = (f32[20,8,2,32,128]{4,3,2,1,0:T(8,128)}, f32[32,2,128]{2,1,0:T(2,128)}, f32[24,128]{1,0:T(8,128)}) custom-call(f32[32,2,128]{2,1,0:T(2,128)} %all_to_all.10.message, f32[20,8,2,32,128]{4,3,2,1,0:T(8,128)} %get-tuple-element.22.basis_hbm), custom_call_target="tpu_custom_call" | custom-call | tf_op jit(solution)/shard_map/pallas_call | solution.py:595
  84.2 10.5 %all_to_all.11.message = f32[32,2,128]{2,1,0:T(2,128)} all-to-all(f32[32,2,128]{2,1,0:T(2,128)} %get-tuple-element.23), channel_id=1, replica_groups=mesh['gx'=2,'gy'=4,'gz'=4] {'gx','gy','gz'}, dimensions={0} | all-to-all | bytes 65536 | tf_op jit(solution)/shard_map/all_to_all | solution.py:516
  94.7 7.9 %shard_map.73 = (f32[20,8,32,256]{3,2,1,0:T(8,128)}, f32[20,20]{1,0:T(8,128)}) custom-call(f32[32,2,128]{2,1,0:T(2,128)} %all_to_all.11.message, f32[24,128]{1,0:T(8,128)} %get-tuple-element.24.factor_one, f32[20,8,2,32,128]{4,3,2,1,0:T(8,128)} %get-tuple-element.25.first_hbm), custom_call_target="tpu_custom_call" | custom-call | tf_op jit(solution)/shard_map/pallas_call | solution.py:611
  (4 shorter events, 0.0 us)
Async XLA Ops:
  3.7 11.4 %collective-permute-start = (f32[8,4,8,256]{3,2,1,0:T(8,128)}, f32[8,4,8,256]{3,2,1,0:T(8,128)S(1)}, u32[]{:S(2)}, u32[]{:S(2)}) collective-permute-start(f32[8,4,8,256]{3,2,1,0:T(8,128)} %get-tuple-element.14), channel_id=1, source_target_pairs={{0,16},{16,0},{1,17},{17,1},{2,18},{18,2},{3,19},{19,3},{4,20},{20... | collective-permute-start | bytes 786440 | tf_op jit(solution)/shard_map/ppermute | solution.py:545
  6.8 32.4 %collective-permute-start.3 = (f32[29,32,256]{2,1,0:T(8,128)}, f32[29,32,256]{2,1,0:T(8,128)}, u32[]{:S(2)}, u32[]{:S(2)}) collective-permute-start(f32[29,32,256]{2,1,0:T(8,128)} %get-tuple-element.19), channel_id=1, source_target_pairs={{0,1},{1,2},{2,3},{4,5},{5,6},{6,7},{8,9},{9,10},{10,11},{12,13},{... | collective-permute-start | bytes 2850824 | tf_op jit(solution)/shard_map/ppermute | solution.py:512
  11.2 28.0 %collective-permute-start.4 = (f32[29,32,256]{2,1,0:T(8,128)}, f32[29,32,256]{2,1,0:T(8,128)}, u32[]{:S(2)}, u32[]{:S(2)}) collective-permute-start(f32[29,32,256]{2,1,0:T(8,128)} %get-tuple-element.20), channel_id=1, source_target_pairs={{1,0},{2,1},{3,2},{5,4},{6,5},{7,6},{9,8},{10,9},{11,10},{13,12},{... | collective-permute-start | bytes 2850824 | tf_op jit(solution)/shard_map/ppermute | solution.py:512
  15.2 0.7 copy-start
  17.7 5.3 %collective-permute-start.1 = (f32[40,256]{1,0:T(8,128)}, f32[40,256]{1,0:T(8,128)S(1)}, u32[]{:S(2)}, u32[]{:S(2)}) collective-permute-start(f32[40,256]{1,0:T(8,128)} %get-tuple-element.17), channel_id=1, source_target_pairs={{4,0},{8,4},{12,8},{5,1},{9,5},{13,9},{6,2},{10,6},{14,10},{7,3},{... | collective-permute-start | bytes 122888 | tf_op jit(solution)/shard_map/ppermute | solution.py:512
  19.0 4.1 %collective-permute-start.2 = (f32[40,256]{1,0:T(8,128)}, f32[40,256]{1,0:T(8,128)S(1)}, u32[]{:S(2)}, u32[]{:S(2)}) collective-permute-start(f32[40,256]{1,0:T(8,128)} %get-tuple-element.18), channel_id=1, source_target_pairs={{0,4},{4,8},{8,12},{1,5},{5,9},{9,13},{2,6},{6,10},{10,14},{3,7},{... | collective-permute-start | bytes 122888 | tf_op jit(solution)/shard_map/ppermute | solution.py:512
  23.0 16.2 %copy-start.3 = (f32[40,256]{1,0:T(8,128)}, f32[40,256]{1,0:T(8,128)S(1)}, u32[]{:S(2)}) copy-start(f32[40,256]{1,0:T(8,128)S(1)} %collective-permute-done.1.rest_1_) | copy-start | bytes 122884
  23.1 16.2 %copy-start.4 = (f32[40,256]{1,0:T(8,128)}, f32[40,256]{1,0:T(8,128)S(1)}, u32[]{:S(2)}) copy-start(f32[40,256]{1,0:T(8,128)S(1)} %collective-permute-done.2.rest_2_) | copy-start | bytes 122884
  23.1 11.1 %collective-permute-start.5 = (f32[168,256]{1,0:T(8,128)S(1)}, f32[168,256]{1,0:T(8,128)S(1)}, u32[]{:S(2)}, u32[]{:S(2)}) collective-permute-start(f32[168,256]{1,0:T(8,128)S(1)} %maximum_maximum_fusion), channel_id=1, source_target_pairs={{0,1},{1,2},{2,3},{4,5},{5,6},{6,7},{8,9},{9,10},{10,11},{12,13},{... | collective-permute-start | bytes 516104 | tf_op jit(solution)/shard_map/ppermute | solution.py:512
  27.7 11.5 %collective-permute-start.6 = (f32[168,256]{1,0:T(8,128)S(1)}, f32[168,256]{1,0:T(8,128)S(1)}, u32[]{:S(2)}, u32[]{:S(2)}) collective-permute-start(f32[168,256]{1,0:T(8,128)S(1)} %maximum_maximum_fusion.1), channel_id=1, source_target_pairs={{1,0},{2,1},{3,2},{5,4},{6,5},{7,6},{9,8},{10,9},{11,10},{13,12},{... | collective-permute-start | bytes 516104 | tf_op jit(solution)/shard_map/ppermute | solution.py:512
  34.1 5.1 %copy-start.1 = (f32[168,256]{1,0:T(8,128)}, f32[168,256]{1,0:T(8,128)S(1)}, u32[]{:S(2)}) copy-start(f32[168,256]{1,0:T(8,128)S(1)} %collective-permute-done.5.rest_5_) | copy-start | bytes 516100
  39.2 0.6 copy-start.2

commit v4 on v3

--- a/solution.py
+++ b/solution.py
@@ -55,15 +55,13 @@
     return rhs.at[f, z] if f < NRHS else (cz, cx, cy, dg)[f - NRHS].at[z]
 
 
-def pack_faces(swap, place, rhs, cz, cx, cy, dg, zlo, zhi, *rest):
-    xmsgs, (whole, loads, saves) = rest[:-3], rest[-3:]
+def pack_faces(rhs, cz, cx, cy, dg, zlo, zhi, token, whole, loads, saves):
     copies = []
     for f in range(FIELDS):
         src = rhs.at[f] if f < NRHS else (cz, cx, cy, dg)[f - NRHS]
         copies.append(pltpu.make_async_copy(src, whole.at[f], loads.at[f]))
         copies[-1].start()
-    low = row_ids((8, NY)) < 4
-    up = place[0] == 0
+    token[0] = 0
     planes = []
     at = 0
     for f in range(FIELDS):
@@ -78,18 +76,35 @@
             )
             planes[-1].start()
         at += depth
+    for copy in planes:
+        copy.wait()
+
+
+def pack_rows(swap, place, token, rhs, cz, cx, cy, dg, *rest):
+    xmsgs, (first_rows, last_rows, loads) = rest[:-3], rest[-3:]
+    copies = []
     for f in range(FIELDS):
+        src = rhs.at[f] if f < NRHS else (cz, cx, cy, dg)[f - NRHS]
+        for side, rows in ((0, first_rows), (1, last_rows)):
+            copies.append(
+                pltpu.make_async_copy(
+                    src.at[:, pl.ds(side * (NX - 8), 8), :], rows.at[f], loads.at[2 * f + side]
+                )
+            )
+            copies[-1].start()
+    low = row_ids((8, NY)) < 4
+    up = place[0] + token[0] == 0
+    for f in range(FIELDS):
+        copies[2 * f].wait()
+        copies[2 * f + 1].wait()
         for m in range(NZ // 2):
-            a, b = whole.at[f, 2 * m], whole.at[f, 2 * m + 1]
-            first = jnp.where(low, a[0:8], pltpu.roll(b[0:8], 4, 0))
-            last = jnp.where(low, pltpu.roll(a[NX - 8 : NX], 4, 0), b[NX - 8 : NX])
+            first = jnp.where(low, first_rows[f, 2 * m], pltpu.roll(first_rows[f, 2 * m + 1], 4, 0))
+            last = jnp.where(low, pltpu.roll(last_rows[f, 2 * m], 4, 0), last_rows[f, 2 * m + 1])
             if swap:
                 xmsgs[0][f, m] = jnp.where(up, last, first)
             else:
                 xmsgs[0][f, m] = first
                 xmsgs[1][f, m] = last
-    for copy in planes:
-        copy.wait()
 
 
 def halo_tile(above, below, odd, keep_up, keep_dn):
@@ -223,169 +238,235 @@
     return jnp.concatenate(tops, 0)
 
 
-def krylov(
-    swap, place, rhs, cz, cx, cy, dg, above, below, yup, ydn, facelo, facehi, rimlo, rimhi,
-    basis, message,
-    store, faces, ysrc, accs, sems,
-):
-    lane = lane_ids((8, 128))
-    keep_up, keep_dn = keep_sides(swap, place)
-    n_x = 1 if swap else 2
-
-    def put(f, z, l, t, value):
-        store[f, z, l, 8 + 8 * t : 16 + 8 * t, :] = value
+def slot(k):
+    return k * NRHS + (NRHS if k else 0)
+
+
+class Block:
+    def __init__(self, store, base, faces, faces_base):
+        self.store, self.base, self.faces, self.faces_base = store, base, faces, faces_base
+        self.lane = lane_ids((8, 128))
+
+    def put(self, f, z, l, t, value):
+        z = z - self.base
+        self.store[f, z, l, 8 + 8 * t : 16 + 8 * t, :] = value
         if t == 0:
-            store[f, z, l, 8 + ROWS : 16 + ROWS, :] = value
+            self.store[f, z, l, 8 + ROWS : 16 + ROWS, :] = value
         if t == ROWS // 8 - 1:
-            store[f, z, l, 0:8, :] = value
-
-    x_rows = FIELDS * 2 * 8
-    for f in range(FIELDS):
-        depth = DEPTH if f <= NRHS else DEPTH - 1
-        start = f * DEPTH if f <= NRHS else NRHS * DEPTH + DEPTH + (f - NRHS - 1) * (DEPTH - 1)
-        for z in range(EZ):
-            own = DEPTH <= z < DEPTH + NZ
-            if own:
-                plane = field_of(rhs, cz, cx, cy, dg, f, z - DEPTH)
-            elif z < DEPTH:
-                d = z - (DEPTH - depth)
-                plane = facelo.at[start + d] if d >= 0 else None
-            else:
-                d = z - DEPTH - NZ
-                plane = facehi.at[start + d] if d < depth else None
-            for l in range(2):
-                lanes = pl.ds(128 * l, 128)
-                for t in range(NX // 8):
-                    if plane is None:
-                        put(f, z, l, t, jnp.zeros((8, 128), F32))
-                    else:
-                        put(f, z, l, t, plane[8 * t : 8 * t + 8, lanes])
-                if own:
-                    m = (z - DEPTH) // 2
-                    a, b = above[f, m, :, lanes], below[f, m, :, lanes]
-                else:
-                    rim, m = (rimlo, z // 2) if z < DEPTH else (rimhi, (z - DEPTH - NZ) // 2)
-                    at = (f * 2 + m) * 8
-                    a = rim[at : at + 8, lanes]
-                    at += x_rows * (n_x - 1)
-                    b = rim[at : at + 8, lanes]
-                put(f, z, l, NX // 8, halo_tile(a, b, z % 2, keep_up, keep_dn))
-
-    at = x_rows * n_x
-    ysrc[0, 0] = rimlo[at : at + ROWS, 0:128]
-    ysrc[1, 0] = rimlo[at : at + ROWS, 128:256]
-    ysrc[0, 1] = yup[:, 0:128]
-    ysrc[0, 2] = yup[:, 128:256]
-    ysrc[1, 1] = ydn[:, 0:128]
-    ysrc[1, 2] = ydn[:, 128:256]
-    ysrc[0, 3] = rimhi[at : at + ROWS, 0:128]
-    ysrc[1, 3] = rimhi[at : at + ROWS, 128:256]
-
-    def place_y(q, carry):
+            self.store[f, z, l, 0:8, :] = value
+
+    def place_y(self, z, up, dn):
         for t in range(ROWS // 8):
-            up = ysrc[0, q, 8 * t : 8 * t + 8, :]
-            dn = ysrc[1, q, 8 * t : 8 * t + 8, :]
+            u_all, d_all = up[8 * t : 8 * t + 8, :], dn[8 * t : 8 * t + 8, :]
             for zz in range(4):
                 for f in range(FIELDS):
                     spot = (zz * FIELDS + f) * 4
-                    u = pltpu.roll(up, (-spot) % 128, 1) if spot else up
-                    d = pltpu.roll(dn, (124 - spot) % 128, 1) if spot != 124 else dn
-                    put(f, 4 * q + zz, 2, t, jnp.where(lane < 4, u, jnp.where(lane >= 124, d, 0.0)))
-        return carry
-
-    lax.fori_loop(0, EZ // 4, place_y, 0)
-
-    def tiles(f, z, t, off):
-        return [store[f, z, l, pl.ds(8 + 8 * t + off, 8), :] for l in range(LT)]
-
-    def lane_up(tri):
+                    u = pltpu.roll(u_all, (-spot) % 128, 1) if spot else u_all
+                    d = pltpu.roll(d_all, (124 - spot) % 128, 1) if spot != 124 else d_all
+                    value = jnp.where(self.lane < 4, u, jnp.where(self.lane >= 124, d, 0.0))
+                    self.put(f, z + zz, 2, t, value)
+
+    def tiles(self, f, z, t, off):
+        return [self.store[f, z - self.base, l, pl.ds(8 + 8 * t + off, 8), :] for l in range(LT)]
+
+    def lane_up(self, tri):
         rolled = [pltpu.roll(v, 127, 1) for v in tri]
-        return [jnp.where(lane == 127, rolled[(l + 1) % LT], rolled[l]) for l in range(LT)]
-
-    def lane_dn(tri):
+        return [jnp.where(self.lane == 127, rolled[(l + 1) % LT], rolled[l]) for l in range(LT)]
+
+    def lane_dn(self, tri):
         rolled = [pltpu.roll(v, 1, 1) for v in tri]
-        return [jnp.where(lane == 0, rolled[(l - 1) % LT], rolled[l]) for l in range(LT)]
-
-    def coefficients(z, carry):
+        return [jnp.where(self.lane == 0, rolled[(l - 1) % LT], rolled[l]) for l in range(LT)]
+
+    def coefficients(self, z):
         for t in range(ROWS // 8):
             kz, kx, ky, kd = (NRHS + i for i in range(4))
-            center_z, center_x, center_y = (tiles(k, z, t, 0) for k in (kz, kx, ky))
-            diag = tiles(kd, z, t, 0)
+            center_z, center_x, center_y = (self.tiles(k, z, t, 0) for k in (kz, kx, ky))
+            diag = self.tiles(kd, z, t, 0)
             sides = [
-                (center_z, tiles(kz, z + 1, t, 0)),
-                (center_z, tiles(kz, z - 1, t, 0)),
-                (center_x, tiles(kx, z, t, 1)),
-                (center_x, tiles(kx, z, t, -1)),
-                (center_y, lane_up(center_y)),
-                (center_y, lane_dn(center_y)),
+                (center_z, self.tiles(kz, z + 1, t, 0)),
+                (center_z, self.tiles(kz, z - 1, t, 0)),
+                (center_x, self.tiles(kx, z, t, 1)),
+                (center_x, self.tiles(kx, z, t, -1)),
+                (center_y, self.lane_up(center_y)),
+                (center_y, self.lane_dn(center_y)),
             ]
+            at = z - self.faces_base
             for l in range(LT):
                 inside = diag[l] > 0.0
                 total = diag[l] * SCALE
                 for k, (mid, side) in enumerate(sides):
                     face = (mid[l] + side[l]) * (0.5 * SCALE)
                     total = total + face
-                    faces[k, z, l, 8 * t : 8 * t + 8, :] = jnp.where(inside, face, 0.0)
-                faces[6, z, l, 8 * t : 8 * t + 8, :] = jnp.where(inside, total, 0.0)
+                    self.faces[k, at, l, 8 * t : 8 * t + 8, :] = jnp.where(inside, face, 0.0)
+                self.faces[6, at, l, 8 * t : 8 * t + 8, :] = jnp.where(inside, total, 0.0)
+
+    def apply(self, k, z):
+        last = k == STEPS - 1
+        at = z - self.faces_base
+        outs = 2 if last else LT
+        for t in range(NX // 8 if last else ROWS // 8):
+            face = [[self.faces[c, at, l, 8 * t : 8 * t + 8, :] for l in range(outs)] for c in range(7)]
+            diag = [face[6][l] - SHIFTS[k] * SCALE for l in range(outs)]
+            for r in range(NRHS):
+                f = slot(k) + r
+                mid = self.tiles(f, z, t, 0)
+                sides = [
+                    self.tiles(f, z + 1, t, 0),
+                    self.tiles(f, z - 1, t, 0),
+                    self.tiles(f, z, t, 1),
+                    self.tiles(f, z, t, -1),
+                    self.lane_up(mid),
+                    self.lane_dn(mid),
+                ]
+                for l in range(outs):
+                    value = diag[l] * mid[l]
+                    for c in range(6):
+                        value = value - face[c][l] * sides[c][l]
+                    self.put(slot(k + 1) + r, z, l, t, value)
+
+
+def loop(start, stop, do):
+    def step(n, carry):
+        do(n)
         return carry
 
-    lax.fori_loop(1, EZ - 1, coefficients, 0)
-
-    def slot(k):
-        return k * NRHS + (NRHS if k else 0)
-
-    copies = []
+    lax.fori_loop(start, stop, step, 0)
+
+
+def inner_planes(k):
+    return DEPTH + k, DEPTH + NZ - k
+
+
+def inner_copies(inner, inner_faces, store, base, faces, faces_base, sems, out):
+    def copy(n, there, here):
+        src, dst = (here, there) if out else (there, here)
+        return pltpu.make_async_copy(src, dst, sems.at[n])
+
+    def planes(ref, f, start, stop, at):
+        return ref.at[pl.ds(f, NRHS), pl.ds(start - at, stop - start)]
+
+    result = []
+    for n, (f, start, stop) in enumerate(
+        [(0, DEPTH, DEPTH + NZ), (NRHS, DEPTH, DEPTH + 2), (NRHS, DEPTH + NZ - 2, DEPTH + NZ)]
+        + [(slot(k), *inner_planes(k)) for k in range(1, STEPS)]
+    ):
+        result.append(copy(n, planes(inner, f, start, stop, DEPTH), planes(store, f, start, stop, base)))
+    start, stop = inner_planes(1)
+    result.append(copy(len(result), inner_faces, faces.at[:, pl.ds(start - faces_base, stop - start)]))
+    return result
+
+
+def krylov_inner(swap, place, rhs, cz, cx, cy, dg, *rest):
+    above, below, yup, ydn, inner, inner_faces, store, faces, sems = rest if not swap else rest[:1] + rest
+    keep_up, keep_dn = keep_sides(swap, place)
+    block = Block(store, DEPTH, faces, DEPTH + 1)
+    for f in range(FIELDS):
+        for z in range(DEPTH, DEPTH + NZ):
+            plane = field_of(rhs, cz, cx, cy, dg, f, z - DEPTH)
+            m = (z - DEPTH) // 2
+            for l in range(2):
+                lanes = pl.ds(128 * l, 128)
+                for t in range(NX // 8):
+                    block.put(f, z, l, t, plane[8 * t : 8 * t + 8, lanes])
+                tile = halo_tile(above[f, m, :, lanes], below[f, m, :, lanes], z % 2, keep_up, keep_dn)
+                block.put(f, z, l, NX // 8, tile)
+    for half in range(2):
+        lanes = pl.ds(128 * half, 128)
+        block.place_y(DEPTH + 4 * half, yup.at[:, lanes], ydn.at[:, lanes])
+    copies = inner_copies(inner, inner_faces, store, DEPTH, faces, DEPTH + 1, sems, True)
+    for n in range(3):
+        copies[n].start()
+    loop(*inner_planes(1), block.coefficients)
+    copies[-1].start()
+    for k in range(STEPS - 1):
+        loop(*inner_planes(k + 1), functools.partial(block.apply, k))
+        copies[3 + k].start()
+    for copy in copies:
+        copy.wait()
+
+
+NEAR, FAR = 8 * FIELDS, 24
+
+
+def krylov_outer(
+    swap, place, inner, inner_faces, facelo, facehi, rimlo, rimhi,
+    basis, message,
+    store, faces, accs, loads, saves,
+):
+    keep_up, keep_dn = keep_sides(swap, place)
+    n_x = 1 if swap else 2
+    block = Block(store, 0, faces, 0)
+    copies = inner_copies(inner, inner_faces, store, 0, faces, 0, loads, False)
+    for copy in copies:
+        copy.start()
+
+    zero = jnp.zeros((8, 128), F32)
+    for f in range(FIELDS):
+        depth = DEPTH if f <= NRHS else DEPTH - 1
+        start = f * DEPTH if f <= NRHS else NRHS * DEPTH + DEPTH + (f - NRHS - 1) * (DEPTH - 1)
+        for face, rim, first in ((facelo, rimlo, 0), (facehi, rimhi, DEPTH + NZ)):
+            for z in range(first, first + DEPTH):
+                far = DEPTH - z if first == 0 else z - first + 1
+                d = start + (depth - far if first == 0 else far - 1)
+                for l in range(2):
+                    lanes = pl.ds(128 * l, 128)
+                    for t in range(NX // 8):
+                        value = face[d, 8 * t : 8 * t + 8, lanes] if far <= depth else zero
+                        block.put(f, z, l, t, value)
+                    if far <= 2:
+                        at, odd = 8 * f, z % 2
+                    elif far == 3 and 8 * (f // 2) < FAR:
+                        at, odd = NEAR + 8 * (f // 2), f % 2
+                    else:
+                        block.put(f, z, l, NX // 8, zero)
+                        continue
+                    other = at + (n_x - 1) * (NEAR + FAR)
+                    tile = halo_tile(rim[at : at + 8, lanes], rim[other : other + 8, lanes], odd, keep_up, keep_dn)
+                    block.put(f, z, l, NX // 8, tile)
+    rows = pl.ds(n_x * (NEAR + FAR), ROWS)
+    for rim, z in ((rimlo, 0), (rimhi, DEPTH + NZ)):
+        block.place_y(z, rim.at[rows, pl.ds(0, 128)], rim.at[rows, pl.ds(128, 128)])
+
+    for n in range(3):
+        copies[n].wait()
+    loop(1, DEPTH + 1, block.coefficients)
+    loop(DEPTH + NZ - 1, EZ - 1, block.coefficients)
+
+    sends = []
 
     def send_block(k):
         copy = pltpu.make_async_copy(
             store.at[pl.ds(slot(k), NRHS), pl.ds(DEPTH, NZ), pl.ds(0, 2), pl.ds(8, NX), :],
             basis.at[pl.ds(k * NRHS, NRHS)],
-            sems.at[k],
+            saves.at[k],
         )
         copy.start()
-        copies.append(copy)
+        sends.append(copy)
 
     send_block(0)
     for k in range(STEPS):
-
-        def apply(z, carry):
-            for t in range(ROWS // 8):
-                face = [[faces[c, z, l, 8 * t : 8 * t + 8, :] for l in range(LT)] for c in range(7)]
-                diag = [face[6][l] - SHIFTS[k] * SCALE for l in range(LT)]
-                for r in range(NRHS):
-                    f = slot(k) + r
-                    mid = tiles(f, z, t, 0)
-                    sides = [
-                        tiles(f, z + 1, t, 0),
-                        tiles(f, z - 1, t, 0),
-                        tiles(f, z, t, 1),
-                        tiles(f, z, t, -1),
-                        lane_up(mid),
-                        lane_dn(mid),
-                    ]
-                    for l in range(LT):
-                        value = diag[l] * mid[l]
-                        for c in range(6):
-                            value = value - face[c][l] * sides[c][l]
-                        put(slot(k + 1) + r, z, l, t, value)
-            return carry
-
-        lax.fori_loop(k + 1, EZ - 1 - k, apply, 0)
+        if k == 1:
+            copies[-1].wait()
+        loop(
+            0,
+            2 * DEPTH,
+            lambda n, k=k: block.apply(k, n + k + 1 + jnp.where(n >= DEPTH, NZ - 2 - 2 * k, 0)),
+        )
+        if k < STEPS - 1:
+            copies[3 + k].wait()
         send_block(k + 1)
-
     gram_zero(accs)
 
-    def products(z, carry):
+    def products(z):
         def tile(i, t):
             f = slot(i // NRHS) + i % NRHS
             return jnp.concatenate([store[f, z, l, 8 + 8 * t : 16 + 8 * t, :] for l in range(2)], 1)
 
         gram_add([jnp.concatenate([tile(i, t) for i in range(COLS)], 0) for t in range(NX // 8)], accs)
-        return carry
-
-    lax.fori_loop(DEPTH, DEPTH + NZ, products, 0)
+
+    loop(DEPTH, DEPTH + NZ, products)
     gram_message(accs, message)
-    for copy in copies:
+    for copy in sends:
         copy.wait()
 
 
@@ -525,22 +606,33 @@
     fields = (rhs, coef_z, coef_x, coef_y, diag_term)
 
     place = at_x.astype(jnp.int32).reshape(1)
-    x_shape = shape(FIELDS, NZ // 2, 8, NY)
     face_shape = shape(FACE, NX, NY)
-    zlo, zhi, *xmsgs = pl.pallas_call(
-        functools.partial(pack_faces, swap),
-        out_shape=(face_shape, face_shape) + (x_shape,) * (1 if swap else 2),
-        in_specs=[smem()] + [hbm()] * 5,
-        out_specs=(hbm(), hbm()) + (vmem(),) * (1 if swap else 2),
+    zlo, zhi, token = pl.pallas_call(
+        pack_faces,
+        out_shape=(face_shape, face_shape, jax.ShapeDtypeStruct((1,), jnp.int32)),
+        in_specs=[hbm()] * 5,
+        out_specs=(hbm(), hbm(), smem()),
         scratch_shapes=[
             pltpu.VMEM((FIELDS, NZ, NX, NY), F32),
             pltpu.SemaphoreType.DMA((FIELDS,)),
             pltpu.SemaphoreType.DMA((2 * FIELDS,)),
         ],
         compiler_params=params(LIMIT),
-    )(place, *fields)
+    )(*fields)
     facehi = move(zlo, "gz", -1)
     facelo = move(zhi, "gz", 1)
+    x_shape = shape(FIELDS, NZ // 2, 8, NY)
+    xmsgs = pl.pallas_call(
+        functools.partial(pack_rows, swap),
+        out_shape=(x_shape,) * (1 if swap else 2),
+        in_specs=[smem(), smem()] + [hbm()] * 5,
+        scratch_shapes=[
+            pltpu.VMEM((FIELDS, NZ, 8, NY), F32),
+            pltpu.VMEM((FIELDS, NZ, 8, NY), F32),
+            pltpu.SemaphoreType.DMA((2 * FIELDS,)),
+        ],
+        compiler_params=params(LIMIT),
+    )(place, token, *fields)
     if swap:
         x_parts = (lax.ppermute(xmsgs[0], "gx", [(0, 1), (1, 0)]),)
     else:
@@ -558,43 +650,57 @@
         functools.partial(pack_rims, swap),
         out_shape=(rim_shape, rim_shape),
         in_specs=[smem()] + [vmem()] * (2 + len(x_parts)),
-        compiler_params=params(LIMIT),
+        compiler_params=params(16),
     )(place, *own_rims, *x_parts)
     yup, ydn = move(ylo, "gy", -1), move(yhi, "gy", 1)
 
     def rim(half):
-        rows = [p[:, 2 * half : 2 * half + 2].reshape(-1, NY) for p in x_parts]
+        near, far, odd = ((0, 1, 0), (3, 2, 1))[half]
+        rows = []
+        for part in x_parts:
+            rows.append(part[:, near].reshape(NEAR, NY))
+            rows.append(part[: FAR // 4, far, 4 * odd : 4 * odd + 4].reshape(FAR, NY))
         lanes = slice(128 * half, 128 * half + 128)
         return jnp.concatenate(rows + [jnp.concatenate([yup[:, lanes], ydn[:, lanes]], 1)], 0)
 
     rimhi, rimlo = move(rim(0), "gz", -1), move(rim(1), "gz", 1)
 
+    inner_shape = shape(COLS, NZ, LT, EROWS, 128)
+    inner_faces_shape = shape(7, NZ - 2, LT, ROWS, 128)
+    inner, inner_faces = pl.pallas_call(
+        functools.partial(krylov_inner, swap),
+        out_shape=(inner_shape, inner_faces_shape),
+        in_specs=[smem()] + [vmem()] * (5 + len(x_parts) + 2),
+        out_specs=(hbm(), hbm()),
+        scratch_shapes=[
+            pltpu.VMEM(inner_shape.shape, F32),
+            pltpu.VMEM(inner_faces_shape.shape, F32),
+            pltpu.SemaphoreType.DMA((7,)),
+        ],
+        compiler_params=params(LIMIT),
+        cost_estimate=pl.CostEstimate(flops=1 << 27, bytes_accessed=25 << 20, transcendentals=0),
+    )(place, *fields, *x_parts, yup, ydn)
+
     block = shape(COLS, NZ, 2, NX, 128)
-
-    def krylov_entry(place, rhs, cz, cx, cy, dg, *rest):
-        if swap:
-            rest = (rest[0],) + rest
-        krylov(swap, place, rhs, cz, cx, cy, dg, *rest)
-
     basis, message = pl.pallas_call(
-        krylov_entry,
+        functools.partial(krylov_outer, swap),
         out_shape=(block, shape(devices, 2, 128)),
-        in_specs=[smem()] + [vmem()] * (5 + len(x_parts) + 6),
+        in_specs=[smem(), hbm(), hbm()] + [vmem()] * 4,
         out_specs=(hbm(), vmem()),
         scratch_shapes=[
             pltpu.VMEM((COLS + NRHS, EZ, LT, EROWS, 128), F32),
             pltpu.VMEM((7, EZ, LT, ROWS, 128), F32),
-            pltpu.VMEM((2, 4, ROWS, 128), F32),
             pltpu.VMEM((2, STACK, STACK), F32),
+            pltpu.SemaphoreType.DMA((7,)),
             pltpu.SemaphoreType.DMA((STEPS + 1,)),
         ],
         compiler_params=params(LIMIT),
-    )(place, *fields, *x_parts, yup, ydn, facelo, facehi, rimlo, rimhi)
+    )(place, inner, inner_faces, facelo, facehi, rimlo, rimhi)
 
     message = exchange(message)
     first, message, factor_one = pl.pallas_call(
         functools.partial(first_pass, cells),
-        out_shape=(block, shape(devices, 2, 128), shape(24, 128)),
+        out_shape=(block, shape(1, 2, 128), shape(24, 128)),
         in_specs=[vmem(), hbm()],
         out_specs=(hbm(), vmem(), vmem()),
         scratch_shapes=[
@@ -607,7 +713,7 @@
         compiler_params=params(LIMIT),
     )(message, basis)
 
-    message = exchange(message)
+    message = lax.all_gather(message[0], AXES)
     return pl.pallas_call(
         functools.partial(second_pass, cells),
         out_shape=(shape(COLS, NZ, NX, NY), shape(COLS, COLS)),

time: 103 us -> 160 us (1.55)
  blocking collectives: 21.1 us -> 81.6 us
  waiting for transfers between devices: 10.3 us -> 3.57 us
  Pallas kernels: 49.2 us -> 52.3 us
    all_gather x0 -> x1, blocking collectives: none -> 68.9 us  [body(): message = lax.all_gather(message[0], AXES)]
    all_to_all x2 -> x1, blocking collectives: 21.1 us -> 12.7 us  [exchange(): return lax.all_to_all(messages, AXES, 0, 0, tiled=True)]
    ppermute x6, waiting for transfers between devices: 10.3 us -> 3.57 us  [move(): return lax.ppermute(value, axis, pairs)]
    pallas_call x2 -> x4, Pallas kernels: 26.2 us -> 31.1 us  [the longest x1 18 us: body(): pl.pallas_call(functools.partial(krylov_outer, swap), out_shape=(block, s...]
    pallas_call x1, Pallas kernels: 1.8 us -> 0.2 us  [body(): pl.pallas_call(functools.partial(pack_rims, swap), out_shape=(rim_shape,...]
  transfers between devices with their start and end apart: 7 -> 7, of which waited for: 2 -> 2; matrix products, arithmetic and copies ran while one was open for 1% -> 0% of each run, Pallas kernels for 4% -> 6%
where the time goes in v4:
time: 160 us
  blocking collectives  81.6 us (51%)
  Pallas kernels  52.3 us (33%)
  starting transfers between devices  18.9 us (12%)
  waiting for transfers between devices  3.57 us (2%)
  local copies, waits for them, and re-layouts  2.22 us (1%)
    all_gather x1, blocking collectives, body(): message = lax.all_gather(message[0], AXES)  68.9 us
    pallas_call x1, Pallas kernels, body(): pl.pallas_call(functools.partial(krylov_outer, swap), out_shape=(block, s...  18 us
    ppermute x6, starting transfers between devices, move(): return lax.ppermute(value, axis, pairs)  15.9 us
    all_to_all x1, blocking collectives, exchange(): return lax.all_to_all(messages, AXES, 0, 0, tiled=True)  12.7 us
    pallas_call x1, Pallas kernels, body(): pl.pallas_call(functools.partial(first_pass, cells), out_shape=(block, sh...  10.5 us
    pallas_call x1, Pallas kernels, body(): pl.pallas_call(functools.partial(second_pass, cells), out_shape=(shape(CO...  7.86 us
    pallas_call x1, Pallas kernels, body(): pl.pallas_call(functools.partial(krylov_inner, swap), out_shape=(inner_sh...  7.45 us
    ppermute x6, waiting for transfers between devices, move(): return lax.ppermute(value, axis, pairs)  3.57 us
  transfers between devices with their start and end apart: 7, of which 2 were waited for; matrix products, arithmetic and copies ran while one was open for 0% of the time, Pallas kernels for 6%

profile of v4, /device:TPU:0, one launch (start us, length us, event | category | flops | bytes accessed | tf_op | source)
XLA Modules:
  0.0 159.5 jit_solution(1617643410382603795)
XLA Ops:
  0.6 2.9 %shard_map.68 = (f32[29,32,256]{2,1,0:T(8,128)}, f32[29,32,256]{2,1,0:T(8,128)}, s32[1]{0:T(128)}) custom-call(f32[4,8,32,256]{3,2,1,0:T(8,128)} %rhs.7, f32[8,32,256]{2,1,0:T(8,128)} %cz.7, f32[8,32,256]{2,1,0:T(8,128)} %cx.7, f32[8,32,256]{2,1,0:T(8,128)} %cy.7, f32[8,32,256]{2,1,0:T(8,128)} %dg.7), custom_call_target="tpu_custom_call" | custom-call | tf_op jit(solution)/shard_map/pallas_call | solution.py:610
  3.5 2.7 %shard_map.69 = f32[8,4,8,256]{3,2,1,0:T(8,128)} custom-call(s32[1]{0:T(128)} %bitcast.place, s32[1]{0:T(128)} %get-tuple-element.16.token, f32[4,8,32,256]{3,2,1,0:T(8,128)} %rhs.7, f32[8,32,256]{2,1,0:T(8,128)} %cz.7, f32[8,32,256]{2,1,0:T(8,128)} %cx.7, f32[8,32,256]{2,1,0:T(8,128)} %cy.7, f32[8,32,256]{2,1,0:T(8,128)} %dg.7), custom_call_target="tpu_custom_call" | custom-call | tf_op jit(solution)/shard_map/pallas_call | solution.py:625
  6.3 3.0 %collective-permute-start = (f32[8,4,8,256]{3,2,1,0:T(8,128)}, f32[8,4,8,256]{3,2,1,0:T(8,128)S(1)}, u32[]{:S(2)}, u32[]{:S(2)}) collective-permute-start(f32[8,4,8,256]{3,2,1,0:T(8,128)} %shard_map.69), channel_id=1, source_target_pairs={{0,16},{16,0},{1,17},{17,1},{2,18},{18,2},{3,19},{19,3},{4,20},{20... | collective-permute-start | bytes 786440 | tf_op jit(solution)/shard_map/ppermute | solution.py:637
  9.3 4.4 %collective-permute-start.3 = (f32[29,32,256]{2,1,0:T(8,128)}, f32[29,32,256]{2,1,0:T(8,128)}, u32[]{:S(2)}, u32[]{:S(2)}) collective-permute-start(f32[29,32,256]{2,1,0:T(8,128)} %get-tuple-element.23), channel_id=1, source_target_pairs={{0,1},{1,2},{2,3},{4,5},{5,6},{6,7},{8,9},{9,10},{10,11},{12,13},{... | collective-permute-start | bytes 2850824 | tf_op jit(solution)/shard_map/ppermute | solution.py:593
  13.7 1.3 collective-permute-start.4
  15.0 2.7 %shard_map.70 = (f32[32,256]{1,0:T(8,128)}, f32[32,256]{1,0:T(8,128)}) custom-call(f32[4,8,32,256]{3,2,1,0:T(8,128)} %rhs.7, f32[8,32,256]{2,1,0:T(8,128)} %cz.7, f32[8,32,256]{2,1,0:T(8,128)} %cx.7, f32[8,32,256]{2,1,0:T(8,128)} %cy.7, f32[8,32,256]{2,1,0:T(8,128)} %dg.7), custom_call_target="tpu_custom_call" | custom-call | tf_op jit(solution)/shard_map/pallas_call | solution.py:642
  17.7 0.0 collective-permute-done.refs_0_.rest_0_
  17.7 0.0 copy-start
  17.7 0.0 copy-start.1
  17.7 0.8 copy-done.1
  18.5 0.0 copy-start.2
  18.5 0.8 copy-done.2
  19.3 0.2 shard_map.71
  19.5 1.3 collective-permute-start.1
  20.8 3.0 %collective-permute-start.2 = (f32[40,256]{1,0:T(8,128)S(1)}, f32[40,256]{1,0:T(8,128)S(1)}, u32[]{:S(2)}, u32[]{:S(2)}) collective-permute-start(f32[40,256]{1,0:T(8,128)S(1)} %get-tuple-element.20), channel_id=1, source_target_pairs={{0,4},{4,8},{8,12},{1,5},{5,9},{9,13},{2,6},{6,10},{10,14},{3,7},{... | collective-permute-start | bytes 122888 | tf_op jit(solution)/shard_map/ppermute | solution.py:593
  23.9 0.0 collective-permute-done.1.rest_1_
  23.9 0.0 copy-start.3
  23.9 0.8 collective-permute-done.2.rest_2_
  24.7 0.0 copy-start.4
  24.7 4.6 %collective-permute-start.5 = (f32[128,256]{1,0:T(8,128)S(1)}, f32[128,256]{1,0:T(8,128)S(1)}, u32[]{:S(2)}, u32[]{:S(2)}) collective-permute-start(f32[128,256]{1,0:T(8,128)S(1)} %maximum_maximum_fusion), channel_id=1, source_target_pairs={{0,1},{1,2},{2,3},{4,5},{5,6},{6,7},{8,9},{9,10},{10,11},{12,13},{... | collective-permute-start | bytes 393224 | tf_op jit(solution)/shard_map/ppermute | solution.py:593
  29.3 1.3 collective-permute-start.6
  30.6 0.0 copy-done
  30.6 0.0 copy-done.3
  30.6 0.0 copy-done.4
  30.7 7.4 %shard_map.72 = (f32[20,8,3,56,128]{4,3,2,1,0:T(8,128)}, f32[7,6,3,40,128]{4,3,2,1,0:T(8,128)}) custom-call(s32[1]{0:T(128)} %bitcast.place, f32[4,8,32,256]{3,2,1,0:T(8,128)} %rhs.7, f32[8,32,256]{2,1,0:T(8,128)} %cz.7, f32[8,32,256]{2,1,0:T(8,128)} %cx.7, f32[8,32,256]{2,1,0:T(8,128)} %cy.7, f32[8,32,256]{2,1,0:T(8,128)} %dg.7, f32[8,4,8,256]{3,2,1,0:T(8,128)} %copy-done, ...), custom_call_target="tpu_custom_call" | custom-call | flops 134217728 | bytes 26214400 | tf_op jit(solution)/shard_map/pallas_call | solution.py:670
  38.1 0.0 collective-permute-done.5.rimlo
  38.1 0.0 copy-start.5
  38.1 2.7 %collective-permute-done.6.rimhi = f32[128,256]{1,0:T(8,128)S(1)} collective-permute-done((f32[128,256]{1,0:T(8,128)S(1)}, f32[128,256]{1,0:T(8,128)S(1)}, u32[]{:S(2)}, u32[]{:S(2)}) %collective-permute-start.6) | collective-permute-done | bytes 131104 | tf_op jit(solution)/shard_map/ppermute | solution.py:593
  40.9 0.0 copy-start.6
  40.9 0.0 collective-permute-done.3.facelo
  40.9 0.0 collective-permute-done.4.facehi
  40.9 0.0 copy-done.5
  40.9 0.6 copy-done.6
  41.5 18.0 %shard_map.73 = (f32[20,8,2,32,128]{4,3,2,1,0:T(8,128)}, f32[32,2,128]{2,1,0:T(2,128)}) custom-call(s32[1]{0:T(128)} %bitcast.place, f32[20,8,3,56,128]{4,3,2,1,0:T(8,128)} %get-tuple-element.21.inner, f32[7,6,3,40,128]{4,3,2,1,0:T(8,128)} %get-tuple-element.22.inner_faces, f32[29,32,256]{2,1,0:T(8,128)} %collective-permute-done.3.facelo, ...), custom_call_target="tpu_custom_call" | custom-call | tf_op jit(solution)/shard_map/pallas_call | solution.py:685
  59.6 12.7 %all_to_all.5.message = f32[32,2,128]{2,1,0:T(2,128)} all-to-all(f32[32,2,128]{2,1,0:T(2,128)} %get-tuple-element.25), channel_id=1, replica_groups=mesh['gx'=2,'gy'=4,'gz'=4] {'gx','gy','gz'}, dimensions={0} | all-to-all | bytes 65536 | tf_op jit(solution)/shard_map/all_to_all | solution.py:597
  72.3 10.5 %shard_map.74 = (f32[20,8,2,32,128]{4,3,2,1,0:T(8,128)}, f32[1,2,128]{2,1,0:T(2,128)}, f32[24,128]{1,0:T(8,128)}) custom-call(f32[32,2,128]{2,1,0:T(2,128)} %all_to_all.5.message, f32[20,8,2,32,128]{4,3,2,1,0:T(8,128)} %get-tuple-element.26.basis_hbm), custom_call_target="tpu_custom_call" | custom-call | tf_op jit(solution)/shard_map/pallas_call | solution.py:701
  82.8 68.9 %all_gather.3.message = f32[32,2,128]{2,1,0:T(2,128)} all-gather(f32[1,2,128]{2,1,0:T(2,128)} %get-tuple-element.27), channel_id=1, replica_groups=mesh['gx'=2,'gy'=4,'gz'=4] {'gx','gy','gz'}, dimensions={0}, use_global_device_ids=true | all-gather | bytes 33792 | tf_op jit(solution)/shard_map/all_gather | solution.py:716
  151.7 7.9 %shard_map.75 = (f32[20,8,32,256]{3,2,1,0:T(8,128)}, f32[20,20]{1,0:T(8,128)}) custom-call(f32[32,2,128]{2,1,0:T(2,128)} %all_gather.3.message, f32[24,128]{1,0:T(8,128)} %get-tuple-element.28.factor_one, f32[20,8,2,32,128]{4,3,2,1,0:T(8,128)} %get-tuple-element.29.first_hbm), custom_call_target="tpu_custom_call" | custom-call | tf_op jit(solution)/shard_map/pallas_call | solution.py:717
  (8 shorter events, 0.1 us)
Async XLA Ops:
  6.3 11.5 %collective-permute-start = (f32[8,4,8,256]{3,2,1,0:T(8,128)}, f32[8,4,8,256]{3,2,1,0:T(8,128)S(1)}, u32[]{:S(2)}, u32[]{:S(2)}) collective-permute-start(f32[8,4,8,256]{3,2,1,0:T(8,128)} %shard_map.69), channel_id=1, source_target_pairs={{0,16},{16,0},{1,17},{17,1},{2,18},{18,2},{3,19},{19,3},{4,20},{20... | collective-permute-start | bytes 786440 | tf_op jit(solution)/shard_map/ppermute | solution.py:637
  9.3 31.6 %collective-permute-start.3 = (f32[29,32,256]{2,1,0:T(8,128)}, f32[29,32,256]{2,1,0:T(8,128)}, u32[]{:S(2)}, u32[]{:S(2)}) collective-permute-start(f32[29,32,256]{2,1,0:T(8,128)} %get-tuple-element.23), channel_id=1, source_target_pairs={{0,1},{1,2},{2,3},{4,5},{5,6},{6,7},{8,9},{9,10},{10,11},{12,13},{... | collective-permute-start | bytes 2850824 | tf_op jit(solution)/shard_map/ppermute | solution.py:593
  13.7 27.1 %collective-permute-start.4 = (f32[29,32,256]{2,1,0:T(8,128)}, f32[29,32,256]{2,1,0:T(8,128)}, u32[]{:S(2)}, u32[]{:S(2)}) collective-permute-start(f32[29,32,256]{2,1,0:T(8,128)} %get-tuple-element.24), channel_id=1, source_target_pairs={{1,0},{2,1},{3,2},{5,4},{6,5},{7,6},{9,8},{10,9},{11,10},{13,12},{... | collective-permute-start | bytes 2850824 | tf_op jit(solution)/shard_map/ppermute | solution.py:593
  17.7 12.9 %copy-start = (f32[8,4,8,256]{3,2,1,0:T(8,128)}, f32[8,4,8,256]{3,2,1,0:T(8,128)S(1)}, u32[]{:S(2)}) copy-start(f32[8,4,8,256]{3,2,1,0:T(8,128)S(1)} %collective-permute-done.refs_0_.rest_0_) | copy-start | bytes 786436
  17.7 0.8 copy-start.1
  18.5 0.8 copy-start.2
  19.5 4.4 %collective-permute-start.1 = (f32[40,256]{1,0:T(8,128)S(1)}, f32[40,256]{1,0:T(8,128)S(1)}, u32[]{:S(2)}, u32[]{:S(2)}) collective-permute-start(f32[40,256]{1,0:T(8,128)S(1)} %get-tuple-element.19), channel_id=1, source_target_pairs={{4,0},{8,4},{12,8},{5,1},{9,5},{13,9},{6,2},{10,6},{14,10},{7,3},{... | collective-permute-start | bytes 122888 | tf_op jit(solution)/shard_map/ppermute | solution.py:593
  20.8 3.9 %collective-permute-start.2 = (f32[40,256]{1,0:T(8,128)S(1)}, f32[40,256]{1,0:T(8,128)S(1)}, u32[]{:S(2)}, u32[]{:S(2)}) collective-permute-start(f32[40,256]{1,0:T(8,128)S(1)} %get-tuple-element.20), channel_id=1, source_target_pairs={{0,4},{4,8},{8,12},{1,5},{5,9},{9,13},{2,6},{6,10},{10,14},{3,7},{... | collective-permute-start | bytes 122888 | tf_op jit(solution)/shard_map/ppermute | solution.py:593
  23.9 6.8 %copy-start.3 = (f32[40,256]{1,0:T(8,128)}, f32[40,256]{1,0:T(8,128)S(1)}, u32[]{:S(2)}) copy-start(f32[40,256]{1,0:T(8,128)S(1)} %collective-permute-done.1.rest_1_) | copy-start | bytes 122884
  24.7 5.9 %copy-start.4 = (f32[40,256]{1,0:T(8,128)}, f32[40,256]{1,0:T(8,128)S(1)}, u32[]{:S(2)}) copy-start(f32[40,256]{1,0:T(8,128)S(1)} %collective-permute-done.2.rest_2_) | copy-start | bytes 122884
  24.7 13.4 %collective-permute-start.5 = (f32[128,256]{1,0:T(8,128)S(1)}, f32[128,256]{1,0:T(8,128)S(1)}, u32[]{:S(2)}, u32[]{:S(2)}) collective-permute-start(f32[128,256]{1,0:T(8,128)S(1)} %maximum_maximum_fusion), channel_id=1, source_target_pairs={{0,1},{1,2},{2,3},{4,5},{5,6},{6,7},{8,9},{9,10},{10,11},{12,13},{... | collective-permute-start | bytes 393224 | tf_op jit(solution)/shard_map/ppermute | solution.py:593
  29.3 11.5 %collective-permute-start.6 = (f32[128,256]{1,0:T(8,128)S(1)}, f32[128,256]{1,0:T(8,128)S(1)}, u32[]{:S(2)}, u32[]{:S(2)}) collective-permute-start(f32[128,256]{1,0:T(8,128)S(1)} %maximum_maximum_fusion.1), channel_id=1, source_target_pairs={{1,0},{2,1},{3,2},{5,4},{6,5},{7,6},{9,8},{10,9},{11,10},{13,12},{... | collective-permute-start | bytes 393224 | tf_op jit(solution)/shard_map/ppermute | solution.py:593
  38.1 2.8 %copy-start.5 = (f32[128,256]{1,0:T(8,128)}, f32[128,256]{1,0:T(8,128)S(1)}, u32[]{:S(2)}) copy-start(f32[128,256]{1,0:T(8,128)S(1)} %collective-permute-done.5.rimlo) | copy-start | bytes 393220
  40.9 0.7 copy-start.6

commit v5 on v4

--- a/solution.py
+++ b/solution.py
@@ -31,6 +31,10 @@
     return pltpu.CompilerParams(vmem_limit_bytes=mb << 20)
 
 
+def cost(us):
+    return pl.CostEstimate(flops=0, bytes_accessed=int(us * 3.6e6), transcendentals=0)
+
+
 def vmem():
     return pl.BlockSpec(memory_space=pltpu.VMEM)
 
@@ -55,13 +59,15 @@
     return rhs.at[f, z] if f < NRHS else (cz, cx, cy, dg)[f - NRHS].at[z]
 
 
-def pack_faces(rhs, cz, cx, cy, dg, zlo, zhi, token, whole, loads, saves):
+def pack_faces(swap, place, rhs, cz, cx, cy, dg, zlo, zhi, *rest):
+    xmsgs, (whole, loads, saves) = rest[:-3], rest[-3:]
     copies = []
     for f in range(FIELDS):
         src = rhs.at[f] if f < NRHS else (cz, cx, cy, dg)[f - NRHS]
         copies.append(pltpu.make_async_copy(src, whole.at[f], loads.at[f]))
         copies[-1].start()
-    token[0] = 0
+    low = row_ids((8, NY)) < 4
+    up = place[0] == 0
     planes = []
     at = 0
     for f in range(FIELDS):
@@ -76,35 +82,17 @@
             )
             planes[-1].start()
         at += depth
-    for copy in planes:
-        copy.wait()
-
-
-def pack_rows(swap, place, token, rhs, cz, cx, cy, dg, *rest):
-    xmsgs, (first_rows, last_rows, loads) = rest[:-3], rest[-3:]
-    copies = []
-    for f in range(FIELDS):
-        src = rhs.at[f] if f < NRHS else (cz, cx, cy, dg)[f - NRHS]
-        for side, rows in ((0, first_rows), (1, last_rows)):
-            copies.append(
-                pltpu.make_async_copy(
-                    src.at[:, pl.ds(side * (NX - 8), 8), :], rows.at[f], loads.at[2 * f + side]
-                )
-            )
-            copies[-1].start()
-    low = row_ids((8, NY)) < 4
-    up = place[0] + token[0] == 0
-    for f in range(FIELDS):
-        copies[2 * f].wait()
-        copies[2 * f + 1].wait()
         for m in range(NZ // 2):
-            first = jnp.where(low, first_rows[f, 2 * m], pltpu.roll(first_rows[f, 2 * m + 1], 4, 0))
-            last = jnp.where(low, pltpu.roll(last_rows[f, 2 * m], 4, 0), last_rows[f, 2 * m + 1])
+            a, b = whole.at[f, 2 * m], whole.at[f, 2 * m + 1]
+            first = jnp.where(low, a[0:8], pltpu.roll(b[0:8], 4, 0))
+            last = jnp.where(low, pltpu.roll(a[NX - 8 : NX], 4, 0), b[NX - 8 : NX])
             if swap:
                 xmsgs[0][f, m] = jnp.where(up, last, first)
             else:
                 xmsgs[0][f, m] = first
                 xmsgs[1][f, m] = last
+    for copy in planes:
+        copy.wait()
 
 
 def halo_tile(above, below, odd, keep_up, keep_dn):
@@ -243,7 +231,8 @@
 
 
 class Block:
-    def __init__(self, store, base, faces, faces_base):
+    def __init__(self, store, base, faces, faces_base, one):
+        self.one = one
         self.store, self.base, self.faces, self.faces_base = store, base, faces, faces_base
         self.lane = lane_ids((8, 128))
 
@@ -267,7 +256,13 @@
                     self.put(f, z + zz, 2, t, value)
 
     def tiles(self, f, z, t, off):
-        return [self.store[f, z - self.base, l, pl.ds(8 + 8 * t + off, 8), :] for l in range(LT)]
+        row = 8 + 8 * t + (off * self.one if off else 0)
+        return [self.store[f, z - self.base, l, pl.ds(row, 8), :] for l in range(LT)]
+
+    def close_ring(self, f, z):
+        z = z - self.base
+        for l in range(2):
+            self.store[f, z, l, 8 + ROWS : 16 + ROWS, :] = self.store[f, z, l, 8:16, :]
 
     def lane_up(self, tri):
         rolled = [pltpu.roll(v, 127, 1) for v in tri]
@@ -325,6 +320,10 @@
                     self.put(slot(k + 1) + r, z, l, t, value)
 
 
+def dynamic_one(place):
+    return (place[0] >> 24) + 1
+
+
 def loop(start, stop, do):
     def step(n, carry):
         do(n)
@@ -357,22 +356,35 @@
 
 
 def krylov_inner(swap, place, rhs, cz, cx, cy, dg, *rest):
-    above, below, yup, ydn, inner, inner_faces, store, faces, sems = rest if not swap else rest[:1] + rest
+    above, below, yup, ydn, inner, inner_faces, store, faces, load_sems, sems = rest if not swap else rest[:1] + rest
     keep_up, keep_dn = keep_sides(swap, place)
-    block = Block(store, DEPTH, faces, DEPTH + 1)
+    block = Block(store, DEPTH, faces, DEPTH + 1, dynamic_one(place))
+    loads = []
+    for n, src in enumerate((rhs, cz, cx, cy, dg)):
+        for l in range(2):
+            lanes = pl.ds(128 * l, 128)
+            rows = pl.ds(8, NX)
+            if n == 0:
+                src_at, dst = src.at[:, :, :, lanes], store.at[pl.ds(0, NRHS), :, l, rows, :]
+            else:
+                src_at, dst = src.at[:, :, lanes], store.at[NRHS + n - 1, :, l, rows, :]
+            loads.append(pltpu.make_async_copy(src_at, dst, load_sems.at[2 * n + l]))
+            loads[-1].start()
     for f in range(FIELDS):
         for z in range(DEPTH, DEPTH + NZ):
-            plane = field_of(rhs, cz, cx, cy, dg, f, z - DEPTH)
             m = (z - DEPTH) // 2
             for l in range(2):
                 lanes = pl.ds(128 * l, 128)
-                for t in range(NX // 8):
-                    block.put(f, z, l, t, plane[8 * t : 8 * t + 8, lanes])
                 tile = halo_tile(above[f, m, :, lanes], below[f, m, :, lanes], z % 2, keep_up, keep_dn)
                 block.put(f, z, l, NX // 8, tile)
     for half in range(2):
         lanes = pl.ds(128 * half, 128)
         block.place_y(DEPTH + 4 * half, yup.at[:, lanes], ydn.at[:, lanes])
+    for copy in loads:
+        copy.wait()
+    for f in range(FIELDS):
+        for z in range(DEPTH, DEPTH + NZ):
+            block.close_ring(f, z)
     copies = inner_copies(inner, inner_faces, store, DEPTH, faces, DEPTH + 1, sems, True)
     for n in range(3):
         copies[n].start()
@@ -389,30 +401,38 @@
 
 
 def krylov_outer(
-    swap, place, inner, inner_faces, facelo, facehi, rimlo, rimhi,
+    swap, facelo, facehi, place, inner, inner_faces, rimlo, rimhi,
     basis, message,
-    store, faces, accs, loads, saves,
+    store, faces, accs, plane_sems, loads, saves,
 ):
     keep_up, keep_dn = keep_sides(swap, place)
     n_x = 1 if swap else 2
-    block = Block(store, 0, faces, 0)
+    block = Block(store, 0, faces, 0, dynamic_one(place))
     copies = inner_copies(inner, inner_faces, store, 0, faces, 0, loads, False)
-    for copy in copies:
+    planes = []
+    start = 0
+    for f in range(FIELDS):
+        depth = DEPTH if f <= NRHS else DEPTH - 1
+        for side, (face, z) in enumerate(((facelo, DEPTH - depth), (facehi, DEPTH + NZ))):
+            for l in range(2):
+                planes.append(
+                    pltpu.make_async_copy(
+                        face.at[pl.ds(start, depth), :, pl.ds(128 * l, 128)],
+                        store.at[f, pl.ds(z, depth), l, pl.ds(8, NX), :],
+                        plane_sems.at[4 * f + 2 * side + l],
+                    )
+                )
+        start += depth
+    for copy in copies[:3] + planes + copies[3:]:
         copy.start()
 
     zero = jnp.zeros((8, 128), F32)
     for f in range(FIELDS):
-        depth = DEPTH if f <= NRHS else DEPTH - 1
-        start = f * DEPTH if f <= NRHS else NRHS * DEPTH + DEPTH + (f - NRHS - 1) * (DEPTH - 1)
-        for face, rim, first in ((facelo, rimlo, 0), (facehi, rimhi, DEPTH + NZ)):
+        for rim, first in ((rimlo, 0), (rimhi, DEPTH + NZ)):
             for z in range(first, first + DEPTH):
                 far = DEPTH - z if first == 0 else z - first + 1
-                d = start + (depth - far if first == 0 else far - 1)
                 for l in range(2):
                     lanes = pl.ds(128 * l, 128)
-                    for t in range(NX // 8):
-                        value = face[d, 8 * t : 8 * t + 8, lanes] if far <= depth else zero
-                        block.put(f, z, l, t, value)
                     if far <= 2:
                         at, odd = 8 * f, z % 2
                     elif far == 3 and 8 * (f // 2) < FAR:
@@ -427,8 +447,13 @@
     for rim, z in ((rimlo, 0), (rimhi, DEPTH + NZ)):
         block.place_y(z, rim.at[rows, pl.ds(0, 128)], rim.at[rows, pl.ds(128, 128)])
 
-    for n in range(3):
-        copies[n].wait()
+    for copy in copies[:3] + planes:
+        copy.wait()
+    for f in range(FIELDS):
+        depth = DEPTH if f <= NRHS else DEPTH - 1
+        for d in range(depth):
+            block.close_ring(f, DEPTH - 1 - d)
+            block.close_ring(f, DEPTH + NZ + d)
     loop(1, DEPTH + 1, block.coefficients)
     loop(DEPTH + NZ - 1, EZ - 1, block.coefficients)
 
@@ -607,32 +632,22 @@
 
     place = at_x.astype(jnp.int32).reshape(1)
     face_shape = shape(FACE, NX, NY)
-    zlo, zhi, token = pl.pallas_call(
-        pack_faces,
-        out_shape=(face_shape, face_shape, jax.ShapeDtypeStruct((1,), jnp.int32)),
-        in_specs=[hbm()] * 5,
-        out_specs=(hbm(), hbm(), smem()),
+    x_shape = shape(FIELDS, NZ // 2, 8, NY)
+    zlo, zhi, *xmsgs = pl.pallas_call(
+        functools.partial(pack_faces, swap),
+        out_shape=(face_shape, face_shape) + (x_shape,) * (1 if swap else 2),
+        in_specs=[smem()] + [hbm()] * 5,
+        out_specs=(hbm(), hbm()) + (vmem(),) * (1 if swap else 2),
         scratch_shapes=[
             pltpu.VMEM((FIELDS, NZ, NX, NY), F32),
             pltpu.SemaphoreType.DMA((FIELDS,)),
             pltpu.SemaphoreType.DMA((2 * FIELDS,)),
         ],
         compiler_params=params(LIMIT),
-    )(*fields)
+        cost_estimate=cost(2.5),
+    )(place, *fields)
     facehi = move(zlo, "gz", -1)
     facelo = move(zhi, "gz", 1)
-    x_shape = shape(FIELDS, NZ // 2, 8, NY)
-    xmsgs = pl.pallas_call(
-        functools.partial(pack_rows, swap),
-        out_shape=(x_shape,) * (1 if swap else 2),
-        in_specs=[smem(), smem()] + [hbm()] * 5,
-        scratch_shapes=[
-            pltpu.VMEM((FIELDS, NZ, 8, NY), F32),
-            pltpu.VMEM((FIELDS, NZ, 8, NY), F32),
-            pltpu.SemaphoreType.DMA((2 * FIELDS,)),
-        ],
-        compiler_params=params(LIMIT),
-    )(place, token, *fields)
     if swap:
         x_parts = (lax.ppermute(xmsgs[0], "gx", [(0, 1), (1, 0)]),)
     else:
@@ -644,6 +659,7 @@
         out_shape=(own_shape, own_shape),
         in_specs=[vmem()] * 5,
         compiler_params=params(LIMIT),
+        cost_estimate=cost(2.5),
     )(*fields)
     rim_shape = shape(ROWS, NY)
     ylo, yhi = pl.pallas_call(
@@ -651,6 +667,7 @@
         out_shape=(rim_shape, rim_shape),
         in_specs=[smem()] + [vmem()] * (2 + len(x_parts)),
         compiler_params=params(16),
+        cost_estimate=cost(1),
     )(place, *own_rims, *x_parts)
     yup, ydn = move(ylo, "gy", -1), move(yhi, "gy", 1)
 
@@ -670,37 +687,40 @@
     inner, inner_faces = pl.pallas_call(
         functools.partial(krylov_inner, swap),
         out_shape=(inner_shape, inner_faces_shape),
-        in_specs=[smem()] + [vmem()] * (5 + len(x_parts) + 2),
+        in_specs=[smem()] + [hbm()] * 5 + [vmem()] * (len(x_parts) + 2),
         out_specs=(hbm(), hbm()),
         scratch_shapes=[
             pltpu.VMEM(inner_shape.shape, F32),
             pltpu.VMEM(inner_faces_shape.shape, F32),
+            pltpu.SemaphoreType.DMA((10,)),
             pltpu.SemaphoreType.DMA((7,)),
         ],
         compiler_params=params(LIMIT),
-        cost_estimate=pl.CostEstimate(flops=1 << 27, bytes_accessed=25 << 20, transcendentals=0),
+        cost_estimate=cost(7),
     )(place, *fields, *x_parts, yup, ydn)
 
     block = shape(COLS, NZ, 2, NX, 128)
     basis, message = pl.pallas_call(
         functools.partial(krylov_outer, swap),
         out_shape=(block, shape(devices, 2, 128)),
-        in_specs=[smem(), hbm(), hbm()] + [vmem()] * 4,
+        in_specs=[hbm(), hbm(), smem(), hbm(), hbm(), vmem(), vmem()],
         out_specs=(hbm(), vmem()),
         scratch_shapes=[
             pltpu.VMEM((COLS + NRHS, EZ, LT, EROWS, 128), F32),
             pltpu.VMEM((7, EZ, LT, ROWS, 128), F32),
             pltpu.VMEM((2, STACK, STACK), F32),
+            pltpu.SemaphoreType.DMA((4 * FIELDS,)),
             pltpu.SemaphoreType.DMA((7,)),
             pltpu.SemaphoreType.DMA((STEPS + 1,)),
         ],
         compiler_params=params(LIMIT),
-    )(place, inner, inner_faces, facelo, facehi, rimlo, rimhi)
+        cost_estimate=cost(15),
+    )(facelo, facehi, place, inner, inner_faces, rimlo, rimhi)
 
     message = exchange(message)
     first, message, factor_one = pl.pallas_call(
         functools.partial(first_pass, cells),
-        out_shape=(block, shape(1, 2, 128), shape(24, 128)),
+        out_shape=(block, shape(devices, 2, 128), shape(24, 128)),
         in_specs=[vmem(), hbm()],
         out_specs=(hbm(), vmem(), vmem()),
         scratch_shapes=[
@@ -713,7 +733,7 @@
         compiler_params=params(LIMIT),
     )(message, basis)
 
-    message = lax.all_gather(message[0], AXES)
+    message = exchange(message)
     return pl.pallas_call(
         functools.partial(second_pass, cells),
         out_shape=(shape(COLS, NZ, NX, NY), shape(COLS, COLS)),

time: 160 us -> 100 us (0.62)
  blocking collectives: 81.6 us -> 23.4 us
  Pallas kernels: 52.3 us -> 50.5 us
    all_gather x1 -> x0, blocking collectives: 68.9 us -> none  [body(): message = lax.all_gather(message[0], AXES)]
    all_to_all x1 -> x2, blocking collectives: 12.7 us -> 23.4 us  [exchange(): return lax.all_to_all(messages, AXES, 0, 0, tiled=True)]
    pallas_call x2 -> x1, Pallas kernels: 5.61 us -> 3.08 us  [body(): pl.pallas_call(functools.partial(pack_faces, swap), out_shape=(face_shape...]
  transfers between devices with their start and end apart: 7 -> 7, of which waited for: 2 -> 2; matrix products, arithmetic and copies ran while one was open for 0% -> 0% of each run, Pallas kernels for 6% -> 10%
where the time goes in v5:
time: 100 us; the launch traced here: 99.3 us
  Pallas kernels  50.5 us (50%)
  blocking collectives  23.4 us (23%)
  starting transfers between devices  18.9 us (19%)
  waiting for transfers between devices  3.55 us (4%)
  local copies, waits for them, and re-layouts  2.22 us (2%)
    all_to_all x2, blocking collectives, exchange(): return lax.all_to_all(messages, AXES, 0, 0, tiled=True)  23.4 us
    pallas_call x1, Pallas kernels, body(): pl.pallas_call(functools.partial(krylov_outer, swap), out_shape=(block, s...  18.6 us
    ppermute x6, starting transfers between devices, move(): return lax.ppermute(value, axis, pairs)  15.9 us
    pallas_call x1, Pallas kernels, body(): pl.pallas_call(functools.partial(first_pass, cells), out_shape=(block, sh...  10.6 us
    pallas_call x1, Pallas kernels, body(): pl.pallas_call(functools.partial(second_pass, cells), out_shape=(shape(CO...  7.86 us
    pallas_call x1, Pallas kernels, body(): pl.pallas_call(functools.partial(krylov_inner, swap), out_shape=(inner_sh...  7.47 us
    ppermute x6, waiting for transfers between devices, move(): return lax.ppermute(value, axis, pairs)  3.54 us
    pallas_call x1, Pallas kernels, body(): pl.pallas_call(functools.partial(pack_faces, swap), out_shape=(face_shape...  3.08 us
  transfers between devices with their start and end apart: 7, of which 2 were waited for; matrix products, arithmetic and copies ran while one was open for 0% of the time, Pallas kernels for 10%

profile of v5, /device:TPU:0, one launch (start us, length us, event | category | flops | bytes accessed | tf_op | source)
XLA Modules:
  0.0 99.3 jit_solution(12393322645461264513)
XLA Ops:
  0.6 3.1 %shard_map.68 = (f32[29,32,256]{2,1,0:T(8,128)}, f32[29,32,256]{2,1,0:T(8,128)}, f32[8,4,8,256]{3,2,1,0:T(8,128)}) custom-call(s32[1]{0:T(128)} %bitcast.place, f32[4,8,32,256]{3,2,1,0:T(8,128)} %rhs.5, f32[8,32,256]{2,1,0:T(8,128)} %cz.5, f32[8,32,256]{2,1,0:T(8,128)} %cx.5, f32[8,32,256]{2,1,0:T(8,128)} %cy.5, f32[8,32,256]{2,1,0:T(8,128)} %dg.5), custom_call_target="tpu_custom_call" | custom-call | bytes 9000000 | tf_op jit(solution)/shard_map/pallas_call | solution.py:636
  3.7 3.0 %collective-permute-start.2 = (f32[8,4,8,256]{3,2,1,0:T(8,128)}, f32[8,4,8,256]{3,2,1,0:T(8,128)S(1)}, u32[]{:S(2)}, u32[]{:S(2)}) collective-permute-start(f32[8,4,8,256]{3,2,1,0:T(8,128)} %get-tuple-element.18), channel_id=1, source_target_pairs={{0,16},{16,0},{1,17},{17,1},{2,18},{18,2},{3,19},{19,3},{4,20},{20... | collective-permute-start | bytes 786440 | tf_op jit(solution)/shard_map/ppermute | solution.py:652
  6.8 4.4 %collective-permute-start = (f32[29,32,256]{2,1,0:T(8,128)}, f32[29,32,256]{2,1,0:T(8,128)}, u32[]{:S(2)}, u32[]{:S(2)}) collective-permute-start(f32[29,32,256]{2,1,0:T(8,128)} %get-tuple-element.16), channel_id=1, source_target_pairs={{0,1},{1,2},{2,3},{4,5},{5,6},{6,7},{8,9},{9,10},{10,11},{12,13},{... | collective-permute-start | bytes 2850824 | tf_op jit(solution)/shard_map/ppermute | solution.py:618
  11.2 1.3 %collective-permute-start.1 = (f32[29,32,256]{2,1,0:T(8,128)}, f32[29,32,256]{2,1,0:T(8,128)}, u32[]{:S(2)}, u32[]{:S(2)}) collective-permute-start(f32[29,32,256]{2,1,0:T(8,128)} %get-tuple-element.17), channel_id=1, source_target_pairs={{1,0},{2,1},{3,2},{5,4},{6,5},{7,6},{9,8},{10,9},{11,10},{13,12},{... | collective-permute-start | bytes 2850824 | tf_op jit(solution)/shard_map/ppermute | solution.py:618
  12.5 2.7 %shard_map.69 = (f32[32,256]{1,0:T(8,128)}, f32[32,256]{1,0:T(8,128)}) custom-call(f32[4,8,32,256]{3,2,1,0:T(8,128)} %rhs.5, f32[8,32,256]{2,1,0:T(8,128)} %cz.5, f32[8,32,256]{2,1,0:T(8,128)} %cx.5, f32[8,32,256]{2,1,0:T(8,128)} %cy.5, f32[8,32,256]{2,1,0:T(8,128)} %dg.5), custom_call_target="tpu_custom_call" | custom-call | bytes 9000000 | tf_op jit(solution)/shard_map/pallas_call | solution.py:657
  15.2 0.0 collective-permute-done.2.refs_0_.rest_0_
  15.2 0.0 copy-start
  15.2 0.0 copy-start.1
  15.2 0.8 copy-done.1
  15.9 0.0 copy-start.2
  15.9 0.8 copy-done.2
  16.7 0.2 shard_map.70
  16.9 1.3 %collective-permute-start.3 = (f32[40,256]{1,0:T(8,128)S(1)}, f32[40,256]{1,0:T(8,128)S(1)}, u32[]{:S(2)}, u32[]{:S(2)}) collective-permute-start(f32[40,256]{1,0:T(8,128)S(1)} %get-tuple-element.21), channel_id=1, source_target_pairs={{4,0},{8,4},{12,8},{5,1},{9,5},{13,9},{6,2},{10,6},{14,10},{7,3},{... | collective-permute-start | bytes 122888 | tf_op jit(solution)/shard_map/ppermute | solution.py:618
  18.3 3.0 %collective-permute-start.4 = (f32[40,256]{1,0:T(8,128)S(1)}, f32[40,256]{1,0:T(8,128)S(1)}, u32[]{:S(2)}, u32[]{:S(2)}) collective-permute-start(f32[40,256]{1,0:T(8,128)S(1)} %get-tuple-element.22), channel_id=1, source_target_pairs={{0,4},{4,8},{8,12},{1,5},{5,9},{9,13},{2,6},{6,10},{10,14},{3,7},{... | collective-permute-start | bytes 122888 | tf_op jit(solution)/shard_map/ppermute | solution.py:618
  21.3 0.0 collective-permute-done.3.rest_1_
  21.3 0.0 copy-start.3
  21.3 0.8 collective-permute-done.4.rest_2_
  22.2 0.0 copy-start.4
  22.2 4.6 %collective-permute-start.5 = (f32[128,256]{1,0:T(8,128)S(1)}, f32[128,256]{1,0:T(8,128)S(1)}, u32[]{:S(2)}, u32[]{:S(2)}) collective-permute-start(f32[128,256]{1,0:T(8,128)S(1)} %maximum_maximum_fusion), channel_id=1, source_target_pairs={{0,1},{1,2},{2,3},{4,5},{5,6},{6,7},{8,9},{9,10},{10,11},{12,13},{... | collective-permute-start | bytes 393224 | tf_op jit(solution)/shard_map/ppermute | solution.py:618
  26.8 1.3 %collective-permute-start.6 = (f32[128,256]{1,0:T(8,128)S(1)}, f32[128,256]{1,0:T(8,128)S(1)}, u32[]{:S(2)}, u32[]{:S(2)}) collective-permute-start(f32[128,256]{1,0:T(8,128)S(1)} %maximum_maximum_fusion.1), channel_id=1, source_target_pairs={{1,0},{2,1},{3,2},{5,4},{6,5},{7,6},{9,8},{10,9},{11,10},{13,12},{... | collective-permute-start | bytes 393224 | tf_op jit(solution)/shard_map/ppermute | solution.py:618
  28.1 0.0 copy-done
  28.1 0.0 copy-done.3
  28.1 0.0 copy-done.4
  28.1 7.5 %shard_map.71 = (f32[20,8,3,56,128]{4,3,2,1,0:T(8,128)}, f32[7,6,3,40,128]{4,3,2,1,0:T(8,128)}) custom-call(s32[1]{0:T(128)} %bitcast.place, f32[4,8,32,256]{3,2,1,0:T(8,128)} %rhs.5, f32[8,32,256]{2,1,0:T(8,128)} %cz.5, f32[8,32,256]{2,1,0:T(8,128)} %cx.5, f32[8,32,256]{2,1,0:T(8,128)} %cy.5, f32[8,32,256]{2,1,0:T(8,128)} %dg.5, f32[8,4,8,256]{3,2,1,0:T(8,128)} %copy-done, ...), custom_call_target="tpu_custom_call" | custom-call | bytes 25200000 | tf_op jit(solution)/shard_map/pallas_call | solution.py:687
  35.6 0.0 collective-permute-done.5.rimlo
  35.6 0.0 copy-start.5
  35.6 2.7 %collective-permute-done.6.rimhi = f32[128,256]{1,0:T(8,128)S(1)} collective-permute-done((f32[128,256]{1,0:T(8,128)S(1)}, f32[128,256]{1,0:T(8,128)S(1)}, u32[]{:S(2)}, u32[]{:S(2)}) %collective-permute-start.6) | collective-permute-done | bytes 131104 | tf_op jit(solution)/shard_map/ppermute | solution.py:618
  38.3 0.0 copy-start.6
  38.3 0.0 collective-permute-done.facelo
  38.3 0.0 collective-permute-done.1.facehi
  38.3 0.0 copy-done.5
  38.3 0.6 copy-done.6
  39.0 18.6 %shard_map.72 = (f32[20,8,2,32,128]{4,3,2,1,0:T(8,128)}, f32[32,2,128]{2,1,0:T(2,128)}) custom-call(f32[29,32,256]{2,1,0:T(8,128)} %collective-permute-done.facelo, f32[29,32,256]{2,1,0:T(8,128)} %collective-permute-done.1.facehi, s32[1]{0:T(128)} %bitcast.place, f32[20,8,3,56,128]{4,3,2,1,0:T(8,128)} %get-tuple-element.23.inner, ...), custom_call_target="tpu_custom_call" | custom-call | bytes 54000000 | tf_op jit(solution)/shard_map/pallas_call | solution.py:703
  57.5 12.8 %all_to_all.10.message = f32[32,2,128]{2,1,0:T(2,128)} all-to-all(f32[32,2,128]{2,1,0:T(2,128)} %get-tuple-element.25), channel_id=1, replica_groups=mesh['gx'=2,'gy'=4,'gz'=4] {'gx','gy','gz'}, dimensions={0} | all-to-all | bytes 65536 | tf_op jit(solution)/shard_map/all_to_all | solution.py:622
  70.3 10.6 %shard_map.73 = (f32[20,8,2,32,128]{4,3,2,1,0:T(8,128)}, f32[32,2,128]{2,1,0:T(2,128)}, f32[24,128]{1,0:T(8,128)}) custom-call(f32[32,2,128]{2,1,0:T(2,128)} %all_to_all.10.message, f32[20,8,2,32,128]{4,3,2,1,0:T(8,128)} %get-tuple-element.26.basis_hbm), custom_call_target="tpu_custom_call" | custom-call | tf_op jit(solution)/shard_map/pallas_call | solution.py:721
  80.9 10.6 %all_to_all.11.message = f32[32,2,128]{2,1,0:T(2,128)} all-to-all(f32[32,2,128]{2,1,0:T(2,128)} %get-tuple-element.27), channel_id=1, replica_groups=mesh['gx'=2,'gy'=4,'gz'=4] {'gx','gy','gz'}, dimensions={0} | all-to-all | bytes 65536 | tf_op jit(solution)/shard_map/all_to_all | solution.py:622
  91.5 7.9 %shard_map.74 = (f32[20,8,32,256]{3,2,1,0:T(8,128)}, f32[20,20]{1,0:T(8,128)}) custom-call(f32[32,2,128]{2,1,0:T(2,128)} %all_to_all.11.message, f32[24,128]{1,0:T(8,128)} %get-tuple-element.28.factor_one, f32[20,8,2,32,128]{4,3,2,1,0:T(8,128)} %get-tuple-element.29.first_hbm), custom_call_target="tpu_custom_call" | custom-call | tf_op jit(solution)/shard_map/pallas_call | solution.py:737
  (8 shorter events, 0.1 us)
Async XLA Ops:
  3.7 11.5 %collective-permute-start.2 = (f32[8,4,8,256]{3,2,1,0:T(8,128)}, f32[8,4,8,256]{3,2,1,0:T(8,128)S(1)}, u32[]{:S(2)}, u32[]{:S(2)}) collective-permute-start(f32[8,4,8,256]{3,2,1,0:T(8,128)} %get-tuple-element.18), channel_id=1, source_target_pairs={{0,16},{16,0},{1,17},{17,1},{2,18},{18,2},{3,19},{19,3},{4,20},{20... | collective-permute-start | bytes 786440 | tf_op jit(solution)/shard_map/ppermute | solution.py:652
  6.8 31.6 %collective-permute-start = (f32[29,32,256]{2,1,0:T(8,128)}, f32[29,32,256]{2,1,0:T(8,128)}, u32[]{:S(2)}, u32[]{:S(2)}) collective-permute-start(f32[29,32,256]{2,1,0:T(8,128)} %get-tuple-element.16), channel_id=1, source_target_pairs={{0,1},{1,2},{2,3},{4,5},{5,6},{6,7},{8,9},{9,10},{10,11},{12,13},{... | collective-permute-start | bytes 2850824 | tf_op jit(solution)/shard_map/ppermute | solution.py:618
  11.2 27.1 %collective-permute-start.1 = (f32[29,32,256]{2,1,0:T(8,128)}, f32[29,32,256]{2,1,0:T(8,128)}, u32[]{:S(2)}, u32[]{:S(2)}) collective-permute-start(f32[29,32,256]{2,1,0:T(8,128)} %get-tuple-element.17), channel_id=1, source_target_pairs={{1,0},{2,1},{3,2},{5,4},{6,5},{7,6},{9,8},{10,9},{11,10},{13,12},{... | collective-permute-start | bytes 2850824 | tf_op jit(solution)/shard_map/ppermute | solution.py:618
  15.2 12.9 %copy-start = (f32[8,4,8,256]{3,2,1,0:T(8,128)}, f32[8,4,8,256]{3,2,1,0:T(8,128)S(1)}, u32[]{:S(2)}) copy-start(f32[8,4,8,256]{3,2,1,0:T(8,128)S(1)} %collective-permute-done.2.refs_0_.rest_0_) | copy-start | bytes 786436
  15.2 0.8 copy-start.1
  15.9 0.8 copy-start.2
  16.9 4.4 %collective-permute-start.3 = (f32[40,256]{1,0:T(8,128)S(1)}, f32[40,256]{1,0:T(8,128)S(1)}, u32[]{:S(2)}, u32[]{:S(2)}) collective-permute-start(f32[40,256]{1,0:T(8,128)S(1)} %get-tuple-element.21), channel_id=1, source_target_pairs={{4,0},{8,4},{12,8},{5,1},{9,5},{13,9},{6,2},{10,6},{14,10},{7,3},{... | collective-permute-start | bytes 122888 | tf_op jit(solution)/shard_map/ppermute | solution.py:618
  18.3 3.9 %collective-permute-start.4 = (f32[40,256]{1,0:T(8,128)S(1)}, f32[40,256]{1,0:T(8,128)S(1)}, u32[]{:S(2)}, u32[]{:S(2)}) collective-permute-start(f32[40,256]{1,0:T(8,128)S(1)} %get-tuple-element.22), channel_id=1, source_target_pairs={{0,4},{4,8},{8,12},{1,5},{5,9},{9,13},{2,6},{6,10},{10,14},{3,7},{... | collective-permute-start | bytes 122888 | tf_op jit(solution)/shard_map/ppermute | solution.py:618
  21.3 6.8 %copy-start.3 = (f32[40,256]{1,0:T(8,128)}, f32[40,256]{1,0:T(8,128)S(1)}, u32[]{:S(2)}) copy-start(f32[40,256]{1,0:T(8,128)S(1)} %collective-permute-done.3.rest_1_) | copy-start | bytes 122884
  22.2 5.9 %copy-start.4 = (f32[40,256]{1,0:T(8,128)}, f32[40,256]{1,0:T(8,128)S(1)}, u32[]{:S(2)}) copy-start(f32[40,256]{1,0:T(8,128)S(1)} %collective-permute-done.4.rest_2_) | copy-start | bytes 122884
  22.2 13.4 %collective-permute-start.5 = (f32[128,256]{1,0:T(8,128)S(1)}, f32[128,256]{1,0:T(8,128)S(1)}, u32[]{:S(2)}, u32[]{:S(2)}) collective-permute-start(f32[128,256]{1,0:T(8,128)S(1)} %maximum_maximum_fusion), channel_id=1, source_target_pairs={{0,1},{1,2},{2,3},{4,5},{5,6},{6,7},{8,9},{9,10},{10,11},{12,13},{... | collective-permute-start | bytes 393224 | tf_op jit(solution)/shard_map/ppermute | solution.py:618
  26.8 11.5 %collective-permute-start.6 = (f32[128,256]{1,0:T(8,128)S(1)}, f32[128,256]{1,0:T(8,128)S(1)}, u32[]{:S(2)}, u32[]{:S(2)}) collective-permute-start(f32[128,256]{1,0:T(8,128)S(1)} %maximum_maximum_fusion.1), channel_id=1, source_target_pairs={{1,0},{2,1},{3,2},{5,4},{6,5},{7,6},{9,8},{10,9},{11,10},{13,12},{... | collective-permute-start | bytes 393224 | tf_op jit(solution)/shard_map/ppermute | solution.py:618
  35.6 2.7 %copy-start.5 = (f32[128,256]{1,0:T(8,128)}, f32[128,256]{1,0:T(8,128)S(1)}, u32[]{:S(2)}) copy-start(f32[128,256]{1,0:T(8,128)S(1)} %collective-permute-done.5.rimlo) | copy-start | bytes 393220
  38.3 0.7 copy-start.6

commit v6 on v5

--- a/solution.py
+++ b/solution.py
@@ -231,18 +231,17 @@
 
 
 class Block:
-    def __init__(self, store, base, faces, faces_base, one):
-        self.one = one
-        self.store, self.base, self.faces, self.faces_base = store, base, faces, faces_base
+    def __init__(self, stores, base, faces, faces_base):
+        self.stores, self.base, self.faces, self.faces_base = stores, base, faces, faces_base
         self.lane = lane_ids((8, 128))
 
     def put(self, f, z, l, t, value):
-        z = z - self.base
-        self.store[f, z, l, 8 + 8 * t : 16 + 8 * t, :] = value
+        store, f, z = self.stores[f // NRHS], f % NRHS, z - self.base
+        store[f, z, l, 8 + 8 * t : 16 + 8 * t, :] = value
         if t == 0:
-            self.store[f, z, l, 8 + ROWS : 16 + ROWS, :] = value
+            store[f, z, l, 8 + ROWS : 16 + ROWS, :] = value
         if t == ROWS // 8 - 1:
-            self.store[f, z, l, 0:8, :] = value
+            store[f, z, l, 0:8, :] = value
 
     def place_y(self, z, up, dn):
         for t in range(ROWS // 8):
@@ -256,13 +255,13 @@
                     self.put(f, z + zz, 2, t, value)
 
     def tiles(self, f, z, t, off):
-        row = 8 + 8 * t + (off * self.one if off else 0)
-        return [self.store[f, z - self.base, l, pl.ds(row, 8), :] for l in range(LT)]
+        store, f, z = self.stores[f // NRHS], f % NRHS, z - self.base
+        return [store[f, z, l, pl.ds(8 + 8 * t + off, 8), :] for l in range(LT)]
 
     def close_ring(self, f, z):
-        z = z - self.base
+        store, f, z = self.stores[f // NRHS], f % NRHS, z - self.base
         for l in range(2):
-            self.store[f, z, l, 8 + ROWS : 16 + ROWS, :] = self.store[f, z, l, 8:16, :]
+            store[f, z, l, 8 + ROWS : 16 + ROWS, :] = store[f, z, l, 8:16, :]
 
     def lane_up(self, tri):
         rolled = [pltpu.roll(v, 127, 1) for v in tri]
@@ -320,10 +319,6 @@
                     self.put(slot(k + 1) + r, z, l, t, value)
 
 
-def dynamic_one(place):
-    return (place[0] >> 24) + 1
-
-
 def loop(start, stop, do):
     def step(n, carry):
         do(n)
@@ -336,7 +331,7 @@
     return DEPTH + k, DEPTH + NZ - k
 
 
-def inner_copies(inner, inner_faces, store, base, faces, faces_base, sems, out):
+def inner_copies(inner, inner_faces, stores, base, faces, faces_base, sems, out):
     def copy(n, there, here):
         src, dst = (here, there) if out else (there, here)
         return pltpu.make_async_copy(src, dst, sems.at[n])
@@ -349,25 +344,26 @@
         [(0, DEPTH, DEPTH + NZ), (NRHS, DEPTH, DEPTH + 2), (NRHS, DEPTH + NZ - 2, DEPTH + NZ)]
         + [(slot(k), *inner_planes(k)) for k in range(1, STEPS)]
     ):
-        result.append(copy(n, planes(inner, f, start, stop, DEPTH), planes(store, f, start, stop, base)))
+        there = planes(inner, f, start, stop, DEPTH)
+        result.append(copy(n, there, stores[f // NRHS].at[:, pl.ds(start - base, stop - start)]))
     start, stop = inner_planes(1)
     result.append(copy(len(result), inner_faces, faces.at[:, pl.ds(start - faces_base, stop - start)]))
     return result
 
 
 def krylov_inner(swap, place, rhs, cz, cx, cy, dg, *rest):
-    above, below, yup, ydn, inner, inner_faces, store, faces, load_sems, sems = rest if not swap else rest[:1] + rest
+    above, below, yup, ydn, inner, inner_faces, *stores, faces, load_sems, sems = rest if not swap else rest[:1] + rest
     keep_up, keep_dn = keep_sides(swap, place)
-    block = Block(store, DEPTH, faces, DEPTH + 1, dynamic_one(place))
+    block = Block(stores, DEPTH, faces, DEPTH + 1)
     loads = []
     for n, src in enumerate((rhs, cz, cx, cy, dg)):
         for l in range(2):
             lanes = pl.ds(128 * l, 128)
             rows = pl.ds(8, NX)
             if n == 0:
-                src_at, dst = src.at[:, :, :, lanes], store.at[pl.ds(0, NRHS), :, l, rows, :]
+                src_at, dst = src.at[:, :, :, lanes], stores[0].at[:, :, l, rows, :]
             else:
-                src_at, dst = src.at[:, :, lanes], store.at[NRHS + n - 1, :, l, rows, :]
+                src_at, dst = src.at[:, :, lanes], stores[1].at[n - 1, :, l, rows, :]
             loads.append(pltpu.make_async_copy(src_at, dst, load_sems.at[2 * n + l]))
             loads[-1].start()
     for f in range(FIELDS):
@@ -385,7 +381,7 @@
     for f in range(FIELDS):
         for z in range(DEPTH, DEPTH + NZ):
             block.close_ring(f, z)
-    copies = inner_copies(inner, inner_faces, store, DEPTH, faces, DEPTH + 1, sems, True)
+    copies = inner_copies(inner, inner_faces, stores, DEPTH, faces, DEPTH + 1, sems, True)
     for n in range(3):
         copies[n].start()
     loop(*inner_planes(1), block.coefficients)
@@ -403,12 +399,13 @@
 def krylov_outer(
     swap, facelo, facehi, place, inner, inner_faces, rimlo, rimhi,
     basis, message,
-    store, faces, accs, plane_sems, loads, saves,
+    *rest,
 ):
     keep_up, keep_dn = keep_sides(swap, place)
     n_x = 1 if swap else 2
-    block = Block(store, 0, faces, 0, dynamic_one(place))
-    copies = inner_copies(inner, inner_faces, store, 0, faces, 0, loads, False)
+    *stores, faces, accs, plane_sems, loads, saves = rest
+    block = Block(stores, 0, faces, 0)
+    copies = inner_copies(inner, inner_faces, stores, 0, faces, 0, loads, False)
     planes = []
     start = 0
     for f in range(FIELDS):
@@ -418,12 +415,12 @@
                 planes.append(
                     pltpu.make_async_copy(
                         face.at[pl.ds(start, depth), :, pl.ds(128 * l, 128)],
-                        store.at[f, pl.ds(z, depth), l, pl.ds(8, NX), :],
+                        stores[f // NRHS].at[f % NRHS, pl.ds(z, depth), l, pl.ds(8, NX), :],
                         plane_sems.at[4 * f + 2 * side + l],
                     )
                 )
         start += depth
-    for copy in copies[:3] + planes + copies[3:]:
+    for copy in copies[:3] + planes:
         copy.start()
 
     zero = jnp.zeros((8, 128), F32)
@@ -449,6 +446,8 @@
 
     for copy in copies[:3] + planes:
         copy.wait()
+    for copy in copies[3:]:
+        copy.start()
     for f in range(FIELDS):
         depth = DEPTH if f <= NRHS else DEPTH - 1
         for d in range(depth):
@@ -461,7 +460,7 @@
 
     def send_block(k):
         copy = pltpu.make_async_copy(
-            store.at[pl.ds(slot(k), NRHS), pl.ds(DEPTH, NZ), pl.ds(0, 2), pl.ds(8, NX), :],
+            stores[slot(k) // NRHS].at[:, pl.ds(DEPTH, NZ), pl.ds(0, 2), pl.ds(8, NX), :],
             basis.at[pl.ds(k * NRHS, NRHS)],
             saves.at[k],
         )
@@ -484,8 +483,8 @@
 
     def products(z):
         def tile(i, t):
-            f = slot(i // NRHS) + i % NRHS
-            return jnp.concatenate([store[f, z, l, 8 + 8 * t : 16 + 8 * t, :] for l in range(2)], 1)
+            store = stores[slot(i // NRHS) // NRHS]
+            return jnp.concatenate([store[i % NRHS, z, l, 8 + 8 * t : 16 + 8 * t, :] for l in range(2)], 1)
 
         gram_add([jnp.concatenate([tile(i, t) for i in range(COLS)], 0) for t in range(NX // 8)], accs)
 
@@ -548,36 +547,44 @@
     return pltpu.make_async_copy(src.at[:, z], dst.at[:, z], sems.at[z])
 
 
-def first_pass(cells, message, basis_hbm, first_hbm, next_message, factor_out, basis, table, accs, loads, saves):
+def first_pass(
+    cells, message, basis_hbm, first_hbm, next_message, factor_out, basis, first, table, accs, loads, saves
+):
     for z in range(NZ):
         plane_copy(basis_hbm, basis, loads, z).start()
     factor_out[...] = factor_gram(message, cells, table)
     gram_zero(accs)
 
-    def chunk(z, carry):
-        plane_copy(basis_hbm, basis, loads, z).wait()
+    def products(z):
+        def tile(i, t):
+            return jnp.concatenate([first[i, z, l, 8 * t : 8 * t + 8, :] for l in range(2)], 1)
+
+        gram_add([jnp.concatenate([tile(i, t) for i in range(COLS)], 0) for t in range(NX // 8)], accs)
+
+    def apply(z):
         for l in range(2):
 
             def read(j, p):
                 return basis[j, z, l, 8 * p : 8 * p + 8, :]
 
             def write(i, p, value):
-                basis[i, z, l, 8 * p : 8 * p + 8, :] = value
+                first[i, z, l, 8 * p : 8 * p + 8, :] = value
 
             apply_rows(table, read, write)
-        plane_copy(basis, first_hbm, saves, z).start()
-
-        def tile(i, t):
-            return jnp.concatenate([basis[i, z, l, 8 * t : 8 * t + 8, :] for l in range(2)], 1)
-
-        gram_add([jnp.concatenate([tile(i, t) for i in range(COLS)], 0) for t in range(NX // 8)], accs)
-        return carry
-
-    lax.fori_loop(0, NZ, chunk, 0)
-
+        plane_copy(first, first_hbm, saves, z).start()
+
+    def both(z):
+        plane_copy(basis_hbm, basis, loads, z).wait()
+        products(z - 1)
+        apply(z)
+
+    plane_copy(basis_hbm, basis, loads, 0).wait()
+    apply(0)
+    loop(1, NZ, both)
+    products(NZ - 1)
     gram_message(accs, next_message)
     for z in range(NZ):
-        plane_copy(basis, first_hbm, saves, z).wait()
+        plane_copy(first, first_hbm, saves, z).wait()
 
 
 def second_pass(cells, message, factor_one, first_hbm, out_hbm, triangle, first, out, table, loads, saves):
@@ -690,7 +697,7 @@
         in_specs=[smem()] + [hbm()] * 5 + [vmem()] * (len(x_parts) + 2),
         out_specs=(hbm(), hbm()),
         scratch_shapes=[
-            pltpu.VMEM(inner_shape.shape, F32),
+            *[pltpu.VMEM((NRHS,) + inner_shape.shape[1:], F32)] * (STEPS + 1),
             pltpu.VMEM(inner_faces_shape.shape, F32),
             pltpu.SemaphoreType.DMA((10,)),
             pltpu.SemaphoreType.DMA((7,)),
@@ -706,7 +713,7 @@
         in_specs=[hbm(), hbm(), smem(), hbm(), hbm(), vmem(), vmem()],
         out_specs=(hbm(), vmem()),
         scratch_shapes=[
-            pltpu.VMEM((COLS + NRHS, EZ, LT, EROWS, 128), F32),
+            *[pltpu.VMEM((NRHS, EZ, LT, EROWS, 128), F32)] * (STEPS + 2),
             pltpu.VMEM((7, EZ, LT, ROWS, 128), F32),
             pltpu.VMEM((2, STACK, STACK), F32),
             pltpu.SemaphoreType.DMA((4 * FIELDS,)),
@@ -724,6 +731,7 @@
         in_specs=[vmem(), hbm()],
         out_specs=(hbm(), vmem(), vmem()),
         scratch_shapes=[
+            pltpu.VMEM(block.shape, F32),
             pltpu.VMEM(block.shape, F32),
             pltpu.VMEM((COLS, 24, 128), F32),
             pltpu.VMEM((2, STACK, STACK), F32),

time: 100 us -> 98.8 us (0.988)
  Pallas kernels: 50.5 us -> 49.2 us
where the time goes in v6:
time: 98.8 us; the launch traced here: 98.1 us
  Pallas kernels  49.2 us (50%)
  blocking collectives  22.8 us (23%)
  starting transfers between devices  18.9 us (19%)
  waiting for transfers between devices  4.13 us (4%)
  local copies, waits for them, and re-layouts  2.22 us (2%)
    all_to_all x2, blocking collectives, exchange(): return lax.all_to_all(messages, AXES, 0, 0, tiled=True)  22.8 us
    pallas_call x1, Pallas kernels, body(): pl.pallas_call(functools.partial(krylov_outer, swap), out_shape=(block, s...  17.7 us
    ppermute x6, starting transfers between devices, move(): return lax.ppermute(value, axis, pairs)  15.9 us
    pallas_call x1, Pallas kernels, body(): pl.pallas_call(functools.partial(first_pass, cells), out_shape=(block, sh...  10.7 us
    pallas_call x1, Pallas kernels, body(): pl.pallas_call(functools.partial(second_pass, cells), out_shape=(shape(CO...  7.86 us
    pallas_call x1, Pallas kernels, body(): pl.pallas_call(functools.partial(krylov_inner, swap), out_shape=(inner_sh...  6.89 us
    ppermute x6, waiting for transfers between devices, move(): return lax.ppermute(value, axis, pairs)  4.13 us
    pallas_call x1, Pallas kernels, body(): pl.pallas_call(functools.partial(pack_faces, swap), out_shape=(face_shape...  3.08 us
  transfers between devices with their start and end apart: 7, of which 2 were waited for; matrix products, arithmetic and copies ran while one was open for 0% of the time, Pallas kernels for 10%

profile of v6, /device:TPU:0, one launch (start us, length us, event | category | flops | bytes accessed | tf_op | source)
XLA Modules:
  0.0 98.1 jit_solution(12366554021934891841)
XLA Ops:
  0.6 3.1 %shard_map.68 = (f32[29,32,256]{2,1,0:T(8,128)}, f32[29,32,256]{2,1,0:T(8,128)}, f32[8,4,8,256]{3,2,1,0:T(8,128)}) custom-call(s32[1]{0:T(128)} %bitcast.place, f32[4,8,32,256]{3,2,1,0:T(8,128)} %rhs.5, f32[8,32,256]{2,1,0:T(8,128)} %cz.5, f32[8,32,256]{2,1,0:T(8,128)} %cx.5, f32[8,32,256]{2,1,0:T(8,128)} %cy.5, f32[8,32,256]{2,1,0:T(8,128)} %dg.5), custom_call_target="tpu_custom_call" | custom-call | bytes 9000000 | tf_op jit(solution)/shard_map/pallas_call | solution.py:643
  3.7 3.0 %collective-permute-start.2 = (f32[8,4,8,256]{3,2,1,0:T(8,128)}, f32[8,4,8,256]{3,2,1,0:T(8,128)S(1)}, u32[]{:S(2)}, u32[]{:S(2)}) collective-permute-start(f32[8,4,8,256]{3,2,1,0:T(8,128)} %get-tuple-element.18), channel_id=1, source_target_pairs={{0,16},{16,0},{1,17},{17,1},{2,18},{18,2},{3,19},{19,3},{4,20},{20... | collective-permute-start | bytes 786440 | tf_op jit(solution)/shard_map/ppermute | solution.py:659
  6.8 4.4 %collective-permute-start = (f32[29,32,256]{2,1,0:T(8,128)}, f32[29,32,256]{2,1,0:T(8,128)}, u32[]{:S(2)}, u32[]{:S(2)}) collective-permute-start(f32[29,32,256]{2,1,0:T(8,128)} %get-tuple-element.16), channel_id=1, source_target_pairs={{0,1},{1,2},{2,3},{4,5},{5,6},{6,7},{8,9},{9,10},{10,11},{12,13},{... | collective-permute-start | bytes 2850824 | tf_op jit(solution)/shard_map/ppermute | solution.py:625
  11.2 1.3 %collective-permute-start.1 = (f32[29,32,256]{2,1,0:T(8,128)}, f32[29,32,256]{2,1,0:T(8,128)}, u32[]{:S(2)}, u32[]{:S(2)}) collective-permute-start(f32[29,32,256]{2,1,0:T(8,128)} %get-tuple-element.17), channel_id=1, source_target_pairs={{1,0},{2,1},{3,2},{5,4},{6,5},{7,6},{9,8},{10,9},{11,10},{13,12},{... | collective-permute-start | bytes 2850824 | tf_op jit(solution)/shard_map/ppermute | solution.py:625
  12.5 2.7 %shard_map.69 = (f32[32,256]{1,0:T(8,128)}, f32[32,256]{1,0:T(8,128)}) custom-call(f32[4,8,32,256]{3,2,1,0:T(8,128)} %rhs.5, f32[8,32,256]{2,1,0:T(8,128)} %cz.5, f32[8,32,256]{2,1,0:T(8,128)} %cx.5, f32[8,32,256]{2,1,0:T(8,128)} %cy.5, f32[8,32,256]{2,1,0:T(8,128)} %dg.5), custom_call_target="tpu_custom_call" | custom-call | bytes 9000000 | tf_op jit(solution)/shard_map/pallas_call | solution.py:664
  15.2 0.0 collective-permute-done.2.refs_0_.rest_0_
  15.2 0.0 copy-start
  15.2 0.0 copy-start.1
  15.2 0.8 copy-done.1
  15.9 0.0 copy-start.2
  15.9 0.8 copy-done.2
  16.7 0.2 shard_map.70
  16.9 1.3 %collective-permute-start.3 = (f32[40,256]{1,0:T(8,128)S(1)}, f32[40,256]{1,0:T(8,128)S(1)}, u32[]{:S(2)}, u32[]{:S(2)}) collective-permute-start(f32[40,256]{1,0:T(8,128)S(1)} %get-tuple-element.21), channel_id=1, source_target_pairs={{4,0},{8,4},{12,8},{5,1},{9,5},{13,9},{6,2},{10,6},{14,10},{7,3},{... | collective-permute-start | bytes 122888 | tf_op jit(solution)/shard_map/ppermute | solution.py:625
  18.3 3.0 %collective-permute-start.4 = (f32[40,256]{1,0:T(8,128)S(1)}, f32[40,256]{1,0:T(8,128)S(1)}, u32[]{:S(2)}, u32[]{:S(2)}) collective-permute-start(f32[40,256]{1,0:T(8,128)S(1)} %get-tuple-element.22), channel_id=1, source_target_pairs={{0,4},{4,8},{8,12},{1,5},{5,9},{9,13},{2,6},{6,10},{10,14},{3,7},{... | collective-permute-start | bytes 122888 | tf_op jit(solution)/shard_map/ppermute | solution.py:625
  21.3 0.0 collective-permute-done.3.rest_1_
  21.3 0.0 copy-start.3
  21.3 0.8 collective-permute-done.4.rest_2_
  22.2 0.0 copy-start.4
  22.2 4.6 %collective-permute-start.5 = (f32[128,256]{1,0:T(8,128)S(1)}, f32[128,256]{1,0:T(8,128)S(1)}, u32[]{:S(2)}, u32[]{:S(2)}) collective-permute-start(f32[128,256]{1,0:T(8,128)S(1)} %maximum_maximum_fusion), channel_id=1, source_target_pairs={{0,1},{1,2},{2,3},{4,5},{5,6},{6,7},{8,9},{9,10},{10,11},{12,13},{... | collective-permute-start | bytes 393224 | tf_op jit(solution)/shard_map/ppermute | solution.py:625
  26.8 1.3 %collective-permute-start.6 = (f32[128,256]{1,0:T(8,128)S(1)}, f32[128,256]{1,0:T(8,128)S(1)}, u32[]{:S(2)}, u32[]{:S(2)}) collective-permute-start(f32[128,256]{1,0:T(8,128)S(1)} %maximum_maximum_fusion.1), channel_id=1, source_target_pairs={{1,0},{2,1},{3,2},{5,4},{6,5},{7,6},{9,8},{10,9},{11,10},{13,12},{... | collective-permute-start | bytes 393224 | tf_op jit(solution)/shard_map/ppermute | solution.py:625
  28.1 0.0 copy-done
  28.1 0.0 copy-done.3
  28.1 0.0 copy-done.4
  28.1 6.9 %shard_map.71 = (f32[20,8,3,56,128]{4,3,2,1,0:T(8,128)}, f32[7,6,3,40,128]{4,3,2,1,0:T(8,128)}) custom-call(s32[1]{0:T(128)} %bitcast.place, f32[4,8,32,256]{3,2,1,0:T(8,128)} %rhs.5, f32[8,32,256]{2,1,0:T(8,128)} %cz.5, f32[8,32,256]{2,1,0:T(8,128)} %cx.5, f32[8,32,256]{2,1,0:T(8,128)} %cy.5, f32[8,32,256]{2,1,0:T(8,128)} %dg.5, f32[8,4,8,256]{3,2,1,0:T(8,128)} %copy-done, ...), custom_call_target="tpu_custom_call" | custom-call | bytes 25200000 | tf_op jit(solution)/shard_map/pallas_call | solution.py:694
  35.0 0.0 collective-permute-done.5.rimlo
  35.0 0.0 copy-start.5
  35.0 3.3 %collective-permute-done.6.rimhi = f32[128,256]{1,0:T(8,128)S(1)} collective-permute-done((f32[128,256]{1,0:T(8,128)S(1)}, f32[128,256]{1,0:T(8,128)S(1)}, u32[]{:S(2)}, u32[]{:S(2)}) %collective-permute-start.6) | collective-permute-done | bytes 131104 | tf_op jit(solution)/shard_map/ppermute | solution.py:625
  38.3 0.0 copy-start.6
  38.3 0.0 collective-permute-done.facelo
  38.3 0.0 collective-permute-done.1.facehi
  38.3 0.0 copy-done.5
  38.3 0.6 copy-done.6
  39.0 17.7 %shard_map.72 = (f32[20,8,2,32,128]{4,3,2,1,0:T(8,128)}, f32[32,2,128]{2,1,0:T(2,128)}) custom-call(f32[29,32,256]{2,1,0:T(8,128)} %collective-permute-done.facelo, f32[29,32,256]{2,1,0:T(8,128)} %collective-permute-done.1.facehi, s32[1]{0:T(128)} %bitcast.place, f32[20,8,3,56,128]{4,3,2,1,0:T(8,128)} %get-tuple-element.23.inner, ...), custom_call_target="tpu_custom_call" | custom-call | bytes 54000000 | tf_op jit(solution)/shard_map/pallas_call | solution.py:710
  56.7 12.2 %all_to_all.10.message = f32[32,2,128]{2,1,0:T(2,128)} all-to-all(f32[32,2,128]{2,1,0:T(2,128)} %get-tuple-element.25), channel_id=1, replica_groups=mesh['gx'=2,'gy'=4,'gz'=4] {'gx','gy','gz'}, dimensions={0} | all-to-all | bytes 65536 | tf_op jit(solution)/shard_map/all_to_all | solution.py:629
  68.9 10.7 %shard_map.73 = (f32[20,8,2,32,128]{4,3,2,1,0:T(8,128)}, f32[32,2,128]{2,1,0:T(2,128)}, f32[24,128]{1,0:T(8,128)}) custom-call(f32[32,2,128]{2,1,0:T(2,128)} %all_to_all.10.message, f32[20,8,2,32,128]{4,3,2,1,0:T(8,128)} %get-tuple-element.26.basis_hbm), custom_call_target="tpu_custom_call" | custom-call | tf_op jit(solution)/shard_map/pallas_call | solution.py:728
  79.7 10.6 %all_to_all.11.message = f32[32,2,128]{2,1,0:T(2,128)} all-to-all(f32[32,2,128]{2,1,0:T(2,128)} %get-tuple-element.27), channel_id=1, replica_groups=mesh['gx'=2,'gy'=4,'gz'=4] {'gx','gy','gz'}, dimensions={0} | all-to-all | bytes 65536 | tf_op jit(solution)/shard_map/all_to_all | solution.py:629
  90.2 7.9 %shard_map.74 = (f32[20,8,32,256]{3,2,1,0:T(8,128)}, f32[20,20]{1,0:T(8,128)}) custom-call(f32[32,2,128]{2,1,0:T(2,128)} %all_to_all.11.message, f32[24,128]{1,0:T(8,128)} %get-tuple-element.28.factor_one, f32[20,8,2,32,128]{4,3,2,1,0:T(8,128)} %get-tuple-element.29.first_hbm), custom_call_target="tpu_custom_call" | custom-call | tf_op jit(solution)/shard_map/pallas_call | solution.py:745
  (8 shorter events, 0.1 us)
Async XLA Ops:
  3.7 11.5 %collective-permute-start.2 = (f32[8,4,8,256]{3,2,1,0:T(8,128)}, f32[8,4,8,256]{3,2,1,0:T(8,128)S(1)}, u32[]{:S(2)}, u32[]{:S(2)}) collective-permute-start(f32[8,4,8,256]{3,2,1,0:T(8,128)} %get-tuple-element.18), channel_id=1, source_target_pairs={{0,16},{16,0},{1,17},{17,1},{2,18},{18,2},{3,19},{19,3},{4,20},{20... | collective-permute-start | bytes 786440 | tf_op jit(solution)/shard_map/ppermute | solution.py:659
  6.8 31.6 %collective-permute-start = (f32[29,32,256]{2,1,0:T(8,128)}, f32[29,32,256]{2,1,0:T(8,128)}, u32[]{:S(2)}, u32[]{:S(2)}) collective-permute-start(f32[29,32,256]{2,1,0:T(8,128)} %get-tuple-element.16), channel_id=1, source_target_pairs={{0,1},{1,2},{2,3},{4,5},{5,6},{6,7},{8,9},{9,10},{10,11},{12,13},{... | collective-permute-start | bytes 2850824 | tf_op jit(solution)/shard_map/ppermute | solution.py:625
  11.2 27.1 %collective-permute-start.1 = (f32[29,32,256]{2,1,0:T(8,128)}, f32[29,32,256]{2,1,0:T(8,128)}, u32[]{:S(2)}, u32[]{:S(2)}) collective-permute-start(f32[29,32,256]{2,1,0:T(8,128)} %get-tuple-element.17), channel_id=1, source_target_pairs={{1,0},{2,1},{3,2},{5,4},{6,5},{7,6},{9,8},{10,9},{11,10},{13,12},{... | collective-permute-start | bytes 2850824 | tf_op jit(solution)/shard_map/ppermute | solution.py:625
  15.2 12.9 %copy-start = (f32[8,4,8,256]{3,2,1,0:T(8,128)}, f32[8,4,8,256]{3,2,1,0:T(8,128)S(1)}, u32[]{:S(2)}) copy-start(f32[8,4,8,256]{3,2,1,0:T(8,128)S(1)} %collective-permute-done.2.refs_0_.rest_0_) | copy-start | bytes 786436
  15.2 0.8 copy-start.1
  15.9 0.8 copy-start.2
  16.9 4.4 %collective-permute-start.3 = (f32[40,256]{1,0:T(8,128)S(1)}, f32[40,256]{1,0:T(8,128)S(1)}, u32[]{:S(2)}, u32[]{:S(2)}) collective-permute-start(f32[40,256]{1,0:T(8,128)S(1)} %get-tuple-element.21), channel_id=1, source_target_pairs={{4,0},{8,4},{12,8},{5,1},{9,5},{13,9},{6,2},{10,6},{14,10},{7,3},{... | collective-permute-start | bytes 122888 | tf_op jit(solution)/shard_map/ppermute | solution.py:625
  18.3 3.9 %collective-permute-start.4 = (f32[40,256]{1,0:T(8,128)S(1)}, f32[40,256]{1,0:T(8,128)S(1)}, u32[]{:S(2)}, u32[]{:S(2)}) collective-permute-start(f32[40,256]{1,0:T(8,128)S(1)} %get-tuple-element.22), channel_id=1, source_target_pairs={{0,4},{4,8},{8,12},{1,5},{5,9},{9,13},{2,6},{6,10},{10,14},{3,7},{... | collective-permute-start | bytes 122888 | tf_op jit(solution)/shard_map/ppermute | solution.py:625
  21.3 6.8 %copy-start.3 = (f32[40,256]{1,0:T(8,128)}, f32[40,256]{1,0:T(8,128)S(1)}, u32[]{:S(2)}) copy-start(f32[40,256]{1,0:T(8,128)S(1)} %collective-permute-done.3.rest_1_) | copy-start | bytes 122884
  22.2 5.9 %copy-start.4 = (f32[40,256]{1,0:T(8,128)}, f32[40,256]{1,0:T(8,128)S(1)}, u32[]{:S(2)}) copy-start(f32[40,256]{1,0:T(8,128)S(1)} %collective-permute-done.4.rest_2_) | copy-start | bytes 122884
  22.2 12.8 %collective-permute-start.5 = (f32[128,256]{1,0:T(8,128)S(1)}, f32[128,256]{1,0:T(8,128)S(1)}, u32[]{:S(2)}, u32[]{:S(2)}) collective-permute-start(f32[128,256]{1,0:T(8,128)S(1)} %maximum_maximum_fusion), channel_id=1, source_target_pairs={{0,1},{1,2},{2,3},{4,5},{5,6},{6,7},{8,9},{9,10},{10,11},{12,13},{... | collective-permute-start | bytes 393224 | tf_op jit(solution)/shard_map/ppermute | solution.py:625
  26.8 11.5 %collective-permute-start.6 = (f32[128,256]{1,0:T(8,128)S(1)}, f32[128,256]{1,0:T(8,128)S(1)}, u32[]{:S(2)}, u32[]{:S(2)}) collective-permute-start(f32[128,256]{1,0:T(8,128)S(1)} %maximum_maximum_fusion.1), channel_id=1, source_target_pairs={{1,0},{2,1},{3,2},{5,4},{6,5},{7,6},{9,8},{10,9},{11,10},{13,12},{... | collective-permute-start | bytes 393224 | tf_op jit(solution)/shard_map/ppermute | solution.py:625
  35.0 3.3 %copy-start.5 = (f32[128,256]{1,0:T(8,128)}, f32[128,256]{1,0:T(8,128)S(1)}, u32[]{:S(2)}) copy-start(f32[128,256]{1,0:T(8,128)S(1)} %collective-permute-done.5.rimlo) | copy-start | bytes 393220
  38.3 0.7 copy-start.6

commit v7 on v6

--- a/solution.py
+++ b/solution.py
@@ -59,7 +59,7 @@
     return rhs.at[f, z] if f < NRHS else (cz, cx, cy, dg)[f - NRHS].at[z]
 
 
-def pack_faces(swap, place, rhs, cz, cx, cy, dg, zlo, zhi, *rest):
+def pack_faces(swap, place, rhs, cz, cx, cy, dg, zlo, zhi, ylo, yhi, *rest):
     xmsgs, (whole, loads, saves) = rest[:-3], rest[-3:]
     copies = []
     for f in range(FIELDS):
@@ -91,6 +91,12 @@
             else:
                 xmsgs[0][f, m] = first
                 xmsgs[1][f, m] = last
+    for t in range(NX // 8):
+        for side, out in ((0, ylo), (1, yhi)):
+            for half in range(2):
+                out[8 * t : 8 * t + 8, 128 * half : 128 * half + 128] = pack_lanes(
+                    lambda f, zz: whole[f, 4 * half + zz, 8 * t : 8 * t + 8, 128 * side : 128 * side + 128], side
+                )
     for copy in planes:
         copy.wait()
 
@@ -124,18 +130,6 @@
                 tile = pltpu.roll(tile, shift, 1)
             acc = jnp.where((lane >= spot) & (lane < spot + 4), tile, acc)
     return acc
-
-
-def pack_own_rims(rhs, cz, cx, cy, dg, ylo, yhi):
-    for t in range(NX // 8):
-        for side, out in ((0, ylo), (1, yhi)):
-            for half in range(2):
-                out[8 * t : 8 * t + 8, 128 * half : 128 * half + 128] = pack_lanes(
-                    lambda f, zz: field_of(rhs, cz, cx, cy, dg, f, 4 * half + zz)[
-                        8 * t : 8 * t + 8, 128 * side : 128 * side + 128
-                    ],
-                    side,
-                )
 
 
 def pack_rims(swap, place, ylo_own, yhi_own, *refs):
@@ -231,7 +225,8 @@
 
 
 class Block:
-    def __init__(self, stores, base, faces, faces_base):
+    def __init__(self, stores, base, faces, faces_base, one):
+        self.one = one
         self.stores, self.base, self.faces, self.faces_base = stores, base, faces, faces_base
         self.lane = lane_ids((8, 128))
 
@@ -256,7 +251,8 @@
 
     def tiles(self, f, z, t, off):
         store, f, z = self.stores[f // NRHS], f % NRHS, z - self.base
-        return [store[f, z, l, pl.ds(8 + 8 * t + off, 8), :] for l in range(LT)]
+        row = 8 + 8 * t + (off * self.one if off else 0)
+        return [store[f, z, l, pl.ds(row, 8), :] for l in range(LT)]
 
     def close_ring(self, f, z):
         store, f, z = self.stores[f // NRHS], f % NRHS, z - self.base
@@ -319,6 +315,10 @@
                     self.put(slot(k + 1) + r, z, l, t, value)
 
 
+def dynamic_one(place):
+    return (place[0] >> 24) + 1
+
+
 def loop(start, stop, do):
     def step(n, carry):
         do(n)
@@ -341,7 +341,8 @@
 
     result = []
     for n, (f, start, stop) in enumerate(
-        [(0, DEPTH, DEPTH + NZ), (NRHS, DEPTH, DEPTH + 2), (NRHS, DEPTH + NZ - 2, DEPTH + NZ)]
+        [(f, z, z + 2) for f in (0, NRHS) for z in (DEPTH, DEPTH + NZ - 2)]
+        + [(0, DEPTH + 2, DEPTH + NZ - 2)]
         + [(slot(k), *inner_planes(k)) for k in range(1, STEPS)]
     ):
         there = planes(inner, f, start, stop, DEPTH)
@@ -354,7 +355,7 @@
 def krylov_inner(swap, place, rhs, cz, cx, cy, dg, *rest):
     above, below, yup, ydn, inner, inner_faces, *stores, faces, load_sems, sems = rest if not swap else rest[:1] + rest
     keep_up, keep_dn = keep_sides(swap, place)
-    block = Block(stores, DEPTH, faces, DEPTH + 1)
+    block = Block(stores, DEPTH, faces, DEPTH + 1, dynamic_one(place))
     loads = []
     for n, src in enumerate((rhs, cz, cx, cy, dg)):
         for l in range(2):
@@ -382,13 +383,13 @@
         for z in range(DEPTH, DEPTH + NZ):
             block.close_ring(f, z)
     copies = inner_copies(inner, inner_faces, stores, DEPTH, faces, DEPTH + 1, sems, True)
-    for n in range(3):
+    for n in range(5):
         copies[n].start()
     loop(*inner_planes(1), block.coefficients)
     copies[-1].start()
     for k in range(STEPS - 1):
         loop(*inner_planes(k + 1), functools.partial(block.apply, k))
-        copies[3 + k].start()
+        copies[5 + k].start()
     for copy in copies:
         copy.wait()
 
@@ -404,7 +405,7 @@
     keep_up, keep_dn = keep_sides(swap, place)
     n_x = 1 if swap else 2
     *stores, faces, accs, plane_sems, loads, saves = rest
-    block = Block(stores, 0, faces, 0)
+    block = Block(stores, 0, faces, 0, dynamic_one(place))
     copies = inner_copies(inner, inner_faces, stores, 0, faces, 0, loads, False)
     planes = []
     start = 0
@@ -420,7 +421,7 @@
                     )
                 )
         start += depth
-    for copy in copies[:3] + planes:
+    for copy in copies[:4] + planes:
         copy.start()
 
     zero = jnp.zeros((8, 128), F32)
@@ -444,9 +445,9 @@
     for rim, z in ((rimlo, 0), (rimhi, DEPTH + NZ)):
         block.place_y(z, rim.at[rows, pl.ds(0, 128)], rim.at[rows, pl.ds(128, 128)])
 
-    for copy in copies[:3] + planes:
+    for copy in copies[:4] + planes:
         copy.wait()
-    for copy in copies[3:]:
+    for copy in [copies[5], copies[-1], copies[6], copies[7], copies[4]]:
         copy.start()
     for f in range(FIELDS):
         depth = DEPTH if f <= NRHS else DEPTH - 1
@@ -467,7 +468,6 @@
         copy.start()
         sends.append(copy)
 
-    send_block(0)
     for k in range(STEPS):
         if k == 1:
             copies[-1].wait()
@@ -477,8 +477,10 @@
             lambda n, k=k: block.apply(k, n + k + 1 + jnp.where(n >= DEPTH, NZ - 2 - 2 * k, 0)),
         )
         if k < STEPS - 1:
-            copies[3 + k].wait()
+            copies[5 + k].wait()
         send_block(k + 1)
+    copies[4].wait()
+    send_block(0)
     gram_zero(accs)
 
     def products(z):
@@ -640,11 +642,12 @@
     place = at_x.astype(jnp.int32).reshape(1)
     face_shape = shape(FACE, NX, NY)
     x_shape = shape(FIELDS, NZ // 2, 8, NY)
-    zlo, zhi, *xmsgs = pl.pallas_call(
+    own_shape = shape(NX, NY)
+    zlo, zhi, ylo_own, yhi_own, *xmsgs = pl.pallas_call(
         functools.partial(pack_faces, swap),
-        out_shape=(face_shape, face_shape) + (x_shape,) * (1 if swap else 2),
+        out_shape=(face_shape, face_shape, own_shape, own_shape) + (x_shape,) * (1 if swap else 2),
         in_specs=[smem()] + [hbm()] * 5,
-        out_specs=(hbm(), hbm()) + (vmem(),) * (1 if swap else 2),
+        out_specs=(hbm(), hbm()) + (vmem(),) * (3 if swap else 4),
         scratch_shapes=[
             pltpu.VMEM((FIELDS, NZ, NX, NY), F32),
             pltpu.SemaphoreType.DMA((FIELDS,)),
@@ -660,14 +663,6 @@
     else:
         x_parts = (move(xmsgs[0], "gx", -1), move(xmsgs[1], "gx", 1))
 
-    own_shape = shape(NX, NY)
-    own_rims = pl.pallas_call(
-        pack_own_rims,
-        out_shape=(own_shape, own_shape),
-        in_specs=[vmem()] * 5,
-        compiler_params=params(LIMIT),
-        cost_estimate=cost(2.5),
-    )(*fields)
     rim_shape = shape(ROWS, NY)
     ylo, yhi = pl.pallas_call(
         functools.partial(pack_rims, swap),
@@ -675,7 +670,7 @@
         in_specs=[smem()] + [vmem()] * (2 + len(x_parts)),
         compiler_params=params(16),
         cost_estimate=cost(1),
-    )(place, *own_rims, *x_parts)
+    )(place, ylo_own, yhi_own, *x_parts)
     yup, ydn = move(ylo, "gy", -1), move(yhi, "gy", 1)
 
     def rim(half):
@@ -700,7 +695,7 @@
             *[pltpu.VMEM((NRHS,) + inner_shape.shape[1:], F32)] * (STEPS + 1),
             pltpu.VMEM(inner_faces_shape.shape, F32),
             pltpu.SemaphoreType.DMA((10,)),
-            pltpu.SemaphoreType.DMA((7,)),
+            pltpu.SemaphoreType.DMA((9,)),
         ],
         compiler_params=params(LIMIT),
         cost_estimate=cost(7),
@@ -717,7 +712,7 @@
             pltpu.VMEM((7, EZ, LT, ROWS, 128), F32),
             pltpu.VMEM((2, STACK, STACK), F32),
             pltpu.SemaphoreType.DMA((4 * FIELDS,)),
-            pltpu.SemaphoreType.DMA((7,)),
+            pltpu.SemaphoreType.DMA((9,)),
             pltpu.SemaphoreType.DMA((STEPS + 1,)),
         ],
         compiler_params=params(LIMIT),

time: 98.8 us -> 96.7 us (0.979)
  waiting for transfers between devices: 4.13 us -> 7.48 us
  Pallas kernels: 49.2 us -> 46.3 us
  blocking collectives: 22.8 us -> 21.1 us
    pallas_call x1 -> x0, Pallas kernels: 2.71 us -> none  [body(): pl.pallas_call(pack_own_rims, out_shape=(own_shape, own_shape), in_specs=...]
    ppermute x6, waiting for transfers between devices: 4.13 us -> 6.68 us  [move(): return lax.ppermute(value, axis, pairs)]
    all_to_all x2, blocking collectives: 22.8 us -> 21.1 us  [exchange(): return lax.all_to_all(messages, AXES, 0, 0, tiled=True)]
  transfers between devices with their start and end apart: 7 -> 7, of which waited for: 2 -> 4; matrix products, arithmetic and copies ran while one was open for 0% -> 0% of each run, Pallas kernels for 10% -> 8%
where the time goes in v7:
time: 96.7 us; the launch traced here: 96 us
  Pallas kernels  46.3 us (48%)
  blocking collectives  21.1 us (22%)
  starting transfers between devices  18.2 us (19%)
  waiting for transfers between devices  7.48 us (8%)
  local copies, waits for them, and re-layouts  2.22 us (2%)
    all_to_all x2, blocking collectives, exchange(): return lax.all_to_all(messages, AXES, 0, 0, tiled=True)  21.1 us
    pallas_call x1, Pallas kernels, body(): pl.pallas_call(functools.partial(krylov_outer, swap), out_shape=(block, s...  16.8 us
    ppermute x6, starting transfers between devices, move(): return lax.ppermute(value, axis, pairs)  15.1 us
    pallas_call x1, Pallas kernels, body(): pl.pallas_call(functools.partial(first_pass, cells), out_shape=(block, sh...  10.7 us
    pallas_call x1, Pallas kernels, body(): pl.pallas_call(functools.partial(second_pass, cells), out_shape=(shape(CO...  7.86 us
    pallas_call x1, Pallas kernels, body(): pl.pallas_call(functools.partial(krylov_inner, swap), out_shape=(inner_sh...  7.01 us
    ppermute x6, waiting for transfers between devices, move(): return lax.ppermute(value, axis, pairs)  6.68 us
    pallas_call x1, Pallas kernels, body(): pl.pallas_call(functools.partial(pack_faces, swap), out_shape=(face_shape...  3.63 us
  transfers between devices with their start and end apart: 7, of which 4 were waited for; matrix products, arithmetic and copies ran while one was open for 0% of the time, Pallas kernels for 8%

profile of v7, /device:TPU:0, one launch (start us, length us, event | category | flops | bytes accessed | tf_op | source)
XLA Modules:
  0.0 96.0 jit_solution(841122210153388233)
XLA Ops:
  0.6 3.6 %shard_map.68 = (f32[29,32,256]{2,1,0:T(8,128)}, f32[29,32,256]{2,1,0:T(8,128)}, f32[32,256]{1,0:T(8,128)}, f32[32,256]{1,0:T(8,128)}, f32[8,4,8,256]{3,2,1,0:T(8,128)}) custom-call(s32[1]{0:T(128)} %bitcast.place, f32[4,8,32,256]{3,2,1,0:T(8,128)} %rhs.3, f32[8,32,256]{2,1,0:T(8,128)} %cz.3, f32[8,32,256]{2,1,0:T(8,128)} %cx.3, f32[8,32,256]{2,1,0:T(8,128)} %cy.3, ...), custom_call_target="tpu_custom_call" | custom-call | bytes 9000000 | tf_op jit(solution)/shard_map/pallas_call | solution.py:646
  4.3 3.0 %collective-permute-start.2 = (f32[8,4,8,256]{3,2,1,0:T(8,128)}, f32[8,4,8,256]{3,2,1,0:T(8,128)S(1)}, u32[]{:S(2)}, u32[]{:S(2)}) collective-permute-start(f32[8,4,8,256]{3,2,1,0:T(8,128)} %get-tuple-element.18), channel_id=1, source_target_pairs={{0,16},{16,0},{1,17},{17,1},{2,18},{18,2},{3,19},{19,3},{4,20},{20... | collective-permute-start | bytes 786440 | tf_op jit(solution)/shard_map/ppermute | solution.py:662
  7.3 4.4 %collective-permute-start = (f32[29,32,256]{2,1,0:T(8,128)}, f32[29,32,256]{2,1,0:T(8,128)}, u32[]{:S(2)}, u32[]{:S(2)}) collective-permute-start(f32[29,32,256]{2,1,0:T(8,128)} %get-tuple-element.16), channel_id=1, source_target_pairs={{0,1},{1,2},{2,3},{4,5},{5,6},{6,7},{8,9},{9,10},{10,11},{12,13},{... | collective-permute-start | bytes 2850824 | tf_op jit(solution)/shard_map/ppermute | solution.py:627
  11.7 1.3 %collective-permute-start.1 = (f32[29,32,256]{2,1,0:T(8,128)}, f32[29,32,256]{2,1,0:T(8,128)}, u32[]{:S(2)}, u32[]{:S(2)}) collective-permute-start(f32[29,32,256]{2,1,0:T(8,128)} %get-tuple-element.17), channel_id=1, source_target_pairs={{1,0},{2,1},{3,2},{5,4},{6,5},{7,6},{9,8},{10,9},{11,10},{13,12},{... | collective-permute-start | bytes 2850824 | tf_op jit(solution)/shard_map/ppermute | solution.py:627
  13.0 0.8 collective-permute-done.2.refs_0_.rest_0_
  13.8 0.0 copy-start
  13.8 0.0 copy-start.1
  13.8 0.8 copy-done.1
  14.6 0.0 copy-start.2
  14.6 0.8 copy-done.2
  15.3 0.2 shard_map.69
  15.5 1.3 %collective-permute-start.3 = (f32[40,256]{1,0:T(8,128)S(1)}, f32[40,256]{1,0:T(8,128)S(1)}, u32[]{:S(2)}, u32[]{:S(2)}) collective-permute-start(f32[40,256]{1,0:T(8,128)S(1)} %get-tuple-element.21), channel_id=1, source_target_pairs={{4,0},{8,4},{12,8},{5,1},{9,5},{13,9},{6,2},{10,6},{14,10},{7,3},{... | collective-permute-start | bytes 122888 | tf_op jit(solution)/shard_map/ppermute | solution.py:627
  16.9 3.0 %collective-permute-start.4 = (f32[40,256]{1,0:T(8,128)S(1)}, f32[40,256]{1,0:T(8,128)S(1)}, u32[]{:S(2)}, u32[]{:S(2)}) collective-permute-start(f32[40,256]{1,0:T(8,128)S(1)} %get-tuple-element.22), channel_id=1, source_target_pairs={{0,4},{4,8},{8,12},{1,5},{5,9},{9,13},{2,6},{6,10},{10,14},{3,7},{... | collective-permute-start | bytes 122888 | tf_op jit(solution)/shard_map/ppermute | solution.py:627
  20.0 0.0 collective-permute-done.3.rest_1_
  20.0 0.0 copy-start.3
  20.0 0.8 collective-permute-done.4.rest_2_
  20.8 0.0 copy-start.4
  20.8 3.8 %collective-permute-start.5 = (f32[128,256]{1,0:T(8,128)S(1)}, f32[128,256]{1,0:T(8,128)S(1)}, u32[]{:S(2)}, u32[]{:S(2)}) collective-permute-start(f32[128,256]{1,0:T(8,128)S(1)} %maximum_maximum_fusion), channel_id=1, source_target_pairs={{0,1},{1,2},{2,3},{4,5},{5,6},{6,7},{8,9},{9,10},{10,11},{12,13},{... | collective-permute-start | bytes 393224 | tf_op jit(solution)/shard_map/ppermute | solution.py:627
  24.7 1.3 %collective-permute-start.6 = (f32[128,256]{1,0:T(8,128)S(1)}, f32[128,256]{1,0:T(8,128)S(1)}, u32[]{:S(2)}, u32[]{:S(2)}) collective-permute-start(f32[128,256]{1,0:T(8,128)S(1)} %maximum_maximum_fusion.1), channel_id=1, source_target_pairs={{1,0},{2,1},{3,2},{5,4},{6,5},{7,6},{9,8},{10,9},{11,10},{13,12},{... | collective-permute-start | bytes 393224 | tf_op jit(solution)/shard_map/ppermute | solution.py:627
  26.0 0.0 copy-done
  26.0 0.0 copy-done.3
  26.0 0.0 copy-done.4
  26.0 7.0 %shard_map.70 = (f32[20,8,3,56,128]{4,3,2,1,0:T(8,128)}, f32[7,6,3,40,128]{4,3,2,1,0:T(8,128)}) custom-call(s32[1]{0:T(128)} %bitcast.place, f32[4,8,32,256]{3,2,1,0:T(8,128)} %rhs.3, f32[8,32,256]{2,1,0:T(8,128)} %cz.3, f32[8,32,256]{2,1,0:T(8,128)} %cx.3, f32[8,32,256]{2,1,0:T(8,128)} %cy.3, f32[8,32,256]{2,1,0:T(8,128)} %dg.3, f32[8,4,8,256]{3,2,1,0:T(8,128)} %copy-done, ...), custom_call_target="tpu_custom_call" | custom-call | bytes 25200000 | tf_op jit(solution)/shard_map/pallas_call | solution.py:689
  33.0 0.8 collective-permute-done.5.rimlo
  33.8 0.0 copy-start.5
  33.8 5.1 %collective-permute-done.6.rimhi = f32[128,256]{1,0:T(8,128)S(1)} collective-permute-done((f32[128,256]{1,0:T(8,128)S(1)}, f32[128,256]{1,0:T(8,128)S(1)}, u32[]{:S(2)}, u32[]{:S(2)}) %collective-permute-start.6) | collective-permute-done | bytes 131104 | tf_op jit(solution)/shard_map/ppermute | solution.py:627
  38.9 0.0 copy-start.6
  38.9 0.0 collective-permute-done.facelo
  38.9 0.0 collective-permute-done.1.facehi
  38.9 0.0 copy-done.5
  38.9 0.6 copy-done.6
  39.5 16.8 %shard_map.71 = (f32[20,8,2,32,128]{4,3,2,1,0:T(8,128)}, f32[32,2,128]{2,1,0:T(2,128)}) custom-call(f32[29,32,256]{2,1,0:T(8,128)} %collective-permute-done.facelo, f32[29,32,256]{2,1,0:T(8,128)} %collective-permute-done.1.facehi, s32[1]{0:T(128)} %bitcast.place, f32[20,8,3,56,128]{4,3,2,1,0:T(8,128)} %get-tuple-element.23.inner, ...), custom_call_target="tpu_custom_call" | custom-call | bytes 54000000 | tf_op jit(solution)/shard_map/pallas_call | solution.py:705
  56.3 10.5 %all_to_all.10.message = f32[32,2,128]{2,1,0:T(2,128)} all-to-all(f32[32,2,128]{2,1,0:T(2,128)} %get-tuple-element.25), channel_id=1, replica_groups=mesh['gx'=2,'gy'=4,'gz'=4] {'gx','gy','gz'}, dimensions={0} | all-to-all | bytes 65536 | tf_op jit(solution)/shard_map/all_to_all | solution.py:631
  66.9 10.7 %shard_map.72 = (f32[20,8,2,32,128]{4,3,2,1,0:T(8,128)}, f32[32,2,128]{2,1,0:T(2,128)}, f32[24,128]{1,0:T(8,128)}) custom-call(f32[32,2,128]{2,1,0:T(2,128)} %all_to_all.10.message, f32[20,8,2,32,128]{4,3,2,1,0:T(8,128)} %get-tuple-element.26.basis_hbm), custom_call_target="tpu_custom_call" | custom-call | tf_op jit(solution)/shard_map/pallas_call | solution.py:723
  77.6 10.5 %all_to_all.11.message = f32[32,2,128]{2,1,0:T(2,128)} all-to-all(f32[32,2,128]{2,1,0:T(2,128)} %get-tuple-element.27), channel_id=1, replica_groups=mesh['gx'=2,'gy'=4,'gz'=4] {'gx','gy','gz'}, dimensions={0} | all-to-all | bytes 65536 | tf_op jit(solution)/shard_map/all_to_all | solution.py:631
  88.2 7.9 %shard_map.73 = (f32[20,8,32,256]{3,2,1,0:T(8,128)}, f32[20,20]{1,0:T(8,128)}) custom-call(f32[32,2,128]{2,1,0:T(2,128)} %all_to_all.11.message, f32[24,128]{1,0:T(8,128)} %get-tuple-element.28.factor_one, f32[20,8,2,32,128]{4,3,2,1,0:T(8,128)} %get-tuple-element.29.first_hbm), custom_call_target="tpu_custom_call" | custom-call | tf_op jit(solution)/shard_map/pallas_call | solution.py:740
  (8 shorter events, 0.1 us)
Async XLA Ops:
  4.3 9.5 %collective-permute-start.2 = (f32[8,4,8,256]{3,2,1,0:T(8,128)}, f32[8,4,8,256]{3,2,1,0:T(8,128)S(1)}, u32[]{:S(2)}, u32[]{:S(2)}) collective-permute-start(f32[8,4,8,256]{3,2,1,0:T(8,128)} %get-tuple-element.18), channel_id=1, source_target_pairs={{0,16},{16,0},{1,17},{17,1},{2,18},{18,2},{3,19},{19,3},{4,20},{20... | collective-permute-start | bytes 786440 | tf_op jit(solution)/shard_map/ppermute | solution.py:662
  7.3 31.6 %collective-permute-start = (f32[29,32,256]{2,1,0:T(8,128)}, f32[29,32,256]{2,1,0:T(8,128)}, u32[]{:S(2)}, u32[]{:S(2)}) collective-permute-start(f32[29,32,256]{2,1,0:T(8,128)} %get-tuple-element.16), channel_id=1, source_target_pairs={{0,1},{1,2},{2,3},{4,5},{5,6},{6,7},{8,9},{9,10},{10,11},{12,13},{... | collective-permute-start | bytes 2850824 | tf_op jit(solution)/shard_map/ppermute | solution.py:627
  11.7 27.1 %collective-permute-start.1 = (f32[29,32,256]{2,1,0:T(8,128)}, f32[29,32,256]{2,1,0:T(8,128)}, u32[]{:S(2)}, u32[]{:S(2)}) collective-permute-start(f32[29,32,256]{2,1,0:T(8,128)} %get-tuple-element.17), channel_id=1, source_target_pairs={{1,0},{2,1},{3,2},{5,4},{6,5},{7,6},{9,8},{10,9},{11,10},{13,12},{... | collective-permute-start | bytes 2850824 | tf_op jit(solution)/shard_map/ppermute | solution.py:627
  13.8 12.1 %copy-start = (f32[8,4,8,256]{3,2,1,0:T(8,128)}, f32[8,4,8,256]{3,2,1,0:T(8,128)S(1)}, u32[]{:S(2)}) copy-start(f32[8,4,8,256]{3,2,1,0:T(8,128)S(1)} %collective-permute-done.2.refs_0_.rest_0_) | copy-start | bytes 786436
  13.8 0.8 copy-start.1
  14.6 0.8 copy-start.2
  15.5 4.4 %collective-permute-start.3 = (f32[40,256]{1,0:T(8,128)S(1)}, f32[40,256]{1,0:T(8,128)S(1)}, u32[]{:S(2)}, u32[]{:S(2)}) collective-permute-start(f32[40,256]{1,0:T(8,128)S(1)} %get-tuple-element.21), channel_id=1, source_target_pairs={{4,0},{8,4},{12,8},{5,1},{9,5},{13,9},{6,2},{10,6},{14,10},{7,3},{... | collective-permute-start | bytes 122888 | tf_op jit(solution)/shard_map/ppermute | solution.py:627
  16.9 3.9 %collective-permute-start.4 = (f32[40,256]{1,0:T(8,128)S(1)}, f32[40,256]{1,0:T(8,128)S(1)}, u32[]{:S(2)}, u32[]{:S(2)}) collective-permute-start(f32[40,256]{1,0:T(8,128)S(1)} %get-tuple-element.22), channel_id=1, source_target_pairs={{0,4},{4,8},{8,12},{1,5},{5,9},{9,13},{2,6},{6,10},{10,14},{3,7},{... | collective-permute-start | bytes 122888 | tf_op jit(solution)/shard_map/ppermute | solution.py:627
  20.0 6.0 %copy-start.3 = (f32[40,256]{1,0:T(8,128)}, f32[40,256]{1,0:T(8,128)S(1)}, u32[]{:S(2)}) copy-start(f32[40,256]{1,0:T(8,128)S(1)} %collective-permute-done.3.rest_1_) | copy-start | bytes 122884
  20.8 5.2 %copy-start.4 = (f32[40,256]{1,0:T(8,128)}, f32[40,256]{1,0:T(8,128)S(1)}, u32[]{:S(2)}) copy-start(f32[40,256]{1,0:T(8,128)S(1)} %collective-permute-done.4.rest_2_) | copy-start | bytes 122884
  20.8 13.0 %collective-permute-start.5 = (f32[128,256]{1,0:T(8,128)S(1)}, f32[128,256]{1,0:T(8,128)S(1)}, u32[]{:S(2)}, u32[]{:S(2)}) collective-permute-start(f32[128,256]{1,0:T(8,128)S(1)} %maximum_maximum_fusion), channel_id=1, source_target_pairs={{0,1},{1,2},{2,3},{4,5},{5,6},{6,7},{8,9},{9,10},{10,11},{12,13},{... | collective-permute-start | bytes 393224 | tf_op jit(solution)/shard_map/ppermute | solution.py:627
  24.7 14.2 %collective-permute-start.6 = (f32[128,256]{1,0:T(8,128)S(1)}, f32[128,256]{1,0:T(8,128)S(1)}, u32[]{:S(2)}, u32[]{:S(2)}) collective-permute-start(f32[128,256]{1,0:T(8,128)S(1)} %maximum_maximum_fusion.1), channel_id=1, source_target_pairs={{1,0},{2,1},{3,2},{5,4},{6,5},{7,6},{9,8},{10,9},{11,10},{13,12},{... | collective-permute-start | bytes 393224 | tf_op jit(solution)/shard_map/ppermute | solution.py:627
  33.8 5.1 %copy-start.5 = (f32[128,256]{1,0:T(8,128)}, f32[128,256]{1,0:T(8,128)S(1)}, u32[]{:S(2)}) copy-start(f32[128,256]{1,0:T(8,128)S(1)} %collective-permute-done.5.rimlo) | copy-start | bytes 393220
  38.9 0.7 copy-start.6

commit v8 on v7

--- a/solution.py
+++ b/solution.py
@@ -59,7 +59,7 @@
     return rhs.at[f, z] if f < NRHS else (cz, cx, cy, dg)[f - NRHS].at[z]
 
 
-def pack_faces(swap, place, rhs, cz, cx, cy, dg, zlo, zhi, ylo, yhi, *rest):
+def pack_faces(swap, place, odd_z, rhs, cz, cx, cy, dg, z_one, z_two, ylo, yhi, *rest):
     xmsgs, (whole, loads, saves) = rest[:-3], rest[-3:]
     copies = []
     for f in range(FIELDS):
@@ -73,8 +73,8 @@
     for f in range(FIELDS):
         copies[f].wait()
         depth = DEPTH if f <= NRHS else DEPTH - 1
-        for side, out in ((0, zlo), (1, zhi)):
-            start = side * (NZ - depth)
+        for side, out in ((0, z_one), (1, z_two)):
+            start = jnp.where(odd_z[0] == side, NZ - depth, 0)
             planes.append(
                 pltpu.make_async_copy(
                     whole.at[f, pl.ds(start, depth)], out.at[pl.ds(at, depth)], saves.at[2 * f + side]
@@ -132,19 +132,32 @@
     return acc
 
 
-def pack_rims(swap, place, ylo_own, yhi_own, *refs):
-    above, below, ylo, yhi = refs if not swap else (refs[0],) + refs
+def pack_rims(swap, place, odd_y, ylo_own, yhi_own, *refs):
+    above, below, one, two = refs if not swap else (refs[0],) + refs
     keep_up, keep_dn = keep_sides(swap, place)
-    for side, own, out in ((0, ylo_own, ylo), (1, yhi_own, yhi)):
-        out[0:NX, :] = own[...]
-        lanes = slice(128 * side, 128 * side + 128)
-        for half in range(2):
-            out[NX:ROWS, 128 * half : 128 * half + 128] = pack_lanes(
-                lambda f, zz: halo_tile(
-                    above[f, 2 * half + zz // 2, :, lanes], below[f, 2 * half + zz // 2, :, lanes], zz % 2, keep_up, keep_dn
-                ),
-                side,
+    odd = odd_y[0] == 1
+    lo, hi = ylo_own[...], yhi_own[...]
+    one[0:NX, :] = jnp.where(odd, lo, hi)
+    two[0:NX, :] = jnp.where(odd, hi, lo)
+    for half in range(2):
+        halves = []
+        for side in range(2):
+            lanes = slice(128 * side, 128 * side + 128)
+            halves.append(
+                pack_lanes(
+                    lambda f, zz: halo_tile(
+                        above[f, 2 * half + zz // 2, :, lanes],
+                        below[f, 2 * half + zz // 2, :, lanes],
+                        zz % 2,
+                        keep_up,
+                        keep_dn,
+                    ),
+                    side,
+                )
             )
+        lo, hi = halves
+        one[NX:ROWS, 128 * half : 128 * half + 128] = jnp.where(odd, lo, hi)
+        two[NX:ROWS, 128 * half : 128 * half + 128] = jnp.where(odd, hi, lo)
 
 
 STACK = 8 * COLS
@@ -398,31 +411,50 @@
 
 
 def krylov_outer(
-    swap, facelo, facehi, place, inner, inner_faces, rimlo, rimhi,
+    swap, face_one, face_two, place, odd_z, inner, inner_faces, rim_one, rim_two,
     basis, message,
     *rest,
 ):
     keep_up, keep_dn = keep_sides(swap, place)
     n_x = 1 if swap else 2
-    *stores, faces, accs, plane_sems, loads, saves = rest
+    *stores, faces, accs, rims, plane_sems, loads, saves = rest
+    odd = odd_z[0] == 1
     block = Block(stores, 0, faces, 0, dynamic_one(place))
     copies = inner_copies(inner, inner_faces, stores, 0, faces, 0, loads, False)
-    planes = []
-    start = 0
-    for f in range(FIELDS):
-        depth = DEPTH if f <= NRHS else DEPTH - 1
-        for side, (face, z) in enumerate(((facelo, DEPTH - depth), (facehi, DEPTH + NZ))):
-            for l in range(2):
-                planes.append(
-                    pltpu.make_async_copy(
-                        face.at[pl.ds(start, depth), :, pl.ds(128 * l, 128)],
-                        stores[f // NRHS].at[f % NRHS, pl.ds(z, depth), l, pl.ds(8, NX), :],
-                        plane_sems.at[4 * f + 2 * side + l],
+    def plane_copies(lower, upper):
+        planes = []
+        start = 0
+        for f in range(FIELDS):
+            depth = DEPTH if f <= NRHS else DEPTH - 1
+            for side, (face, z) in enumerate(((lower, DEPTH - depth), (upper, DEPTH + NZ))):
+                for l in range(2):
+                    planes.append(
+                        pltpu.make_async_copy(
+                            face.at[pl.ds(start, depth), :, pl.ds(128 * l, 128)],
+                            stores[f // NRHS].at[f % NRHS, pl.ds(z, depth), l, pl.ds(8, NX), :],
+                            plane_sems.at[4 * f + 2 * side + l],
+                        )
                     )
-                )
-        start += depth
-    for copy in copies[:4] + planes:
+            start += depth
+        return planes
+
+    for copy in copies[:4]:
         copy.start()
+
+    @pl.when(odd)
+    def _():
+        for copy in plane_copies(face_one, face_two):
+            copy.start()
+
+    @pl.when(jnp.logical_not(odd))
+    def _():
+        for copy in plane_copies(face_two, face_one):
+            copy.start()
+
+    one, two = rim_one[...], rim_two[...]
+    rims[0] = jnp.where(odd, one, two)
+    rims[1] = jnp.where(odd, two, one)
+    rimlo, rimhi = rims.at[0], rims.at[1]
 
     zero = jnp.zeros((8, 128), F32)
     for f in range(FIELDS):
@@ -445,7 +477,7 @@
     for rim, z in ((rimlo, 0), (rimhi, DEPTH + NZ)):
         block.place_y(z, rim.at[rows, pl.ds(0, 128)], rim.at[rows, pl.ds(128, 128)])
 
-    for copy in copies[:4] + planes:
+    for copy in copies[:4] + plane_copies(face_one, face_two):
         copy.wait()
     for copy in [copies[5], copies[-1], copies[6], copies[7], copies[4]]:
         copy.start()
@@ -627,6 +659,11 @@
     return lax.ppermute(value, axis, pairs)
 
 
+def swap_pairs(value, axis, first):
+    pairs = [(i, i + 1) for i in range(first, lax.axis_size(axis) - 1, 2)]
+    return lax.ppermute(value, axis, pairs + [(j, i) for i, j in pairs])
+
+
 def exchange(messages):
     return lax.all_to_all(messages, AXES, 0, 0, tiled=True)
 
@@ -640,13 +677,14 @@
     fields = (rhs, coef_z, coef_x, coef_y, diag_term)
 
     place = at_x.astype(jnp.int32).reshape(1)
+    odd_z, odd_y = ((lax.axis_index(axis) & 1).astype(jnp.int32).reshape(1) for axis in ("gz", "gy"))
     face_shape = shape(FACE, NX, NY)
     x_shape = shape(FIELDS, NZ // 2, 8, NY)
     own_shape = shape(NX, NY)
-    zlo, zhi, ylo_own, yhi_own, *xmsgs = pl.pallas_call(
+    z_one, z_two, ylo_own, yhi_own, *xmsgs = pl.pallas_call(
         functools.partial(pack_faces, swap),
         out_shape=(face_shape, face_shape, own_shape, own_shape) + (x_shape,) * (1 if swap else 2),
-        in_specs=[smem()] + [hbm()] * 5,
+        in_specs=[smem()] * 2 + [hbm()] * 5,
         out_specs=(hbm(), hbm()) + (vmem(),) * (3 if swap else 4),
         scratch_shapes=[
             pltpu.VMEM((FIELDS, NZ, NX, NY), F32),
@@ -655,23 +693,23 @@
         ],
         compiler_params=params(LIMIT),
         cost_estimate=cost(2.5),
-    )(place, *fields)
-    facehi = move(zlo, "gz", -1)
-    facelo = move(zhi, "gz", 1)
+    )(place, odd_z, *fields)
+    face_one, face_two = swap_pairs(z_one, "gz", 0), swap_pairs(z_two, "gz", 1)
     if swap:
         x_parts = (lax.ppermute(xmsgs[0], "gx", [(0, 1), (1, 0)]),)
     else:
         x_parts = (move(xmsgs[0], "gx", -1), move(xmsgs[1], "gx", 1))
 
     rim_shape = shape(ROWS, NY)
-    ylo, yhi = pl.pallas_call(
+    y_one, y_two = pl.pallas_call(
         functools.partial(pack_rims, swap),
         out_shape=(rim_shape, rim_shape),
-        in_specs=[smem()] + [vmem()] * (2 + len(x_parts)),
+        in_specs=[smem()] * 2 + [vmem()] * (2 + len(x_parts)),
         compiler_params=params(16),
         cost_estimate=cost(1),
-    )(place, ylo_own, yhi_own, *x_parts)
-    yup, ydn = move(ylo, "gy", -1), move(yhi, "gy", 1)
+    )(place, odd_y, ylo_own, yhi_own, *x_parts)
+    y_one, y_two = swap_pairs(y_one, "gy", 0), swap_pairs(y_two, "gy", 1)
+    yup, ydn = jnp.where(odd_y == 1, y_two, y_one), jnp.where(odd_y == 1, y_one, y_two)
 
     def rim(half):
         near, far, odd = ((0, 1, 0), (3, 2, 1))[half]
@@ -682,7 +720,9 @@
         lanes = slice(128 * half, 128 * half + 128)
         return jnp.concatenate(rows + [jnp.concatenate([yup[:, lanes], ydn[:, lanes]], 1)], 0)
 
-    rimhi, rimlo = move(rim(0), "gz", -1), move(rim(1), "gz", 1)
+    low, high = rim(0), rim(1)
+    rim_one = swap_pairs(jnp.where(odd_z == 1, low, high), "gz", 0)
+    rim_two = swap_pairs(jnp.where(odd_z == 1, high, low), "gz", 1)
 
     inner_shape = shape(COLS, NZ, LT, EROWS, 128)
     inner_faces_shape = shape(7, NZ - 2, LT, ROWS, 128)
@@ -705,19 +745,20 @@
     basis, message = pl.pallas_call(
         functools.partial(krylov_outer, swap),
         out_shape=(block, shape(devices, 2, 128)),
-        in_specs=[hbm(), hbm(), smem(), hbm(), hbm(), vmem(), vmem()],
+        in_specs=[hbm(), hbm(), smem(), smem(), hbm(), hbm(), vmem(), vmem()],
         out_specs=(hbm(), vmem()),
         scratch_shapes=[
             *[pltpu.VMEM((NRHS, EZ, LT, EROWS, 128), F32)] * (STEPS + 2),
             pltpu.VMEM((7, EZ, LT, ROWS, 128), F32),
             pltpu.VMEM((2, STACK, STACK), F32),
+            pltpu.VMEM((2,) + rim_one.shape, F32),
             pltpu.SemaphoreType.DMA((4 * FIELDS,)),
             pltpu.SemaphoreType.DMA((9,)),
             pltpu.SemaphoreType.DMA((STEPS + 1,)),
         ],
         compiler_params=params(LIMIT),
         cost_estimate=cost(15),
-    )(facelo, facehi, place, inner, inner_faces, rimlo, rimhi)
+    )(face_one, face_two, place, odd_z, inner, inner_faces, rim_one, rim_two)
 
     message = exchange(message)
     first, message, factor_one = pl.pallas_call(

time: 96.7 us -> 94.5 us (0.977)
  blocking collectives: 21.1 us -> 25.1 us
  starting transfers between devices: 18.2 us -> 15.2 us
  waiting for transfers between devices: 7.48 us -> 4.49 us
    ppermute x6, waiting for transfers between devices: 6.68 us -> 1.18 us  [swap_pairs(): return lax.ppermute(value, axis, pairs + [(j, i) for i, j in pairs])]
    all_to_all x2, blocking collectives: 21.1 us -> 25.1 us  [exchange(): return lax.all_to_all(messages, AXES, 0, 0, tiled=True)]
    ppermute x6, starting transfers between devices: 15.1 us -> 12.1 us  [swap_pairs(): return lax.ppermute(value, axis, pairs + [(j, i) for i, j in pairs])]
    ppermute x1, waiting for transfers between devices: 0.8 us -> 3.31 us  [body(): x_parts = (lax.ppermute(xmsgs[0], 'gx', [(0, 1), (1, 0)]),)]
  transfers between devices with their start and end apart: 7 -> 7, of which waited for: 4 -> 3; matrix products, arithmetic and copies ran while one was open for 0% -> 0% of each run, Pallas kernels for 8% -> 8%
where the time goes in v8:
time: 94.5 us; the launch traced here: 93.9 us
  Pallas kernels  46.1 us (49%)
  blocking collectives  25.1 us (27%)
  starting transfers between devices  15.2 us (16%)
  waiting for transfers between devices  4.49 us (5%)
  local copies, waits for them, and re-layouts  2.23 us (2%)
    all_to_all x2, blocking collectives, exchange(): return lax.all_to_all(messages, AXES, 0, 0, tiled=True)  25.1 us
    pallas_call x1, Pallas kernels, body(): pl.pallas_call(functools.partial(krylov_outer, swap), out_shape=(block, s...  16.7 us
    ppermute x6, starting transfers between devices, swap_pairs(): return lax.ppermute(value, axis, pairs + [(j, i) for i, j in pairs])  12.1 us
    pallas_call x1, Pallas kernels, body(): pl.pallas_call(functools.partial(first_pass, cells), out_shape=(block, sh...  10.7 us
    pallas_call x1, Pallas kernels, body(): pl.pallas_call(functools.partial(second_pass, cells), out_shape=(shape(CO...  7.86 us
    pallas_call x1, Pallas kernels, body(): pl.pallas_call(functools.partial(krylov_inner, swap), out_shape=(inner_sh...  6.99 us
    pallas_call x1, Pallas kernels, body(): pl.pallas_call(functools.partial(pack_faces, swap), out_shape=(face_shape...  3.63 us
    ppermute x1, waiting for transfers between devices, body(): x_parts = (lax.ppermute(xmsgs[0], 'gx', [(0, 1), (1, 0)]),)  3.31 us
  transfers between devices with their start and end apart: 7, of which 3 were waited for; matrix products, arithmetic and copies ran while one was open for 0% of the time, Pallas kernels for 8%

profile of v8, /device:TPU:0, one launch (start us, length us, event | category | flops | bytes accessed | tf_op | source)
XLA Modules:
  0.0 93.9 jit_solution(8363079174518120030)
XLA Ops:
  0.6 3.6 %shard_map.68 = (f32[29,32,256]{2,1,0:T(8,128)}, f32[29,32,256]{2,1,0:T(8,128)}, f32[32,256]{1,0:T(8,128)}, f32[32,256]{1,0:T(8,128)}, f32[8,4,8,256]{3,2,1,0:T(8,128)}) custom-call(s32[1]{0:T(128)} %bitcast.place, s32[1]{0:T(128)} %bitcast.1.odd_z, f32[4,8,32,256]{3,2,1,0:T(8,128)} %rhs.3, f32[8,32,256]{2,1,0:T(8,128)} %cz.3, f32[8,32,256]{2,1,0:T(8,128)} %cx.3, ...), custom_call_target="tpu_custom_call" | custom-call | bytes 9000000 | tf_op jit(solution)/shard_map/pallas_call | solution.py:684
  4.3 3.0 %collective-permute-start.2 = (f32[8,4,8,256]{3,2,1,0:T(8,128)}, f32[8,4,8,256]{3,2,1,0:T(8,128)S(1)}, u32[]{:S(2)}, u32[]{:S(2)}) collective-permute-start(f32[8,4,8,256]{3,2,1,0:T(8,128)} %get-tuple-element.18), channel_id=1, source_target_pairs={{0,16},{16,0},{1,17},{17,1},{2,18},{18,2},{3,19},{19,3},{4,20},{20... | collective-permute-start | bytes 786440 | tf_op jit(solution)/shard_map/ppermute | solution.py:699
  7.3 1.6 %collective-permute-start = (f32[29,32,256]{2,1,0:T(8,128)}, f32[29,32,256]{2,1,0:T(8,128)}, u32[]{:S(2)}, u32[]{:S(2)}) collective-permute-start(f32[29,32,256]{2,1,0:T(8,128)} %get-tuple-element.16), channel_id=1, source_target_pairs={{0,1},{2,3},{1,0},{3,2},{4,5},{6,7},{5,4},{7,6},{8,9},{10,11},{9,8... | collective-permute-start | bytes 2850824 | tf_op jit(solution)/shard_map/ppermute | solution.py:664
  8.9 1.6 %collective-permute-start.1 = (f32[29,32,256]{2,1,0:T(8,128)}, f32[29,32,256]{2,1,0:T(8,128)}, u32[]{:S(2)}, u32[]{:S(2)}) collective-permute-start(f32[29,32,256]{2,1,0:T(8,128)} %get-tuple-element.17), channel_id=1, source_target_pairs={{1,2},{2,1},{5,6},{6,5},{9,10},{10,9},{13,14},{14,13},{17,18},{18,... | collective-permute-start | bytes 2850824 | tf_op jit(solution)/shard_map/ppermute | solution.py:664
  10.5 3.3 %collective-permute-done.2.refs_0_.rest_0_ = f32[8,4,8,256]{3,2,1,0:T(8,128)S(1)} collective-permute-done((f32[8,4,8,256]{3,2,1,0:T(8,128)}, f32[8,4,8,256]{3,2,1,0:T(8,128)S(1)}, u32[]{:S(2)}, u32[]{:S(2)}) %collective-permute-start.2) | collective-permute-done | bytes 262176 | tf_op jit(solution)/shard_map/ppermute | solution.py:699
  13.8 0.0 copy-start
  13.8 0.0 copy-start.1
  13.8 0.8 copy-done.1
  14.6 0.0 copy-start.2
  14.6 0.8 copy-done.2
  15.3 0.2 shard_map.69
  15.5 0.7 collective-permute-start.3
  16.2 3.1 %collective-permute-start.4 = (f32[40,256]{1,0:T(8,128)S(1)}, f32[40,256]{1,0:T(8,128)S(1)}, u32[]{:S(2)}, u32[]{:S(2)}) collective-permute-start(f32[40,256]{1,0:T(8,128)S(1)} %get-tuple-element.22), channel_id=1, source_target_pairs={{0,4},{8,12},{4,0},{12,8},{1,5},{9,13},{5,1},{13,9},{2,6},{10,14},... | collective-permute-start | bytes 122888 | tf_op jit(solution)/shard_map/ppermute | solution.py:664
  19.4 0.0 collective-permute-done.3
  19.4 0.8 collective-permute-done.4
  20.2 0.0 copy-start.3
  20.2 0.0 copy-start.4
  20.3 0.7 collective-permute-start.6
  21.0 4.5 %collective-permute-start.5 = (f32[128,256]{1,0:T(8,128)S(1)}, f32[128,256]{1,0:T(8,128)S(1)}, u32[]{:S(2)}, u32[]{:S(2)}) collective-permute-start(f32[128,256]{1,0:T(8,128)S(1)} %get-tuple-element.31), channel_id=1, source_target_pairs={{0,1},{2,3},{1,0},{3,2},{4,5},{6,7},{5,4},{7,6},{8,9},{10,11},{9,8... | collective-permute-start | bytes 393224 | tf_op jit(solution)/shard_map/ppermute | solution.py:664
  25.4 0.0 copy-done
  25.4 0.0 copy-done.3
  25.4 0.0 copy-done.4
  25.4 7.0 %shard_map.70 = (f32[20,8,3,56,128]{4,3,2,1,0:T(8,128)}, f32[7,6,3,40,128]{4,3,2,1,0:T(8,128)}) custom-call(s32[1]{0:T(128)} %bitcast.place, f32[4,8,32,256]{3,2,1,0:T(8,128)} %rhs.3, f32[8,32,256]{2,1,0:T(8,128)} %cz.3, f32[8,32,256]{2,1,0:T(8,128)} %cx.3, f32[8,32,256]{2,1,0:T(8,128)} %cy.3, f32[8,32,256]{2,1,0:T(8,128)} %dg.3, f32[8,4,8,256]{3,2,1,0:T(8,128)} %copy-done, ...), custom_call_target="tpu_custom_call" | custom-call | bytes 25200000 | tf_op jit(solution)/shard_map/pallas_call | solution.py:729
  32.4 0.0 collective-permute-done.6.rim_two
  32.4 0.0 copy-start.5
  32.5 0.4 collective-permute-done.5.rim_one
  32.8 0.0 copy-start.6
  32.8 0.0 collective-permute-done.face_one
  32.8 0.0 collective-permute-done.1.face_two
  32.8 0.3 copy-done.5
  33.1 0.4 copy-done.6
  33.5 16.7 %shard_map.71 = (f32[20,8,2,32,128]{4,3,2,1,0:T(8,128)}, f32[32,2,128]{2,1,0:T(2,128)}) custom-call(f32[29,32,256]{2,1,0:T(8,128)} %collective-permute-done.face_one, f32[29,32,256]{2,1,0:T(8,128)} %collective-permute-done.1.face_two, s32[1]{0:T(128)} %bitcast.place, s32[1]{0:T(128)} %bitcast.1.odd_z, f32[20,8,3,56,128]{4,3,2,1,0:T(8,128)} %get-tuple-element.23.inner, ...), custom_call_target="tpu_custom_call" | custom-call | bytes 54000000 | tf_op jit(solution)/shard_map/pallas_call | solution.py:745
  50.2 14.5 %all_to_all.10.message = f32[32,2,128]{2,1,0:T(2,128)} all-to-all(f32[32,2,128]{2,1,0:T(2,128)} %get-tuple-element.25), channel_id=1, replica_groups=mesh['gx'=2,'gy'=4,'gz'=4] {'gx','gy','gz'}, dimensions={0} | all-to-all | bytes 65536 | tf_op jit(solution)/shard_map/all_to_all | solution.py:668
  64.7 10.7 %shard_map.72 = (f32[20,8,2,32,128]{4,3,2,1,0:T(8,128)}, f32[32,2,128]{2,1,0:T(2,128)}, f32[24,128]{1,0:T(8,128)}) custom-call(f32[32,2,128]{2,1,0:T(2,128)} %all_to_all.10.message, f32[20,8,2,32,128]{4,3,2,1,0:T(8,128)} %get-tuple-element.26.basis_hbm), custom_call_target="tpu_custom_call" | custom-call | tf_op jit(solution)/shard_map/pallas_call | solution.py:764
  75.5 10.6 %all_to_all.11.message = f32[32,2,128]{2,1,0:T(2,128)} all-to-all(f32[32,2,128]{2,1,0:T(2,128)} %get-tuple-element.27), channel_id=1, replica_groups=mesh['gx'=2,'gy'=4,'gz'=4] {'gx','gy','gz'}, dimensions={0} | all-to-all | bytes 65536 | tf_op jit(solution)/shard_map/all_to_all | solution.py:668
  86.0 7.9 %shard_map.73 = (f32[20,8,32,256]{3,2,1,0:T(8,128)}, f32[20,20]{1,0:T(8,128)}) custom-call(f32[32,2,128]{2,1,0:T(2,128)} %all_to_all.11.message, f32[24,128]{1,0:T(8,128)} %get-tuple-element.28.factor_one, f32[20,8,2,32,128]{4,3,2,1,0:T(8,128)} %get-tuple-element.29.first_hbm), custom_call_target="tpu_custom_call" | custom-call | tf_op jit(solution)/shard_map/pallas_call | solution.py:781
  (7 shorter events, 0.1 us)
Async XLA Ops:
  4.3 9.5 %collective-permute-start.2 = (f32[8,4,8,256]{3,2,1,0:T(8,128)}, f32[8,4,8,256]{3,2,1,0:T(8,128)S(1)}, u32[]{:S(2)}, u32[]{:S(2)}) collective-permute-start(f32[8,4,8,256]{3,2,1,0:T(8,128)} %get-tuple-element.18), channel_id=1, source_target_pairs={{0,16},{16,0},{1,17},{17,1},{2,18},{18,2},{3,19},{19,3},{4,20},{20... | collective-permute-start | bytes 786440 | tf_op jit(solution)/shard_map/ppermute | solution.py:699
  7.3 25.5 %collective-permute-start = (f32[29,32,256]{2,1,0:T(8,128)}, f32[29,32,256]{2,1,0:T(8,128)}, u32[]{:S(2)}, u32[]{:S(2)}) collective-permute-start(f32[29,32,256]{2,1,0:T(8,128)} %get-tuple-element.16), channel_id=1, source_target_pairs={{0,1},{2,3},{1,0},{3,2},{4,5},{6,7},{5,4},{7,6},{8,9},{10,11},{9,8... | collective-permute-start | bytes 2850824 | tf_op jit(solution)/shard_map/ppermute | solution.py:664
  8.9 24.0 %collective-permute-start.1 = (f32[29,32,256]{2,1,0:T(8,128)}, f32[29,32,256]{2,1,0:T(8,128)}, u32[]{:S(2)}, u32[]{:S(2)}) collective-permute-start(f32[29,32,256]{2,1,0:T(8,128)} %get-tuple-element.17), channel_id=1, source_target_pairs={{1,2},{2,1},{5,6},{6,5},{9,10},{10,9},{13,14},{14,13},{17,18},{18,... | collective-permute-start | bytes 2850824 | tf_op jit(solution)/shard_map/ppermute | solution.py:664
  13.8 11.6 %copy-start = (f32[8,4,8,256]{3,2,1,0:T(8,128)}, f32[8,4,8,256]{3,2,1,0:T(8,128)S(1)}, u32[]{:S(2)}) copy-start(f32[8,4,8,256]{3,2,1,0:T(8,128)S(1)} %collective-permute-done.2.refs_0_.rest_0_) | copy-start | bytes 786436
  13.8 0.8 copy-start.1
  14.6 0.8 copy-start.2
  15.5 3.9 %collective-permute-start.3 = (f32[40,256]{1,0:T(8,128)S(1)}, f32[40,256]{1,0:T(8,128)S(1)}, u32[]{:S(2)}, u32[]{:S(2)}) collective-permute-start(f32[40,256]{1,0:T(8,128)S(1)} %get-tuple-element.21), channel_id=1, source_target_pairs={{4,8},{8,4},{5,9},{9,5},{6,10},{10,6},{7,11},{11,7},{20,24},{24,20... | collective-permute-start | bytes 122888 | tf_op jit(solution)/shard_map/ppermute | solution.py:664
  16.2 4.0 %collective-permute-start.4 = (f32[40,256]{1,0:T(8,128)S(1)}, f32[40,256]{1,0:T(8,128)S(1)}, u32[]{:S(2)}, u32[]{:S(2)}) collective-permute-start(f32[40,256]{1,0:T(8,128)S(1)} %get-tuple-element.22), channel_id=1, source_target_pairs={{0,4},{8,12},{4,0},{12,8},{1,5},{9,13},{5,1},{13,9},{2,6},{10,14},... | collective-permute-start | bytes 122888 | tf_op jit(solution)/shard_map/ppermute | solution.py:664
  20.2 5.2 %copy-start.3 = (f32[40,256]{1,0:T(8,128)}, f32[40,256]{1,0:T(8,128)S(1)}, u32[]{:S(2)}) copy-start(f32[40,256]{1,0:T(8,128)S(1)} %get-tuple-element.36.rest_2_) | copy-start | bytes 122884
  20.2 5.2 %copy-start.4 = (f32[40,256]{1,0:T(8,128)}, f32[40,256]{1,0:T(8,128)S(1)}, u32[]{:S(2)}) copy-start(f32[40,256]{1,0:T(8,128)S(1)} %get-tuple-element.37.rest_1_) | copy-start | bytes 122884
  20.3 12.1 %collective-permute-start.6 = (f32[128,256]{1,0:T(8,128)S(1)}, f32[128,256]{1,0:T(8,128)S(1)}, u32[]{:S(2)}, u32[]{:S(2)}) collective-permute-start(f32[128,256]{1,0:T(8,128)S(1)} %get-tuple-element.30), channel_id=1, source_target_pairs={{1,2},{2,1},{5,6},{6,5},{9,10},{10,9},{13,14},{14,13},{17,18},{18,... | collective-permute-start | bytes 393224 | tf_op jit(solution)/shard_map/ppermute | solution.py:664
  21.0 11.9 %collective-permute-start.5 = (f32[128,256]{1,0:T(8,128)S(1)}, f32[128,256]{1,0:T(8,128)S(1)}, u32[]{:S(2)}, u32[]{:S(2)}) collective-permute-start(f32[128,256]{1,0:T(8,128)S(1)} %get-tuple-element.31), channel_id=1, source_target_pairs={{0,1},{2,3},{1,0},{3,2},{4,5},{6,7},{5,4},{7,6},{8,9},{10,11},{9,8... | collective-permute-start | bytes 393224 | tf_op jit(solution)/shard_map/ppermute | solution.py:664
  32.4 0.7 copy-start.5
  32.8 0.7 copy-start.6

commit v9 on v8

--- a/solution.py
+++ b/solution.py
@@ -59,7 +59,7 @@
     return rhs.at[f, z] if f < NRHS else (cz, cx, cy, dg)[f - NRHS].at[z]
 
 
-def pack_faces(swap, place, odd_z, rhs, cz, cx, cy, dg, z_one, z_two, ylo, yhi, *rest):
+def pack_faces(swap, place, odd_z, odd_y, rhs, cz, cx, cy, dg, z_one, z_two, y_one, y_two, *rest):
     xmsgs, (whole, loads, saves) = rest[:-3], rest[-3:]
     copies = []
     for f in range(FIELDS):
@@ -91,12 +91,17 @@
             else:
                 xmsgs[0][f, m] = first
                 xmsgs[1][f, m] = last
+    odd = odd_y[0] == 1
     for t in range(NX // 8):
-        for side, out in ((0, ylo), (1, yhi)):
-            for half in range(2):
-                out[8 * t : 8 * t + 8, 128 * half : 128 * half + 128] = pack_lanes(
+        for half in range(2):
+            lo, hi = (
+                pack_lanes(
                     lambda f, zz: whole[f, 4 * half + zz, 8 * t : 8 * t + 8, 128 * side : 128 * side + 128], side
                 )
+                for side in range(2)
+            )
+            y_one[8 * t : 8 * t + 8, 128 * half : 128 * half + 128] = jnp.where(odd, lo, hi)
+            y_two[8 * t : 8 * t + 8, 128 * half : 128 * half + 128] = jnp.where(odd, hi, lo)
     for copy in planes:
         copy.wait()
 
@@ -132,13 +137,10 @@
     return acc
 
 
-def pack_rims(swap, place, odd_y, ylo_own, yhi_own, *refs):
+def pack_rims(swap, place, odd_y, *refs):
     above, below, one, two = refs if not swap else (refs[0],) + refs
     keep_up, keep_dn = keep_sides(swap, place)
     odd = odd_y[0] == 1
-    lo, hi = ylo_own[...], yhi_own[...]
-    one[0:NX, :] = jnp.where(odd, lo, hi)
-    two[0:NX, :] = jnp.where(odd, hi, lo)
     for half in range(2):
         halves = []
         for side in range(2):
@@ -156,8 +158,8 @@
                 )
             )
         lo, hi = halves
-        one[NX:ROWS, 128 * half : 128 * half + 128] = jnp.where(odd, lo, hi)
-        two[NX:ROWS, 128 * half : 128 * half + 128] = jnp.where(odd, hi, lo)
+        one[:, 128 * half : 128 * half + 128] = jnp.where(odd, lo, hi)
+        two[:, 128 * half : 128 * half + 128] = jnp.where(odd, hi, lo)
 
 
 STACK = 8 * COLS
@@ -677,14 +679,15 @@
     fields = (rhs, coef_z, coef_x, coef_y, diag_term)
 
     place = at_x.astype(jnp.int32).reshape(1)
-    odd_z, odd_y = ((lax.axis_index(axis) & 1).astype(jnp.int32).reshape(1) for axis in ("gz", "gy"))
+    odd_z = ((lax.axis_index("gz") + 1) & 1).astype(jnp.int32).reshape(1)
+    odd_y = (lax.axis_index("gy") & 1).astype(jnp.int32).reshape(1)
     face_shape = shape(FACE, NX, NY)
     x_shape = shape(FIELDS, NZ // 2, 8, NY)
     own_shape = shape(NX, NY)
-    z_one, z_two, ylo_own, yhi_own, *xmsgs = pl.pallas_call(
+    z_one, z_two, own_one, own_two, *xmsgs = pl.pallas_call(
         functools.partial(pack_faces, swap),
         out_shape=(face_shape, face_shape, own_shape, own_shape) + (x_shape,) * (1 if swap else 2),
-        in_specs=[smem()] * 2 + [hbm()] * 5,
+        in_specs=[smem()] * 3 + [hbm()] * 5,
         out_specs=(hbm(), hbm()) + (vmem(),) * (3 if swap else 4),
         scratch_shapes=[
             pltpu.VMEM((FIELDS, NZ, NX, NY), F32),
@@ -693,22 +696,23 @@
         ],
         compiler_params=params(LIMIT),
         cost_estimate=cost(2.5),
-    )(place, odd_z, *fields)
-    face_one, face_two = swap_pairs(z_one, "gz", 0), swap_pairs(z_two, "gz", 1)
+    )(place, odd_z, odd_y, *fields)
+    face_one, face_two = swap_pairs(z_one, "gz", 1), swap_pairs(z_two, "gz", 0)
     if swap:
         x_parts = (lax.ppermute(xmsgs[0], "gx", [(0, 1), (1, 0)]),)
     else:
         x_parts = (move(xmsgs[0], "gx", -1), move(xmsgs[1], "gx", 1))
 
-    rim_shape = shape(ROWS, NY)
-    y_one, y_two = pl.pallas_call(
+    halo_shape = shape(ROWS - NX, NY)
+    halo_one, halo_two = pl.pallas_call(
         functools.partial(pack_rims, swap),
-        out_shape=(rim_shape, rim_shape),
-        in_specs=[smem()] * 2 + [vmem()] * (2 + len(x_parts)),
+        out_shape=(halo_shape, halo_shape),
+        in_specs=[smem()] * 2 + [vmem()] * len(x_parts),
         compiler_params=params(16),
         cost_estimate=cost(1),
-    )(place, odd_y, ylo_own, yhi_own, *x_parts)
-    y_one, y_two = swap_pairs(y_one, "gy", 0), swap_pairs(y_two, "gy", 1)
+    )(place, odd_y, *x_parts)
+    y_one = swap_pairs(jnp.concatenate([own_one, halo_one], 0), "gy", 0)
+    y_two = swap_pairs(jnp.concatenate([own_two, halo_two], 0), "gy", 1)
     yup, ydn = jnp.where(odd_y == 1, y_two, y_one), jnp.where(odd_y == 1, y_one, y_two)
 
     def rim(half):
@@ -721,8 +725,8 @@
         return jnp.concatenate(rows + [jnp.concatenate([yup[:, lanes], ydn[:, lanes]], 1)], 0)
 
     low, high = rim(0), rim(1)
-    rim_one = swap_pairs(jnp.where(odd_z == 1, low, high), "gz", 0)
-    rim_two = swap_pairs(jnp.where(odd_z == 1, high, low), "gz", 1)
+    rim_one = swap_pairs(jnp.where(odd_z == 1, low, high), "gz", 1)
+    rim_two = swap_pairs(jnp.where(odd_z == 1, high, low), "gz", 0)
 
     inner_shape = shape(COLS, NZ, LT, EROWS, 128)
     inner_faces_shape = shape(7, NZ - 2, LT, ROWS, 128)

time: 94.5 us -> 94 us (level)
  waiting for transfers between devices: 4.49 us -> 11.4 us
  starting transfers between devices: 15.2 us -> 11.3 us
  blocking collectives: 25.1 us -> 21.4 us
  other arithmetic: 0.04 us -> 1.56 us
  local copies, waits for them, and re-layouts: 2.23 us -> 0.76 us
    ppermute x6, waiting for transfers between devices: 1.18 us -> 9.98 us  [swap_pairs(): return lax.ppermute(value, axis, pairs + [(j, i) for i, j in pairs])]
    ppermute x6, starting transfers between devices: 12.1 us -> 8.3 us  [swap_pairs(): return lax.ppermute(value, axis, pairs + [(j, i) for i, j in pairs])]
    all_to_all x2, blocking collectives: 25.1 us -> 21.4 us  [exchange(): return lax.all_to_all(messages, AXES, 0, 0, tiled=True)]
    ppermute x1, waiting for transfers between devices: 3.31 us -> 1.39 us  [body(): x_parts = (lax.ppermute(xmsgs[0], 'gx', [(0, 1), (1, 0)]),)]
    concatenate x0 -> x2, other arithmetic: none -> 1.52 us  [the longest x1 0.76 us: body(): y_one = swap_pairs(jnp.concatenate([own_one, halo_one], 0), 'gy', 0)]
    unnamed x14 -> x10, local copies, waits for them, and re-layouts: 2.17 us -> 0.7 us
  transfers between devices with their start and end apart: 7 -> 7, of which waited for: 3 -> 2; matrix products, arithmetic and copies ran while one was open for 0% -> 2% of each run, Pallas kernels for 8% -> 8%
where the time goes in v9:
time: 94 us; the launch traced here: 93.3 us
  Pallas kernels  46.1 us (49%)
  blocking collectives  21.4 us (23%)
  waiting for transfers between devices  11.4 us (12%)
  starting transfers between devices  11.3 us (12%)
  other arithmetic  1.56 us (2%)
    all_to_all x2, blocking collectives, exchange(): return lax.all_to_all(messages, AXES, 0, 0, tiled=True)  21.4 us
    pallas_call x1, Pallas kernels, body(): pl.pallas_call(functools.partial(krylov_outer, swap), out_shape=(block, s...  16.7 us
    pallas_call x1, Pallas kernels, body(): pl.pallas_call(functools.partial(first_pass, cells), out_shape=(block, sh...  10.7 us
    ppermute x6, waiting for transfers between devices, swap_pairs(): return lax.ppermute(value, axis, pairs + [(j, i) for i, j in pairs])  9.98 us
    ppermute x6, starting transfers between devices, swap_pairs(): return lax.ppermute(value, axis, pairs + [(j, i) for i, j in pairs])  8.3 us
    pallas_call x1, Pallas kernels, body(): pl.pallas_call(functools.partial(second_pass, cells), out_shape=(shape(CO...  7.86 us
    pallas_call x1, Pallas kernels, body(): pl.pallas_call(functools.partial(krylov_inner, swap), out_shape=(inner_sh...  7.02 us
    pallas_call x1, Pallas kernels, body(): pl.pallas_call(functools.partial(pack_faces, swap), out_shape=(face_shape...  3.64 us
  transfers between devices with their start and end apart: 7, of which 2 were waited for; matrix products, arithmetic and copies ran while one was open for 2% of the time, Pallas kernels for 8%

profile of v9, /device:TPU:0, one launch (start us, length us, event | category | flops | bytes accessed | tf_op | source)
XLA Modules:
  0.0 93.3 jit_solution(15058971829234115961)
XLA Ops:
  0.6 3.6 %shard_map.68 = (f32[29,32,256]{2,1,0:T(8,128)}, f32[29,32,256]{2,1,0:T(8,128)}, f32[32,256]{1,0:T(8,128)}, f32[32,256]{1,0:T(8,128)}, f32[8,4,8,256]{3,2,1,0:T(8,128)}) custom-call(s32[1]{0:T(128)} %bitcast.place, s32[1]{0:T(128)} %bitcast.1.odd_z, s32[1]{0:T(128)} %bitcast.2.odd_y, f32[4,8,32,256]{3,2,1,0:T(8,128)} %rhs.3, f32[8,32,256]{2,1,0:T(8,128)} %cz.3, ...), custom_call_target="tpu_custom_call" | custom-call | bytes 9000000 | tf_op jit(solution)/shard_map/pallas_call | solution.py:687
  4.3 3.0 %collective-permute-start.2 = (f32[8,4,8,256]{3,2,1,0:T(8,128)}, f32[8,4,8,256]{3,2,1,0:T(8,128)S(1)}, u32[]{:S(2)}, u32[]{:S(2)}) collective-permute-start(f32[8,4,8,256]{3,2,1,0:T(8,128)} %get-tuple-element.18), channel_id=1, source_target_pairs={{0,16},{16,0},{1,17},{17,1},{2,18},{18,2},{3,19},{19,3},{4,20},{20... | collective-permute-start | bytes 786440 | tf_op jit(solution)/shard_map/ppermute | solution.py:702
  7.3 1.6 %collective-permute-start = (f32[29,32,256]{2,1,0:T(8,128)}, f32[29,32,256]{2,1,0:T(8,128)}, u32[]{:S(2)}, u32[]{:S(2)}) collective-permute-start(f32[29,32,256]{2,1,0:T(8,128)} %get-tuple-element.16), channel_id=1, source_target_pairs={{1,2},{2,1},{5,6},{6,5},{9,10},{10,9},{13,14},{14,13},{17,18},{18,... | collective-permute-start | bytes 2850824 | tf_op jit(solution)/shard_map/ppermute | solution.py:666
  8.9 3.5 %collective-permute-start.1 = (f32[29,32,256]{2,1,0:T(8,128)}, f32[29,32,256]{2,1,0:T(8,128)}, u32[]{:S(2)}, u32[]{:S(2)}) collective-permute-start(f32[29,32,256]{2,1,0:T(8,128)} %get-tuple-element.17), channel_id=1, source_target_pairs={{0,1},{2,3},{1,0},{3,2},{4,5},{6,7},{5,4},{7,6},{8,9},{10,11},{9,8... | collective-permute-start | bytes 2850824 | tf_op jit(solution)/shard_map/ppermute | solution.py:666
  12.4 1.4 %collective-permute-done.2.refs_0_.rest_0_ = f32[8,4,8,256]{3,2,1,0:T(8,128)S(1)} collective-permute-done((f32[8,4,8,256]{3,2,1,0:T(8,128)}, f32[8,4,8,256]{3,2,1,0:T(8,128)S(1)}, u32[]{:S(2)}, u32[]{:S(2)}) %collective-permute-start.2) | collective-permute-done | bytes 262176 | tf_op jit(solution)/shard_map/ppermute | solution.py:702
  13.8 0.0 copy-start
  13.8 0.2 shard_map.69
  14.0 0.8 pad_maximum_fusion.1
  14.8 0.0 collective-permute-start.4
  14.8 0.8 pad_maximum_fusion
  15.6 0.7 collective-permute-start.3
  16.3 0.0 collective-permute-done.4
  16.3 0.0 collective-permute-done.3
  16.3 0.0 copy-start.1
  16.4 0.0 copy-start.2
  16.4 1.9 %collective-permute-start.6 = (f32[128,256]{1,0:T(8,128)S(1)}, f32[128,256]{1,0:T(8,128)S(1)}, u32[]{:S(2)}, u32[]{:S(2)}) collective-permute-start(f32[128,256]{1,0:T(8,128)S(1)} %get-tuple-element.30), channel_id=1, source_target_pairs={{0,1},{2,3},{1,0},{3,2},{4,5},{6,7},{5,4},{7,6},{8,9},{10,11},{9,8... | collective-permute-start | bytes 393224 | tf_op jit(solution)/shard_map/ppermute | solution.py:666
  18.3 0.7 collective-permute-start.5
  18.9 0.0 copy-done
  18.9 0.0 copy-done.1
  19.0 0.0 copy-done.2
  19.0 7.0 %shard_map.70 = (f32[20,8,3,56,128]{4,3,2,1,0:T(8,128)}, f32[7,6,3,40,128]{4,3,2,1,0:T(8,128)}) custom-call(s32[1]{0:T(128)} %bitcast.place, f32[4,8,32,256]{3,2,1,0:T(8,128)} %rhs.3, f32[8,32,256]{2,1,0:T(8,128)} %cz.3, f32[8,32,256]{2,1,0:T(8,128)} %cx.3, f32[8,32,256]{2,1,0:T(8,128)} %cy.3, f32[8,32,256]{2,1,0:T(8,128)} %dg.3, f32[8,4,8,256]{3,2,1,0:T(8,128)} %copy-done, ...), custom_call_target="tpu_custom_call" | custom-call | bytes 25200000 | tf_op jit(solution)/shard_map/pallas_call | solution.py:733
  26.0 10.0 %collective-permute-done.6.rim_two = f32[128,256]{1,0:T(8,128)S(1)} collective-permute-done((f32[128,256]{1,0:T(8,128)S(1)}, f32[128,256]{1,0:T(8,128)S(1)}, u32[]{:S(2)}, u32[]{:S(2)}) %collective-permute-start.6) | collective-permute-done | bytes 131104 | tf_op jit(solution)/shard_map/ppermute | solution.py:666
  36.0 0.0 copy-start.3
  36.0 0.0 collective-permute-done.5.rim_one
  36.0 0.0 copy-start.4
  36.0 0.0 collective-permute-done.face_one
  36.0 0.0 collective-permute-done.1.face_two
  36.0 0.6 copy-done.3
  36.6 0.1 copy-done.4
  36.7 16.7 %shard_map.71 = (f32[20,8,2,32,128]{4,3,2,1,0:T(8,128)}, f32[32,2,128]{2,1,0:T(2,128)}) custom-call(f32[29,32,256]{2,1,0:T(8,128)} %collective-permute-done.face_one, f32[29,32,256]{2,1,0:T(8,128)} %collective-permute-done.1.face_two, s32[1]{0:T(128)} %bitcast.place, s32[1]{0:T(128)} %bitcast.1.odd_z, f32[20,8,3,56,128]{4,3,2,1,0:T(8,128)} %get-tuple-element.23.inner, ...), custom_call_target="tpu_custom_call" | custom-call | bytes 54000000 | tf_op jit(solution)/shard_map/pallas_call | solution.py:749
  53.4 10.8 %all_to_all.10.message = f32[32,2,128]{2,1,0:T(2,128)} all-to-all(f32[32,2,128]{2,1,0:T(2,128)} %get-tuple-element.25), channel_id=1, replica_groups=mesh['gx'=2,'gy'=4,'gz'=4] {'gx','gy','gz'}, dimensions={0} | all-to-all | bytes 65536 | tf_op jit(solution)/shard_map/all_to_all | solution.py:670
  64.2 10.7 %shard_map.72 = (f32[20,8,2,32,128]{4,3,2,1,0:T(8,128)}, f32[32,2,128]{2,1,0:T(2,128)}, f32[24,128]{1,0:T(8,128)}) custom-call(f32[32,2,128]{2,1,0:T(2,128)} %all_to_all.10.message, f32[20,8,2,32,128]{4,3,2,1,0:T(8,128)} %get-tuple-element.26.basis_hbm), custom_call_target="tpu_custom_call" | custom-call | tf_op jit(solution)/shard_map/pallas_call | solution.py:768
  74.9 10.5 %all_to_all.11.message = f32[32,2,128]{2,1,0:T(2,128)} all-to-all(f32[32,2,128]{2,1,0:T(2,128)} %get-tuple-element.27), channel_id=1, replica_groups=mesh['gx'=2,'gy'=4,'gz'=4] {'gx','gy','gz'}, dimensions={0} | all-to-all | bytes 65536 | tf_op jit(solution)/shard_map/all_to_all | solution.py:670
  85.5 7.9 %shard_map.73 = (f32[20,8,32,256]{3,2,1,0:T(8,128)}, f32[20,20]{1,0:T(8,128)}) custom-call(f32[32,2,128]{2,1,0:T(2,128)} %all_to_all.11.message, f32[24,128]{1,0:T(8,128)} %get-tuple-element.28.factor_one, f32[20,8,2,32,128]{4,3,2,1,0:T(8,128)} %get-tuple-element.29.first_hbm), custom_call_target="tpu_custom_call" | custom-call | tf_op jit(solution)/shard_map/pallas_call | solution.py:785
  (7 shorter events, 0.1 us)
Async XLA Ops:
  4.3 9.5 %collective-permute-start.2 = (f32[8,4,8,256]{3,2,1,0:T(8,128)}, f32[8,4,8,256]{3,2,1,0:T(8,128)S(1)}, u32[]{:S(2)}, u32[]{:S(2)}) collective-permute-start(f32[8,4,8,256]{3,2,1,0:T(8,128)} %get-tuple-element.18), channel_id=1, source_target_pairs={{0,16},{16,0},{1,17},{17,1},{2,18},{18,2},{3,19},{19,3},{4,20},{20... | collective-permute-start | bytes 786440 | tf_op jit(solution)/shard_map/ppermute | solution.py:702
  7.3 28.6 %collective-permute-start = (f32[29,32,256]{2,1,0:T(8,128)}, f32[29,32,256]{2,1,0:T(8,128)}, u32[]{:S(2)}, u32[]{:S(2)}) collective-permute-start(f32[29,32,256]{2,1,0:T(8,128)} %get-tuple-element.16), channel_id=1, source_target_pairs={{1,2},{2,1},{5,6},{6,5},{9,10},{10,9},{13,14},{14,13},{17,18},{18,... | collective-permute-start | bytes 2850824 | tf_op jit(solution)/shard_map/ppermute | solution.py:666
  8.9 27.0 %collective-permute-start.1 = (f32[29,32,256]{2,1,0:T(8,128)}, f32[29,32,256]{2,1,0:T(8,128)}, u32[]{:S(2)}, u32[]{:S(2)}) collective-permute-start(f32[29,32,256]{2,1,0:T(8,128)} %get-tuple-element.17), channel_id=1, source_target_pairs={{0,1},{2,3},{1,0},{3,2},{4,5},{6,7},{5,4},{7,6},{8,9},{10,11},{9,8... | collective-permute-start | bytes 2850824 | tf_op jit(solution)/shard_map/ppermute | solution.py:666
  13.8 5.1 %copy-start = (f32[8,4,8,256]{3,2,1,0:T(8,128)}, f32[8,4,8,256]{3,2,1,0:T(8,128)S(1)}, u32[]{:S(2)}) copy-start(f32[8,4,8,256]{3,2,1,0:T(8,128)S(1)} %collective-permute-done.2.refs_0_.rest_0_) | copy-start | bytes 786436
  14.8 1.5 %collective-permute-start.4 = (f32[40,256]{1,0:T(8,128)S(1)}, f32[40,256]{1,0:T(8,128)S(1)}, u32[]{:S(2)}, u32[]{:S(2)}) collective-permute-start(f32[40,256]{1,0:T(8,128)S(1)} %pad_maximum_fusion.1), channel_id=1, source_target_pairs={{0,4},{8,12},{4,0},{12,8},{1,5},{9,13},{5,1},{13,9},{2,6},{10,14},... | collective-permute-start | bytes 122888 | tf_op jit(solution)/shard_map/ppermute | solution.py:666
  15.6 0.7 collective-permute-start.3
  16.3 2.6 %copy-start.1 = (f32[40,256]{1,0:T(8,128)}, f32[40,256]{1,0:T(8,128)S(1)}, u32[]{:S(2)}) copy-start(f32[40,256]{1,0:T(8,128)S(1)} %get-tuple-element.36.rest_2_) | copy-start | bytes 122884
  16.4 2.6 %copy-start.2 = (f32[40,256]{1,0:T(8,128)}, f32[40,256]{1,0:T(8,128)S(1)}, u32[]{:S(2)}) copy-start(f32[40,256]{1,0:T(8,128)S(1)} %get-tuple-element.37.rest_1_) | copy-start | bytes 122884
  16.4 19.5 %collective-permute-start.6 = (f32[128,256]{1,0:T(8,128)S(1)}, f32[128,256]{1,0:T(8,128)S(1)}, u32[]{:S(2)}, u32[]{:S(2)}) collective-permute-start(f32[128,256]{1,0:T(8,128)S(1)} %get-tuple-element.30), channel_id=1, source_target_pairs={{0,1},{2,3},{1,0},{3,2},{4,5},{6,7},{5,4},{7,6},{8,9},{10,11},{9,8... | collective-permute-start | bytes 393224 | tf_op jit(solution)/shard_map/ppermute | solution.py:666
  18.3 17.7 %collective-permute-start.5 = (f32[128,256]{1,0:T(8,128)S(1)}, f32[128,256]{1,0:T(8,128)S(1)}, u32[]{:S(2)}, u32[]{:S(2)}) collective-permute-start(f32[128,256]{1,0:T(8,128)S(1)} %get-tuple-element.31), channel_id=1, source_target_pairs={{1,2},{2,1},{5,6},{6,5},{9,10},{10,9},{13,14},{14,13},{17,18},{18,... | collective-permute-start | bytes 393224 | tf_op jit(solution)/shard_map/ppermute | solution.py:666
  36.0 0.7 copy-start.3
  36.0 0.7 copy-start.4

commit v10 on v9

--- a/solution.py
+++ b/solution.py
@@ -59,7 +59,7 @@
     return rhs.at[f, z] if f < NRHS else (cz, cx, cy, dg)[f - NRHS].at[z]
 
 
-def pack_faces(swap, place, odd_z, odd_y, rhs, cz, cx, cy, dg, z_one, z_two, y_one, y_two, *rest):
+def pack_faces(swap, place, odd_z, rhs, cz, cx, cy, dg, z_one, z_two, *rest):
     xmsgs, (whole, loads, saves) = rest[:-3], rest[-3:]
     copies = []
     for f in range(FIELDS):
@@ -91,17 +91,6 @@
             else:
                 xmsgs[0][f, m] = first
                 xmsgs[1][f, m] = last
-    odd = odd_y[0] == 1
-    for t in range(NX // 8):
-        for half in range(2):
-            lo, hi = (
-                pack_lanes(
-                    lambda f, zz: whole[f, 4 * half + zz, 8 * t : 8 * t + 8, 128 * side : 128 * side + 128], side
-                )
-                for side in range(2)
-            )
-            y_one[8 * t : 8 * t + 8, 128 * half : 128 * half + 128] = jnp.where(odd, lo, hi)
-            y_two[8 * t : 8 * t + 8, 128 * half : 128 * half + 128] = jnp.where(odd, hi, lo)
     for copy in planes:
         copy.wait()
 
@@ -135,6 +124,23 @@
                 tile = pltpu.roll(tile, shift, 1)
             acc = jnp.where((lane >= spot) & (lane < spot + 4), tile, acc)
     return acc
+
+
+def pack_own_rims(odd_y, rhs, cz, cx, cy, dg, one, two):
+    odd = odd_y[0] == 1
+    for t in range(NX // 8):
+        for half in range(2):
+            lo, hi = (
+                pack_lanes(
+                    lambda f, zz: field_of(rhs, cz, cx, cy, dg, f, 4 * half + zz)[
+                        8 * t : 8 * t + 8, 128 * side : 128 * side + 128
+                    ],
+                    side,
+                )
+                for side in range(2)
+            )
+            one[8 * t : 8 * t + 8, 128 * half : 128 * half + 128] = jnp.where(odd, lo, hi)
+            two[8 * t : 8 * t + 8, 128 * half : 128 * half + 128] = jnp.where(odd, hi, lo)
 
 
 def pack_rims(swap, place, odd_y, *refs):
@@ -235,8 +241,11 @@
     return jnp.concatenate(tops, 0)
 
 
-def slot(k):
-    return k * NRHS + (NRHS if k else 0)
+GROUPS = (9, 12, 9, 9, 9, 9)
+
+
+def group(k):
+    return k + 1 if k else 0
 
 
 class Block:
@@ -245,55 +254,87 @@
         self.stores, self.base, self.faces, self.faces_base = stores, base, faces, faces_base
         self.lane = lane_ids((8, 128))
 
-    def put(self, f, z, l, t, value):
-        store, f, z = self.stores[f // NRHS], f % NRHS, z - self.base
-        store[f, z, l, 8 + 8 * t : 16 + 8 * t, :] = value
+    def where(self, f, l):
+        return (0, 2 * f + l) if f < NRHS else (1, 3 * (f - NRHS) + l)
+
+    def put(self, g, n, z, t, value):
+        store, z = self.stores[g], z - self.base
+        store[n, z, 8 + 8 * t : 16 + 8 * t, :] = value
         if t == 0:
-            store[f, z, l, 8 + ROWS : 16 + ROWS, :] = value
+            store[n, z, 8 + ROWS : 16 + ROWS, :] = value
         if t == ROWS // 8 - 1:
-            store[f, z, l, 0:8, :] = value
+            store[n, z, 0:8, :] = value
+
+    def get(self, g, n, z, t, off=0):
+        row = 8 + 8 * t + (off * self.one if off else 0)
+        return self.stores[g][n, z - self.base, pl.ds(row, 8), :]
+
+    def close_ring(self, f, z):
+        z = z - self.base
+        for l in range(2):
+            g, n = self.where(f, l)
+            self.stores[g][n, z, 8 + ROWS : 16 + ROWS, :] = self.stores[g][n, z, 8:16, :]
 
     def place_y(self, z, up, dn):
+        lane = self.lane
         for t in range(ROWS // 8):
             u_all, d_all = up[8 * t : 8 * t + 8, :], dn[8 * t : 8 * t + 8, :]
+
+            def turned(value, shift):
+                return pltpu.roll(value, shift % 128, 1) if shift % 128 else value
+
+            def pair(f, zz, r, rest):
+                spot = (zz * FIELDS + f) * 4
+                u = turned(u_all, 32 * r - spot)
+                d = turned(d_all, 32 * r + 28 - spot)
+                rest = jnp.where((lane >= 32 * r) & (lane < 32 * r + 4), u, rest)
+                return jnp.where((lane >= 32 * r + 28) & (lane < 32 * r + 32), d, rest)
+
+            zero = jnp.zeros((8, 128), F32)
             for zz in range(4):
-                for f in range(FIELDS):
-                    spot = (zz * FIELDS + f) * 4
-                    u = pltpu.roll(u_all, (-spot) % 128, 1) if spot else u_all
-                    d = pltpu.roll(d_all, (124 - spot) % 128, 1) if spot != 124 else d_all
-                    value = jnp.where(self.lane < 4, u, jnp.where(self.lane >= 124, d, 0.0))
-                    self.put(f, z + zz, 2, t, value)
-
-    def tiles(self, f, z, t, off):
-        store, f, z = self.stores[f // NRHS], f % NRHS, z - self.base
-        row = 8 + 8 * t + (off * self.one if off else 0)
-        return [store[f, z, l, pl.ds(row, 8), :] for l in range(LT)]
-
-    def close_ring(self, f, z):
-        store, f, z = self.stores[f // NRHS], f % NRHS, z - self.base
-        for l in range(2):
-            store[f, z, l, 8 + ROWS : 16 + ROWS, :] = store[f, z, l, 8:16, :]
-
-    def lane_up(self, tri):
-        rolled = [pltpu.roll(v, 127, 1) for v in tri]
-        return [jnp.where(self.lane == 127, rolled[(l + 1) % LT], rolled[l]) for l in range(LT)]
-
-    def lane_dn(self, tri):
-        rolled = [pltpu.roll(v, 1, 1) for v in tri]
-        return [jnp.where(self.lane == 0, rolled[(l - 1) % LT], rolled[l]) for l in range(LT)]
+                value = zero
+                for r in range(NRHS):
+                    value = pair(r, zz, r, value)
+                self.put(0, 2 * NRHS, z + zz, t, value)
+                for c in range(4):
+                    value = pair(NRHS + c, zz, 0, zero)
+                    value = value + turned(value, 32)
+                    value = value + turned(value, 64)
+                    self.put(1, 3 * c + 2, z + zz, t, value)
 
     def coefficients(self, z):
+        lane = self.lane
         for t in range(ROWS // 8):
-            kz, kx, ky, kd = (NRHS + i for i in range(4))
-            center_z, center_x, center_y = (self.tiles(k, z, t, 0) for k in (kz, kx, ky))
-            diag = self.tiles(kd, z, t, 0)
+
+            def tiles(c, z, off=0):
+                return [self.get(1, 3 * c + l, z, t, off) for l in range(LT)]
+
+            center_z, center_x, center_y, diag = (tiles(c, z) for c in range(4))
+            up = [pltpu.roll(v, 127, 1) for v in center_y]
+            dn = [pltpu.roll(v, 1, 1) for v in center_y]
+            first = jnp.broadcast_to(center_y[0][:, 0:1], (8, 128))
+            last = jnp.broadcast_to(center_y[1][:, 127:128], (8, 128))
             sides = [
-                (center_z, self.tiles(kz, z + 1, t, 0)),
-                (center_z, self.tiles(kz, z - 1, t, 0)),
-                (center_x, self.tiles(kx, z, t, 1)),
-                (center_x, self.tiles(kx, z, t, -1)),
-                (center_y, self.lane_up(center_y)),
-                (center_y, self.lane_dn(center_y)),
+                (center_z, tiles(0, z + 1)),
+                (center_z, tiles(0, z - 1)),
+                (center_x, tiles(1, z, 1)),
+                (center_x, tiles(1, z, -1)),
+                (
+                    center_y,
+                    [
+                        jnp.where(lane == 127, up[1], up[0]),
+                        jnp.where(lane == 127, up[2], up[1]),
+                        jnp.where((lane & 31) == 31, first, up[2]),
+                    ],
+                ),
+                (
+                    center_y,
+                    [
+                        jnp.where(lane == 0, dn[2], dn[0]),
+                        jnp.where(lane == 0, dn[0], dn[1]),
+                        jnp.where((lane & 31) == 0, last, dn[2]),
+                    ],
+                ),
             ]
             at = z - self.faces_base
             for l in range(LT):
@@ -307,27 +348,46 @@
 
     def apply(self, k, z):
         last = k == STEPS - 1
-        at = z - self.faces_base
-        outs = 2 if last else LT
+        at, lane, edge = z - self.faces_base, self.lane, 2 * NRHS
+        src, dst = group(k), group(k + 1)
         for t in range(NX // 8 if last else ROWS // 8):
-            face = [[self.faces[c, at, l, 8 * t : 8 * t + 8, :] for l in range(outs)] for c in range(7)]
-            diag = [face[6][l] - SHIFTS[k] * SCALE for l in range(outs)]
+            face = [
+                [self.faces[c, at, l, 8 * t : 8 * t + 8, :] for l in range(2 if last else LT)] for c in range(7)
+            ]
+            diag = [d - SHIFTS[k] * SCALE for d in face[6]]
+
+            def image(n, l, mid, up, dn):
+                sides = (
+                    self.get(src, n, z + 1, t),
+                    self.get(src, n, z - 1, t),
+                    self.get(src, n, z, t, 1),
+                    self.get(src, n, z, t, -1),
+                    up,
+                    dn,
+                )
+                value = diag[l] * mid
+                for c, side in enumerate(sides):
+                    value = value - face[c][l] * side
+                self.put(dst, n, z, t, value)
+
+            rim = self.get(src, edge, z, t)
+            rim_up, rim_dn = pltpu.roll(rim, 127, 1), pltpu.roll(rim, 1, 1)
+            edge_up, edge_dn = rim_up, rim_dn
             for r in range(NRHS):
-                f = slot(k) + r
-                mid = self.tiles(f, z, t, 0)
-                sides = [
-                    self.tiles(f, z + 1, t, 0),
-                    self.tiles(f, z - 1, t, 0),
-                    self.tiles(f, z, t, 1),
-                    self.tiles(f, z, t, -1),
-                    self.lane_up(mid),
-                    self.lane_dn(mid),
-                ]
-                for l in range(outs):
-                    value = diag[l] * mid[l]
-                    for c in range(6):
-                        value = value - face[c][l] * sides[c][l]
-                    self.put(slot(k + 1) + r, z, l, t, value)
+                one, two = self.get(src, 2 * r, z, t), self.get(src, 2 * r + 1, z, t)
+                one_up, two_up = pltpu.roll(one, 127, 1), pltpu.roll(two, 127, 1)
+                one_dn, two_dn = pltpu.roll(one, 1, 1), pltpu.roll(two, 1, 1)
+                above = rim_up if r == 0 else pltpu.roll(rim, 127 - 32 * r, 1)
+                below = rim_dn if r == NRHS - 1 else pltpu.roll(rim, 97 - 32 * r, 1)
+                image(2 * r, 0, one, jnp.where(lane == 127, two_up, one_up), jnp.where(lane == 0, below, one_dn))
+                image(2 * r + 1, 1, two, jnp.where(lane == 127, above, two_up), jnp.where(lane == 0, one_dn, two_dn))
+                if not last:
+                    start = one_up if r == NRHS - 1 else pltpu.roll(one, 32 * r + 31, 1)
+                    end = two_dn if r == 0 else pltpu.roll(two, 32 * r + 1, 1)
+                    edge_up = jnp.where(lane == 32 * r + 31, start, edge_up)
+                    edge_dn = jnp.where(lane == 32 * r, end, edge_dn)
+            if not last:
+                image(edge, 2, rim, edge_up, edge_dn)
 
 
 def dynamic_one(place):
@@ -351,17 +411,14 @@
         src, dst = (here, there) if out else (there, here)
         return pltpu.make_async_copy(src, dst, sems.at[n])
 
-    def planes(ref, f, start, stop, at):
-        return ref.at[pl.ds(f, NRHS), pl.ds(start - at, stop - start)]
-
     result = []
-    for n, (f, start, stop) in enumerate(
-        [(f, z, z + 2) for f in (0, NRHS) for z in (DEPTH, DEPTH + NZ - 2)]
+    for n, (g, start, stop) in enumerate(
+        [(g, z, z + 2) for g in (0, 1) for z in (DEPTH, DEPTH + NZ - 2)]
         + [(0, DEPTH + 2, DEPTH + NZ - 2)]
-        + [(slot(k), *inner_planes(k)) for k in range(1, STEPS)]
+        + [(group(k), *inner_planes(k)) for k in range(1, STEPS)]
     ):
-        there = planes(inner, f, start, stop, DEPTH)
-        result.append(copy(n, there, stores[f // NRHS].at[:, pl.ds(start - base, stop - start)]))
+        there = inner.at[pl.ds(sum(GROUPS[:g]), GROUPS[g]), pl.ds(start - DEPTH, stop - start)]
+        result.append(copy(n, there, stores[g].at[:, pl.ds(start - base, stop - start)]))
     start, stop = inner_planes(1)
     result.append(copy(len(result), inner_faces, faces.at[:, pl.ds(start - faces_base, stop - start)]))
     return result
@@ -372,15 +429,15 @@
     keep_up, keep_dn = keep_sides(swap, place)
     block = Block(stores, DEPTH, faces, DEPTH + 1, dynamic_one(place))
     loads = []
-    for n, src in enumerate((rhs, cz, cx, cy, dg)):
+    for f in range(FIELDS):
+        src = rhs.at[f] if f < NRHS else (cz, cx, cy, dg)[f - NRHS]
         for l in range(2):
-            lanes = pl.ds(128 * l, 128)
-            rows = pl.ds(8, NX)
-            if n == 0:
-                src_at, dst = src.at[:, :, :, lanes], stores[0].at[:, :, l, rows, :]
-            else:
-                src_at, dst = src.at[:, :, lanes], stores[1].at[n - 1, :, l, rows, :]
-            loads.append(pltpu.make_async_copy(src_at, dst, load_sems.at[2 * n + l]))
+            g, n = block.where(f, l)
+            loads.append(
+                pltpu.make_async_copy(
+                    src.at[:, :, pl.ds(128 * l, 128)], stores[g].at[n, :, pl.ds(8, NX), :], load_sems.at[2 * f + l]
+                )
+            )
             loads[-1].start()
     for f in range(FIELDS):
         for z in range(DEPTH, DEPTH + NZ):
@@ -388,7 +445,7 @@
             for l in range(2):
                 lanes = pl.ds(128 * l, 128)
                 tile = halo_tile(above[f, m, :, lanes], below[f, m, :, lanes], z % 2, keep_up, keep_dn)
-                block.put(f, z, l, NX // 8, tile)
+                block.put(*block.where(f, l), z, NX // 8, tile)
     for half in range(2):
         lanes = pl.ds(128 * half, 128)
         block.place_y(DEPTH + 4 * half, yup.at[:, lanes], ydn.at[:, lanes])
@@ -430,10 +487,11 @@
             depth = DEPTH if f <= NRHS else DEPTH - 1
             for side, (face, z) in enumerate(((lower, DEPTH - depth), (upper, DEPTH + NZ))):
                 for l in range(2):
+                    g, n = block.where(f, l)
                     planes.append(
                         pltpu.make_async_copy(
                             face.at[pl.ds(start, depth), :, pl.ds(128 * l, 128)],
-                            stores[f // NRHS].at[f % NRHS, pl.ds(z, depth), l, pl.ds(8, NX), :],
+                            stores[g].at[n, pl.ds(z, depth), pl.ds(8, NX), :],
                             plane_sems.at[4 * f + 2 * side + l],
                         )
                     )
@@ -470,11 +528,11 @@
                     elif far == 3 and 8 * (f // 2) < FAR:
                         at, odd = NEAR + 8 * (f // 2), f % 2
                     else:
-                        block.put(f, z, l, NX // 8, zero)
+                        block.put(*block.where(f, l), z, NX // 8, zero)
                         continue
                     other = at + (n_x - 1) * (NEAR + FAR)
                     tile = halo_tile(rim[at : at + 8, lanes], rim[other : other + 8, lanes], odd, keep_up, keep_dn)
-                    block.put(f, z, l, NX // 8, tile)
+                    block.put(*block.where(f, l), z, NX // 8, tile)
     rows = pl.ds(n_x * (NEAR + FAR), ROWS)
     for rim, z in ((rimlo, 0), (rimhi, DEPTH + NZ)):
         block.place_y(z, rim.at[rows, pl.ds(0, 128)], rim.at[rows, pl.ds(128, 128)])
@@ -495,8 +553,8 @@
 
     def send_block(k):
         copy = pltpu.make_async_copy(
-            stores[slot(k) // NRHS].at[:, pl.ds(DEPTH, NZ), pl.ds(0, 2), pl.ds(8, NX), :],
-            basis.at[pl.ds(k * NRHS, NRHS)],
+            stores[group(k)].at[pl.ds(0, 2 * NRHS), pl.ds(DEPTH, NZ), pl.ds(8, NX), :],
+            basis.at[pl.ds(k * 2 * NRHS, 2 * NRHS)],
             saves.at[k],
         )
         copy.start()
@@ -519,8 +577,8 @@
 
     def products(z):
         def tile(i, t):
-            store = stores[slot(i // NRHS) // NRHS]
-            return jnp.concatenate([store[i % NRHS, z, l, 8 + 8 * t : 16 + 8 * t, :] for l in range(2)], 1)
+            store = stores[group(i // NRHS)]
+            return jnp.concatenate([store[2 * (i % NRHS) + l, z, 8 + 8 * t : 16 + 8 * t, :] for l in range(2)], 1)
 
         gram_add([jnp.concatenate([tile(i, t) for i in range(COLS)], 0) for t in range(NX // 8)], accs)
 
@@ -537,28 +595,35 @@
     square = jnp.concatenate([upper, jnp.zeros((104, 128), F32)], 0).T
     whole = jnp.where(rows <= lanes, upper, square[0:24, :])
 
-    def splat(value):
-        return jnp.broadcast_to(value, (24, 128))
-
-    columns = [splat(whole[:, c : c + 1]) for c in range(COLS)]
-    inverse = [jnp.where(rows == c, 1.0, 0.0) for c in range(COLS)]
-    pivots = jnp.ones((24, 128), F32)
+    tile_rows = row_ids((8, 128))
+    tiles = range(3)
+
+    def split(value):
+        return [value[8 * k : 8 * k + 8] for k in tiles]
+
+    def row_of(column, j):
+        return jnp.broadcast_to(column[j // 8][j % 8 : j % 8 + 1, :], (8, 128))
+
+    columns = [split(jnp.broadcast_to(whole[:, c : c + 1], (24, 128))) for c in range(COLS)]
+    inverse = [[jnp.where(tile_rows + 8 * k == c, 1.0, 0.0) for k in tiles] for c in range(COLS)]
+    pivots = [jnp.ones((8, 128), F32) for k in tiles]
+    for j in range(COLS):
+        pivot = row_of(columns[j], j)
+        first = j // 8
+        pivots[first] = jnp.where(tile_rows == j % 8, pivot, pivots[first])
+        below = {k: columns[j][k] / pivot for k in tiles if k >= first}
+        below[first] = jnp.where(tile_rows > j % 8, below[first], 0.0)
+        for c in range(COLS):
+            change = columns[c] if c > j else inverse[c]
+            row = row_of(change, j)
+            for k in below:
+                change[k] = change[k] - below[k] * row
+    scales = [1.0 / jnp.sqrt(p) for p in pivots]
     factor = jnp.zeros((24, 128), F32)
-    for j in range(COLS):
-        pivot = splat(columns[j][j : j + 1, :])
-        pivots = jnp.where(rows == j, pivot, pivots)
-        below = jnp.where(rows > j, columns[j] / pivot, 0.0)
-        for c in range(j, COLS):
-            row = splat(columns[c][j : j + 1, :])
-            factor = jnp.where((rows == j) & (lanes == c), row, factor)
-            if c > j:
-                columns[c] = columns[c] - below * row
-        for c in range(j + 1):
-            inverse[c] = inverse[c] - below * splat(inverse[c][j : j + 1, :])
-    roots = jnp.sqrt(pivots)
     for c in range(COLS):
-        table[c] = inverse[c] / roots
-    return factor / roots
+        table[c] = jnp.concatenate([inverse[c][k] * scales[k] for k in tiles], 0)
+        factor = jnp.where(lanes == c, jnp.concatenate(columns[c], 0), factor)
+    return jnp.where((rows <= lanes) & (rows < COLS), factor * jnp.concatenate(scales, 0), 0.0)
 
 
 def apply_rows(table, read, write):
@@ -593,7 +658,7 @@
 
     def products(z):
         def tile(i, t):
-            return jnp.concatenate([first[i, z, l, 8 * t : 8 * t + 8, :] for l in range(2)], 1)
+            return jnp.concatenate([first[2 * i + l, z, 8 * t : 8 * t + 8, :] for l in range(2)], 1)
 
         gram_add([jnp.concatenate([tile(i, t) for i in range(COLS)], 0) for t in range(NX // 8)], accs)
 
@@ -601,10 +666,10 @@
         for l in range(2):
 
             def read(j, p):
-                return basis[j, z, l, 8 * p : 8 * p + 8, :]
+                return basis[2 * j + l, z, 8 * p : 8 * p + 8, :]
 
             def write(i, p, value):
-                first[i, z, l, 8 * p : 8 * p + 8, :] = value
+                first[2 * i + l, z, 8 * p : 8 * p + 8, :] = value
 
             apply_rows(table, read, write)
         plane_copy(first, first_hbm, saves, z).start()
@@ -637,7 +702,7 @@
         for l in range(2):
 
             def read(j, p):
-                return first[j, z, l, 8 * p : 8 * p + 8, :]
+                return first[2 * j + l, z, 8 * p : 8 * p + 8, :]
 
             def write(i, p, value):
                 out[i, z, 8 * p : 8 * p + 8, 128 * l : 128 * l + 128] = value
@@ -679,16 +744,14 @@
     fields = (rhs, coef_z, coef_x, coef_y, diag_term)
 
     place = at_x.astype(jnp.int32).reshape(1)
-    odd_z = ((lax.axis_index("gz") + 1) & 1).astype(jnp.int32).reshape(1)
-    odd_y = (lax.axis_index("gy") & 1).astype(jnp.int32).reshape(1)
+    odd_z, odd_y = ((lax.axis_index(axis) & 1).astype(jnp.int32).reshape(1) for axis in ("gz", "gy"))
     face_shape = shape(FACE, NX, NY)
     x_shape = shape(FIELDS, NZ // 2, 8, NY)
-    own_shape = shape(NX, NY)
-    z_one, z_two, own_one, own_two, *xmsgs = pl.pallas_call(
+    z_one, z_two, *xmsgs = pl.pallas_call(
         functools.partial(pack_faces, swap),
-        out_shape=(face_shape, face_shape, own_shape, own_shape) + (x_shape,) * (1 if swap else 2),
-        in_specs=[smem()] * 3 + [hbm()] * 5,
-        out_specs=(hbm(), hbm()) + (vmem(),) * (3 if swap else 4),
+        out_shape=(face_shape, face_shape) + (x_shape,) * (1 if swap else 2),
+        in_specs=[smem()] * 2 + [hbm()] * 5,
+        out_specs=(hbm(), hbm()) + (vmem(),) * (1 if swap else 2),
         scratch_shapes=[
             pltpu.VMEM((FIELDS, NZ, NX, NY), F32),
             pltpu.SemaphoreType.DMA((FIELDS,)),
@@ -696,14 +759,21 @@
         ],
         compiler_params=params(LIMIT),
         cost_estimate=cost(2.5),
-    )(place, odd_z, odd_y, *fields)
-    face_one, face_two = swap_pairs(z_one, "gz", 1), swap_pairs(z_two, "gz", 0)
+    )(place, odd_z, *fields)
+    face_one, face_two = swap_pairs(z_one, "gz", 0), swap_pairs(z_two, "gz", 1)
     if swap:
         x_parts = (lax.ppermute(xmsgs[0], "gx", [(0, 1), (1, 0)]),)
     else:
         x_parts = (move(xmsgs[0], "gx", -1), move(xmsgs[1], "gx", 1))
 
-    halo_shape = shape(ROWS - NX, NY)
+    own_shape, halo_shape = shape(NX, NY), shape(ROWS - NX, NY)
+    own_one, own_two = pl.pallas_call(
+        pack_own_rims,
+        out_shape=(own_shape, own_shape),
+        in_specs=[smem()] + [vmem()] * 5,
+        compiler_params=params(LIMIT),
+        cost_estimate=cost(2.5),
+    )(odd_y, *fields)
     halo_one, halo_two = pl.pallas_call(
         functools.partial(pack_rims, swap),
         out_shape=(halo_shape, halo_shape),
@@ -725,10 +795,10 @@
         return jnp.concatenate(rows + [jnp.concatenate([yup[:, lanes], ydn[:, lanes]], 1)], 0)
 
     low, high = rim(0), rim(1)
-    rim_one = swap_pairs(jnp.where(odd_z == 1, low, high), "gz", 1)
-    rim_two = swap_pairs(jnp.where(odd_z == 1, high, low), "gz", 0)
-
-    inner_shape = shape(COLS, NZ, LT, EROWS, 128)
+    rim_one = swap_pairs(jnp.where(odd_z == 1, low, high), "gz", 0)
+    rim_two = swap_pairs(jnp.where(odd_z == 1, high, low), "gz", 1)
+
+    inner_shape = shape(sum(GROUPS[:-1]), NZ, EROWS, 128)
     inner_faces_shape = shape(7, NZ - 2, LT, ROWS, 128)
     inner, inner_faces = pl.pallas_call(
         functools.partial(krylov_inner, swap),
@@ -736,23 +806,23 @@
         in_specs=[smem()] + [hbm()] * 5 + [vmem()] * (len(x_parts) + 2),
         out_specs=(hbm(), hbm()),
         scratch_shapes=[
-            *[pltpu.VMEM((NRHS,) + inner_shape.shape[1:], F32)] * (STEPS + 1),
+            *[pltpu.VMEM((tiles, NZ, EROWS, 128), F32) for tiles in GROUPS[:-1]],
             pltpu.VMEM(inner_faces_shape.shape, F32),
-            pltpu.SemaphoreType.DMA((10,)),
+            pltpu.SemaphoreType.DMA((2 * FIELDS,)),
             pltpu.SemaphoreType.DMA((9,)),
         ],
         compiler_params=params(LIMIT),
         cost_estimate=cost(7),
     )(place, *fields, *x_parts, yup, ydn)
 
-    block = shape(COLS, NZ, 2, NX, 128)
+    block = shape(2 * COLS, NZ, NX, 128)
     basis, message = pl.pallas_call(
         functools.partial(krylov_outer, swap),
         out_shape=(block, shape(devices, 2, 128)),
         in_specs=[hbm(), hbm(), smem(), smem(), hbm(), hbm(), vmem(), vmem()],
         out_specs=(hbm(), vmem()),
         scratch_shapes=[
-            *[pltpu.VMEM((NRHS, EZ, LT, EROWS, 128), F32)] * (STEPS + 2),
+            *[pltpu.VMEM((tiles, EZ, EROWS, 128), F32) for tiles in GROUPS],
             pltpu.VMEM((7, EZ, LT, ROWS, 128), F32),
             pltpu.VMEM((2, STACK, STACK), F32),
             pltpu.VMEM((2,) + rim_one.shape, F32),

time: 94 us -> 123 us (1.31)
  Pallas kernels: 46.1 us -> 80 us
  waiting for transfers between devices: 11.4 us -> 0.61 us
  blocking collectives: 21.4 us -> 26.2 us
    pallas_call x1, Pallas kernels: 16.7 us -> 32.7 us  [body(): pl.pallas_call(functools.partial(krylov_outer, swap), out_shape=(block, s...]
    pallas_call x1, Pallas kernels: 7.02 us -> 22.6 us  [body(): pl.pallas_call(functools.partial(krylov_inner, swap), out_shape=(inner_sh...]
    ppermute x6, waiting for transfers between devices: 9.98 us -> 0.02 us  [swap_pairs(): return lax.ppermute(value, axis, pairs + [(j, i) for i, j in pairs])]
    all_to_all x2, blocking collectives: 21.4 us -> 26.2 us  [exchange(): return lax.all_to_all(messages, AXES, 0, 0, tiled=True)]
    pallas_call x0 -> x1, Pallas kernels: none -> 2.72 us  [body(): pl.pallas_call(pack_own_rims, out_shape=(own_shape, own_shape), in_specs=...]
  transfers between devices with their start and end apart: 7 -> 7, of which waited for: 2 -> 1; matrix products, arithmetic and copies ran while one was open for 2% -> 1% of each run, Pallas kernels for 8% -> 21%
where the time goes in v10:
time: 123 us; the launch traced here: 122 us
  Pallas kernels  80 us (65%)
  blocking collectives  26.2 us (21%)
  starting transfers between devices  12.2 us (10%)
  other arithmetic  1.56 us (1%)
    pallas_call x1, Pallas kernels, body(): pl.pallas_call(functools.partial(krylov_outer, swap), out_shape=(block, s...  32.7 us
    all_to_all x2, blocking collectives, exchange(): return lax.all_to_all(messages, AXES, 0, 0, tiled=True)  26.2 us
    pallas_call x1, Pallas kernels, body(): pl.pallas_call(functools.partial(krylov_inner, swap), out_shape=(inner_sh...  22.6 us
    pallas_call x1, Pallas kernels, body(): pl.pallas_call(functools.partial(first_pass, cells), out_shape=(block, sh...  10.8 us
    ppermute x6, starting transfers between devices, swap_pairs(): return lax.ppermute(value, axis, pairs + [(j, i) for i, j in pairs])  9.2 us
    pallas_call x1, Pallas kernels, body(): pl.pallas_call(functools.partial(second_pass, cells), out_shape=(shape(CO...  7.86 us
    pallas_call x1, Pallas kernels, body(): pl.pallas_call(functools.partial(pack_faces, swap), out_shape=(face_shape...  3.11 us
    ppermute x1, starting transfers between devices, body(): x_parts = (lax.ppermute(xmsgs[0], 'gx', [(0, 1), (1, 0)]),)  3.03 us
  transfers between devices with their start and end apart: 7, of which 1 were waited for; matrix products, arithmetic and copies ran while one was open for 1% of the time, Pallas kernels for 21%

profile of v10, /device:TPU:0, one launch (start us, length us, event | category | flops | bytes accessed | tf_op | source)
XLA Modules:
  0.0 122.1 jit_solution(15024231189038124013)
XLA Ops:
  0.6 3.1 %shard_map.68 = (f32[29,32,256]{2,1,0:T(8,128)}, f32[29,32,256]{2,1,0:T(8,128)}, f32[8,4,8,256]{3,2,1,0:T(8,128)}) custom-call(s32[1]{0:T(128)} %bitcast.place, s32[1]{0:T(128)} %bitcast.1.odd_z, f32[4,8,32,256]{3,2,1,0:T(8,128)} %rhs.5, f32[8,32,256]{2,1,0:T(8,128)} %cz.5, f32[8,32,256]{2,1,0:T(8,128)} %cx.5, f32[8,32,256]{2,1,0:T(8,128)} %cy.5, ...), custom_call_target="tpu_custom_call" | custom-call | bytes 9000000 | tf_op jit(solution)/shard_map/pallas_call | solution.py:750
  3.8 3.0 %collective-permute-start.2 = (f32[8,4,8,256]{3,2,1,0:T(8,128)}, f32[8,4,8,256]{3,2,1,0:T(8,128)S(1)}, u32[]{:S(2)}, u32[]{:S(2)}) collective-permute-start(f32[8,4,8,256]{3,2,1,0:T(8,128)} %get-tuple-element.18), channel_id=1, source_target_pairs={{0,16},{16,0},{1,17},{17,1},{2,18},{18,2},{3,19},{19,3},{4,20},{20... | collective-permute-start | bytes 786440 | tf_op jit(solution)/shard_map/ppermute | solution.py:765
  6.8 1.6 %collective-permute-start = (f32[29,32,256]{2,1,0:T(8,128)}, f32[29,32,256]{2,1,0:T(8,128)}, u32[]{:S(2)}, u32[]{:S(2)}) collective-permute-start(f32[29,32,256]{2,1,0:T(8,128)} %get-tuple-element.16), channel_id=1, source_target_pairs={{0,1},{2,3},{1,0},{3,2},{4,5},{6,7},{5,4},{7,6},{8,9},{10,11},{9,8... | collective-permute-start | bytes 2850824 | tf_op jit(solution)/shard_map/ppermute | solution.py:731
  8.4 1.6 %collective-permute-start.1 = (f32[29,32,256]{2,1,0:T(8,128)}, f32[29,32,256]{2,1,0:T(8,128)}, u32[]{:S(2)}, u32[]{:S(2)}) collective-permute-start(f32[29,32,256]{2,1,0:T(8,128)} %get-tuple-element.17), channel_id=1, source_target_pairs={{1,2},{2,1},{5,6},{6,5},{9,10},{10,9},{13,14},{14,13},{17,18},{18,... | collective-permute-start | bytes 2850824 | tf_op jit(solution)/shard_map/ppermute | solution.py:731
  10.0 2.7 %shard_map.69 = (f32[32,256]{1,0:T(8,128)}, f32[32,256]{1,0:T(8,128)}) custom-call(s32[1]{0:T(128)} %bitcast.2.odd_y, f32[4,8,32,256]{3,2,1,0:T(8,128)} %rhs.5, f32[8,32,256]{2,1,0:T(8,128)} %cz.5, f32[8,32,256]{2,1,0:T(8,128)} %cx.5, f32[8,32,256]{2,1,0:T(8,128)} %cy.5, f32[8,32,256]{2,1,0:T(8,128)} %dg.5), custom_call_target="tpu_custom_call" | custom-call | bytes 9000000 | tf_op jit(solution)/shard_map/pallas_call | solution.py:770
  12.7 0.6 collective-permute-done.2.refs_0_.rest_0_
  13.3 0.0 copy-start
  13.3 0.2 shard_map.70
  13.5 0.8 pad_maximum_fusion.1
  14.3 0.0 collective-permute-start.4
  14.3 0.8 pad_maximum_fusion
  15.0 0.7 collective-permute-start.3
  15.8 0.0 collective-permute-done.4
  15.8 0.0 collective-permute-done.3
  15.8 0.0 copy-start.1
  15.8 0.0 copy-start.2
  15.9 0.7 collective-permute-start.6
  16.6 4.7 %collective-permute-start.5 = (f32[128,256]{1,0:T(8,128)S(1)}, f32[128,256]{1,0:T(8,128)S(1)}, u32[]{:S(2)}, u32[]{:S(2)}) collective-permute-start(f32[128,256]{1,0:T(8,128)S(1)} %get-tuple-element.31), channel_id=1, source_target_pairs={{0,1},{2,3},{1,0},{3,2},{4,5},{6,7},{5,4},{7,6},{8,9},{10,11},{9,8... | collective-permute-start | bytes 393224 | tf_op jit(solution)/shard_map/ppermute | solution.py:731
  21.2 0.0 copy-done
  21.2 0.0 copy-done.1
  21.2 0.0 copy-done.2
  21.2 22.6 %shard_map.71 = (f32[48,8,56,128]{3,2,1,0:T(8,128)}, f32[7,6,3,40,128]{4,3,2,1,0:T(8,128)}) custom-call(s32[1]{0:T(128)} %bitcast.place, f32[4,8,32,256]{3,2,1,0:T(8,128)} %rhs.5, f32[8,32,256]{2,1,0:T(8,128)} %cz.5, f32[8,32,256]{2,1,0:T(8,128)} %cx.5, f32[8,32,256]{2,1,0:T(8,128)} %cy.5, f32[8,32,256]{2,1,0:T(8,128)} %dg.5, f32[8,4,8,256]{3,2,1,0:T(8,128)} %copy-done, ...), custom_call_target="tpu_custom_call" | custom-call | bytes 25200000 | tf_op jit(solution)/shard_map/pallas_call | solution.py:803
  43.9 0.0 collective-permute-done.6.rim_two
  43.9 0.0 copy-start.3
  43.9 0.0 collective-permute-done.5.rim_one
  43.9 0.0 copy-start.4
  43.9 0.0 collective-permute-done.face_one
  43.9 0.0 collective-permute-done.1.face_two
  43.9 0.6 copy-done.3
  44.5 0.1 copy-done.4
  44.6 32.7 %shard_map.72 = (f32[40,8,32,128]{3,2,1,0:T(8,128)}, f32[32,2,128]{2,1,0:T(2,128)}) custom-call(f32[29,32,256]{2,1,0:T(8,128)} %collective-permute-done.face_one, f32[29,32,256]{2,1,0:T(8,128)} %collective-permute-done.1.face_two, s32[1]{0:T(128)} %bitcast.place, s32[1]{0:T(128)} %bitcast.1.odd_z, f32[48,8,56,128]{3,2,1,0:T(8,128)} %get-tuple-element.23.inner, ...), custom_call_target="tpu_custom_call" | custom-call | bytes 54000000 | tf_op jit(solution)/shard_map/pallas_call | solution.py:819
  77.3 15.7 %all_to_all.10.message = f32[32,2,128]{2,1,0:T(2,128)} all-to-all(f32[32,2,128]{2,1,0:T(2,128)} %get-tuple-element.25), channel_id=1, replica_groups=mesh['gx'=2,'gy'=4,'gz'=4] {'gx','gy','gz'}, dimensions={0} | all-to-all | bytes 65536 | tf_op jit(solution)/shard_map/all_to_all | solution.py:735
  93.0 10.8 %shard_map.73 = (f32[40,8,32,128]{3,2,1,0:T(8,128)}, f32[32,2,128]{2,1,0:T(2,128)}, f32[24,128]{1,0:T(8,128)}) custom-call(f32[32,2,128]{2,1,0:T(2,128)} %all_to_all.10.message, f32[40,8,32,128]{3,2,1,0:T(8,128)} %get-tuple-element.26.basis_hbm), custom_call_target="tpu_custom_call" | custom-call | tf_op jit(solution)/shard_map/pallas_call | solution.py:838
  103.8 10.5 %all_to_all.11.message = f32[32,2,128]{2,1,0:T(2,128)} all-to-all(f32[32,2,128]{2,1,0:T(2,128)} %get-tuple-element.27), channel_id=1, replica_groups=mesh['gx'=2,'gy'=4,'gz'=4] {'gx','gy','gz'}, dimensions={0} | all-to-all | bytes 65536 | tf_op jit(solution)/shard_map/all_to_all | solution.py:735
  114.3 7.9 %shard_map.74 = (f32[20,8,32,256]{3,2,1,0:T(8,128)}, f32[20,20]{1,0:T(8,128)}) custom-call(f32[32,2,128]{2,1,0:T(2,128)} %all_to_all.11.message, f32[24,128]{1,0:T(8,128)} %get-tuple-element.28.factor_one, f32[40,8,32,128]{3,2,1,0:T(8,128)} %get-tuple-element.29.first_hbm), custom_call_target="tpu_custom_call" | custom-call | tf_op jit(solution)/shard_map/pallas_call | solution.py:855
  (7 shorter events, 0.1 us)
Async XLA Ops:
  3.8 9.5 %collective-permute-start.2 = (f32[8,4,8,256]{3,2,1,0:T(8,128)}, f32[8,4,8,256]{3,2,1,0:T(8,128)S(1)}, u32[]{:S(2)}, u32[]{:S(2)}) collective-permute-start(f32[8,4,8,256]{3,2,1,0:T(8,128)} %get-tuple-element.18), channel_id=1, source_target_pairs={{0,16},{16,0},{1,17},{17,1},{2,18},{18,2},{3,19},{19,3},{4,20},{20... | collective-permute-start | bytes 786440 | tf_op jit(solution)/shard_map/ppermute | solution.py:765
  6.8 37.1 %collective-permute-start = (f32[29,32,256]{2,1,0:T(8,128)}, f32[29,32,256]{2,1,0:T(8,128)}, u32[]{:S(2)}, u32[]{:S(2)}) collective-permute-start(f32[29,32,256]{2,1,0:T(8,128)} %get-tuple-element.16), channel_id=1, source_target_pairs={{0,1},{2,3},{1,0},{3,2},{4,5},{6,7},{5,4},{7,6},{8,9},{10,11},{9,8... | collective-permute-start | bytes 2850824 | tf_op jit(solution)/shard_map/ppermute | solution.py:731
  8.4 35.6 %collective-permute-start.1 = (f32[29,32,256]{2,1,0:T(8,128)}, f32[29,32,256]{2,1,0:T(8,128)}, u32[]{:S(2)}, u32[]{:S(2)}) collective-permute-start(f32[29,32,256]{2,1,0:T(8,128)} %get-tuple-element.17), channel_id=1, source_target_pairs={{1,2},{2,1},{5,6},{6,5},{9,10},{10,9},{13,14},{14,13},{17,18},{18,... | collective-permute-start | bytes 2850824 | tf_op jit(solution)/shard_map/ppermute | solution.py:731
  13.3 7.9 %copy-start = (f32[8,4,8,256]{3,2,1,0:T(8,128)}, f32[8,4,8,256]{3,2,1,0:T(8,128)S(1)}, u32[]{:S(2)}) copy-start(f32[8,4,8,256]{3,2,1,0:T(8,128)S(1)} %collective-permute-done.2.refs_0_.rest_0_) | copy-start | bytes 786436
  14.3 1.5 %collective-permute-start.4 = (f32[40,256]{1,0:T(8,128)S(1)}, f32[40,256]{1,0:T(8,128)S(1)}, u32[]{:S(2)}, u32[]{:S(2)}) collective-permute-start(f32[40,256]{1,0:T(8,128)S(1)} %pad_maximum_fusion.1), channel_id=1, source_target_pairs={{0,4},{8,12},{4,0},{12,8},{1,5},{9,13},{5,1},{13,9},{2,6},{10,14},... | collective-permute-start | bytes 122888 | tf_op jit(solution)/shard_map/ppermute | solution.py:731
  15.0 0.7 collective-permute-start.3
  15.8 5.4 %copy-start.1 = (f32[40,256]{1,0:T(8,128)}, f32[40,256]{1,0:T(8,128)S(1)}, u32[]{:S(2)}) copy-start(f32[40,256]{1,0:T(8,128)S(1)} %get-tuple-element.36.rest_2_) | copy-start | bytes 122884
  15.8 5.4 %copy-start.2 = (f32[40,256]{1,0:T(8,128)}, f32[40,256]{1,0:T(8,128)S(1)}, u32[]{:S(2)}) copy-start(f32[40,256]{1,0:T(8,128)S(1)} %get-tuple-element.37.rest_1_) | copy-start | bytes 122884
  15.9 28.0 %collective-permute-start.6 = (f32[128,256]{1,0:T(8,128)S(1)}, f32[128,256]{1,0:T(8,128)S(1)}, u32[]{:S(2)}, u32[]{:S(2)}) collective-permute-start(f32[128,256]{1,0:T(8,128)S(1)} %get-tuple-element.30), channel_id=1, source_target_pairs={{1,2},{2,1},{5,6},{6,5},{9,10},{10,9},{13,14},{14,13},{17,18},{18,... | collective-permute-start | bytes 393224 | tf_op jit(solution)/shard_map/ppermute | solution.py:731
  16.6 27.4 %collective-permute-start.5 = (f32[128,256]{1,0:T(8,128)S(1)}, f32[128,256]{1,0:T(8,128)S(1)}, u32[]{:S(2)}, u32[]{:S(2)}) collective-permute-start(f32[128,256]{1,0:T(8,128)S(1)} %get-tuple-element.31), channel_id=1, source_target_pairs={{0,1},{2,3},{1,0},{3,2},{4,5},{6,7},{5,4},{7,6},{8,9},{10,11},{9,8... | collective-permute-start | bytes 393224 | tf_op jit(solution)/shard_map/ppermute | solution.py:731
  43.9 0.6 copy-start.3
  43.9 0.7 copy-start.4

commit v11 on v10

--- a/solution.py
+++ b/solution.py
@@ -276,31 +276,34 @@
             self.stores[g][n, z, 8 + ROWS : 16 + ROWS, :] = self.stores[g][n, z, 8:16, :]
 
     def place_y(self, z, up, dn):
-        lane = self.lane
+        part, place = self.lane & 31, self.lane >> 5
+        upper, lower = part < 4, part >= 28
         for t in range(ROWS // 8):
             u_all, d_all = up[8 * t : 8 * t + 8, :], dn[8 * t : 8 * t + 8, :]
 
             def turned(value, shift):
                 return pltpu.roll(value, shift % 128, 1) if shift % 128 else value
 
-            def pair(f, zz, r, rest):
-                spot = (zz * FIELDS + f) * 4
-                u = turned(u_all, 32 * r - spot)
-                d = turned(d_all, 32 * r + 28 - spot)
-                rest = jnp.where((lane >= 32 * r) & (lane < 32 * r + 4), u, rest)
-                return jnp.where((lane >= 32 * r + 28) & (lane < 32 * r + 32), d, rest)
-
-            zero = jnp.zeros((8, 128), F32)
+            def copies(f):
+                result = []
+                for m in range(4):
+                    u, d = turned(u_all, 32 * m - 4 * f), turned(d_all, 32 * m + 28 - 4 * f)
+                    result.append(jnp.where(upper, u, jnp.where(lower, d, 0.0)))
+                return result
+
+            def pick(tiles):
+                value = tiles[0]
+                for r in range(1, 4):
+                    value = jnp.where(place == r, tiles[r], value)
+                return value
+
+            fields = [copies(r) for r in range(NRHS)]
             for zz in range(4):
-                value = zero
-                for r in range(NRHS):
-                    value = pair(r, zz, r, value)
-                self.put(0, 2 * NRHS, z + zz, t, value)
-                for c in range(4):
-                    value = pair(NRHS + c, zz, 0, zero)
-                    value = value + turned(value, 32)
-                    value = value + turned(value, 64)
-                    self.put(1, 3 * c + 2, z + zz, t, value)
+                self.put(0, 2 * NRHS, z + zz, t, pick([fields[r][(r - zz) % 4] for r in range(4)]))
+            for c in range(4):
+                mine = copies(NRHS + c)
+                for zz in range(4):
+                    self.put(1, 3 * c + 2, z + zz, t, pick([mine[(r - zz) % 4] for r in range(4)]))
 
     def coefficients(self, z):
         lane = self.lane

time: 123 us -> 94.4 us (0.77)
  Pallas kernels: 80 us -> 49.2 us
  waiting for transfers between devices: 0.61 us -> 4.26 us
    pallas_call x1, Pallas kernels: 32.7 us -> 17.1 us  [body(): pl.pallas_call(functools.partial(krylov_outer, swap), out_shape=(block, s...]
    pallas_call x1, Pallas kernels: 22.6 us -> 7.4 us  [body(): pl.pallas_call(functools.partial(krylov_inner, swap), out_shape=(inner_sh...]
    ppermute x6, waiting for transfers between devices: 0.02 us -> 3.66 us  [swap_pairs(): return lax.ppermute(value, axis, pairs + [(j, i) for i, j in pairs])]
  transfers between devices with their start and end apart: 7 -> 7, of which waited for: 1 -> 2; matrix products, arithmetic and copies ran while one was open for 1% -> 2% of each run, Pallas kernels for 21% -> 11%
where the time goes in v11:
time: 94.4 us; the launch traced here: 93.8 us
  Pallas kernels  49.2 us (52%)
  blocking collectives  25 us (26%)
  starting transfers between devices  12.2 us (13%)
  waiting for transfers between devices  4.26 us (5%)
  other arithmetic  1.56 us (2%)
    all_to_all x2, blocking collectives, exchange(): return lax.all_to_all(messages, AXES, 0, 0, tiled=True)  25 us
    pallas_call x1, Pallas kernels, body(): pl.pallas_call(functools.partial(krylov_outer, swap), out_shape=(block, s...  17.1 us
    pallas_call x1, Pallas kernels, body(): pl.pallas_call(functools.partial(first_pass, cells), out_shape=(block, sh...  10.8 us
    ppermute x6, starting transfers between devices, swap_pairs(): return lax.ppermute(value, axis, pairs + [(j, i) for i, j in pairs])  9.2 us
    pallas_call x1, Pallas kernels, body(): pl.pallas_call(functools.partial(second_pass, cells), out_shape=(shape(CO...  7.86 us
    pallas_call x1, Pallas kernels, body(): pl.pallas_call(functools.partial(krylov_inner, swap), out_shape=(inner_sh...  7.4 us
    ppermute x6, waiting for transfers between devices, swap_pairs(): return lax.ppermute(value, axis, pairs + [(j, i) for i, j in pairs])  3.66 us
    pallas_call x1, Pallas kernels, body(): pl.pallas_call(functools.partial(pack_faces, swap), out_shape=(face_shape...  3.11 us
  transfers between devices with their start and end apart: 7, of which 2 were waited for; matrix products, arithmetic and copies ran while one was open for 2% of the time, Pallas kernels for 11%

profile of v11, /device:TPU:0, one launch (start us, length us, event | category | flops | bytes accessed | tf_op | source)
XLA Modules:
  0.0 93.8 jit_solution(13453793834317411170)
XLA Ops:
  0.6 3.1 %shard_map.68 = (f32[29,32,256]{2,1,0:T(8,128)}, f32[29,32,256]{2,1,0:T(8,128)}, f32[8,4,8,256]{3,2,1,0:T(8,128)}) custom-call(s32[1]{0:T(128)} %bitcast.place, s32[1]{0:T(128)} %bitcast.1.odd_z, f32[4,8,32,256]{3,2,1,0:T(8,128)} %rhs.5, f32[8,32,256]{2,1,0:T(8,128)} %cz.5, f32[8,32,256]{2,1,0:T(8,128)} %cx.5, f32[8,32,256]{2,1,0:T(8,128)} %cy.5, ...), custom_call_target="tpu_custom_call" | custom-call | bytes 9000000 | tf_op jit(solution)/shard_map/pallas_call | solution.py:753
  3.8 3.0 %collective-permute-start.2 = (f32[8,4,8,256]{3,2,1,0:T(8,128)}, f32[8,4,8,256]{3,2,1,0:T(8,128)S(1)}, u32[]{:S(2)}, u32[]{:S(2)}) collective-permute-start(f32[8,4,8,256]{3,2,1,0:T(8,128)} %get-tuple-element.18), channel_id=1, source_target_pairs={{0,16},{16,0},{1,17},{17,1},{2,18},{18,2},{3,19},{19,3},{4,20},{20... | collective-permute-start | bytes 786440 | tf_op jit(solution)/shard_map/ppermute | solution.py:768
  6.8 1.6 %collective-permute-start = (f32[29,32,256]{2,1,0:T(8,128)}, f32[29,32,256]{2,1,0:T(8,128)}, u32[]{:S(2)}, u32[]{:S(2)}) collective-permute-start(f32[29,32,256]{2,1,0:T(8,128)} %get-tuple-element.16), channel_id=1, source_target_pairs={{0,1},{2,3},{1,0},{3,2},{4,5},{6,7},{5,4},{7,6},{8,9},{10,11},{9,8... | collective-permute-start | bytes 2850824 | tf_op jit(solution)/shard_map/ppermute | solution.py:734
  8.4 1.6 %collective-permute-start.1 = (f32[29,32,256]{2,1,0:T(8,128)}, f32[29,32,256]{2,1,0:T(8,128)}, u32[]{:S(2)}, u32[]{:S(2)}) collective-permute-start(f32[29,32,256]{2,1,0:T(8,128)} %get-tuple-element.17), channel_id=1, source_target_pairs={{1,2},{2,1},{5,6},{6,5},{9,10},{10,9},{13,14},{14,13},{17,18},{18,... | collective-permute-start | bytes 2850824 | tf_op jit(solution)/shard_map/ppermute | solution.py:734
  10.0 2.7 %shard_map.69 = (f32[32,256]{1,0:T(8,128)}, f32[32,256]{1,0:T(8,128)}) custom-call(s32[1]{0:T(128)} %bitcast.2.odd_y, f32[4,8,32,256]{3,2,1,0:T(8,128)} %rhs.5, f32[8,32,256]{2,1,0:T(8,128)} %cz.5, f32[8,32,256]{2,1,0:T(8,128)} %cx.5, f32[8,32,256]{2,1,0:T(8,128)} %cy.5, f32[8,32,256]{2,1,0:T(8,128)} %dg.5), custom_call_target="tpu_custom_call" | custom-call | bytes 9000000 | tf_op jit(solution)/shard_map/pallas_call | solution.py:773
  12.7 0.6 collective-permute-done.2.refs_0_.rest_0_
  13.3 0.0 copy-start
  13.3 0.2 shard_map.70
  13.5 0.8 pad_maximum_fusion.1
  14.3 0.0 collective-permute-start.4
  14.3 0.8 pad_maximum_fusion
  15.0 0.7 collective-permute-start.3
  15.8 0.0 collective-permute-done.4
  15.8 0.0 collective-permute-done.3
  15.8 0.0 copy-start.1
  15.8 0.0 copy-start.2
  15.9 0.7 collective-permute-start.6
  16.6 4.7 %collective-permute-start.5 = (f32[128,256]{1,0:T(8,128)S(1)}, f32[128,256]{1,0:T(8,128)S(1)}, u32[]{:S(2)}, u32[]{:S(2)}) collective-permute-start(f32[128,256]{1,0:T(8,128)S(1)} %get-tuple-element.31), channel_id=1, source_target_pairs={{0,1},{2,3},{1,0},{3,2},{4,5},{6,7},{5,4},{7,6},{8,9},{10,11},{9,8... | collective-permute-start | bytes 393224 | tf_op jit(solution)/shard_map/ppermute | solution.py:734
  21.2 0.0 copy-done
  21.2 0.0 copy-done.1
  21.2 0.0 copy-done.2
  21.2 7.4 %shard_map.71 = (f32[48,8,56,128]{3,2,1,0:T(8,128)}, f32[7,6,3,40,128]{4,3,2,1,0:T(8,128)}) custom-call(s32[1]{0:T(128)} %bitcast.place, f32[4,8,32,256]{3,2,1,0:T(8,128)} %rhs.5, f32[8,32,256]{2,1,0:T(8,128)} %cz.5, f32[8,32,256]{2,1,0:T(8,128)} %cx.5, f32[8,32,256]{2,1,0:T(8,128)} %cy.5, f32[8,32,256]{2,1,0:T(8,128)} %dg.5, f32[8,4,8,256]{3,2,1,0:T(8,128)} %copy-done, ...), custom_call_target="tpu_custom_call" | custom-call | bytes 25200000 | tf_op jit(solution)/shard_map/pallas_call | solution.py:806
  28.6 0.0 collective-permute-done.6.rim_two
  28.7 0.0 copy-start.3
  28.7 3.6 %collective-permute-done.5.rim_one = f32[128,256]{1,0:T(8,128)S(1)} collective-permute-done((f32[128,256]{1,0:T(8,128)S(1)}, f32[128,256]{1,0:T(8,128)S(1)}, u32[]{:S(2)}, u32[]{:S(2)}) %collective-permute-start.5) | collective-permute-done | bytes 131104 | tf_op jit(solution)/shard_map/ppermute | solution.py:734
  32.3 0.0 copy-start.4
  32.3 0.0 collective-permute-done.face_one
  32.3 0.0 collective-permute-done.1.face_two
  32.3 0.0 copy-done.3
  32.3 0.6 copy-done.4
  33.0 17.1 %shard_map.72 = (f32[40,8,32,128]{3,2,1,0:T(8,128)}, f32[32,2,128]{2,1,0:T(2,128)}) custom-call(f32[29,32,256]{2,1,0:T(8,128)} %collective-permute-done.face_one, f32[29,32,256]{2,1,0:T(8,128)} %collective-permute-done.1.face_two, s32[1]{0:T(128)} %bitcast.place, s32[1]{0:T(128)} %bitcast.1.odd_z, f32[48,8,56,128]{3,2,1,0:T(8,128)} %get-tuple-element.23.inner, ...), custom_call_target="tpu_custom_call" | custom-call | bytes 54000000 | tf_op jit(solution)/shard_map/pallas_call | solution.py:822
  50.1 14.5 %all_to_all.10.message = f32[32,2,128]{2,1,0:T(2,128)} all-to-all(f32[32,2,128]{2,1,0:T(2,128)} %get-tuple-element.25), channel_id=1, replica_groups=mesh['gx'=2,'gy'=4,'gz'=4] {'gx','gy','gz'}, dimensions={0} | all-to-all | bytes 65536 | tf_op jit(solution)/shard_map/all_to_all | solution.py:738
  64.6 10.8 %shard_map.73 = (f32[40,8,32,128]{3,2,1,0:T(8,128)}, f32[32,2,128]{2,1,0:T(2,128)}, f32[24,128]{1,0:T(8,128)}) custom-call(f32[32,2,128]{2,1,0:T(2,128)} %all_to_all.10.message, f32[40,8,32,128]{3,2,1,0:T(8,128)} %get-tuple-element.26.basis_hbm), custom_call_target="tpu_custom_call" | custom-call | tf_op jit(solution)/shard_map/pallas_call | solution.py:841
  75.4 10.5 %all_to_all.11.message = f32[32,2,128]{2,1,0:T(2,128)} all-to-all(f32[32,2,128]{2,1,0:T(2,128)} %get-tuple-element.27), channel_id=1, replica_groups=mesh['gx'=2,'gy'=4,'gz'=4] {'gx','gy','gz'}, dimensions={0} | all-to-all | bytes 65536 | tf_op jit(solution)/shard_map/all_to_all | solution.py:738
  85.9 7.9 %shard_map.74 = (f32[20,8,32,256]{3,2,1,0:T(8,128)}, f32[20,20]{1,0:T(8,128)}) custom-call(f32[32,2,128]{2,1,0:T(2,128)} %all_to_all.11.message, f32[24,128]{1,0:T(8,128)} %get-tuple-element.28.factor_one, f32[40,8,32,128]{3,2,1,0:T(8,128)} %get-tuple-element.29.first_hbm), custom_call_target="tpu_custom_call" | custom-call | tf_op jit(solution)/shard_map/pallas_call | solution.py:858
  (7 shorter events, 0.1 us)
Async XLA Ops:
  3.8 9.5 %collective-permute-start.2 = (f32[8,4,8,256]{3,2,1,0:T(8,128)}, f32[8,4,8,256]{3,2,1,0:T(8,128)S(1)}, u32[]{:S(2)}, u32[]{:S(2)}) collective-permute-start(f32[8,4,8,256]{3,2,1,0:T(8,128)} %get-tuple-element.18), channel_id=1, source_target_pairs={{0,16},{16,0},{1,17},{17,1},{2,18},{18,2},{3,19},{19,3},{4,20},{20... | collective-permute-start | bytes 786440 | tf_op jit(solution)/shard_map/ppermute | solution.py:768
  6.8 25.5 %collective-permute-start = (f32[29,32,256]{2,1,0:T(8,128)}, f32[29,32,256]{2,1,0:T(8,128)}, u32[]{:S(2)}, u32[]{:S(2)}) collective-permute-start(f32[29,32,256]{2,1,0:T(8,128)} %get-tuple-element.16), channel_id=1, source_target_pairs={{0,1},{2,3},{1,0},{3,2},{4,5},{6,7},{5,4},{7,6},{8,9},{10,11},{9,8... | collective-permute-start | bytes 2850824 | tf_op jit(solution)/shard_map/ppermute | solution.py:734
  8.4 24.0 %collective-permute-start.1 = (f32[29,32,256]{2,1,0:T(8,128)}, f32[29,32,256]{2,1,0:T(8,128)}, u32[]{:S(2)}, u32[]{:S(2)}) collective-permute-start(f32[29,32,256]{2,1,0:T(8,128)} %get-tuple-element.17), channel_id=1, source_target_pairs={{1,2},{2,1},{5,6},{6,5},{9,10},{10,9},{13,14},{14,13},{17,18},{18,... | collective-permute-start | bytes 2850824 | tf_op jit(solution)/shard_map/ppermute | solution.py:734
  13.3 7.9 %copy-start = (f32[8,4,8,256]{3,2,1,0:T(8,128)}, f32[8,4,8,256]{3,2,1,0:T(8,128)S(1)}, u32[]{:S(2)}) copy-start(f32[8,4,8,256]{3,2,1,0:T(8,128)S(1)} %collective-permute-done.2.refs_0_.rest_0_) | copy-start | bytes 786436
  14.3 1.5 %collective-permute-start.4 = (f32[40,256]{1,0:T(8,128)S(1)}, f32[40,256]{1,0:T(8,128)S(1)}, u32[]{:S(2)}, u32[]{:S(2)}) collective-permute-start(f32[40,256]{1,0:T(8,128)S(1)} %pad_maximum_fusion.1), channel_id=1, source_target_pairs={{0,4},{8,12},{4,0},{12,8},{1,5},{9,13},{5,1},{13,9},{2,6},{10,14},... | collective-permute-start | bytes 122888 | tf_op jit(solution)/shard_map/ppermute | solution.py:734
  15.0 0.7 collective-permute-start.3
  15.8 5.4 %copy-start.1 = (f32[40,256]{1,0:T(8,128)}, f32[40,256]{1,0:T(8,128)S(1)}, u32[]{:S(2)}) copy-start(f32[40,256]{1,0:T(8,128)S(1)} %get-tuple-element.36.rest_2_) | copy-start | bytes 122884
  15.8 5.4 %copy-start.2 = (f32[40,256]{1,0:T(8,128)}, f32[40,256]{1,0:T(8,128)S(1)}, u32[]{:S(2)}) copy-start(f32[40,256]{1,0:T(8,128)S(1)} %get-tuple-element.37.rest_1_) | copy-start | bytes 122884
  15.9 12.8 %collective-permute-start.6 = (f32[128,256]{1,0:T(8,128)S(1)}, f32[128,256]{1,0:T(8,128)S(1)}, u32[]{:S(2)}, u32[]{:S(2)}) collective-permute-start(f32[128,256]{1,0:T(8,128)S(1)} %get-tuple-element.30), channel_id=1, source_target_pairs={{1,2},{2,1},{5,6},{6,5},{9,10},{10,9},{13,14},{14,13},{17,18},{18,... | collective-permute-start | bytes 393224 | tf_op jit(solution)/shard_map/ppermute | solution.py:734
  16.6 15.8 %collective-permute-start.5 = (f32[128,256]{1,0:T(8,128)S(1)}, f32[128,256]{1,0:T(8,128)S(1)}, u32[]{:S(2)}, u32[]{:S(2)}) collective-permute-start(f32[128,256]{1,0:T(8,128)S(1)} %get-tuple-element.31), channel_id=1, source_target_pairs={{0,1},{2,3},{1,0},{3,2},{4,5},{6,7},{5,4},{7,6},{8,9},{10,11},{9,8... | collective-permute-start | bytes 393224 | tf_op jit(solution)/shard_map/ppermute | solution.py:734
  28.7 3.7 %copy-start.3 = (f32[128,256]{1,0:T(8,128)}, f32[128,256]{1,0:T(8,128)S(1)}, u32[]{:S(2)}) copy-start(f32[128,256]{1,0:T(8,128)S(1)} %collective-permute-done.6.rim_two) | copy-start | bytes 393220
  32.3 0.7 copy-start.4

commit v12 on v11

--- a/solution.py
+++ b/solution.py
@@ -24,7 +24,7 @@
 LT = 3
 FACE = NRHS * 4 + 3 * 4 + 1
 F32 = jnp.float32
-LIMIT = 63
+LIMIT, ROOMY = 63, 52
 
 
 def params(mb):
@@ -833,7 +833,7 @@
             pltpu.SemaphoreType.DMA((9,)),
             pltpu.SemaphoreType.DMA((STEPS + 1,)),
         ],
-        compiler_params=params(LIMIT),
+        compiler_params=params(ROOMY),
         cost_estimate=cost(15),
     )(face_one, face_two, place, odd_z, inner, inner_faces, rim_one, rim_two)
 
@@ -851,7 +851,7 @@
             pltpu.SemaphoreType.DMA((NZ,)),
             pltpu.SemaphoreType.DMA((NZ,)),
         ],
-        compiler_params=params(LIMIT),
+        compiler_params=params(ROOMY),
     )(message, basis)
 
     message = exchange(message)
@@ -867,7 +867,7 @@
             pltpu.SemaphoreType.DMA((NZ,)),
             pltpu.SemaphoreType.DMA((NZ,)),
         ],
-        compiler_params=params(LIMIT),
+        compiler_params=params(ROOMY),
     )(message, factor_one, first)
 
 

time: 94.4 us -> 88.3 us (0.935)
  Pallas kernels: 49.2 us -> 45.8 us
  blocking collectives: 25 us -> 23.2 us
    all_to_all x2, blocking collectives: 25 us -> 23.2 us  [exchange(): return lax.all_to_all(messages, AXES, 0, 0, tiled=True)]
    pallas_call x1, Pallas kernels: 17.1 us -> 15.6 us  [body(): pl.pallas_call(functools.partial(krylov_outer, swap), out_shape=(block, s...]
    pallas_call x1, Pallas kernels: 10.8 us -> 9.41 us  [body(): pl.pallas_call(functools.partial(first_pass, cells), out_shape=(block, sh...]
  transfers between devices with their start and end apart: 7 -> 7, of which waited for: 2 -> 2; matrix products, arithmetic and copies ran while one was open for 2% -> 2% of each run, Pallas kernels for 11% -> 12%
where the time goes in v12:
time: 88.3 us; the launch traced here: 87.9 us
  Pallas kernels  45.8 us (52%)
  blocking collectives  23.2 us (26%)
  starting transfers between devices  12.2 us (14%)
  waiting for transfers between devices  4.24 us (5%)
  other arithmetic  1.56 us (2%)
    all_to_all x2, blocking collectives, exchange(): return lax.all_to_all(messages, AXES, 0, 0, tiled=True)  23.2 us
    pallas_call x1, Pallas kernels, body(): pl.pallas_call(functools.partial(krylov_outer, swap), out_shape=(block, s...  15.6 us
    pallas_call x1, Pallas kernels, body(): pl.pallas_call(functools.partial(first_pass, cells), out_shape=(block, sh...  9.41 us
    ppermute x6, starting transfers between devices, swap_pairs(): return lax.ppermute(value, axis, pairs + [(j, i) for i, j in pairs])  9.21 us
    pallas_call x1, Pallas kernels, body(): pl.pallas_call(functools.partial(krylov_inner, swap), out_shape=(inner_sh...  7.42 us
    pallas_call x1, Pallas kernels, body(): pl.pallas_call(functools.partial(second_pass, cells), out_shape=(shape(CO...  7.37 us
    ppermute x6, waiting for transfers between devices, swap_pairs(): return lax.ppermute(value, axis, pairs + [(j, i) for i, j in pairs])  3.66 us
    pallas_call x1, Pallas kernels, body(): pl.pallas_call(functools.partial(pack_faces, swap), out_shape=(face_shape...  3.11 us
  transfers between devices with their start and end apart: 7, of which 2 were waited for; matrix products, arithmetic and copies ran while one was open for 2% of the time, Pallas kernels for 12%

profile of v12, /device:TPU:0, one launch (start us, length us, event | category | flops | bytes accessed | tf_op | source)
XLA Modules:
  0.0 87.9 jit_solution(4803394615435932224)
XLA Ops:
  0.6 3.1 %shard_map.68 = (f32[29,32,256]{2,1,0:T(8,128)}, f32[29,32,256]{2,1,0:T(8,128)}, f32[8,4,8,256]{3,2,1,0:T(8,128)}) custom-call(s32[1]{0:T(128)} %bitcast.place, s32[1]{0:T(128)} %bitcast.1.odd_z, f32[4,8,32,256]{3,2,1,0:T(8,128)} %rhs.5, f32[8,32,256]{2,1,0:T(8,128)} %cz.5, f32[8,32,256]{2,1,0:T(8,128)} %cx.5, f32[8,32,256]{2,1,0:T(8,128)} %cy.5, ...), custom_call_target="tpu_custom_call" | custom-call | bytes 9000000 | tf_op jit(solution)/shard_map/pallas_call | solution.py:753
  3.8 3.0 %collective-permute-start.2 = (f32[8,4,8,256]{3,2,1,0:T(8,128)}, f32[8,4,8,256]{3,2,1,0:T(8,128)S(1)}, u32[]{:S(2)}, u32[]{:S(2)}) collective-permute-start(f32[8,4,8,256]{3,2,1,0:T(8,128)} %get-tuple-element.18), channel_id=1, source_target_pairs={{0,16},{16,0},{1,17},{17,1},{2,18},{18,2},{3,19},{19,3},{4,20},{20... | collective-permute-start | bytes 786440 | tf_op jit(solution)/shard_map/ppermute | solution.py:768
  6.8 1.6 %collective-permute-start = (f32[29,32,256]{2,1,0:T(8,128)}, f32[29,32,256]{2,1,0:T(8,128)}, u32[]{:S(2)}, u32[]{:S(2)}) collective-permute-start(f32[29,32,256]{2,1,0:T(8,128)} %get-tuple-element.16), channel_id=1, source_target_pairs={{0,1},{2,3},{1,0},{3,2},{4,5},{6,7},{5,4},{7,6},{8,9},{10,11},{9,8... | collective-permute-start | bytes 2850824 | tf_op jit(solution)/shard_map/ppermute | solution.py:734
  8.4 1.6 %collective-permute-start.1 = (f32[29,32,256]{2,1,0:T(8,128)}, f32[29,32,256]{2,1,0:T(8,128)}, u32[]{:S(2)}, u32[]{:S(2)}) collective-permute-start(f32[29,32,256]{2,1,0:T(8,128)} %get-tuple-element.17), channel_id=1, source_target_pairs={{1,2},{2,1},{5,6},{6,5},{9,10},{10,9},{13,14},{14,13},{17,18},{18,... | collective-permute-start | bytes 2850824 | tf_op jit(solution)/shard_map/ppermute | solution.py:734
  10.0 2.7 %shard_map.69 = (f32[32,256]{1,0:T(8,128)}, f32[32,256]{1,0:T(8,128)}) custom-call(s32[1]{0:T(128)} %bitcast.2.odd_y, f32[4,8,32,256]{3,2,1,0:T(8,128)} %rhs.5, f32[8,32,256]{2,1,0:T(8,128)} %cz.5, f32[8,32,256]{2,1,0:T(8,128)} %cx.5, f32[8,32,256]{2,1,0:T(8,128)} %cy.5, f32[8,32,256]{2,1,0:T(8,128)} %dg.5), custom_call_target="tpu_custom_call" | custom-call | bytes 9000000 | tf_op jit(solution)/shard_map/pallas_call | solution.py:773
  12.7 0.6 collective-permute-done.2.refs_0_.rest_0_
  13.3 0.0 copy-start
  13.3 0.2 shard_map.70
  13.5 0.8 pad_maximum_fusion.1
  14.3 0.0 collective-permute-start.4
  14.3 0.8 pad_maximum_fusion
  15.0 0.7 collective-permute-start.3
  15.8 0.0 collective-permute-done.4
  15.8 0.0 collective-permute-done.3
  15.8 0.0 copy-start.1
  15.8 0.0 copy-start.2
  15.9 0.7 collective-permute-start.6
  16.6 4.7 %collective-permute-start.5 = (f32[128,256]{1,0:T(8,128)S(1)}, f32[128,256]{1,0:T(8,128)S(1)}, u32[]{:S(2)}, u32[]{:S(2)}) collective-permute-start(f32[128,256]{1,0:T(8,128)S(1)} %get-tuple-element.31), channel_id=1, source_target_pairs={{0,1},{2,3},{1,0},{3,2},{4,5},{6,7},{5,4},{7,6},{8,9},{10,11},{9,8... | collective-permute-start | bytes 393224 | tf_op jit(solution)/shard_map/ppermute | solution.py:734
  21.2 0.0 copy-done
  21.2 0.0 copy-done.1
  21.2 0.0 copy-done.2
  21.2 7.4 %shard_map.71 = (f32[48,8,56,128]{3,2,1,0:T(8,128)}, f32[7,6,3,40,128]{4,3,2,1,0:T(8,128)}) custom-call(s32[1]{0:T(128)} %bitcast.place, f32[4,8,32,256]{3,2,1,0:T(8,128)} %rhs.5, f32[8,32,256]{2,1,0:T(8,128)} %cz.5, f32[8,32,256]{2,1,0:T(8,128)} %cx.5, f32[8,32,256]{2,1,0:T(8,128)} %cy.5, f32[8,32,256]{2,1,0:T(8,128)} %dg.5, f32[8,4,8,256]{3,2,1,0:T(8,128)} %copy-done, ...), custom_call_target="tpu_custom_call" | custom-call | bytes 25200000 | tf_op jit(solution)/shard_map/pallas_call | solution.py:806
  28.7 0.0 collective-permute-done.6.rim_two
  28.7 3.6 %collective-permute-done.5.rim_one = f32[128,256]{1,0:T(8,128)S(1)} collective-permute-done((f32[128,256]{1,0:T(8,128)S(1)}, f32[128,256]{1,0:T(8,128)S(1)}, u32[]{:S(2)}, u32[]{:S(2)}) %collective-permute-start.5) | collective-permute-done | bytes 131104 | tf_op jit(solution)/shard_map/ppermute | solution.py:734
  32.3 0.0 collective-permute-done.face_one
  32.3 0.0 collective-permute-done.1.face_two
  32.3 15.6 %shard_map.72 = (f32[40,8,32,128]{3,2,1,0:T(8,128)}, f32[32,2,128]{2,1,0:T(2,128)S(1)}) custom-call(f32[29,32,256]{2,1,0:T(8,128)} %collective-permute-done.face_one, f32[29,32,256]{2,1,0:T(8,128)} %collective-permute-done.1.face_two, s32[1]{0:T(128)} %bitcast.place, s32[1]{0:T(128)} %bitcast.1.odd_z, f32[48,8,56,128]{3,2,1,0:T(8,128)} %get-tuple-element.23.inner, ...), custom_call_target="tpu_custom_call" | custom-call | bytes 54000000 | tf_op jit(solution)/shard_map/pallas_call | solution.py:822
  47.9 14.2 %all_to_all.10.message = f32[32,2,128]{2,1,0:T(2,128)S(1)} all-to-all(f32[32,2,128]{2,1,0:T(2,128)S(1)} %get-tuple-element.25), channel_id=1, replica_groups=mesh['gx'=2,'gy'=4,'gz'=4] {'gx','gy','gz'}, dimensions={0} | all-to-all | bytes 65536 | tf_op jit(solution)/shard_map/all_to_all | solution.py:738
  62.1 9.4 %shard_map.73 = (f32[40,8,32,128]{3,2,1,0:T(8,128)}, f32[32,2,128]{2,1,0:T(2,128)S(1)}, f32[24,128]{1,0:T(8,128)S(1)}) custom-call(f32[32,2,128]{2,1,0:T(2,128)S(1)} %all_to_all.10.message, f32[40,8,32,128]{3,2,1,0:T(8,128)} %get-tuple-element.26.basis_hbm), custom_call_target="tpu_custom_call" | custom-call | tf_op jit(solution)/shard_map/pallas_call | solution.py:841
  71.5 9.0 %all_to_all.11.message = f32[32,2,128]{2,1,0:T(2,128)S(1)} all-to-all(f32[32,2,128]{2,1,0:T(2,128)S(1)} %get-tuple-element.27), channel_id=1, replica_groups=mesh['gx'=2,'gy'=4,'gz'=4] {'gx','gy','gz'}, dimensions={0} | all-to-all | bytes 65536 | tf_op jit(solution)/shard_map/all_to_all | solution.py:738
  80.5 7.4 %shard_map.74 = (f32[20,8,32,256]{3,2,1,0:T(8,128)}, f32[20,20]{1,0:T(8,128)}) custom-call(f32[32,2,128]{2,1,0:T(2,128)S(1)} %all_to_all.11.message, f32[24,128]{1,0:T(8,128)S(1)} %get-tuple-element.28.factor_one, f32[40,8,32,128]{3,2,1,0:T(8,128)} %get-tuple-element.29.first_hbm), custom_call_target="tpu_custom_call" | custom-call | tf_op jit(solution)/shard_map/pallas_call | solution.py:858
  (7 shorter events, 0.1 us)
Async XLA Ops:
  3.8 9.5 %collective-permute-start.2 = (f32[8,4,8,256]{3,2,1,0:T(8,128)}, f32[8,4,8,256]{3,2,1,0:T(8,128)S(1)}, u32[]{:S(2)}, u32[]{:S(2)}) collective-permute-start(f32[8,4,8,256]{3,2,1,0:T(8,128)} %get-tuple-element.18), channel_id=1, source_target_pairs={{0,16},{16,0},{1,17},{17,1},{2,18},{18,2},{3,19},{19,3},{4,20},{20... | collective-permute-start | bytes 786440 | tf_op jit(solution)/shard_map/ppermute | solution.py:768
  6.8 25.5 %collective-permute-start = (f32[29,32,256]{2,1,0:T(8,128)}, f32[29,32,256]{2,1,0:T(8,128)}, u32[]{:S(2)}, u32[]{:S(2)}) collective-permute-start(f32[29,32,256]{2,1,0:T(8,128)} %get-tuple-element.16), channel_id=1, source_target_pairs={{0,1},{2,3},{1,0},{3,2},{4,5},{6,7},{5,4},{7,6},{8,9},{10,11},{9,8... | collective-permute-start | bytes 2850824 | tf_op jit(solution)/shard_map/ppermute | solution.py:734
  8.4 24.0 %collective-permute-start.1 = (f32[29,32,256]{2,1,0:T(8,128)}, f32[29,32,256]{2,1,0:T(8,128)}, u32[]{:S(2)}, u32[]{:S(2)}) collective-permute-start(f32[29,32,256]{2,1,0:T(8,128)} %get-tuple-element.17), channel_id=1, source_target_pairs={{1,2},{2,1},{5,6},{6,5},{9,10},{10,9},{13,14},{14,13},{17,18},{18,... | collective-permute-start | bytes 2850824 | tf_op jit(solution)/shard_map/ppermute | solution.py:734
  13.3 7.9 %copy-start = (f32[8,4,8,256]{3,2,1,0:T(8,128)}, f32[8,4,8,256]{3,2,1,0:T(8,128)S(1)}, u32[]{:S(2)}) copy-start(f32[8,4,8,256]{3,2,1,0:T(8,128)S(1)} %collective-permute-done.2.refs_0_.rest_0_) | copy-start | bytes 786436
  14.3 1.5 %collective-permute-start.4 = (f32[40,256]{1,0:T(8,128)S(1)}, f32[40,256]{1,0:T(8,128)S(1)}, u32[]{:S(2)}, u32[]{:S(2)}) collective-permute-start(f32[40,256]{1,0:T(8,128)S(1)} %pad_maximum_fusion.1), channel_id=1, source_target_pairs={{0,4},{8,12},{4,0},{12,8},{1,5},{9,13},{5,1},{13,9},{2,6},{10,14},... | collective-permute-start | bytes 122888 | tf_op jit(solution)/shard_map/ppermute | solution.py:734
  15.0 0.7 collective-permute-start.3
  15.8 5.4 %copy-start.1 = (f32[40,256]{1,0:T(8,128)}, f32[40,256]{1,0:T(8,128)S(1)}, u32[]{:S(2)}) copy-start(f32[40,256]{1,0:T(8,128)S(1)} %get-tuple-element.36.rest_2_) | copy-start | bytes 122884
  15.8 5.4 %copy-start.2 = (f32[40,256]{1,0:T(8,128)}, f32[40,256]{1,0:T(8,128)S(1)}, u32[]{:S(2)}) copy-start(f32[40,256]{1,0:T(8,128)S(1)} %get-tuple-element.37.rest_1_) | copy-start | bytes 122884
  15.9 12.8 %collective-permute-start.6 = (f32[128,256]{1,0:T(8,128)S(1)}, f32[128,256]{1,0:T(8,128)S(1)}, u32[]{:S(2)}, u32[]{:S(2)}) collective-permute-start(f32[128,256]{1,0:T(8,128)S(1)} %get-tuple-element.30), channel_id=1, source_target_pairs={{1,2},{2,1},{5,6},{6,5},{9,10},{10,9},{13,14},{14,13},{17,18},{18,... | collective-permute-start | bytes 393224 | tf_op jit(solution)/shard_map/ppermute | solution.py:734
  16.6 15.8 %collective-permute-start.5 = (f32[128,256]{1,0:T(8,128)S(1)}, f32[128,256]{1,0:T(8,128)S(1)}, u32[]{:S(2)}, u32[]{:S(2)}) collective-permute-start(f32[128,256]{1,0:T(8,128)S(1)} %get-tuple-element.31), channel_id=1, source_target_pairs={{0,1},{2,3},{1,0},{3,2},{4,5},{6,7},{5,4},{7,6},{8,9},{10,11},{9,8... | collective-permute-start | bytes 393224 | tf_op jit(solution)/shard_map/ppermute | solution.py:734

commit v13 on v12

--- a/solution.py
+++ b/solution.py
@@ -60,7 +60,7 @@
 
 
 def pack_faces(swap, place, odd_z, rhs, cz, cx, cy, dg, z_one, z_two, *rest):
-    xmsgs, (whole, loads, saves) = rest[:-3], rest[-3:]
+    xmsgs, (xrows, whole, loads, saves, xsaves) = rest[:-5], rest[-5:]
     copies = []
     for f in range(FIELDS):
         src = rhs.at[f] if f < NRHS else (cz, cx, cy, dg)[f - NRHS]
@@ -87,10 +87,13 @@
             first = jnp.where(low, a[0:8], pltpu.roll(b[0:8], 4, 0))
             last = jnp.where(low, pltpu.roll(a[NX - 8 : NX], 4, 0), b[NX - 8 : NX])
             if swap:
-                xmsgs[0][f, m] = jnp.where(up, last, first)
+                xrows[0, f, m] = jnp.where(up, last, first)
             else:
-                xmsgs[0][f, m] = first
-                xmsgs[1][f, m] = last
+                xrows[0, f, m] = first
+                xrows[1, f, m] = last
+        for n, xmsg in enumerate(xmsgs):
+            planes.append(pltpu.make_async_copy(xrows.at[n, f], xmsg.at[f], xsaves.at[n, f]))
+            planes[-1].start()
     for copy in planes:
         copy.wait()
 
@@ -224,10 +227,10 @@
 
 
 def gram_of(messages):
-    total = messages[0]
-    for n in range(1, messages.shape[0]):
-        total = total + messages[n]
-    total = jnp.concatenate([total] * 4, 0)
+    parts = [messages[n] for n in range(messages.shape[0])]
+    while len(parts) > 1:
+        parts = [sum(parts[n : n + 2][1:], parts[n]) for n in range(0, len(parts), 2)]
+    total = jnp.concatenate(parts * 4, 0)
     rows, lanes = row_ids((8, 128)), lane_ids((8, 128))
     tile = total
     for q in range(1, 4):
@@ -624,7 +627,9 @@
     scales = [1.0 / jnp.sqrt(p) for p in pivots]
     factor = jnp.zeros((24, 128), F32)
     for c in range(COLS):
-        table[c] = jnp.concatenate([inverse[c][k] * scales[k] for k in tiles], 0)
+        scaled = [inverse[c][k] * scales[k] for k in tiles]
+        for i in range(c, COLS):
+            table[c, i] = row_of(scaled, i)
         factor = jnp.where(lanes == c, jnp.concatenate(columns[c], 0), factor)
     return jnp.where((rows <= lanes) & (rows < COLS), factor * jnp.concatenate(scales, 0), 0.0)
 
@@ -639,7 +644,7 @@
             value = [read(j, p) for p in range(pieces)]
             for i in mine:
                 if j <= i:
-                    weight = jnp.broadcast_to(table[j, i : i + 1, :], (8, 128))
+                    weight = table[j, i]
                     terms = [weight * v for v in value]
                     sums[i] = terms if sums[i] is None else [s + t for s, t in zip(sums[i], terms)]
         for i in mine:
@@ -754,11 +759,13 @@
         functools.partial(pack_faces, swap),
         out_shape=(face_shape, face_shape) + (x_shape,) * (1 if swap else 2),
         in_specs=[smem()] * 2 + [hbm()] * 5,
-        out_specs=(hbm(), hbm()) + (vmem(),) * (1 if swap else 2),
+        out_specs=(hbm(), hbm()) + (hbm(),) * (1 if swap else 2),
         scratch_shapes=[
+            pltpu.VMEM((1 if swap else 2,) + x_shape.shape, F32),
             pltpu.VMEM((FIELDS, NZ, NX, NY), F32),
             pltpu.SemaphoreType.DMA((FIELDS,)),
             pltpu.SemaphoreType.DMA((2 * FIELDS,)),
+            pltpu.SemaphoreType.DMA((1 if swap else 2, FIELDS)),
         ],
         compiler_params=params(LIMIT),
         cost_estimate=cost(2.5),
@@ -846,7 +853,7 @@
         scratch_shapes=[
             pltpu.VMEM(block.shape, F32),
             pltpu.VMEM(block.shape, F32),
-            pltpu.VMEM((COLS, 24, 128), F32),
+            pltpu.VMEM((COLS, COLS, 8, 128), F32),
             pltpu.VMEM((2, STACK, STACK), F32),
             pltpu.SemaphoreType.DMA((NZ,)),
             pltpu.SemaphoreType.DMA((NZ,)),
@@ -863,7 +870,7 @@
         scratch_shapes=[
             pltpu.VMEM(block.shape, F32),
             pltpu.VMEM((COLS, NZ, NX, NY), F32),
-            pltpu.VMEM((COLS, 24, 128), F32),
+            pltpu.VMEM((COLS, COLS, 8, 128), F32),
             pltpu.SemaphoreType.DMA((NZ,)),
             pltpu.SemaphoreType.DMA((NZ,)),
         ],

time: 88.3 us -> 89.4 us (1.012)
  Pallas kernels: 45.8 us -> 46.9 us
    pallas_call x1, Pallas kernels: 7.37 us -> 9 us  [body(): pl.pallas_call(functools.partial(second_pass, cells), out_shape=(shape(CO...]
where the time goes in v13:
time: 89.4 us; the launch traced here: 88.9 us
  Pallas kernels  46.9 us (52%)
  blocking collectives  23.2 us (26%)
  starting transfers between devices  12.2 us (14%)
  waiting for transfers between devices  4.24 us (5%)
  other arithmetic  1.56 us (2%)
    all_to_all x2, blocking collectives, exchange(): return lax.all_to_all(messages, AXES, 0, 0, tiled=True)  23.2 us
    pallas_call x1, Pallas kernels, body(): pl.pallas_call(functools.partial(krylov_outer, swap), out_shape=(block, s...  15.6 us
    pallas_call x1, Pallas kernels, body(): pl.pallas_call(functools.partial(first_pass, cells), out_shape=(block, sh...  9.4 us
    ppermute x6, starting transfers between devices, swap_pairs(): return lax.ppermute(value, axis, pairs + [(j, i) for i, j in pairs])  9.21 us
    pallas_call x1, Pallas kernels, body(): pl.pallas_call(functools.partial(second_pass, cells), out_shape=(shape(CO...  9 us
    pallas_call x1, Pallas kernels, body(): pl.pallas_call(functools.partial(krylov_inner, swap), out_shape=(inner_sh...  7.42 us
    ppermute x6, waiting for transfers between devices, swap_pairs(): return lax.ppermute(value, axis, pairs + [(j, i) for i, j in pairs])  3.66 us
    ppermute x1, starting transfers between devices, body(): x_parts = (lax.ppermute(xmsgs[0], 'gx', [(0, 1), (1, 0)]),)  3.03 us
  transfers between devices with their start and end apart: 7, of which 2 were waited for; matrix products, arithmetic and copies ran while one was open for 2% of the time, Pallas kernels for 12%

profile of v13, /device:TPU:0, one launch (start us, length us, event | category | flops | bytes accessed | tf_op | source)
XLA Modules:
  0.0 88.9 jit_solution(9473412400125822847)
XLA Ops:
  0.6 2.6 %shard_map.68 = (f32[29,32,256]{2,1,0:T(8,128)}, f32[29,32,256]{2,1,0:T(8,128)}, f32[8,4,8,256]{3,2,1,0:T(8,128)}) custom-call(s32[1]{0:T(128)} %bitcast.place, s32[1]{0:T(128)} %bitcast.1.odd_z, f32[4,8,32,256]{3,2,1,0:T(8,128)} %rhs.5, f32[8,32,256]{2,1,0:T(8,128)} %cz.5, f32[8,32,256]{2,1,0:T(8,128)} %cx.5, f32[8,32,256]{2,1,0:T(8,128)} %cy.5, ...), custom_call_target="tpu_custom_call" | custom-call | bytes 9000000 | tf_op jit(solution)/shard_map/pallas_call | solution.py:758
  3.2 3.0 %collective-permute-start.2 = (f32[8,4,8,256]{3,2,1,0:T(8,128)}, f32[8,4,8,256]{3,2,1,0:T(8,128)S(1)}, u32[]{:S(2)}, u32[]{:S(2)}) collective-permute-start(f32[8,4,8,256]{3,2,1,0:T(8,128)} %get-tuple-element.18), channel_id=1, source_target_pairs={{0,16},{16,0},{1,17},{17,1},{2,18},{18,2},{3,19},{19,3},{4,20},{20... | collective-permute-start | bytes 786440 | tf_op jit(solution)/shard_map/ppermute | solution.py:775
  6.2 1.6 %collective-permute-start = (f32[29,32,256]{2,1,0:T(8,128)}, f32[29,32,256]{2,1,0:T(8,128)}, u32[]{:S(2)}, u32[]{:S(2)}) collective-permute-start(f32[29,32,256]{2,1,0:T(8,128)} %get-tuple-element.16), channel_id=1, source_target_pairs={{0,1},{2,3},{1,0},{3,2},{4,5},{6,7},{5,4},{7,6},{8,9},{10,11},{9,8... | collective-permute-start | bytes 2850824 | tf_op jit(solution)/shard_map/ppermute | solution.py:739
  7.8 1.6 %collective-permute-start.1 = (f32[29,32,256]{2,1,0:T(8,128)}, f32[29,32,256]{2,1,0:T(8,128)}, u32[]{:S(2)}, u32[]{:S(2)}) collective-permute-start(f32[29,32,256]{2,1,0:T(8,128)} %get-tuple-element.17), channel_id=1, source_target_pairs={{1,2},{2,1},{5,6},{6,5},{9,10},{10,9},{13,14},{14,13},{17,18},{18,... | collective-permute-start | bytes 2850824 | tf_op jit(solution)/shard_map/ppermute | solution.py:739
  9.4 2.7 %shard_map.69 = (f32[32,256]{1,0:T(8,128)}, f32[32,256]{1,0:T(8,128)}) custom-call(s32[1]{0:T(128)} %bitcast.2.odd_y, f32[4,8,32,256]{3,2,1,0:T(8,128)} %rhs.5, f32[8,32,256]{2,1,0:T(8,128)} %cz.5, f32[8,32,256]{2,1,0:T(8,128)} %cx.5, f32[8,32,256]{2,1,0:T(8,128)} %cy.5, f32[8,32,256]{2,1,0:T(8,128)} %dg.5), custom_call_target="tpu_custom_call" | custom-call | bytes 9000000 | tf_op jit(solution)/shard_map/pallas_call | solution.py:780
  12.2 0.6 collective-permute-done.2.refs_0_.rest_0_
  12.7 0.0 copy-start
  12.7 0.2 shard_map.70
  13.0 0.8 pad_maximum_fusion.1
  13.7 0.0 collective-permute-start.4
  13.7 0.8 pad_maximum_fusion
  14.5 0.7 collective-permute-start.3
  15.2 0.0 collective-permute-done.4
  15.2 0.0 collective-permute-done.3
  15.3 0.0 copy-start.1
  15.3 0.0 copy-start.2
  15.3 0.7 collective-permute-start.6
  16.0 4.7 %collective-permute-start.5 = (f32[128,256]{1,0:T(8,128)S(1)}, f32[128,256]{1,0:T(8,128)S(1)}, u32[]{:S(2)}, u32[]{:S(2)}) collective-permute-start(f32[128,256]{1,0:T(8,128)S(1)} %get-tuple-element.31), channel_id=1, source_target_pairs={{0,1},{2,3},{1,0},{3,2},{4,5},{6,7},{5,4},{7,6},{8,9},{10,11},{9,8... | collective-permute-start | bytes 393224 | tf_op jit(solution)/shard_map/ppermute | solution.py:739
  20.7 0.0 copy-done
  20.7 0.0 copy-done.1
  20.7 0.0 copy-done.2
  20.7 7.4 %shard_map.71 = (f32[48,8,56,128]{3,2,1,0:T(8,128)}, f32[7,6,3,40,128]{4,3,2,1,0:T(8,128)}) custom-call(s32[1]{0:T(128)} %bitcast.place, f32[4,8,32,256]{3,2,1,0:T(8,128)} %rhs.5, f32[8,32,256]{2,1,0:T(8,128)} %cz.5, f32[8,32,256]{2,1,0:T(8,128)} %cx.5, f32[8,32,256]{2,1,0:T(8,128)} %cy.5, f32[8,32,256]{2,1,0:T(8,128)} %dg.5, f32[8,4,8,256]{3,2,1,0:T(8,128)} %copy-done, ...), custom_call_target="tpu_custom_call" | custom-call | bytes 25200000 | tf_op jit(solution)/shard_map/pallas_call | solution.py:813
  28.1 0.0 collective-permute-done.6.rim_two
  28.1 3.6 %collective-permute-done.5.rim_one = f32[128,256]{1,0:T(8,128)S(1)} collective-permute-done((f32[128,256]{1,0:T(8,128)S(1)}, f32[128,256]{1,0:T(8,128)S(1)}, u32[]{:S(2)}, u32[]{:S(2)}) %collective-permute-start.5) | collective-permute-done | bytes 131104 | tf_op jit(solution)/shard_map/ppermute | solution.py:739
  31.8 0.0 collective-permute-done.face_one
  31.8 0.0 collective-permute-done.1.face_two
  31.8 15.6 %shard_map.72 = (f32[40,8,32,128]{3,2,1,0:T(8,128)}, f32[32,2,128]{2,1,0:T(2,128)S(1)}) custom-call(f32[29,32,256]{2,1,0:T(8,128)} %collective-permute-done.face_one, f32[29,32,256]{2,1,0:T(8,128)} %collective-permute-done.1.face_two, s32[1]{0:T(128)} %bitcast.place, s32[1]{0:T(128)} %bitcast.1.odd_z, f32[48,8,56,128]{3,2,1,0:T(8,128)} %get-tuple-element.23.inner, ...), custom_call_target="tpu_custom_call" | custom-call | bytes 54000000 | tf_op jit(solution)/shard_map/pallas_call | solution.py:829
  47.4 14.2 %all_to_all.10.message = f32[32,2,128]{2,1,0:T(2,128)S(1)} all-to-all(f32[32,2,128]{2,1,0:T(2,128)S(1)} %get-tuple-element.25), channel_id=1, replica_groups=mesh['gx'=2,'gy'=4,'gz'=4] {'gx','gy','gz'}, dimensions={0} | all-to-all | bytes 65536 | tf_op jit(solution)/shard_map/all_to_all | solution.py:743
  61.5 9.4 %shard_map.73 = (f32[40,8,32,128]{3,2,1,0:T(8,128)}, f32[32,2,128]{2,1,0:T(2,128)S(1)}, f32[24,128]{1,0:T(8,128)S(1)}) custom-call(f32[32,2,128]{2,1,0:T(2,128)S(1)} %all_to_all.10.message, f32[40,8,32,128]{3,2,1,0:T(8,128)} %get-tuple-element.26.basis_hbm), custom_call_target="tpu_custom_call" | custom-call | tf_op jit(solution)/shard_map/pallas_call | solution.py:848
  70.9 9.0 %all_to_all.11.message = f32[32,2,128]{2,1,0:T(2,128)S(1)} all-to-all(f32[32,2,128]{2,1,0:T(2,128)S(1)} %get-tuple-element.27), channel_id=1, replica_groups=mesh['gx'=2,'gy'=4,'gz'=4] {'gx','gy','gz'}, dimensions={0} | all-to-all | bytes 65536 | tf_op jit(solution)/shard_map/all_to_all | solution.py:743
  79.9 9.0 %shard_map.74 = (f32[20,8,32,256]{3,2,1,0:T(8,128)}, f32[20,20]{1,0:T(8,128)}) custom-call(f32[32,2,128]{2,1,0:T(2,128)S(1)} %all_to_all.11.message, f32[24,128]{1,0:T(8,128)S(1)} %get-tuple-element.28.factor_one, f32[40,8,32,128]{3,2,1,0:T(8,128)} %get-tuple-element.29.first_hbm), custom_call_target="tpu_custom_call" | custom-call | tf_op jit(solution)/shard_map/pallas_call | solution.py:865
  (7 shorter events, 0.1 us)
Async XLA Ops:
  3.2 9.5 %collective-permute-start.2 = (f32[8,4,8,256]{3,2,1,0:T(8,128)}, f32[8,4,8,256]{3,2,1,0:T(8,128)S(1)}, u32[]{:S(2)}, u32[]{:S(2)}) collective-permute-start(f32[8,4,8,256]{3,2,1,0:T(8,128)} %get-tuple-element.18), channel_id=1, source_target_pairs={{0,16},{16,0},{1,17},{17,1},{2,18},{18,2},{3,19},{19,3},{4,20},{20... | collective-permute-start | bytes 786440 | tf_op jit(solution)/shard_map/ppermute | solution.py:775
  6.2 25.5 %collective-permute-start = (f32[29,32,256]{2,1,0:T(8,128)}, f32[29,32,256]{2,1,0:T(8,128)}, u32[]{:S(2)}, u32[]{:S(2)}) collective-permute-start(f32[29,32,256]{2,1,0:T(8,128)} %get-tuple-element.16), channel_id=1, source_target_pairs={{0,1},{2,3},{1,0},{3,2},{4,5},{6,7},{5,4},{7,6},{8,9},{10,11},{9,8... | collective-permute-start | bytes 2850824 | tf_op jit(solution)/shard_map/ppermute | solution.py:739
  7.8 24.0 %collective-permute-start.1 = (f32[29,32,256]{2,1,0:T(8,128)}, f32[29,32,256]{2,1,0:T(8,128)}, u32[]{:S(2)}, u32[]{:S(2)}) collective-permute-start(f32[29,32,256]{2,1,0:T(8,128)} %get-tuple-element.17), channel_id=1, source_target_pairs={{1,2},{2,1},{5,6},{6,5},{9,10},{10,9},{13,14},{14,13},{17,18},{18,... | collective-permute-start | bytes 2850824 | tf_op jit(solution)/shard_map/ppermute | solution.py:739
  12.7 7.9 %copy-start = (f32[8,4,8,256]{3,2,1,0:T(8,128)}, f32[8,4,8,256]{3,2,1,0:T(8,128)S(1)}, u32[]{:S(2)}) copy-start(f32[8,4,8,256]{3,2,1,0:T(8,128)S(1)} %collective-permute-done.2.refs_0_.rest_0_) | copy-start | bytes 786436
  13.7 1.5 %collective-permute-start.4 = (f32[40,256]{1,0:T(8,128)S(1)}, f32[40,256]{1,0:T(8,128)S(1)}, u32[]{:S(2)}, u32[]{:S(2)}) collective-permute-start(f32[40,256]{1,0:T(8,128)S(1)} %pad_maximum_fusion.1), channel_id=1, source_target_pairs={{0,4},{8,12},{4,0},{12,8},{1,5},{9,13},{5,1},{13,9},{2,6},{10,14},... | collective-permute-start | bytes 122888 | tf_op jit(solution)/shard_map/ppermute | solution.py:739
  14.5 0.7 collective-permute-start.3
  15.3 5.4 %copy-start.1 = (f32[40,256]{1,0:T(8,128)}, f32[40,256]{1,0:T(8,128)S(1)}, u32[]{:S(2)}) copy-start(f32[40,256]{1,0:T(8,128)S(1)} %get-tuple-element.36.rest_2_) | copy-start | bytes 122884
  15.3 5.4 %copy-start.2 = (f32[40,256]{1,0:T(8,128)}, f32[40,256]{1,0:T(8,128)S(1)}, u32[]{:S(2)}) copy-start(f32[40,256]{1,0:T(8,128)S(1)} %get-tuple-element.37.rest_1_) | copy-start | bytes 122884
  15.3 12.8 %collective-permute-start.6 = (f32[128,256]{1,0:T(8,128)S(1)}, f32[128,256]{1,0:T(8,128)S(1)}, u32[]{:S(2)}, u32[]{:S(2)}) collective-permute-start(f32[128,256]{1,0:T(8,128)S(1)} %get-tuple-element.30), channel_id=1, source_target_pairs={{1,2},{2,1},{5,6},{6,5},{9,10},{10,9},{13,14},{14,13},{17,18},{18,... | collective-permute-start | bytes 393224 | tf_op jit(solution)/shard_map/ppermute | solution.py:739
  16.0 15.8 %collective-permute-start.5 = (f32[128,256]{1,0:T(8,128)S(1)}, f32[128,256]{1,0:T(8,128)S(1)}, u32[]{:S(2)}, u32[]{:S(2)}) collective-permute-start(f32[128,256]{1,0:T(8,128)S(1)} %get-tuple-element.31), channel_id=1, source_target_pairs={{0,1},{2,3},{1,0},{3,2},{4,5},{6,7},{5,4},{7,6},{8,9},{10,11},{9,8... | collective-permute-start | bytes 393224 | tf_op jit(solution)/shard_map/ppermute | solution.py:739

commit v14 on v13

--- a/solution.py
+++ b/solution.py
@@ -627,16 +627,14 @@
     scales = [1.0 / jnp.sqrt(p) for p in pivots]
     factor = jnp.zeros((24, 128), F32)
     for c in range(COLS):
-        scaled = [inverse[c][k] * scales[k] for k in tiles]
-        for i in range(c, COLS):
-            table[c, i] = row_of(scaled, i)
+        table[c] = jnp.concatenate([inverse[c][k] * scales[k] for k in tiles], 0)
         factor = jnp.where(lanes == c, jnp.concatenate(columns[c], 0), factor)
     return jnp.where((rows <= lanes) & (rows < COLS), factor * jnp.concatenate(scales, 0), 0.0)
 
 
 def apply_rows(table, read, write):
     group = 5
-    pieces = NX // 8
+    pieces = NX // 4
     for g in reversed(range(COLS // group)):
         mine = range(group * g, group * g + group)
         sums = {i: None for i in mine}
@@ -644,7 +642,7 @@
             value = [read(j, p) for p in range(pieces)]
             for i in mine:
                 if j <= i:
-                    weight = table[j, i]
+                    weight = jnp.broadcast_to(table[j, i : i + 1, :], (8, 128))
                     terms = [weight * v for v in value]
                     sums[i] = terms if sums[i] is None else [s + t for s, t in zip(sums[i], terms)]
         for i in mine:
@@ -671,15 +669,15 @@
         gram_add([jnp.concatenate([tile(i, t) for i in range(COLS)], 0) for t in range(NX // 8)], accs)
 
     def apply(z):
-        for l in range(2):
-
-            def read(j, p):
-                return basis[2 * j + l, z, 8 * p : 8 * p + 8, :]
-
-            def write(i, p, value):
-                first[2 * i + l, z, 8 * p : 8 * p + 8, :] = value
-
-            apply_rows(table, read, write)
+        def read(j, n):
+            l, p = n % 2, n // 2
+            return basis[2 * j + l, z, 8 * p : 8 * p + 8, :]
+
+        def write(i, n, value):
+            l, p = n % 2, n // 2
+            first[2 * i + l, z, 8 * p : 8 * p + 8, :] = value
+
+        apply_rows(table, read, write)
         plane_copy(first, first_hbm, saves, z).start()
 
     def both(z):
@@ -707,15 +705,16 @@
 
     def chunk(z, carry):
         plane_copy(first_hbm, first, loads, z).wait()
-        for l in range(2):
-
-            def read(j, p):
-                return first[2 * j + l, z, 8 * p : 8 * p + 8, :]
-
-            def write(i, p, value):
-                out[i, z, 8 * p : 8 * p + 8, 128 * l : 128 * l + 128] = value
-
-            apply_rows(table, read, write)
+
+        def read(j, n):
+            l, p = n % 2, n // 2
+            return first[2 * j + l, z, 8 * p : 8 * p + 8, :]
+
+        def write(i, n, value):
+            l, p = n % 2, n // 2
+            out[i, z, 8 * p : 8 * p + 8, 128 * l : 128 * l + 128] = value
+
+        apply_rows(table, read, write)
         plane_copy(out, out_hbm, saves, z).start()
         return carry
 
@@ -853,7 +852,7 @@
         scratch_shapes=[
             pltpu.VMEM(block.shape, F32),
             pltpu.VMEM(block.shape, F32),
-            pltpu.VMEM((COLS, COLS, 8, 128), F32),
+            pltpu.VMEM((COLS, 24, 128), F32),
             pltpu.VMEM((2, STACK, STACK), F32),
             pltpu.SemaphoreType.DMA((NZ,)),
             pltpu.SemaphoreType.DMA((NZ,)),
@@ -870,7 +869,7 @@
         scratch_shapes=[
             pltpu.VMEM(block.shape, F32),
             pltpu.VMEM((COLS, NZ, NX, NY), F32),
-            pltpu.VMEM((COLS, COLS, 8, 128), F32),
+            pltpu.VMEM((COLS, 24, 128), F32),
             pltpu.SemaphoreType.DMA((NZ,)),
             pltpu.SemaphoreType.DMA((NZ,)),
         ],

time: 89.4 us -> 88.5 us (0.990)
  Pallas kernels: 46.9 us -> 46 us
    pallas_call x1, Pallas kernels: 9 us -> 7.98 us  [body(): pl.pallas_call(functools.partial(second_pass, cells), out_shape=(shape(CO...]
where the time goes in v14:
time: 88.5 us; the launch traced here: 88 us
  Pallas kernels  46 us (52%)
  blocking collectives  23.2 us (26%)
  starting transfers between devices  12.2 us (14%)
  waiting for transfers between devices  4.24 us (5%)
  other arithmetic  1.56 us (2%)
    all_to_all x2, blocking collectives, exchange(): return lax.all_to_all(messages, AXES, 0, 0, tiled=True)  23.2 us
    pallas_call x1, Pallas kernels, body(): pl.pallas_call(functools.partial(krylov_outer, swap), out_shape=(block, s...  15.6 us
    pallas_call x1, Pallas kernels, body(): pl.pallas_call(functools.partial(first_pass, cells), out_shape=(block, sh...  9.51 us
    ppermute x6, starting transfers between devices, swap_pairs(): return lax.ppermute(value, axis, pairs + [(j, i) for i, j in pairs])  9.21 us
    pallas_call x1, Pallas kernels, body(): pl.pallas_call(functools.partial(second_pass, cells), out_shape=(shape(CO...  7.98 us
    pallas_call x1, Pallas kernels, body(): pl.pallas_call(functools.partial(krylov_inner, swap), out_shape=(inner_sh...  7.42 us
    ppermute x6, waiting for transfers between devices, swap_pairs(): return lax.ppermute(value, axis, pairs + [(j, i) for i, j in pairs])  3.66 us
    ppermute x1, starting transfers between devices, body(): x_parts = (lax.ppermute(xmsgs[0], 'gx', [(0, 1), (1, 0)]),)  3.03 us
  transfers between devices with their start and end apart: 7, of which 2 were waited for; matrix products, arithmetic and copies ran while one was open for 2% of the time, Pallas kernels for 12%

profile of v14, /device:TPU:0, one launch (start us, length us, event | category | flops | bytes accessed | tf_op | source)
XLA Modules:
  0.0 88.0 jit_solution(6104509085730981233)
XLA Ops:
  0.6 2.6 %shard_map.68 = (f32[29,32,256]{2,1,0:T(8,128)}, f32[29,32,256]{2,1,0:T(8,128)}, f32[8,4,8,256]{3,2,1,0:T(8,128)}) custom-call(s32[1]{0:T(128)} %bitcast.place, s32[1]{0:T(128)} %bitcast.1.odd_z, f32[4,8,32,256]{3,2,1,0:T(8,128)} %rhs.5, f32[8,32,256]{2,1,0:T(8,128)} %cz.5, f32[8,32,256]{2,1,0:T(8,128)} %cx.5, f32[8,32,256]{2,1,0:T(8,128)} %cy.5, ...), custom_call_target="tpu_custom_call" | custom-call | bytes 9000000 | tf_op jit(solution)/shard_map/pallas_call | solution.py:757
  3.2 3.0 %collective-permute-start.2 = (f32[8,4,8,256]{3,2,1,0:T(8,128)}, f32[8,4,8,256]{3,2,1,0:T(8,128)S(1)}, u32[]{:S(2)}, u32[]{:S(2)}) collective-permute-start(f32[8,4,8,256]{3,2,1,0:T(8,128)} %get-tuple-element.18), channel_id=1, source_target_pairs={{0,16},{16,0},{1,17},{17,1},{2,18},{18,2},{3,19},{19,3},{4,20},{20... | collective-permute-start | bytes 786440 | tf_op jit(solution)/shard_map/ppermute | solution.py:774
  6.2 1.6 %collective-permute-start = (f32[29,32,256]{2,1,0:T(8,128)}, f32[29,32,256]{2,1,0:T(8,128)}, u32[]{:S(2)}, u32[]{:S(2)}) collective-permute-start(f32[29,32,256]{2,1,0:T(8,128)} %get-tuple-element.16), channel_id=1, source_target_pairs={{0,1},{2,3},{1,0},{3,2},{4,5},{6,7},{5,4},{7,6},{8,9},{10,11},{9,8... | collective-permute-start | bytes 2850824 | tf_op jit(solution)/shard_map/ppermute | solution.py:738
  7.8 1.6 %collective-permute-start.1 = (f32[29,32,256]{2,1,0:T(8,128)}, f32[29,32,256]{2,1,0:T(8,128)}, u32[]{:S(2)}, u32[]{:S(2)}) collective-permute-start(f32[29,32,256]{2,1,0:T(8,128)} %get-tuple-element.17), channel_id=1, source_target_pairs={{1,2},{2,1},{5,6},{6,5},{9,10},{10,9},{13,14},{14,13},{17,18},{18,... | collective-permute-start | bytes 2850824 | tf_op jit(solution)/shard_map/ppermute | solution.py:738
  9.4 2.7 %shard_map.69 = (f32[32,256]{1,0:T(8,128)}, f32[32,256]{1,0:T(8,128)}) custom-call(s32[1]{0:T(128)} %bitcast.2.odd_y, f32[4,8,32,256]{3,2,1,0:T(8,128)} %rhs.5, f32[8,32,256]{2,1,0:T(8,128)} %cz.5, f32[8,32,256]{2,1,0:T(8,128)} %cx.5, f32[8,32,256]{2,1,0:T(8,128)} %cy.5, f32[8,32,256]{2,1,0:T(8,128)} %dg.5), custom_call_target="tpu_custom_call" | custom-call | bytes 9000000 | tf_op jit(solution)/shard_map/pallas_call | solution.py:779
  12.2 0.6 collective-permute-done.2.refs_0_.rest_0_
  12.7 0.0 copy-start
  12.7 0.2 shard_map.70
  13.0 0.8 pad_maximum_fusion.1
  13.7 0.0 collective-permute-start.4
  13.7 0.8 pad_maximum_fusion
  14.5 0.7 collective-permute-start.3
  15.2 0.0 collective-permute-done.4
  15.2 0.0 collective-permute-done.3
  15.3 0.0 copy-start.1
  15.3 0.0 copy-start.2
  15.3 0.7 collective-permute-start.6
  16.0 4.7 %collective-permute-start.5 = (f32[128,256]{1,0:T(8,128)S(1)}, f32[128,256]{1,0:T(8,128)S(1)}, u32[]{:S(2)}, u32[]{:S(2)}) collective-permute-start(f32[128,256]{1,0:T(8,128)S(1)} %get-tuple-element.31), channel_id=1, source_target_pairs={{0,1},{2,3},{1,0},{3,2},{4,5},{6,7},{5,4},{7,6},{8,9},{10,11},{9,8... | collective-permute-start | bytes 393224 | tf_op jit(solution)/shard_map/ppermute | solution.py:738
  20.7 0.0 copy-done
  20.7 0.0 copy-done.1
  20.7 0.0 copy-done.2
  20.7 7.4 %shard_map.71 = (f32[48,8,56,128]{3,2,1,0:T(8,128)}, f32[7,6,3,40,128]{4,3,2,1,0:T(8,128)}) custom-call(s32[1]{0:T(128)} %bitcast.place, f32[4,8,32,256]{3,2,1,0:T(8,128)} %rhs.5, f32[8,32,256]{2,1,0:T(8,128)} %cz.5, f32[8,32,256]{2,1,0:T(8,128)} %cx.5, f32[8,32,256]{2,1,0:T(8,128)} %cy.5, f32[8,32,256]{2,1,0:T(8,128)} %dg.5, f32[8,4,8,256]{3,2,1,0:T(8,128)} %copy-done, ...), custom_call_target="tpu_custom_call" | custom-call | bytes 25200000 | tf_op jit(solution)/shard_map/pallas_call | solution.py:812
  28.1 0.0 collective-permute-done.6.rim_two
  28.1 3.6 %collective-permute-done.5.rim_one = f32[128,256]{1,0:T(8,128)S(1)} collective-permute-done((f32[128,256]{1,0:T(8,128)S(1)}, f32[128,256]{1,0:T(8,128)S(1)}, u32[]{:S(2)}, u32[]{:S(2)}) %collective-permute-start.5) | collective-permute-done | bytes 131104 | tf_op jit(solution)/shard_map/ppermute | solution.py:738
  31.8 0.0 collective-permute-done.face_one
  31.8 0.0 collective-permute-done.1.face_two
  31.8 15.6 %shard_map.72 = (f32[40,8,32,128]{3,2,1,0:T(8,128)}, f32[32,2,128]{2,1,0:T(2,128)S(1)}) custom-call(f32[29,32,256]{2,1,0:T(8,128)} %collective-permute-done.face_one, f32[29,32,256]{2,1,0:T(8,128)} %collective-permute-done.1.face_two, s32[1]{0:T(128)} %bitcast.place, s32[1]{0:T(128)} %bitcast.1.odd_z, f32[48,8,56,128]{3,2,1,0:T(8,128)} %get-tuple-element.23.inner, ...), custom_call_target="tpu_custom_call" | custom-call | bytes 54000000 | tf_op jit(solution)/shard_map/pallas_call | solution.py:828
  47.4 14.2 %all_to_all.10.message = f32[32,2,128]{2,1,0:T(2,128)S(1)} all-to-all(f32[32,2,128]{2,1,0:T(2,128)S(1)} %get-tuple-element.25), channel_id=1, replica_groups=mesh['gx'=2,'gy'=4,'gz'=4] {'gx','gy','gz'}, dimensions={0} | all-to-all | bytes 65536 | tf_op jit(solution)/shard_map/all_to_all | solution.py:742
  61.5 9.5 %shard_map.73 = (f32[40,8,32,128]{3,2,1,0:T(8,128)}, f32[32,2,128]{2,1,0:T(2,128)S(1)}, f32[24,128]{1,0:T(8,128)S(1)}) custom-call(f32[32,2,128]{2,1,0:T(2,128)S(1)} %all_to_all.10.message, f32[40,8,32,128]{3,2,1,0:T(8,128)} %get-tuple-element.26.basis_hbm), custom_call_target="tpu_custom_call" | custom-call | tf_op jit(solution)/shard_map/pallas_call | solution.py:847
  71.0 9.0 %all_to_all.11.message = f32[32,2,128]{2,1,0:T(2,128)S(1)} all-to-all(f32[32,2,128]{2,1,0:T(2,128)S(1)} %get-tuple-element.27), channel_id=1, replica_groups=mesh['gx'=2,'gy'=4,'gz'=4] {'gx','gy','gz'}, dimensions={0} | all-to-all | bytes 65536 | tf_op jit(solution)/shard_map/all_to_all | solution.py:742
  80.0 8.0 %shard_map.74 = (f32[20,8,32,256]{3,2,1,0:T(8,128)}, f32[20,20]{1,0:T(8,128)}) custom-call(f32[32,2,128]{2,1,0:T(2,128)S(1)} %all_to_all.11.message, f32[24,128]{1,0:T(8,128)S(1)} %get-tuple-element.28.factor_one, f32[40,8,32,128]{3,2,1,0:T(8,128)} %get-tuple-element.29.first_hbm), custom_call_target="tpu_custom_call" | custom-call | tf_op jit(solution)/shard_map/pallas_call | solution.py:864
  (7 shorter events, 0.1 us)
Async XLA Ops:
  3.2 9.5 %collective-permute-start.2 = (f32[8,4,8,256]{3,2,1,0:T(8,128)}, f32[8,4,8,256]{3,2,1,0:T(8,128)S(1)}, u32[]{:S(2)}, u32[]{:S(2)}) collective-permute-start(f32[8,4,8,256]{3,2,1,0:T(8,128)} %get-tuple-element.18), channel_id=1, source_target_pairs={{0,16},{16,0},{1,17},{17,1},{2,18},{18,2},{3,19},{19,3},{4,20},{20... | collective-permute-start | bytes 786440 | tf_op jit(solution)/shard_map/ppermute | solution.py:774
  6.2 25.5 %collective-permute-start = (f32[29,32,256]{2,1,0:T(8,128)}, f32[29,32,256]{2,1,0:T(8,128)}, u32[]{:S(2)}, u32[]{:S(2)}) collective-permute-start(f32[29,32,256]{2,1,0:T(8,128)} %get-tuple-element.16), channel_id=1, source_target_pairs={{0,1},{2,3},{1,0},{3,2},{4,5},{6,7},{5,4},{7,6},{8,9},{10,11},{9,8... | collective-permute-start | bytes 2850824 | tf_op jit(solution)/shard_map/ppermute | solution.py:738
  7.8 24.0 %collective-permute-start.1 = (f32[29,32,256]{2,1,0:T(8,128)}, f32[29,32,256]{2,1,0:T(8,128)}, u32[]{:S(2)}, u32[]{:S(2)}) collective-permute-start(f32[29,32,256]{2,1,0:T(8,128)} %get-tuple-element.17), channel_id=1, source_target_pairs={{1,2},{2,1},{5,6},{6,5},{9,10},{10,9},{13,14},{14,13},{17,18},{18,... | collective-permute-start | bytes 2850824 | tf_op jit(solution)/shard_map/ppermute | solution.py:738
  12.7 7.9 %copy-start = (f32[8,4,8,256]{3,2,1,0:T(8,128)}, f32[8,4,8,256]{3,2,1,0:T(8,128)S(1)}, u32[]{:S(2)}) copy-start(f32[8,4,8,256]{3,2,1,0:T(8,128)S(1)} %collective-permute-done.2.refs_0_.rest_0_) | copy-start | bytes 786436
  13.7 1.5 %collective-permute-start.4 = (f32[40,256]{1,0:T(8,128)S(1)}, f32[40,256]{1,0:T(8,128)S(1)}, u32[]{:S(2)}, u32[]{:S(2)}) collective-permute-start(f32[40,256]{1,0:T(8,128)S(1)} %pad_maximum_fusion.1), channel_id=1, source_target_pairs={{0,4},{8,12},{4,0},{12,8},{1,5},{9,13},{5,1},{13,9},{2,6},{10,14},... | collective-permute-start | bytes 122888 | tf_op jit(solution)/shard_map/ppermute | solution.py:738
  14.5 0.7 collective-permute-start.3
  15.3 5.4 %copy-start.1 = (f32[40,256]{1,0:T(8,128)}, f32[40,256]{1,0:T(8,128)S(1)}, u32[]{:S(2)}) copy-start(f32[40,256]{1,0:T(8,128)S(1)} %get-tuple-element.36.rest_2_) | copy-start | bytes 122884
  15.3 5.4 %copy-start.2 = (f32[40,256]{1,0:T(8,128)}, f32[40,256]{1,0:T(8,128)S(1)}, u32[]{:S(2)}) copy-start(f32[40,256]{1,0:T(8,128)S(1)} %get-tuple-element.37.rest_1_) | copy-start | bytes 122884
  15.3 12.8 %collective-permute-start.6 = (f32[128,256]{1,0:T(8,128)S(1)}, f32[128,256]{1,0:T(8,128)S(1)}, u32[]{:S(2)}, u32[]{:S(2)}) collective-permute-start(f32[128,256]{1,0:T(8,128)S(1)} %get-tuple-element.30), channel_id=1, source_target_pairs={{1,2},{2,1},{5,6},{6,5},{9,10},{10,9},{13,14},{14,13},{17,18},{18,... | collective-permute-start | bytes 393224 | tf_op jit(solution)/shard_map/ppermute | solution.py:738
  16.0 15.8 %collective-permute-start.5 = (f32[128,256]{1,0:T(8,128)S(1)}, f32[128,256]{1,0:T(8,128)S(1)}, u32[]{:S(2)}, u32[]{:S(2)}) collective-permute-start(f32[128,256]{1,0:T(8,128)S(1)} %get-tuple-element.31), channel_id=1, source_target_pairs={{0,1},{2,3},{1,0},{3,2},{4,5},{6,7},{5,4},{7,6},{8,9},{10,11},{9,8... | collective-permute-start | bytes 393224 | tf_op jit(solution)/shard_map/ppermute | solution.py:738

commit v15 on v13

--- a/solution.py
+++ b/solution.py
@@ -627,15 +627,12 @@
     scales = [1.0 / jnp.sqrt(p) for p in pivots]
     factor = jnp.zeros((24, 128), F32)
     for c in range(COLS):
-        scaled = [inverse[c][k] * scales[k] for k in tiles]
-        for i in range(c, COLS):
-            table[c, i] = row_of(scaled, i)
+        table[c] = jnp.concatenate([inverse[c][k] * scales[k] for k in tiles], 0)
         factor = jnp.where(lanes == c, jnp.concatenate(columns[c], 0), factor)
     return jnp.where((rows <= lanes) & (rows < COLS), factor * jnp.concatenate(scales, 0), 0.0)
 
 
-def apply_rows(table, read, write):
-    group = 5
+def apply_rows(table, group, read, write):
     pieces = NX // 8
     for g in reversed(range(COLS // group)):
         mine = range(group * g, group * g + group)
@@ -644,7 +641,7 @@
             value = [read(j, p) for p in range(pieces)]
             for i in mine:
                 if j <= i:
-                    weight = table[j, i]
+                    weight = jnp.broadcast_to(table[j, i : i + 1, :], (8, 128))
                     terms = [weight * v for v in value]
                     sums[i] = terms if sums[i] is None else [s + t for s, t in zip(sums[i], terms)]
         for i in mine:
@@ -679,7 +676,7 @@
             def write(i, p, value):
                 first[2 * i + l, z, 8 * p : 8 * p + 8, :] = value
 
-            apply_rows(table, read, write)
+            apply_rows(table, 5, read, write)
         plane_copy(first, first_hbm, saves, z).start()
 
     def both(z):
@@ -715,7 +712,7 @@
             def write(i, p, value):
                 out[i, z, 8 * p : 8 * p + 8, 128 * l : 128 * l + 128] = value
 
-            apply_rows(table, read, write)
+            apply_rows(table, 4, read, write)
         plane_copy(out, out_hbm, saves, z).start()
         return carry
 
@@ -853,7 +850,7 @@
         scratch_shapes=[
             pltpu.VMEM(block.shape, F32),
             pltpu.VMEM(block.shape, F32),
-            pltpu.VMEM((COLS, COLS, 8, 128), F32),
+            pltpu.VMEM((COLS, 24, 128), F32),
             pltpu.VMEM((2, STACK, STACK), F32),
             pltpu.SemaphoreType.DMA((NZ,)),
             pltpu.SemaphoreType.DMA((NZ,)),
@@ -870,7 +867,7 @@
         scratch_shapes=[
             pltpu.VMEM(block.shape, F32),
             pltpu.VMEM((COLS, NZ, NX, NY), F32),
-            pltpu.VMEM((COLS, COLS, 8, 128), F32),
+            pltpu.VMEM((COLS, 24, 128), F32),
             pltpu.SemaphoreType.DMA((NZ,)),
             pltpu.SemaphoreType.DMA((NZ,)),
         ],

time: 89.4 us -> 87.7 us (0.981)
  Pallas kernels: 46.9 us -> 45.1 us
    pallas_call x1, Pallas kernels: 9 us -> 7.28 us  [body(): pl.pallas_call(functools.partial(second_pass, cells), out_shape=(shape(CO...]
where the time goes in v15:
time: 87.7 us; the launch traced here: 87.2 us
  Pallas kernels  45.1 us (51%)
  blocking collectives  23.2 us (26%)
  starting transfers between devices  12.2 us (14%)
  waiting for transfers between devices  4.24 us (5%)
  other arithmetic  1.56 us (2%)
    all_to_all x2, blocking collectives, exchange(): return lax.all_to_all(messages, AXES, 0, 0, tiled=True)  23.2 us
    pallas_call x1, Pallas kernels, body(): pl.pallas_call(functools.partial(krylov_outer, swap), out_shape=(block, s...  15.6 us
    pallas_call x1, Pallas kernels, body(): pl.pallas_call(functools.partial(first_pass, cells), out_shape=(block, sh...  9.37 us
    ppermute x6, starting transfers between devices, swap_pairs(): return lax.ppermute(value, axis, pairs + [(j, i) for i, j in pairs])  9.21 us
    pallas_call x1, Pallas kernels, body(): pl.pallas_call(functools.partial(krylov_inner, swap), out_shape=(inner_sh...  7.42 us
    pallas_call x1, Pallas kernels, body(): pl.pallas_call(functools.partial(second_pass, cells), out_shape=(shape(CO...  7.28 us
    ppermute x6, waiting for transfers between devices, swap_pairs(): return lax.ppermute(value, axis, pairs + [(j, i) for i, j in pairs])  3.66 us
    ppermute x1, starting transfers between devices, body(): x_parts = (lax.ppermute(xmsgs[0], 'gx', [(0, 1), (1, 0)]),)  3.03 us
  transfers between devices with their start and end apart: 7, of which 2 were waited for; matrix products, arithmetic and copies ran while one was open for 2% of the time, Pallas kernels for 12%

profile of v15, /device:TPU:0, one launch (start us, length us, event | category | flops | bytes accessed | tf_op | source)
XLA Modules:
  0.0 87.2 jit_solution(10996742376203465407)
XLA Ops:
  0.6 2.6 %shard_map.68 = (f32[29,32,256]{2,1,0:T(8,128)}, f32[29,32,256]{2,1,0:T(8,128)}, f32[8,4,8,256]{3,2,1,0:T(8,128)}) custom-call(s32[1]{0:T(128)} %bitcast.place, s32[1]{0:T(128)} %bitcast.1.odd_z, f32[4,8,32,256]{3,2,1,0:T(8,128)} %rhs.5, f32[8,32,256]{2,1,0:T(8,128)} %cz.5, f32[8,32,256]{2,1,0:T(8,128)} %cx.5, f32[8,32,256]{2,1,0:T(8,128)} %cy.5, ...), custom_call_target="tpu_custom_call" | custom-call | bytes 9000000 | tf_op jit(solution)/shard_map/pallas_call | solution.py:755
  3.2 3.0 %collective-permute-start.2 = (f32[8,4,8,256]{3,2,1,0:T(8,128)}, f32[8,4,8,256]{3,2,1,0:T(8,128)S(1)}, u32[]{:S(2)}, u32[]{:S(2)}) collective-permute-start(f32[8,4,8,256]{3,2,1,0:T(8,128)} %get-tuple-element.18), channel_id=1, source_target_pairs={{0,16},{16,0},{1,17},{17,1},{2,18},{18,2},{3,19},{19,3},{4,20},{20... | collective-permute-start | bytes 786440 | tf_op jit(solution)/shard_map/ppermute | solution.py:772
  6.2 1.6 %collective-permute-start = (f32[29,32,256]{2,1,0:T(8,128)}, f32[29,32,256]{2,1,0:T(8,128)}, u32[]{:S(2)}, u32[]{:S(2)}) collective-permute-start(f32[29,32,256]{2,1,0:T(8,128)} %get-tuple-element.16), channel_id=1, source_target_pairs={{0,1},{2,3},{1,0},{3,2},{4,5},{6,7},{5,4},{7,6},{8,9},{10,11},{9,8... | collective-permute-start | bytes 2850824 | tf_op jit(solution)/shard_map/ppermute | solution.py:736
  7.8 1.6 %collective-permute-start.1 = (f32[29,32,256]{2,1,0:T(8,128)}, f32[29,32,256]{2,1,0:T(8,128)}, u32[]{:S(2)}, u32[]{:S(2)}) collective-permute-start(f32[29,32,256]{2,1,0:T(8,128)} %get-tuple-element.17), channel_id=1, source_target_pairs={{1,2},{2,1},{5,6},{6,5},{9,10},{10,9},{13,14},{14,13},{17,18},{18,... | collective-permute-start | bytes 2850824 | tf_op jit(solution)/shard_map/ppermute | solution.py:736
  9.4 2.7 %shard_map.69 = (f32[32,256]{1,0:T(8,128)}, f32[32,256]{1,0:T(8,128)}) custom-call(s32[1]{0:T(128)} %bitcast.2.odd_y, f32[4,8,32,256]{3,2,1,0:T(8,128)} %rhs.5, f32[8,32,256]{2,1,0:T(8,128)} %cz.5, f32[8,32,256]{2,1,0:T(8,128)} %cx.5, f32[8,32,256]{2,1,0:T(8,128)} %cy.5, f32[8,32,256]{2,1,0:T(8,128)} %dg.5), custom_call_target="tpu_custom_call" | custom-call | bytes 9000000 | tf_op jit(solution)/shard_map/pallas_call | solution.py:777
  12.2 0.6 collective-permute-done.2.refs_0_.rest_0_
  12.7 0.0 copy-start
  12.7 0.2 shard_map.70
  13.0 0.8 pad_maximum_fusion.1
  13.7 0.0 collective-permute-start.4
  13.7 0.8 pad_maximum_fusion
  14.5 0.7 collective-permute-start.3
  15.2 0.0 collective-permute-done.4
  15.2 0.0 collective-permute-done.3
  15.3 0.0 copy-start.1
  15.3 0.0 copy-start.2
  15.3 0.7 collective-permute-start.6
  16.0 4.7 %collective-permute-start.5 = (f32[128,256]{1,0:T(8,128)S(1)}, f32[128,256]{1,0:T(8,128)S(1)}, u32[]{:S(2)}, u32[]{:S(2)}) collective-permute-start(f32[128,256]{1,0:T(8,128)S(1)} %get-tuple-element.31), channel_id=1, source_target_pairs={{0,1},{2,3},{1,0},{3,2},{4,5},{6,7},{5,4},{7,6},{8,9},{10,11},{9,8... | collective-permute-start | bytes 393224 | tf_op jit(solution)/shard_map/ppermute | solution.py:736
  20.7 0.0 copy-done
  20.7 0.0 copy-done.1
  20.7 0.0 copy-done.2
  20.7 7.4 %shard_map.71 = (f32[48,8,56,128]{3,2,1,0:T(8,128)}, f32[7,6,3,40,128]{4,3,2,1,0:T(8,128)}) custom-call(s32[1]{0:T(128)} %bitcast.place, f32[4,8,32,256]{3,2,1,0:T(8,128)} %rhs.5, f32[8,32,256]{2,1,0:T(8,128)} %cz.5, f32[8,32,256]{2,1,0:T(8,128)} %cx.5, f32[8,32,256]{2,1,0:T(8,128)} %cy.5, f32[8,32,256]{2,1,0:T(8,128)} %dg.5, f32[8,4,8,256]{3,2,1,0:T(8,128)} %copy-done, ...), custom_call_target="tpu_custom_call" | custom-call | bytes 25200000 | tf_op jit(solution)/shard_map/pallas_call | solution.py:810
  28.1 0.0 collective-permute-done.6.rim_two
  28.1 3.6 %collective-permute-done.5.rim_one = f32[128,256]{1,0:T(8,128)S(1)} collective-permute-done((f32[128,256]{1,0:T(8,128)S(1)}, f32[128,256]{1,0:T(8,128)S(1)}, u32[]{:S(2)}, u32[]{:S(2)}) %collective-permute-start.5) | collective-permute-done | bytes 131104 | tf_op jit(solution)/shard_map/ppermute | solution.py:736
  31.8 0.0 collective-permute-done.face_one
  31.8 0.0 collective-permute-done.1.face_two
  31.8 15.6 %shard_map.72 = (f32[40,8,32,128]{3,2,1,0:T(8,128)}, f32[32,2,128]{2,1,0:T(2,128)S(1)}) custom-call(f32[29,32,256]{2,1,0:T(8,128)} %collective-permute-done.face_one, f32[29,32,256]{2,1,0:T(8,128)} %collective-permute-done.1.face_two, s32[1]{0:T(128)} %bitcast.place, s32[1]{0:T(128)} %bitcast.1.odd_z, f32[48,8,56,128]{3,2,1,0:T(8,128)} %get-tuple-element.23.inner, ...), custom_call_target="tpu_custom_call" | custom-call | bytes 54000000 | tf_op jit(solution)/shard_map/pallas_call | solution.py:826
  47.4 14.2 %all_to_all.10.message = f32[32,2,128]{2,1,0:T(2,128)S(1)} all-to-all(f32[32,2,128]{2,1,0:T(2,128)S(1)} %get-tuple-element.25), channel_id=1, replica_groups=mesh['gx'=2,'gy'=4,'gz'=4] {'gx','gy','gz'}, dimensions={0} | all-to-all | bytes 65536 | tf_op jit(solution)/shard_map/all_to_all | solution.py:740
  61.5 9.4 %shard_map.73 = (f32[40,8,32,128]{3,2,1,0:T(8,128)}, f32[32,2,128]{2,1,0:T(2,128)S(1)}, f32[24,128]{1,0:T(8,128)S(1)}) custom-call(f32[32,2,128]{2,1,0:T(2,128)S(1)} %all_to_all.10.message, f32[40,8,32,128]{3,2,1,0:T(8,128)} %get-tuple-element.26.basis_hbm), custom_call_target="tpu_custom_call" | custom-call | tf_op jit(solution)/shard_map/pallas_call | solution.py:845
  70.9 9.0 %all_to_all.11.message = f32[32,2,128]{2,1,0:T(2,128)S(1)} all-to-all(f32[32,2,128]{2,1,0:T(2,128)S(1)} %get-tuple-element.27), channel_id=1, replica_groups=mesh['gx'=2,'gy'=4,'gz'=4] {'gx','gy','gz'}, dimensions={0} | all-to-all | bytes 65536 | tf_op jit(solution)/shard_map/all_to_all | solution.py:740
  79.9 7.3 %shard_map.74 = (f32[20,8,32,256]{3,2,1,0:T(8,128)}, f32[20,20]{1,0:T(8,128)}) custom-call(f32[32,2,128]{2,1,0:T(2,128)S(1)} %all_to_all.11.message, f32[24,128]{1,0:T(8,128)S(1)} %get-tuple-element.28.factor_one, f32[40,8,32,128]{3,2,1,0:T(8,128)} %get-tuple-element.29.first_hbm), custom_call_target="tpu_custom_call" | custom-call | tf_op jit(solution)/shard_map/pallas_call | solution.py:862
  (7 shorter events, 0.1 us)
Async XLA Ops:
  3.2 9.5 %collective-permute-start.2 = (f32[8,4,8,256]{3,2,1,0:T(8,128)}, f32[8,4,8,256]{3,2,1,0:T(8,128)S(1)}, u32[]{:S(2)}, u32[]{:S(2)}) collective-permute-start(f32[8,4,8,256]{3,2,1,0:T(8,128)} %get-tuple-element.18), channel_id=1, source_target_pairs={{0,16},{16,0},{1,17},{17,1},{2,18},{18,2},{3,19},{19,3},{4,20},{20... | collective-permute-start | bytes 786440 | tf_op jit(solution)/shard_map/ppermute | solution.py:772
  6.2 25.5 %collective-permute-start = (f32[29,32,256]{2,1,0:T(8,128)}, f32[29,32,256]{2,1,0:T(8,128)}, u32[]{:S(2)}, u32[]{:S(2)}) collective-permute-start(f32[29,32,256]{2,1,0:T(8,128)} %get-tuple-element.16), channel_id=1, source_target_pairs={{0,1},{2,3},{1,0},{3,2},{4,5},{6,7},{5,4},{7,6},{8,9},{10,11},{9,8... | collective-permute-start | bytes 2850824 | tf_op jit(solution)/shard_map/ppermute | solution.py:736
  7.8 24.0 %collective-permute-start.1 = (f32[29,32,256]{2,1,0:T(8,128)}, f32[29,32,256]{2,1,0:T(8,128)}, u32[]{:S(2)}, u32[]{:S(2)}) collective-permute-start(f32[29,32,256]{2,1,0:T(8,128)} %get-tuple-element.17), channel_id=1, source_target_pairs={{1,2},{2,1},{5,6},{6,5},{9,10},{10,9},{13,14},{14,13},{17,18},{18,... | collective-permute-start | bytes 2850824 | tf_op jit(solution)/shard_map/ppermute | solution.py:736
  12.7 7.9 %copy-start = (f32[8,4,8,256]{3,2,1,0:T(8,128)}, f32[8,4,8,256]{3,2,1,0:T(8,128)S(1)}, u32[]{:S(2)}) copy-start(f32[8,4,8,256]{3,2,1,0:T(8,128)S(1)} %collective-permute-done.2.refs_0_.rest_0_) | copy-start | bytes 786436
  13.7 1.5 %collective-permute-start.4 = (f32[40,256]{1,0:T(8,128)S(1)}, f32[40,256]{1,0:T(8,128)S(1)}, u32[]{:S(2)}, u32[]{:S(2)}) collective-permute-start(f32[40,256]{1,0:T(8,128)S(1)} %pad_maximum_fusion.1), channel_id=1, source_target_pairs={{0,4},{8,12},{4,0},{12,8},{1,5},{9,13},{5,1},{13,9},{2,6},{10,14},... | collective-permute-start | bytes 122888 | tf_op jit(solution)/shard_map/ppermute | solution.py:736
  14.5 0.7 collective-permute-start.3
  15.3 5.4 %copy-start.1 = (f32[40,256]{1,0:T(8,128)}, f32[40,256]{1,0:T(8,128)S(1)}, u32[]{:S(2)}) copy-start(f32[40,256]{1,0:T(8,128)S(1)} %get-tuple-element.36.rest_2_) | copy-start | bytes 122884
  15.3 5.4 %copy-start.2 = (f32[40,256]{1,0:T(8,128)}, f32[40,256]{1,0:T(8,128)S(1)}, u32[]{:S(2)}) copy-start(f32[40,256]{1,0:T(8,128)S(1)} %get-tuple-element.37.rest_1_) | copy-start | bytes 122884
  15.3 12.8 %collective-permute-start.6 = (f32[128,256]{1,0:T(8,128)S(1)}, f32[128,256]{1,0:T(8,128)S(1)}, u32[]{:S(2)}, u32[]{:S(2)}) collective-permute-start(f32[128,256]{1,0:T(8,128)S(1)} %get-tuple-element.30), channel_id=1, source_target_pairs={{1,2},{2,1},{5,6},{6,5},{9,10},{10,9},{13,14},{14,13},{17,18},{18,... | collective-permute-start | bytes 393224 | tf_op jit(solution)/shard_map/ppermute | solution.py:736
  16.0 15.8 %collective-permute-start.5 = (f32[128,256]{1,0:T(8,128)S(1)}, f32[128,256]{1,0:T(8,128)S(1)}, u32[]{:S(2)}, u32[]{:S(2)}) collective-permute-start(f32[128,256]{1,0:T(8,128)S(1)} %get-tuple-element.31), channel_id=1, source_target_pairs={{0,1},{2,3},{1,0},{3,2},{4,5},{6,7},{5,4},{7,6},{8,9},{10,11},{9,8... | collective-permute-start | bytes 393224 | tf_op jit(solution)/shard_map/ppermute | solution.py:736

commit v16 on v15

--- a/solution.py
+++ b/solution.py
@@ -676,7 +676,7 @@
             def write(i, p, value):
                 first[2 * i + l, z, 8 * p : 8 * p + 8, :] = value
 
-            apply_rows(table, 5, read, write)
+            apply_rows(table, 4, read, write)
         plane_copy(first, first_hbm, saves, z).start()
 
     def both(z):
@@ -749,7 +749,8 @@
     fields = (rhs, coef_z, coef_x, coef_y, diag_term)
 
     place = at_x.astype(jnp.int32).reshape(1)
-    odd_z, odd_y = ((lax.axis_index(axis) & 1).astype(jnp.int32).reshape(1) for axis in ("gz", "gy"))
+    odd_z = ((lax.axis_index("gz") + 1) & 1).astype(jnp.int32).reshape(1)
+    odd_y = (lax.axis_index("gy") & 1).astype(jnp.int32).reshape(1)
     face_shape = shape(FACE, NX, NY)
     x_shape = shape(FIELDS, NZ // 2, 8, NY)
     z_one, z_two, *xmsgs = pl.pallas_call(
@@ -767,7 +768,7 @@
         compiler_params=params(LIMIT),
         cost_estimate=cost(2.5),
     )(place, odd_z, *fields)
-    face_one, face_two = swap_pairs(z_one, "gz", 0), swap_pairs(z_two, "gz", 1)
+    face_one, face_two = swap_pairs(z_one, "gz", 1), swap_pairs(z_two, "gz", 0)
     if swap:
         x_parts = (lax.ppermute(xmsgs[0], "gx", [(0, 1), (1, 0)]),)
     else:
@@ -802,8 +803,8 @@
         return jnp.concatenate(rows + [jnp.concatenate([yup[:, lanes], ydn[:, lanes]], 1)], 0)
 
     low, high = rim(0), rim(1)
-    rim_one = swap_pairs(jnp.where(odd_z == 1, low, high), "gz", 0)
-    rim_two = swap_pairs(jnp.where(odd_z == 1, high, low), "gz", 1)
+    rim_one = swap_pairs(jnp.where(odd_z == 1, low, high), "gz", 1)
+    rim_two = swap_pairs(jnp.where(odd_z == 1, high, low), "gz", 0)
 
     inner_shape = shape(sum(GROUPS[:-1]), NZ, EROWS, 128)
     inner_faces_shape = shape(7, NZ - 2, LT, ROWS, 128)

time: 87.7 us -> 87.1 us (level)
  waiting for transfers between devices: 4.24 us -> 9.58 us
  blocking collectives: 23.2 us -> 19.5 us
  starting transfers between devices: 12.2 us -> 9.99 us
    ppermute x6, waiting for transfers between devices: 3.66 us -> 9.57 us  [swap_pairs(): return lax.ppermute(value, axis, pairs + [(j, i) for i, j in pairs])]
    all_to_all x2, blocking collectives: 23.2 us -> 19.5 us  [exchange(): return lax.all_to_all(messages, AXES, 0, 0, tiled=True)]
    ppermute x6, starting transfers between devices: 9.21 us -> 6.96 us  [swap_pairs(): return lax.ppermute(value, axis, pairs + [(j, i) for i, j in pairs])]
  transfers between devices with their start and end apart: 7 -> 7, of which waited for: 2 -> 1; matrix products, arithmetic and copies ran while one was open for 2% -> 2% of each run, Pallas kernels for 12% -> 12%
where the time goes in v16:
time: 87.1 us; the launch traced here: 86.6 us
  Pallas kernels  45.1 us (52%)
  blocking collectives  19.5 us (22%)
  starting transfers between devices  9.99 us (11%)
  waiting for transfers between devices  9.58 us (11%)
  other arithmetic  1.56 us (2%)
    all_to_all x2, blocking collectives, exchange(): return lax.all_to_all(messages, AXES, 0, 0, tiled=True)  19.5 us
    pallas_call x1, Pallas kernels, body(): pl.pallas_call(functools.partial(krylov_outer, swap), out_shape=(block, s...  15.6 us
    ppermute x6, waiting for transfers between devices, swap_pairs(): return lax.ppermute(value, axis, pairs + [(j, i) for i, j in pairs])  9.57 us
    pallas_call x1, Pallas kernels, body(): pl.pallas_call(functools.partial(first_pass, cells), out_shape=(block, sh...  9.38 us
    pallas_call x1, Pallas kernels, body(): pl.pallas_call(functools.partial(krylov_inner, swap), out_shape=(inner_sh...  7.42 us
    pallas_call x1, Pallas kernels, body(): pl.pallas_call(functools.partial(second_pass, cells), out_shape=(shape(CO...  7.28 us
    ppermute x6, starting transfers between devices, swap_pairs(): return lax.ppermute(value, axis, pairs + [(j, i) for i, j in pairs])  6.96 us
    ppermute x1, starting transfers between devices, body(): x_parts = (lax.ppermute(xmsgs[0], 'gx', [(0, 1), (1, 0)]),)  3.03 us
  transfers between devices with their start and end apart: 7, of which 1 were waited for; matrix products, arithmetic and copies ran while one was open for 2% of the time, Pallas kernels for 12%

profile of v16, /device:TPU:0, one launch (start us, length us, event | category | flops | bytes accessed | tf_op | source)
XLA Modules:
  0.0 86.6 jit_solution(12849950104800576525)
XLA Ops:
  0.6 2.6 %shard_map.68 = (f32[29,32,256]{2,1,0:T(8,128)}, f32[29,32,256]{2,1,0:T(8,128)}, f32[8,4,8,256]{3,2,1,0:T(8,128)}) custom-call(s32[1]{0:T(128)} %bitcast.place, s32[1]{0:T(128)} %bitcast.1.odd_z, f32[4,8,32,256]{3,2,1,0:T(8,128)} %rhs.5, f32[8,32,256]{2,1,0:T(8,128)} %cz.5, f32[8,32,256]{2,1,0:T(8,128)} %cx.5, f32[8,32,256]{2,1,0:T(8,128)} %cy.5, ...), custom_call_target="tpu_custom_call" | custom-call | bytes 9000000 | tf_op jit(solution)/shard_map/pallas_call | solution.py:756
  3.2 3.0 %collective-permute-start.2 = (f32[8,4,8,256]{3,2,1,0:T(8,128)}, f32[8,4,8,256]{3,2,1,0:T(8,128)S(1)}, u32[]{:S(2)}, u32[]{:S(2)}) collective-permute-start(f32[8,4,8,256]{3,2,1,0:T(8,128)} %get-tuple-element.18), channel_id=1, source_target_pairs={{0,16},{16,0},{1,17},{17,1},{2,18},{18,2},{3,19},{19,3},{4,20},{20... | collective-permute-start | bytes 786440 | tf_op jit(solution)/shard_map/ppermute | solution.py:773
  6.2 1.6 %collective-permute-start = (f32[29,32,256]{2,1,0:T(8,128)}, f32[29,32,256]{2,1,0:T(8,128)}, u32[]{:S(2)}, u32[]{:S(2)}) collective-permute-start(f32[29,32,256]{2,1,0:T(8,128)} %get-tuple-element.16), channel_id=1, source_target_pairs={{1,2},{2,1},{5,6},{6,5},{9,10},{10,9},{13,14},{14,13},{17,18},{18,... | collective-permute-start | bytes 2850824 | tf_op jit(solution)/shard_map/ppermute | solution.py:736
  7.8 3.5 %collective-permute-start.1 = (f32[29,32,256]{2,1,0:T(8,128)}, f32[29,32,256]{2,1,0:T(8,128)}, u32[]{:S(2)}, u32[]{:S(2)}) collective-permute-start(f32[29,32,256]{2,1,0:T(8,128)} %get-tuple-element.17), channel_id=1, source_target_pairs={{0,1},{2,3},{1,0},{3,2},{4,5},{6,7},{5,4},{7,6},{8,9},{10,11},{9,8... | collective-permute-start | bytes 2850824 | tf_op jit(solution)/shard_map/ppermute | solution.py:736
  11.4 2.7 %shard_map.69 = (f32[32,256]{1,0:T(8,128)}, f32[32,256]{1,0:T(8,128)}) custom-call(s32[1]{0:T(128)} %bitcast.2.odd_y, f32[4,8,32,256]{3,2,1,0:T(8,128)} %rhs.5, f32[8,32,256]{2,1,0:T(8,128)} %cz.5, f32[8,32,256]{2,1,0:T(8,128)} %cx.5, f32[8,32,256]{2,1,0:T(8,128)} %cy.5, f32[8,32,256]{2,1,0:T(8,128)} %dg.5), custom_call_target="tpu_custom_call" | custom-call | bytes 9000000 | tf_op jit(solution)/shard_map/pallas_call | solution.py:778
  14.1 0.0 collective-permute-done.2.refs_0_.rest_0_
  14.1 0.0 copy-start
  14.1 0.2 shard_map.70
  14.3 0.8 pad_maximum_fusion.1
  15.1 0.0 collective-permute-start.4
  15.1 0.8 pad_maximum_fusion
  15.8 0.7 collective-permute-start.3
  16.6 0.0 collective-permute-done.4
  16.6 0.0 collective-permute-done.3
  16.6 0.0 copy-start.1
  16.6 0.0 copy-start.2
  16.7 0.5 collective-permute-start.6
  17.2 0.7 collective-permute-start.5
  17.9 0.0 copy-done
  17.9 0.0 copy-done.1
  17.9 0.0 copy-done.2
  17.9 7.4 %shard_map.71 = (f32[48,8,56,128]{3,2,1,0:T(8,128)}, f32[7,6,3,40,128]{4,3,2,1,0:T(8,128)}) custom-call(s32[1]{0:T(128)} %bitcast.place, f32[4,8,32,256]{3,2,1,0:T(8,128)} %rhs.5, f32[8,32,256]{2,1,0:T(8,128)} %cz.5, f32[8,32,256]{2,1,0:T(8,128)} %cx.5, f32[8,32,256]{2,1,0:T(8,128)} %cy.5, f32[8,32,256]{2,1,0:T(8,128)} %dg.5, f32[8,4,8,256]{3,2,1,0:T(8,128)} %copy-done, ...), custom_call_target="tpu_custom_call" | custom-call | bytes 25200000 | tf_op jit(solution)/shard_map/pallas_call | solution.py:811
  25.3 9.6 %collective-permute-done.6.rim_two = f32[128,256]{1,0:T(8,128)S(1)} collective-permute-done((f32[128,256]{1,0:T(8,128)S(1)}, f32[128,256]{1,0:T(8,128)S(1)}, u32[]{:S(2)}, u32[]{:S(2)}) %collective-permute-start.6) | collective-permute-done | bytes 131104 | tf_op jit(solution)/shard_map/ppermute | solution.py:736
  34.9 0.0 collective-permute-done.5.rim_one
  34.9 0.0 collective-permute-done.face_one
  34.9 0.0 collective-permute-done.1.face_two
  34.9 15.6 %shard_map.72 = (f32[40,8,32,128]{3,2,1,0:T(8,128)}, f32[32,2,128]{2,1,0:T(2,128)S(1)}) custom-call(f32[29,32,256]{2,1,0:T(8,128)} %collective-permute-done.face_one, f32[29,32,256]{2,1,0:T(8,128)} %collective-permute-done.1.face_two, s32[1]{0:T(128)} %bitcast.place, s32[1]{0:T(128)} %bitcast.1.odd_z, f32[48,8,56,128]{3,2,1,0:T(8,128)} %get-tuple-element.23.inner, ...), custom_call_target="tpu_custom_call" | custom-call | bytes 54000000 | tf_op jit(solution)/shard_map/pallas_call | solution.py:827
  50.5 10.5 %all_to_all.10.message = f32[32,2,128]{2,1,0:T(2,128)S(1)} all-to-all(f32[32,2,128]{2,1,0:T(2,128)S(1)} %get-tuple-element.25), channel_id=1, replica_groups=mesh['gx'=2,'gy'=4,'gz'=4] {'gx','gy','gz'}, dimensions={0} | all-to-all | bytes 65536 | tf_op jit(solution)/shard_map/all_to_all | solution.py:740
  60.9 9.4 %shard_map.73 = (f32[40,8,32,128]{3,2,1,0:T(8,128)}, f32[32,2,128]{2,1,0:T(2,128)S(1)}, f32[24,128]{1,0:T(8,128)S(1)}) custom-call(f32[32,2,128]{2,1,0:T(2,128)S(1)} %all_to_all.10.message, f32[40,8,32,128]{3,2,1,0:T(8,128)} %get-tuple-element.26.basis_hbm), custom_call_target="tpu_custom_call" | custom-call | tf_op jit(solution)/shard_map/pallas_call | solution.py:846
  70.3 9.0 %all_to_all.11.message = f32[32,2,128]{2,1,0:T(2,128)S(1)} all-to-all(f32[32,2,128]{2,1,0:T(2,128)S(1)} %get-tuple-element.27), channel_id=1, replica_groups=mesh['gx'=2,'gy'=4,'gz'=4] {'gx','gy','gz'}, dimensions={0} | all-to-all | bytes 65536 | tf_op jit(solution)/shard_map/all_to_all | solution.py:740
  79.3 7.3 %shard_map.74 = (f32[20,8,32,256]{3,2,1,0:T(8,128)}, f32[20,20]{1,0:T(8,128)}) custom-call(f32[32,2,128]{2,1,0:T(2,128)S(1)} %all_to_all.11.message, f32[24,128]{1,0:T(8,128)S(1)} %get-tuple-element.28.factor_one, f32[40,8,32,128]{3,2,1,0:T(8,128)} %get-tuple-element.29.first_hbm), custom_call_target="tpu_custom_call" | custom-call | tf_op jit(solution)/shard_map/pallas_call | solution.py:863
  (7 shorter events, 0.1 us)
Async XLA Ops:
  3.2 10.9 %collective-permute-start.2 = (f32[8,4,8,256]{3,2,1,0:T(8,128)}, f32[8,4,8,256]{3,2,1,0:T(8,128)S(1)}, u32[]{:S(2)}, u32[]{:S(2)}) collective-permute-start(f32[8,4,8,256]{3,2,1,0:T(8,128)} %get-tuple-element.18), channel_id=1, source_target_pairs={{0,16},{16,0},{1,17},{17,1},{2,18},{18,2},{3,19},{19,3},{4,20},{20... | collective-permute-start | bytes 786440 | tf_op jit(solution)/shard_map/ppermute | solution.py:773
  6.2 28.6 %collective-permute-start = (f32[29,32,256]{2,1,0:T(8,128)}, f32[29,32,256]{2,1,0:T(8,128)}, u32[]{:S(2)}, u32[]{:S(2)}) collective-permute-start(f32[29,32,256]{2,1,0:T(8,128)} %get-tuple-element.16), channel_id=1, source_target_pairs={{1,2},{2,1},{5,6},{6,5},{9,10},{10,9},{13,14},{14,13},{17,18},{18,... | collective-permute-start | bytes 2850824 | tf_op jit(solution)/shard_map/ppermute | solution.py:736
  7.8 27.1 %collective-permute-start.1 = (f32[29,32,256]{2,1,0:T(8,128)}, f32[29,32,256]{2,1,0:T(8,128)}, u32[]{:S(2)}, u32[]{:S(2)}) collective-permute-start(f32[29,32,256]{2,1,0:T(8,128)} %get-tuple-element.17), channel_id=1, source_target_pairs={{0,1},{2,3},{1,0},{3,2},{4,5},{6,7},{5,4},{7,6},{8,9},{10,11},{9,8... | collective-permute-start | bytes 2850824 | tf_op jit(solution)/shard_map/ppermute | solution.py:736
  14.1 3.8 %copy-start = (f32[8,4,8,256]{3,2,1,0:T(8,128)}, f32[8,4,8,256]{3,2,1,0:T(8,128)S(1)}, u32[]{:S(2)}) copy-start(f32[8,4,8,256]{3,2,1,0:T(8,128)S(1)} %collective-permute-done.2.refs_0_.rest_0_) | copy-start | bytes 786436
  15.1 1.5 %collective-permute-start.4 = (f32[40,256]{1,0:T(8,128)S(1)}, f32[40,256]{1,0:T(8,128)S(1)}, u32[]{:S(2)}, u32[]{:S(2)}) collective-permute-start(f32[40,256]{1,0:T(8,128)S(1)} %pad_maximum_fusion.1), channel_id=1, source_target_pairs={{0,4},{8,12},{4,0},{12,8},{1,5},{9,13},{5,1},{13,9},{2,6},{10,14},... | collective-permute-start | bytes 122888 | tf_op jit(solution)/shard_map/ppermute | solution.py:736
  15.8 0.7 collective-permute-start.3
  16.6 1.3 %copy-start.1 = (f32[40,256]{1,0:T(8,128)}, f32[40,256]{1,0:T(8,128)S(1)}, u32[]{:S(2)}) copy-start(f32[40,256]{1,0:T(8,128)S(1)} %get-tuple-element.36.rest_2_) | copy-start | bytes 122884
  16.6 1.3 %copy-start.2 = (f32[40,256]{1,0:T(8,128)}, f32[40,256]{1,0:T(8,128)S(1)}, u32[]{:S(2)}) copy-start(f32[40,256]{1,0:T(8,128)S(1)} %get-tuple-element.37.rest_1_) | copy-start | bytes 122884
  16.7 18.2 %collective-permute-start.6 = (f32[128,256]{1,0:T(8,128)S(1)}, f32[128,256]{1,0:T(8,128)S(1)}, u32[]{:S(2)}, u32[]{:S(2)}) collective-permute-start(f32[128,256]{1,0:T(8,128)S(1)} %get-tuple-element.30), channel_id=1, source_target_pairs={{0,1},{2,3},{1,0},{3,2},{4,5},{6,7},{5,4},{7,6},{8,9},{10,11},{9,8... | collective-permute-start | bytes 393224 | tf_op jit(solution)/shard_map/ppermute | solution.py:736
  17.2 17.7 %collective-permute-start.5 = (f32[128,256]{1,0:T(8,128)S(1)}, f32[128,256]{1,0:T(8,128)S(1)}, u32[]{:S(2)}, u32[]{:S(2)}) collective-permute-start(f32[128,256]{1,0:T(8,128)S(1)} %get-tuple-element.31), channel_id=1, source_target_pairs={{1,2},{2,1},{5,6},{6,5},{9,10},{10,9},{13,14},{14,13},{17,18},{18,... | collective-permute-start | bytes 393224 | tf_op jit(solution)/shard_map/ppermute | solution.py:736
